TPU v7x, 32 devices: a whole 2x2x4 slice. The times are simulated.
32 devices in a mesh: group: 8 (over z, y), head: 4 (over x, core).
Axes of the slice: x: 2, y: 2, z: 4, core: 2. Of those that a mesh axis runs over, the one named last changes fastest.
Arguments:
- tokens: bfloat16 [4, 1024, 1536], P(None, 'group'), may hold values from -6 to 6
- parents: int32 [3, 1024], P(None, 'group'), may hold values from 0 to 7
- page_request: int32 [384], P('group'), may hold values from 0 to 127, as said below
- page_fill: int32 [384], P('group'), may hold values from 1 to 128, as said below
- keys_pool: bfloat16 [384, 1536, 128], P('group', 'head'), may hold values from -600 to 600
- values_pool: bfloat16 [384, 1536, 128], P('group', 'head'), may hold values from -6 to 6
- decay_pool: bfloat16 [384, 24, 128], P('group', 'head'), may hold values from -494.52 to 0
- gain_attn: float32 [1536], replicated, may hold values from 0.1 to 1.9
- w_query: bfloat16 [1536, 1536], P('head'), may hold values from -0.15625 to 0.15625
- w_key: bfloat16 [1536, 1536], P('head'), may hold values from -0.15625 to 0.15625
- w_value: bfloat16 [1536, 1536], P('head'), may hold values from -0.15625 to 0.15625
- w_forget: bfloat16 [1536, 24], P(None, 'head'), may hold values from -0.15625 to 0.15625
- forget_bias: float32 [24], P('head'), may hold values from -2 to 6
- w_out: bfloat16 [1536, 1536], P('head'), may hold values from -0.15625 to 0.15625
- gain_ffn: float32 [1536], replicated, may hold values from 0.1 to 1.9
- w_gate: bfloat16 [1536, 4096], P(None, 'head'), may hold values from -0.15625 to 0.15625
- w_up: bfloat16 [1536, 4096], P(None, 'head'), may hold values from -0.15625 to 0.15625
- w_down: bfloat16 [4096, 1536], P('head'), may hold values from -0.09375 to 0.09375
Outputs:
- outputs: bfloat16 [4, 1024, 1536], P(None, 'group')
Inputs may be any that keep to these rules, and one draw needn't show every extreme that they name: `page_request`: request ids g * 16 to g * 16 + 15 are the requests owned by group g, and pages g * 48 to g * 48 + 47 are the page slots of group g. The first 32 slots of a group hold pages of its own requests; its other 16 slots hold pages of other groups' requests, at most 3 from the requests of one group. Every request has at least one page. `page_fill`: the valid positions of a page are its first ones.
All inputs are finite; a program needn't handle non-finite values.
Results may differ from a plain program's by a relative error of at most 0.0095.
Values may be sent and summed in bfloat16 or wider, within the bound.
No kernel may reach another device: no remote copies, remote signals or barrier semaphores. Data moves between devices by JAX's collectives and lax.ppermute only.
A program may use at most 192 MiB of HBM per device.

v0:
```python
import jax
import jax.numpy as jnp
from jax import lax
from jax.sharding import PartitionSpec as P

BEAMS = 8
OWNED_SLOTS = 32
SPILL = 16


epsilon = 1e-05
masked_score = -1e30


def rms_scale(values, gain_vector):
    widened = values.astype(jnp.float32)
    return (
        widened
        * lax.rsqrt(jnp.mean(widened * widened, axis=-1, keepdims=True) + epsilon)
        * gain_vector
    )


def page_partials(page_keys, page_values, page_decay, fill_count, asked_rows, head_count):
    page_count, inner_width, length = page_keys.shape
    head_size = inner_width // head_count
    keys_split = page_keys.reshape(page_count, head_count, head_size, length)
    values_split = page_values.reshape(page_count, head_count, head_size, length)
    asked_split = asked_rows.reshape(asked_rows.shape[:3] + (head_count, head_size))
    scores = jnp.einsum(
        "pbshd,phdt->pbsht", asked_split, keys_split, preferred_element_type=jnp.float32
    ) * head_size ** (-0.5)
    scores = scores + page_decay.astype(jnp.float32)[:, None, None, :, :]
    valid_mask = jnp.arange(length)[None, :] < fill_count[:, None]
    scores = jnp.where(valid_mask[:, None, None, None, :], scores, masked_score)
    page_top = jnp.max(scores, axis=-1)
    weights = jnp.exp(scores - page_top[..., None])
    page_total = jnp.sum(weights, axis=-1)
    numerator = jnp.einsum(
        "pbsht,phdt->pbshd",
        weights.astype(jnp.bfloat16),
        values_split,
        preferred_element_type=jnp.float32,
    )
    return (page_top, page_total, numerator.reshape(numerator.shape[:3] + (inner_width,)))


def by_request(current_request, page_top, page_total, numerator, request_count, head_count):
    matches = current_request[None, :] == jnp.arange(request_count)[:, None]
    wide_match = matches[:, :, None, None, None]
    best_top = jnp.max(jnp.where(wide_match, page_top[None], masked_score), axis=1)
    factor = jnp.where(wide_match, jnp.exp(page_top[None] - best_top[:, None]), 0.0)
    summed = jnp.sum(factor * page_total[None], axis=1)
    numer_split = numerator.reshape(numerator.shape[:3] + (head_count, -1))
    combined = jnp.sum(factor[..., None] * numer_split[None], axis=1)
    return (best_top, summed, combined.reshape(combined.shape[:3] + (-1,)))


def shards(
    tokens,
    parents,
    page_request,
    page_fill,
    keys_pool,
    values_pool,
    decay_pool,
    gain_attn,
    w_query,
    w_key,
    w_value,
    w_forget,
    forget_bias,
    w_out,
    gain_ffn,
    w_gate,
    w_up,
    w_down,
):
    step_count, row_count, model_width = tokens.shape
    head_count = w_forget.shape[1]
    inner_width = w_query.shape[0]
    head_size = inner_width // head_count
    local_count = row_count // BEAMS
    groups = lax.axis_size("group")
    own_group = lax.axis_index("group")
    capacity = (SPILL + groups - 2) // (groups - 1)
    flat_tokens = tokens.reshape(step_count * row_count, model_width)
    normed = rms_scale(flat_tokens, gain_attn).astype(jnp.bfloat16)

    def project(weight):
        product = lax.dot_general(
            normed, weight, (((1,), (1,)), ((), ())), preferred_element_type=jnp.float32
        )
        return product.astype(jnp.bfloat16).reshape(step_count, row_count, -1)

    queries = project(w_query)
    key_new = project(w_key)
    value_new = project(w_value)
    forget = jax.nn.log_sigmoid(
        jnp.dot(normed, w_forget, preferred_element_type=jnp.float32) + forget_bias
    ).reshape(step_count, row_count, head_count)
    by_row = queries.transpose(1, 0, 2)
    by_request_rows = by_row.reshape(local_count, BEAMS, step_count, inner_width)
    own_request = page_request[:OWNED_SLOTS] - own_group * local_count
    own_parts = page_partials(
        keys_pool[:OWNED_SLOTS],
        values_pool[:OWNED_SLOTS],
        decay_pool[:OWNED_SLOTS],
        page_fill[:OWNED_SLOTS],
        by_request_rows[own_request],
        head_count,
    )
    hosted_request = page_request[OWNED_SLOTS:]
    hosted_owner = hosted_request // local_count
    hosted_local = hosted_request % local_count
    hosted_index = jnp.arange(hosted_request.shape[0])
    earlier = (hosted_owner[:, None] == hosted_owner[None, :]) & (
        hosted_index[None, :] < hosted_index[:, None]
    )
    hosted_rank = jnp.sum(earlier, axis=1)
    slot_match = (hosted_owner[None, None, :] == jnp.arange(groups)[:, None, None]) & (
        hosted_rank[None, None, :] == jnp.arange(capacity)[None, :, None]
    )
    slot_full = jnp.any(slot_match, axis=2)
    slot_source = jnp.sum(jnp.where(slot_match, hosted_index[None, None, :], 0), axis=2)
    slot_local = jnp.sum(jnp.where(slot_match, hosted_local[None, None, :], 0), axis=2)
    slot_count = groups * capacity
    base_rows = jnp.arange(row_count) // BEAMS * BEAMS
    hist_keys = jnp.zeros((0, row_count, inner_width), jnp.bfloat16)
    hist_values = jnp.zeros((0, row_count, inner_width), jnp.bfloat16)
    hist_totals = jnp.zeros((0, row_count, head_count), jnp.float32)
    running = jnp.zeros((row_count, head_count), jnp.float32)
    finished = []
    for step_index in range(step_count):
        query_block = by_row[:, step_index : step_index + 1]
        step_span = query_block.shape[1]
        gathered = lax.all_gather(query_block, "group", axis=0, tiled=True)
        asked_rows = gathered.reshape(groups * local_count, BEAMS, step_span, inner_width)[
            hosted_request
        ]
        page_top, page_total, numerator = page_partials(
            keys_pool[OWNED_SLOTS:],
            values_pool[OWNED_SLOTS:],
            decay_pool[OWNED_SLOTS:],
            page_fill[OWNED_SLOTS:],
            asked_rows,
            head_count,
        )
        full_slot = slot_full[:, :, None, None, None]
        own_now = tuple((member[:, :, step_index : step_index + 1] for member in own_parts))
        all_request = jnp.concatenate(
            [
                own_request,
                lax.all_to_all(
                    slot_local.astype(jnp.float32), "group", split_axis=0, concat_axis=0, tiled=True
                )
                .reshape(slot_count)
                .astype(jnp.int32),
            ],
            axis=0,
        )
        all_top = jnp.concatenate(
            [
                own_now[0],
                lax.all_to_all(
                    jnp.where(full_slot, page_top[slot_source], masked_score),
                    "group",
                    split_axis=0,
                    concat_axis=0,
                    tiled=True,
                ).reshape((slot_count,) + page_top.shape[1:]),
            ],
            axis=0,
        )
        all_total = jnp.concatenate(
            [
                own_now[1],
                lax.all_to_all(
                    jnp.where(full_slot, page_total[slot_source], 0.0),
                    "group",
                    split_axis=0,
                    concat_axis=0,
                    tiled=True,
                ).reshape((slot_count,) + page_total.shape[1:]),
            ],
            axis=0,
        )
        all_numer = jnp.concatenate(
            [
                own_now[2],
                lax.all_to_all(
                    jnp.where(full_slot, numerator[slot_source], 0.0),
                    "group",
                    split_axis=0,
                    concat_axis=0,
                    tiled=True,
                ).reshape((slot_count,) + numerator.shape[1:]),
            ],
            axis=0,
        )
        page_top, page_total, page_numer = by_request(
            all_request, all_top, all_total, all_numer, local_count, head_count
        )
        page_top = page_top.reshape(row_count, head_count)
        page_total = page_total.reshape(row_count, head_count)
        page_numer = page_numer.reshape(row_count, head_count, head_size)
        if step_index > 0:
            source = base_rows + parents[step_index - 1]
            hist_keys = hist_keys[:, source]
            hist_values = hist_values[:, source]
            hist_totals = hist_totals[:, source]
            running = running[source]
        running = running + forget[step_index]
        hist_keys = jnp.concatenate([hist_keys, key_new[step_index][None]], axis=0)
        hist_values = jnp.concatenate([hist_values, value_new[step_index][None]], axis=0)
        hist_totals = jnp.concatenate([hist_totals, running[None]], axis=0)
        asked_now = queries[step_index].reshape(row_count, head_count, head_size)
        keys_now = hist_keys.reshape(step_index + 1, row_count, head_count, head_size)
        values_now = hist_values.reshape(step_index + 1, row_count, head_count, head_size)
        scores = jnp.einsum(
            "rhd,urhd->rhu", asked_now, keys_now, preferred_element_type=jnp.float32
        ) * head_size ** (-0.5) - hist_totals.transpose(1, 2, 0)
        history_top = jnp.max(scores, axis=-1)
        weights = jnp.exp(scores - history_top[..., None])
        history_total = jnp.sum(weights, axis=-1)
        history_numer = jnp.einsum(
            "rhu,urhd->rhd",
            weights.astype(jnp.bfloat16),
            values_now,
            preferred_element_type=jnp.float32,
        )
        best_top = jnp.maximum(page_top, history_top)
        page_scale = jnp.exp(page_top - best_top)
        history_scale = jnp.exp(history_top - best_top)
        total_sum = page_total * page_scale + history_total * history_scale
        numer_sum = page_numer * page_scale[..., None] + history_numer * history_scale[..., None]
        attended = (
            (numer_sum / total_sum[..., None]).astype(jnp.bfloat16).reshape(row_count, inner_width)
        )
        mixed_sum = lax.psum(jnp.dot(attended, w_out, preferred_element_type=jnp.float32), "head")
        residual = tokens[step_index].astype(jnp.float32) + mixed_sum
        normed_ffn = rms_scale(residual, gain_ffn).astype(jnp.bfloat16)
        gate_proj = jnp.dot(normed_ffn, w_gate, preferred_element_type=jnp.float32)
        up_proj = jnp.dot(normed_ffn, w_up, preferred_element_type=jnp.float32)
        hidden = (jax.nn.silu(gate_proj) * up_proj).astype(jnp.bfloat16)
        down_sum = lax.psum(jnp.dot(hidden, w_down, preferred_element_type=jnp.float32), "head")
        finished.append((residual + down_sum).astype(jnp.bfloat16))
    result = jnp.stack(finished, axis=0)
    return result


def solution(mesh):
    return jax.shard_map(
        shards,
        mesh=mesh,
        in_specs=(
            P(None, "group", None),
            P(None, "group"),
            P("group"),
            P("group"),
            P("group", "head", None),
            P("group", "head", None),
            P("group", "head", None),
            P(),
            P("head", None),
            P("head", None),
            P("head", None),
            P(None, "head"),
            P("head"),
            P("head", None),
            P(),
            P(None, "head"),
            P(None, "head"),
            P("head", None),
        ),
        out_specs=P(None, "group", None),
        check_vma=False,
    )
```

profile of v0, /device:TPU:0, one launch (start us, length us, event | category | flops | bytes accessed | tf_op | source)
XLA Modules:
  0.0 889.7 jit_solution(15058536475737486428)
XLA Ops:
  8.5 7.3 all-to-all-start
  31.2 34.6 %all_gather.15 = bf16[1024,1,384]{2,0,1:T(8,128)(2,1)} all-gather(bf16[128,1,384]{2,0,1:T(8,128)(2,1)S(1)} %get-tuple-element.84), channel_id=1, replica_groups=mesh['group'=8,'head'=4] {'group'}, dimensions={0}, use_global_device_ids=true | all-gather | bytes 884736 | tf_op jit(solution)/shard_map/all_gather | solution.py:137
  76.1 34.0 %all_gather.12 = bf16[1024,1,384]{2,0,1:T(8,128)(2,1)} all-gather(bf16[128,1,384]{2,0,1:T(8,128)(2,1)S(1)} %copy-done.37), channel_id=1, replica_groups=mesh['group'=8,'head'=4] {'group'}, dimensions={0}, use_global_device_ids=true | all-gather | bytes 884736 | tf_op jit(solution)/shard_map/all_gather | solution.py:137
  120.4 34.0 %all_gather.13 = bf16[1024,1,384]{2,0,1:T(8,128)(2,1)} all-gather(bf16[128,1,384]{2,0,1:T(8,128)(2,1)S(1)} %copy-done.36), channel_id=1, replica_groups=mesh['group'=8,'head'=4] {'group'}, dimensions={0}, use_global_device_ids=true | all-gather | bytes 884736 | tf_op jit(solution)/shard_map/all_gather | solution.py:137
  168.7 34.9 %all_gather.14 = bf16[1024,1,384]{2,0,1:T(8,128)(2,1)} all-gather(bf16[128,1,384]{2,0,1:T(8,128)(2,1)} %get-tuple-element.85), channel_id=1, replica_groups=mesh['group'=8,'head'=4] {'group'}, dimensions={0}, use_global_device_ids=true | all-gather | bytes 884736 | tf_op jit(solution)/shard_map/all_gather | solution.py:137
  266.0 4.8 copy.717
  270.8 4.6 reshape.1017
  397.1 6.1 all-to-all-start.1
  412.5 6.0 all-to-all-start.3
  425.8 6.0 all-to-all-start.4
  482.4 6.0 all-to-all-start.7
  489.8 5.1 all-to-all-done.7
  500.1 5.2 all-to-all-done.10
  505.3 3.9 all-to-all-start.12
  534.1 5.9 all-to-all-start.6
  550.8 6.0 all-to-all-start.9
  576.1 6.0 all-to-all-start.2
  609.6 7.3 exponential_select_fusion.1
  616.9 6.0 all-to-all-start.5
  631.5 5.6 all-to-all-start.11
  642.1 6.8 multiply_reduce_fusion.3
  648.9 7.6 multiply_reduce_fusion.2
  663.3 6.0 all-to-all-start.8
  674.0 6.8 multiply_reduce_fusion
  694.7 6.8 multiply_reduce_fusion.1
  706.4 70.2 %all-reduce.7.cloned.1.call-done = (f32[128,1536]{1,0:T(8,128)}, f32[128,1536]{1,0:T(8,128)}, f32[128,1536]{1,0:T(8,128)}, f32[128,1536]{1,0:T(8,128)}) async-done(((f32[128,1536]{1,0:T(8,128)}, f32[128,1536]{1,0:T(8,128)}, f32[128,1536]{1,0:T(8,128)}, f32[128,1536]{1,0:T(8,128)}), (f32[128,1536]{1,0:T(8,128)}, f32[128,1536]{1,0:T(8,128)}, f32[128,1536]{1,0:T(8,128)}, ...) | async-done | bytes 3145744 | tf_op jit(solution)/shard_map/psum | solution.py:240
  785.2 4.1 fusion.33
  789.2 4.1 fusion.34
  796.7 4.0 fusion.35
  804.0 4.0 fusion.36
  808.1 69.2 %all-reduce.5.cloned.1.call-done = (f32[128,1536]{1,0:T(8,128)}, f32[128,1536]{1,0:T(8,128)}, f32[128,1536]{1,0:T(8,128)}, f32[128,1536]{1,0:T(8,128)}) async-done(((f32[128,1536]{1,0:T(8,128)}, f32[128,1536]{1,0:T(8,128)}, f32[128,1536]{1,0:T(8,128)}, f32[128,1536]{1,0:T(8,128)}), (f32[128,1536]{1,0:T(8,128)}, f32[128,1536]{1,0:T(8,128)}, f32[128,1536]{1,0:T(8,128)}, ...) | async-done | bytes 3145744 | tf_op jit(solution)/shard_map/psum | solution.py:246
  877.3 4.1 fusion.58
  (468 shorter events, 452.4 us)
Async XLA Ops:
  6.5 778.7 %copy-start = (bf16[1024,1536]{1,0:T(8,128)(2,1)S(1)}, bf16[1024,1536]{1,0:T(8,128)(2,1)}, u32[]{:S(2)}) copy-start(bf16[1024,1536]{1,0:T(8,128)(2,1)} %param.35) | copy-start | bytes 9437188
  8.5 388.6 %all-to-all-start = ((f32[8,1,3]{2,1,0:T(1,128)}), f32[8,1,3]{2,1,0:T(1,128)}, u32[]{:S(2)}, u32[]{:S(2)}) async-start(f32[8,1,3]{2,1,0:T(1,128)} %copy.702), calls=%async_computation | async-start | bytes 8192 | tf_op jit(solution)/shard_map/all_to_all | solution.py:154
  211.0 15.9 %copy-start.68 = (pred[8,3]{0,1:T(4,128)(4,1)S(1)}, pred[8,3]{0,1:T(4,128)(4,1)}, u32[]{:S(2)}) copy-start(pred[8,3]{0,1:T(4,128)(4,1)} %and_reduce_fusion) | copy-start | bytes 76
  227.0 88.5 %copy-start.63 = (pred[8,3]{1,0:T(8,128)(4,1)}, pred[8,3]{1,0:T(8,128)(4,1)S(1)}, u32[]{:S(2)}) copy-start(pred[8,3]{1,0:T(8,128)(4,1)S(1)} %copy.707) | copy-start | bytes 76
  232.9 17.2 %copy-start.64 = (s32[48]{0:T(128)S(1)}, s32[48]{0:T(128)}, u32[]{:S(2)}) copy-start(s32[48]{0:T(128)} %param.20) | copy-start | bytes 580
  333.3 22.7 %copy-start.40 = (bf16[128,384]{0,1:T(8,128)(2,1)S(1)}, bf16[128,384]{0,1:T(8,128)(2,1)}, u32[]{:S(2)}) copy-start(bf16[128,384]{0,1:T(8,128)(2,1)} %get-tuple-element.63) | copy-start | bytes 294916
  351.0 28.7 %copy-start.17 = (bf16[128,2,384]{2,1,0:T(2,128)(2,1)}, bf16[128,2,384]{2,1,0:T(2,128)(2,1)S(1)}, u32[]{:S(2)}) copy-start(bf16[128,2,384]{2,1,0:T(2,128)(2,1)S(1)} %gather_fusion.18) | copy-start | bytes 589828
  358.0 26.0 %copy-start.26 = (f32[1,128,6]{2,0,1:T(1,128)}, f32[1,128,6]{2,0,1:T(1,128)S(1)}, u32[]{:S(2)}) copy-start(f32[1,128,6]{2,0,1:T(1,128)S(1)} %copy.776) | copy-start | bytes 9220
  390.3 14.7 %copy-start.18 = (bf16[128,2,384]{2,1,0:T(2,128)(2,1)S(1)}, bf16[128,2,384]{2,1,0:T(2,128)(2,1)}, u32[]{:S(2)}) copy-start(bf16[128,2,384]{2,1,0:T(2,128)(2,1)} %copy-done.17) | copy-start | bytes 589828
  390.3 41.5 %copy-start.30 = (bf16[128,384]{0,1:T(8,128)(2,1)S(1)}, bf16[128,384]{0,1:T(8,128)(2,1)}, u32[]{:S(2)}) copy-start(bf16[128,384]{0,1:T(8,128)(2,1)} %copy-done.29) | copy-start | bytes 294916
  392.2 41.2 %copy-start.34 = (f32[128,6]{1,0:T(8,128)S(1)}, f32[128,6]{1,0:T(8,128)}, u32[]{:S(2)}) copy-start(f32[128,6]{1,0:T(8,128)} %copy-done.33) | copy-start | bytes 9220
  397.1 15.3 %all-to-all-start.1 = ((f32[8,1,144]{2,1,0:T(1,128)}), f32[8,1,144]{2,1,0:T(1,128)S(1)}, u32[]{:S(2)}, u32[]{:S(2)}) async-start(f32[8,1,144]{2,1,0:T(1,128)} %reshape.1407), calls=%async_computation.1 | async-start | bytes 16384 | tf_op jit(solution)/shard_map/all_to_all | solution.py:165
  405.9 37.6 %copy-start.39 = (f32[32,8,1,6]{1,2,3,0:T(1,128)S(1)}, f32[32,8,1,6]{1,2,3,0:T(1,128)}, u32[]{:S(2)}) copy-start(f32[32,8,1,6]{1,2,3,0:T(1,128)} %get-tuple-element.81) | copy-start | bytes 18436
  405.9 40.8 %copy-start.38 = (f32[32,8,1,6]{1,2,3,0:T(1,128)S(1)}, f32[32,8,1,6]{1,2,3,0:T(1,128)}, u32[]{:S(2)}) copy-start(f32[32,8,1,6]{1,2,3,0:T(1,128)} %get-tuple-element.80) | copy-start | bytes 18436
  412.5 13.3 %all-to-all-start.3 = ((f32[8,1,144]{2,1,0:T(1,128)}), f32[8,1,144]{2,1,0:T(1,128)S(1)}, u32[]{:S(2)}, u32[]{:S(2)}) async-start(f32[8,1,144]{2,1,0:T(1,128)} %reshape.1409), calls=%async_computation.3 | async-start | bytes 16384 | tf_op jit(solution)/shard_map/all_to_all | solution.py:178
  425.8 21.6 %copy-start.47 = (f32[8,1,144]{2,1,0:T(1,128)}, f32[8,1,144]{2,1,0:T(1,128)S(1)}, u32[]{:S(2)}) copy-start(f32[8,1,144]{2,1,0:T(1,128)S(1)} %all-to-all-done.3) | copy-start | bytes 13828
  425.8 56.7 %all-to-all-start.4 = ((f32[8,1,144]{2,1,0:T(1,128)}), f32[8,1,144]{2,1,0:T(1,128)}, u32[]{:S(2)}, u32[]{:S(2)}) async-start(f32[8,1,144]{2,1,0:T(1,128)} %reshape.1411), calls=%async_computation.4 | async-start | bytes 16384 | tf_op jit(solution)/shard_map/all_to_all | solution.py:165
  447.3 31.3 %copy-start.19 = (f32[32,8,1,384]{3,1,2,0:T(8,128)S(1)}, f32[32,8,1,384]{3,1,2,0:T(8,128)}, u32[]{:S(2)}) copy-start(f32[32,8,1,384]{3,1,2,0:T(8,128)} %get-tuple-element.54) | copy-start | bytes 1179652
  482.4 12.5 %all-to-all-start.7 = ((f32[8,1,144]{2,1,0:T(1,128)}), f32[8,1,144]{2,1,0:T(1,128)}, u32[]{:S(2)}, u32[]{:S(2)}) async-start(f32[8,1,144]{2,1,0:T(1,128)} %reshape.1413), calls=%async_computation.7 | async-start | bytes 16384 | tf_op jit(solution)/shard_map/all_to_all | solution.py:165
  494.9 10.4 %all-to-all-start.10 = ((f32[8,1,144]{2,1,0:T(1,128)}), f32[8,1,144]{2,1,0:T(1,128)}, u32[]{:S(2)}, u32[]{:S(2)}) async-start(f32[8,1,144]{2,1,0:T(1,128)} %reshape.1415), calls=%async_computation.10 | async-start | bytes 16384 | tf_op jit(solution)/shard_map/all_to_all | solution.py:165
  505.3 28.8 %all-to-all-start.12 = ((f32[8,1,144]{2,1,0:T(1,128)}), f32[8,1,144]{2,1,0:T(1,128)}, u32[]{:S(2)}, u32[]{:S(2)}) async-start(f32[8,1,144]{2,1,0:T(1,128)} %reshape.1421), calls=%async_computation.12 | async-start | bytes 16384 | tf_op jit(solution)/shard_map/all_to_all | solution.py:178
  511.2 95.9 %copy-start.58 = (f32[128,6]{0,1:T(8,128)S(1)}, f32[128,6]{0,1:T(8,128)}, u32[]{:S(2)}) copy-start(f32[128,6]{0,1:T(8,128)} %get-tuple-element.88) | copy-start | bytes 9220
  511.2 97.2 %copy-start.45 = (f32[128,6]{0,1:T(8,128)S(1)}, f32[128,6]{0,1:T(8,128)}, u32[]{:S(2)}) copy-start(f32[128,6]{0,1:T(8,128)} %copy-done.44) | copy-start | bytes 9220
  534.1 16.7 %all-to-all-start.6 = ((f32[8,1,144]{2,1,0:T(1,128)}), f32[8,1,144]{2,1,0:T(1,128)}, u32[]{:S(2)}, u32[]{:S(2)}) async-start(f32[8,1,144]{2,1,0:T(1,128)} %reshape.1417), calls=%async_computation.6 | async-start | bytes 16384 | tf_op jit(solution)/shard_map/all_to_all | solution.py:178
  550.8 25.3 %all-to-all-start.9 = ((f32[8,1,144]{2,1,0:T(1,128)}), f32[8,1,144]{2,1,0:T(1,128)}, u32[]{:S(2)}, u32[]{:S(2)}) async-start(f32[8,1,144]{2,1,0:T(1,128)} %reshape.1419), calls=%async_computation.9 | async-start | bytes 16384 | tf_op jit(solution)/shard_map/all_to_all | solution.py:178
  576.1 40.8 %all-to-all-start.2 = ((f32[8,3,8,1,384]{4,2,1,3,0:T(8,128)}), f32[8,3,8,1,384]{4,2,1,3,0:T(8,128)}, u32[]{:S(2)}, u32[]{:S(2)}) async-start(f32[8,3,8,1,384]{4,2,1,3,0:T(8,128)} %get-tuple-element.103), calls=%async_computation.2 | async-start | bytes 589824 | tf_op jit(solution)/shard_map/all_to_all | solution.py:191
  616.9 14.6 %all-to-all-start.5 = ((f32[8,3,8,1,384]{4,2,1,3,0:T(8,128)}), f32[8,3,8,1,384]{4,2,1,3,0:T(8,128)}, u32[]{:S(2)}, u32[]{:S(2)}) async-start(f32[8,3,8,1,384]{4,2,1,3,0:T(8,128)} %get-tuple-element.101), calls=%async_computation.5 | async-start | bytes 589824 | tf_op jit(solution)/shard_map/all_to_all | solution.py:191
  631.5 31.8 %all-to-all-start.11 = ((f32[8,3,8,1,384]{4,2,1,3,0:T(8,128)}), f32[8,3,8,1,384]{4,2,1,3,0:T(8,128)}, u32[]{:S(2)}, u32[]{:S(2)}) async-start(f32[8,3,8,1,384]{4,2,1,3,0:T(8,128)} %get-tuple-element.102), calls=%async_computation.11 | async-start | bytes 589824 | tf_op jit(solution)/shard_map/all_to_all | solution.py:191
  663.3 26.8 %all-to-all-start.8 = ((f32[8,3,8,1,384]{4,2,1,3,0:T(8,128)}), f32[8,3,8,1,384]{4,2,1,3,0:T(8,128)}, u32[]{:S(2)}, u32[]{:S(2)}) async-start(f32[8,3,8,1,384]{4,2,1,3,0:T(8,128)} %get-tuple-element.100), calls=%async_computation.8 | async-start | bytes 589824 | tf_op jit(solution)/shard_map/all_to_all | solution.py:191
  669.3 107.3 %all-reduce.7.cloned.1.call-start = ((), (), s32[]{:S(2)}) async-start(), calls=%async_computation.14 | async-start | bytes 6291456 | tf_op jit(solution)/shard_map/psum | solution.py:240
  706.2 73.4 %copy-start.62 = (f32[1536]{0:T(1024)S(1)}, f32[1536]{0:T(1024)}, u32[]{:S(2)}) copy-start(f32[1536]{0:T(1024)} %param.32) | copy-start | bytes 18436
  706.2 171.1 %all-reduce.5.cloned.1.call-start = ((), (), s32[]{:S(2)}) async-start(), calls=%async_computation.13 | async-start | bytes 6291456 | tf_op jit(solution)/shard_map/psum | solution.py:246
  (55 other events, 262.6 us)
Sparse Core Ops, SparseCore 0:
  706.3 70.2 all-reduce.6
  808.2 69.0 all-reduce.4
where the time goes:
time: 905 us; the launch traced here: 890 us
  local copies, waits for them, and re-layouts  290 us (32%)
  other arithmetic  152 us (17%)
  waiting for transfers between devices  151 us (17%)
  blocking collectives  137 us (15%)
  starting transfers between devices  75 us (8%)
  matrix products  70 us (8%)
  between operations  14.5 us (2%)
    all_gather x4, blocking collectives, shards(): gathered = lax.all_gather(query_block, 'group', axis=0, tiled=True)  137 us
    psum x1, waiting for transfers between devices, shards(): lax.psum(jnp.dot(attended, w_out, preferred_element_type=jnp.float32), 'h...  70.2 us
    psum x1, waiting for transfers between devices, shards(): lax.psum(jnp.dot(hidden, w_down, preferred_element_type=jnp.float32), 'he...  69.2 us
    unnamed x161, local copies, waits for them, and re-layouts  31.9 us
    reduce_sum x4, other arithmetic, by_request(): combined = jnp.sum(factor[..., None] * numer_split[None], axis=1)  28 us
    unnamed x16, other arithmetic  27 us
    all_to_all x4, starting transfers between devices, shards(): lax.all_to_all(jnp.where(full_slot, numerator[slot_source], 0.0), 'group'...  23.6 us
    all_to_all x4, starting transfers between devices, shards(): lax.all_to_all(jnp.where(full_slot, page_top[slot_source], masked_score),...  22 us
  transfers between devices with their start and end apart: 15, of which 5 were waited for; matrix products, arithmetic and copies ran while one was open for 51% of the time, Pallas kernels for 0%

commit v1 on v0

v1 whole, which is shorter than its diff:
```python
import functools

import jax
import jax.numpy as jnp
from jax import lax
from jax.experimental import pallas as pl
from jax.experimental.pallas import tpu as pltpu
from jax.sharding import PartitionSpec as P

BEAMS = 8
OWNED_SLOTS = 32
SPILL = 16
PAGE_BLOCK = 4
TAIL_ROWS = 16
MIB = 1 << 20

epsilon = 1e-05
masked_score = -1e30
f32 = jnp.float32
bf16 = jnp.bfloat16

NN = (((1,), (0,)), ((), ()))
NT = (((1,), (1,)), ((), ()))
SMEM = pl.BlockSpec(memory_space=pltpu.SMEM)


def dot(a, b, dims=NN):
    return lax.dot_general(a, b, dims, preferred_element_type=f32)


def lanes(shape):
    return lax.broadcasted_iota(jnp.int32, shape, len(shape) - 1)


def sublanes(shape):
    return lax.broadcasted_iota(jnp.int32, shape, len(shape) - 2)


def route_kernel(local_count, capacity, request_ref, table_ref, slot_ref, count_ref):
    for owner in range(count_ref.shape[0]):
        count_ref[owner] = 0
    for slot in range(table_ref.shape[0]):
        table_ref[slot] = -1
    for page in range(SPILL):
        request = request_ref[OWNED_SLOTS + page]
        owner = request // local_count
        rank = count_ref[owner]
        slot = owner * capacity + rank
        table_ref[slot] = request - owner * local_count
        slot_ref[page] = slot
        count_ref[owner] = rank + 1


def route(page_request, groups, local_count, capacity):
    return pl.pallas_call(
        functools.partial(route_kernel, local_count, capacity),
        in_specs=[SMEM],
        out_specs=[SMEM, SMEM],
        out_shape=[
            jax.ShapeDtypeStruct((groups * capacity,), jnp.int32),
            jax.ShapeDtypeStruct((SPILL,), jnp.int32),
        ],
        scratch_shapes=[pltpu.SMEM((groups,), jnp.int32)],
        name="route",
    )(page_request)


def project_kernel(
    tokens_ref, gain_ref, wq_ref, wk_ref, wv_ref, wf_ref, bias_ref,
    q_ref, k_ref, v_ref, forget_ref, normed_ref,
):
    steps, rows, _ = tokens_ref.shape
    span = steps * BEAMS
    gain = gain_ref[...]

    def pair(index, carry):
        slabs = []
        for step in range(steps):
            x = tokens_ref[step, pl.ds(pl.multiple_of(index * 16, 16), 16), :].astype(f32)
            scale = lax.rsqrt(jnp.mean(x * x, axis=-1, keepdims=True) + epsilon)
            slabs.append(x * scale * gain)
        for half in range(2):
            part = jnp.concatenate([s[half * 8 : half * 8 + 8] for s in slabs], axis=0)
            start = pl.multiple_of((index * 2 + half) * span, span)
            normed_ref[pl.ds(start, span), :] = part.astype(bf16)
        return carry

    lax.fori_loop(0, rows // 16, pair, 0)
    normed = normed_ref[...]
    query = dot(normed, wq_ref[...], NT).astype(bf16)
    q_ref[...] = (query.astype(f32) * 0.125).astype(bf16)
    k_ref[...] = dot(normed, wk_ref[...], NT).astype(bf16)
    v_ref[...] = dot(normed, wv_ref[...], NT).astype(bf16)
    gate = dot(normed, wf_ref[...]) + bias_ref[...]
    forget = jnp.minimum(gate, 0.0) - jnp.log1p(jnp.exp(-jnp.abs(gate)))
    forget_ref[...] = jnp.zeros_like(forget_ref)
    forget_ref[:, : forget.shape[1]] = forget


def project(tokens, gain, w_query, w_key, w_value, w_forget, forget_bias):
    steps, rows, width = tokens.shape
    inner = w_query.shape[0]
    total = steps * rows
    flat = jax.ShapeDtypeStruct((total, inner), bf16)
    flops = 2 * total * width * inner * 3
    return pl.pallas_call(
        project_kernel,
        out_shape=[flat, flat, flat, jax.ShapeDtypeStruct((total, 128), f32)],
        scratch_shapes=[pltpu.VMEM((total, width), bf16)],
        compiler_params=pltpu.CompilerParams(vmem_limit_bytes=32 * MIB),
        cost_estimate=pl.CostEstimate(
            flops=flops, bytes_accessed=8 * MIB, transcendentals=total
        ),
        name="project",
    )(
        tokens, gain.reshape(1, -1), w_query, w_key, w_value, w_forget,
        forget_bias.reshape(1, -1),
    )


def half_masks(rows):
    low = lanes((rows, 128)) < 64
    return low.astype(f32).astype(bf16), jnp.logical_not(low).astype(f32).astype(bf16)


def stacked(pair_rows, masks):
    return jnp.concatenate([pair_rows * masks[0], pair_rows * masks[1]], axis=0)


def side_by_side(values, rows):
    low = lanes((rows, 128)) < 64
    top = jnp.broadcast_to(values[:rows], (rows, 128))
    bottom = jnp.broadcast_to(values[rows:], (rows, 128))
    return jnp.where(low, top, bottom)


def page_pair(query_pair, keys_pair, values_pair, decay_low, decay_high, masks):
    rows = query_pair.shape[0]
    raw = dot(stacked(query_pair, masks), keys_pair)
    scores = jnp.concatenate([raw[:rows] + decay_low, raw[rows:] + decay_high], axis=0)
    top = jnp.max(scores, axis=-1, keepdims=True)
    weights = jnp.exp(scores - top)
    total = jnp.sum(weights, axis=-1, keepdims=True)
    numer = dot(weights.astype(bf16), values_pair, NT)
    return top, total, side_by_side(numer, rows)


def absorb(state, rows, columns, top, total, numer):
    top_ref, total_ref, numer_ref = state
    old = top_ref[rows, columns]
    new = jnp.maximum(old, top)
    keep = jnp.exp(old - new)
    add = jnp.exp(top - new)
    top_ref[rows, columns] = new
    total_ref[rows, columns] = total_ref[rows, columns] * keep + total * add
    numer_ref[rows, columns] = numer_ref[rows, columns] * keep + numer * add


def history(parents_ref, q_ref, k_ref, v_ref, forget_ref, state):
    transitions, rows = parents_ref.shape
    span = (transitions + 1) * BEAMS
    pack = 128 // span
    square = (128, 128)
    down, across = sublanes(square), lanes(square)
    diagonal = down == across
    columns = []
    for step in range(transitions):
        row = parents_ref[step : step + 1, :].astype(f32)
        columns.append(
            jnp.sum(jnp.where(diagonal, jnp.broadcast_to(row, square), 0.0), axis=1, keepdims=True)
        )
    lane8 = lanes((8, 128)).astype(f32)
    masks = half_masks(128)
    top_ref, total_ref, numer_ref = state
    for group in range(rows // BEAMS // pack):
        slabs = []
        for member in range(pack):
            first = (group * pack + member) * BEAMS
            slabs.append(jnp.zeros((8, 128), f32))
            for step in range(transitions):
                wanted = columns[step][first : first + 8] + float(member * span + step * 8)
                slabs.append(jnp.where(lane8 == wanted, 1.0, 0.0))
        parent = jnp.concatenate(slabs, axis=0)
        same = diagonal.astype(f32)
        parent16 = parent.astype(bf16)
        one = same + parent
        two = dot(parent16, parent16)
        ancestors = one + dot(two.astype(bf16), one.astype(bf16))
        here = pl.ds(group * 128, 128)
        running = lax.dot_general(
            ancestors, forget_ref[here, :], NN,
            precision=lax.Precision.HIGHEST, preferred_element_type=f32,
        ).T
        hidden = jnp.where(ancestors > 0.5, 0.0, masked_score)
        for pair in range(q_ref.shape[1] // 128):
            cols = pl.ds(pair * 128, 128)
            raw = dot(stacked(q_ref[here, cols], masks), k_ref[here, cols], NT)
            low = raw[:128] + (hidden - running[2 * pair : 2 * pair + 1])
            high = raw[128:] + (hidden - running[2 * pair + 1 : 2 * pair + 2])
            scores = jnp.concatenate([low, high], axis=0)
            top = jnp.max(scores, axis=-1, keepdims=True)
            weights = jnp.exp(scores - top)
            total = jnp.sum(weights, axis=-1, keepdims=True)
            numer = dot(weights.astype(bf16), v_ref[here, cols])
            top_ref[here, cols] = side_by_side(top, 128)
            total_ref[here, cols] = side_by_side(total, 128)
            numer_ref[here, cols] = side_by_side(numer, 128)


def masked_decay(decay, fill):
    valid = lanes(decay.shape) < fill
    return jnp.where(valid, decay.astype(f32), masked_score)


def own_kernel(
    request_ref, fill_ref, parents_ref, q_ref, k_ref, v_ref, forget_ref,
    keys_ref, values_ref, decay_ref, top_ref, total_ref, numer_ref,
):
    state = (top_ref, total_ref, numer_ref)
    block = pl.program_id(0)
    local_count = parents_ref.shape[1] // BEAMS
    span = (parents_ref.shape[0] + 1) * BEAMS

    @pl.when(block == 0)
    def _():
        history(parents_ref, q_ref, k_ref, v_ref, forget_ref, state)

    masks = half_masks(span)
    pairs = q_ref.shape[1] // 128
    found = []
    for page in range(PAGE_BLOCK):
        index = block * PAGE_BLOCK + page
        local = lax.rem(request_ref[index], local_count)
        rows = pl.ds(pl.multiple_of(local * span, span), span)
        decay = masked_decay(decay_ref[page], fill_ref[index])
        for pair in range(pairs):
            cols = pl.ds(pair * 128, 128)
            top, total, numer = page_pair(
                q_ref[rows, cols],
                keys_ref[page, cols, :],
                values_ref[page, cols, :],
                decay[2 * pair : 2 * pair + 1],
                decay[2 * pair + 1 : 2 * pair + 2],
                masks,
            )
            found.append(
                (rows, cols, side_by_side(top, span), side_by_side(total, span), numer)
            )
    for rows, cols, top, total, numer in found:
        absorb(state, rows, cols, top, total, numer)


def whole(array):
    return pl.BlockSpec(array.shape, lambda *_: (0,) * array.ndim)


def page_specs(keys, decay, first):
    shift = first // PAGE_BLOCK
    pool = pl.BlockSpec((PAGE_BLOCK,) + keys.shape[1:], lambda i: (i + shift, 0, 0))
    return [pool, pool, pl.BlockSpec((PAGE_BLOCK,) + decay.shape[1:], lambda i: (i + shift, 0, 0))]


def page_cost(pages, keys, rows):
    inner, length = keys.shape[1:]
    return pl.CostEstimate(
        flops=pages * rows * inner * length * 8,
        bytes_accessed=pages * inner * length * 4,
        transcendentals=pages * rows * inner * length // 64,
    )


def own_pages(request, fill, parents, q, k, v, forget, keys, values, decay):
    state = jax.ShapeDtypeStruct(q.shape, f32)
    out_spec = pl.BlockSpec(q.shape, lambda *_: (0, 0))
    return pl.pallas_call(
        own_kernel,
        grid=(OWNED_SLOTS // PAGE_BLOCK,),
        in_specs=[SMEM, SMEM, whole(parents), whole(q), whole(k), whole(v), whole(forget)]
        + page_specs(keys, decay, 0),
        out_specs=[out_spec] * 3,
        out_shape=[state] * 3,
        compiler_params=pltpu.CompilerParams(vmem_limit_bytes=32 * MIB),
        cost_estimate=page_cost(OWNED_SLOTS, keys, 64),
        name="own_pages",
    )(request, fill, parents, q, k, v, forget, keys, values, decay)


def ask_kernel(asked_ref, q_ref, out_ref):
    slots, span, _ = out_ref.shape
    for slot in range(slots):
        local = jnp.maximum(asked_ref[slot], 0)
        out_ref[slot] = q_ref[pl.ds(pl.multiple_of(local * span, span), span), :]


def ask(asked, q, span):
    slots = asked.shape[0]
    return pl.pallas_call(
        ask_kernel,
        in_specs=[SMEM, pl.BlockSpec(memory_space=pltpu.VMEM)],
        out_shape=jax.ShapeDtypeStruct((slots, span, q.shape[1]), bf16),
        name="ask",
    )(asked, q)


def hosted_kernel(
    capacity, fill_ref, slot_ref, q_ref, keys_ref, values_ref, decay_ref, out_ref, tail_ref
):
    block = pl.program_id(0)
    span = q_ref.shape[1]
    inner = q_ref.shape[2]
    pairs = inner // 128
    heads = inner // 64

    @pl.when(block == 0)
    def _():
        out_ref[...] = jnp.zeros_like(out_ref)
        tail_ref[...] = jnp.zeros_like(tail_ref)

    masks = half_masks(span)
    lane = lanes((span, 128))
    found = []
    for page in range(PAGE_BLOCK):
        index = block * PAGE_BLOCK + page
        slot = slot_ref[index]
        decay = masked_decay(decay_ref[page], fill_ref[OWNED_SLOTS + index])
        logs, averages = [], []
        for pair in range(pairs):
            cols = pl.ds(pair * 128, 128)
            top, total, numer = page_pair(
                q_ref[slot, :, cols],
                keys_ref[page, cols, :],
                values_ref[page, cols, :],
                decay[2 * pair : 2 * pair + 1],
                decay[2 * pair + 1 : 2 * pair + 2],
                masks,
            )
            averages.append((numer / side_by_side(total, span)).astype(bf16))
            log_total = top + jnp.log(total)
            logs.extend([log_total[:span], log_total[span:]])
        found.append((slot, logs, averages))
    for slot, logs, averages in found:
        owner = slot // capacity
        rank = slot - owner * capacity
        for pair in range(pairs):
            out_ref[owner, pl.ds(pl.multiple_of(rank * span, span), span), pl.ds(pair * 128, 128)] = averages[pair]
        tail = tail_ref[owner]
        base = rank * (3 * heads)
        for head, value in enumerate(logs):
            rest = jnp.broadcast_to(value, (span, 128))
            for piece in range(3):
                part = rest.astype(bf16).astype(f32)
                rest = rest - part
                tail = jnp.where(lane == base + piece * heads + head, part, tail)
        tail_ref[owner] = tail

    @pl.when(block == pl.num_programs(0) - 1)
    def _():
        first = capacity * span
        for owner in range(out_ref.shape[0]):
            tail = tail_ref[owner].astype(bf16)
            for part in range(span // TAIL_ROWS):
                out_ref[owner, first : first + TAIL_ROWS, part * 128 : part * 128 + 128] = tail[
                    part * TAIL_ROWS : part * TAIL_ROWS + TAIL_ROWS
                ]


def hosted_pages(fill, slots, asked_rows, keys, values, decay, groups, capacity):
    count, span, inner = asked_rows.shape
    out_shape = (groups, capacity * span + TAIL_ROWS, inner)
    return pl.pallas_call(
        functools.partial(hosted_kernel, capacity),
        grid=(SPILL // PAGE_BLOCK,),
        in_specs=[SMEM, SMEM, whole(asked_rows)] + page_specs(keys, decay, OWNED_SLOTS),
        out_specs=pl.BlockSpec(out_shape, lambda *_: (0, 0, 0)),
        out_shape=jax.ShapeDtypeStruct(out_shape, bf16),
        scratch_shapes=[pltpu.VMEM((groups, span, 128), f32)],
        compiler_params=pltpu.CompilerParams(vmem_limit_bytes=32 * MIB),
        cost_estimate=page_cost(SPILL, keys, 64),
        name="hosted_pages",
    )(fill, slots, asked_rows, keys, values, decay)


def merge_kernel(capacity, steps, asked_ref, back_ref, top_in, total_in, numer_in, out_ref,
                 top_ref, total_ref, numer_ref):
    groups, _, inner = back_ref.shape
    span = steps * BEAMS
    heads = inner // 64
    state = (top_ref, total_ref, numer_ref)
    top_ref[...] = top_in[...]
    total_ref[...] = total_in[...]
    numer_ref[...] = numer_in[...]
    source, target = sublanes((128, inner)), lanes((128, inner)) // 64
    spread = []
    for rank in range(capacity):
        hit = source < 0
        for piece in range(3):
            hit = hit | (source == target + (rank * 3 + piece) * heads)
        spread.append(hit.astype(f32).astype(bf16))

    for owner in range(groups):
        first = capacity * span
        for rank in range(capacity):
            local = asked_ref[owner * capacity + rank]

            @pl.when(local >= 0)
            def _():
                tail = jnp.concatenate(
                    [
                        back_ref[owner, first : first + TAIL_ROWS, part * 128 : part * 128 + 128]
                        for part in range(span // TAIL_ROWS)
                    ],
                    axis=0,
                )
                top = dot(tail, spread[rank])
                average = back_ref[owner, rank * span : rank * span + span, :].astype(f32)
                rows = pl.ds(pl.multiple_of(local * span, span), span)
                absorb(state, rows, slice(None), top, 1.0, average)

    for index in range(out_ref.shape[1] // 16):
        parts = []
        for half in range(2):
            rows = slice((index * 2 + half) * span, (index * 2 + half + 1) * span)
            parts.append(numer_ref[rows, :] / total_ref[rows, :])
        for step in range(steps):
            both = jnp.concatenate([p[step * 8 : step * 8 + 8] for p in parts], axis=0)
            out_ref[step, index * 16 : index * 16 + 16, :] = both.astype(bf16)


def merge(asked, back, top, total, numer, steps, capacity):
    rows, inner = top.shape
    vmem = pl.BlockSpec(memory_space=pltpu.VMEM)
    return pl.pallas_call(
        functools.partial(merge_kernel, capacity, steps),
        in_specs=[SMEM, vmem, vmem, vmem, vmem],
        out_shape=jax.ShapeDtypeStruct((steps, rows // steps, inner), bf16),
        scratch_shapes=[pltpu.VMEM((rows, inner), f32)] * 3,
        compiler_params=pltpu.CompilerParams(vmem_limit_bytes=32 * MIB),
        name="merge",
    )(asked, back, top, total, numer)


def rms_scale(values, gain_vector):
    return (
        values
        * lax.rsqrt(jnp.mean(values * values, axis=-1, keepdims=True) + epsilon)
        * gain_vector
    )


def swap_core(value):
    return lax.ppermute(value, "head", [(i, i ^ 1) for i in range(4)])


def swap_chip(value):
    return lax.ppermute(value, "head", [(i, i ^ 2) for i in range(4)])


def shards(
    tokens, parents, page_request, page_fill, keys_pool, values_pool, decay_pool,
    gain_attn, w_query, w_key, w_value, w_forget, forget_bias, w_out,
    gain_ffn, w_gate, w_up, w_down,
):
    steps, rows, width = tokens.shape
    inner = w_query.shape[0]
    local_count = rows // BEAMS
    span = steps * BEAMS
    groups = lax.axis_size("group")
    capacity = (SPILL + groups - 2) // (groups - 1)
    core = lax.axis_index("head") % 2

    table, slots = route(page_request, groups, local_count, capacity)
    asked = lax.all_to_all(
        table.reshape(groups, 1, capacity), "group", split_axis=0, concat_axis=0, tiled=True
    ).reshape(groups * capacity)
    w_out_far = swap_chip(w_out)
    q, k, v, forget = project(tokens, gain_attn, w_query, w_key, w_value, w_forget, forget_bias)
    asked_rows = lax.all_to_all(
        ask(asked, q, span).reshape(groups, capacity * span, inner),
        "group", split_axis=0, concat_axis=0, tiled=True,
    ).reshape(groups * capacity, span, inner)
    top, total, numer = own_pages(
        page_request, page_fill, parents, q, k, v, forget, keys_pool, values_pool, decay_pool
    )
    back = lax.all_to_all(
        hosted_pages(
            page_fill, slots, asked_rows, keys_pool, values_pool, decay_pool, groups, capacity
        ),
        "group", split_axis=0, concat_axis=0, tiled=True,
    )
    w_out_near, w_out_cross = swap_core(w_out), swap_core(w_out_far)
    attended = merge(asked, back, top, total, numer, steps, capacity).reshape(steps * rows, inner)
    far = swap_chip(attended)
    near, cross = swap_core(attended), swap_core(far)

    mixed = (dot(attended, w_out) + dot(near, w_out_near)) + (
        dot(far, w_out_far) + dot(cross, w_out_cross)
    )
    residual = tokens.reshape(steps * rows, width).astype(f32) + mixed
    normed = rms_scale(residual, gain_ffn).astype(bf16)
    hidden = (jax.nn.silu(dot(normed, w_gate)) * dot(normed, w_up)).astype(bf16)
    partial = dot(hidden, w_down)
    half = steps * rows // 2
    mine = lax.dynamic_slice_in_dim(partial, core * half, half, 0)
    other = lax.dynamic_slice_in_dim(partial, (1 - core) * half, half, 0).astype(bf16)
    chip = (mine + swap_core(other).astype(f32)).astype(bf16)
    both = chip.astype(f32) + swap_chip(chip).astype(f32)
    done = (lax.dynamic_slice_in_dim(residual, core * half, half, 0) + both).astype(bf16)
    theirs = swap_core(done)
    first = jnp.where(core == 0, done, theirs)
    second = jnp.where(core == 0, theirs, done)
    return jnp.concatenate([first, second], axis=0).reshape(steps, rows, width)


def solution(mesh):
    return jax.shard_map(
        shards,
        mesh=mesh,
        in_specs=(
            P(None, "group", None),
            P(None, "group"),
            P("group"),
            P("group"),
            P("group", "head", None),
            P("group", "head", None),
            P("group", "head", None),
            P(),
            P("head", None),
            P("head", None),
            P("head", None),
            P(None, "head"),
            P("head"),
            P("head", None),
            P(),
            P(None, "head"),
            P(None, "head"),
            P("head", None),
        ),
        out_specs=P(None, "group", None),
        check_vma=False,
    )
```

time: 905 us -> 174 us (0.19); the launches traced: 890 us -> 173 us
  local copies, waits for them, and re-layouts: 290 us -> 37.9 us
  other arithmetic: 152 us -> 7.82 us
  blocking collectives: 137 us -> 0 us
  waiting for transfers between devices: 151 us -> 43.1 us
  starting transfers between devices: 75 us -> 23.2 us
  matrix products: 70 us -> 25.1 us
  Pallas kernels: 0 us -> 35.4 us
  between operations: 14.5 us -> 0.24 us
    psum x2 -> x0, waiting for transfers between devices: 139 us -> none  [the longest x1 70.2 us: shards(): lax.psum(jnp.dot(attended, w_out, preferred_element_type=jnp.float32), 'h...]
    all_gather x4 -> x0, blocking collectives: 137 us -> none  [shards(): gathered = lax.all_gather(query_block, 'group', axis=0, tiled=True)]
    gather x46 -> x0, local copies, waits for them, and re-layouts: 83.1 us -> none  [the longest x8 15.5 us: shards(): page_top[slot_source]]
    all_to_all x13 -> x3, starting transfers between devices: 74.7 us -> 17.5 us  [the longest x1 7.28 us: shards(): lax.all_to_all(table.reshape(groups, 1, capacity), 'group', split_axis=0,...]
    reduce_sum x18 -> x0, other arithmetic: 48.3 us -> none  [the longest x4 28 us: by_request(): combined = jnp.sum(factor[..., None] * numer_split[None], axis=1)]
    dot_general x26 -> x6, matrix products: 70 us -> 25.1 us  [dot(): return lax.dot_general(a, b, dims, preferred_element_type=f32)]
    reshape x24 -> x3, local copies, waits for them, and re-layouts: 42 us -> 2.6 us  [the longest x1 1.29 us: shards(): table.reshape(groups, 1, capacity)]
    pallas_call x0 -> x6, Pallas kernels: none -> 35.4 us  [the longest x1 16.2 us: own_pages(): pl.pallas_call(own_kernel, grid=(OWNED_SLOTS // PAGE_BLOCK,), in_specs=[S...]
  transfers between devices with their start and end apart: 15 -> 12, of which waited for: 5 -> 5; matrix products, arithmetic and copies ran while one was open for 51% -> 6% of each run, Pallas kernels for 0% -> 19%
where the time goes in v1:
time: 174 us; the launch traced here: 173 us
  waiting for transfers between devices  43.1 us (25%)
  local copies, waits for them, and re-layouts  37.9 us (22%)
  Pallas kernels  35.4 us (20%)
  matrix products  25.1 us (14%)
  starting transfers between devices  23.2 us (13%)
  other arithmetic  7.82 us (4%)
    unnamed x72, local copies, waits for them, and re-layouts  32.4 us
    ppermute x3, waiting for transfers between devices, swap_chip(): return lax.ppermute(value, 'head', [(i, i ^ 2) for i in range(4)])  25.8 us
    dot_general x6, matrix products, dot(): return lax.dot_general(a, b, dims, preferred_element_type=f32)  25.1 us
    pallas_call x1, Pallas kernels, own_pages(): pl.pallas_call(own_kernel, grid=(OWNED_SLOTS // PAGE_BLOCK,), in_specs=[S...  16.2 us
    all_to_all x1, waiting for transfers between devices, shards(): lax.all_to_all(ask(asked, q, span).reshape(groups, capacity * span, inner...  12.4 us
    pallas_call x1, Pallas kernels, hosted_pages(): pl.pallas_call(functools.partial(hosted_kernel, capacity), grid=(SPILL //...  7.54 us
    all_to_all x1, starting transfers between devices, shards(): lax.all_to_all(table.reshape(groups, 1, capacity), 'group', split_axis=0,...  7.28 us
    all_to_all x1, starting transfers between devices, shards(): lax.all_to_all(ask(asked, q, span).reshape(groups, capacity * span, inner...  6 us
  transfers between devices with their start and end apart: 12, of which 5 were waited for; matrix products, arithmetic and copies ran while one was open for 6% of the time, Pallas kernels for 19%

profile of v1, /device:TPU:0, one launch (start us, length us, event | category | flops | bytes accessed | tf_op | source)
XLA Modules:
  0.0 172.7 jit_solution(4675101290245524440)
XLA Ops:
  0.0 1.4 route.1
  2.7 7.3 %all-to-all-start = ((s32[8,1,3]{2,1,0:T(1,128)}), s32[8,1,3]{2,1,0:T(1,128)S(1)}, u32[]{:S(2)}, u32[]{:S(2)}) async-start(s32[8,1,3]{2,1,0:T(1,128)} %bitcast.1), calls=%async_computation | async-start | bytes 8192 | tf_op jit(solution)/shard_map/all_to_all | solution.py:472
  17.6 4.2 %project.1 = (bf16[512,384]{1,0:T(8,128)(2,1)S(1)}, bf16[512,384]{1,0:T(8,128)(2,1)S(1)}, bf16[512,384]{1,0:T(8,128)(2,1)S(1)}, f32[512,128]{1,0:T(8,128)S(1)}) custom-call(bf16[4,128,1536]{2,1,0:T(8,128)(2,1)S(1)} %copy-done.8, f32[1,1536]{1,0:T(1,128)S(1)} %reshape.38.gain_ref, bf16[384,1536]{1,0:T(8,128)(2,1)S(1)} %copy-done.29, ...), custom_call_target="tpu_custom_call" | custom-call | flops 1811939328 | bytes 8388608 | tf_op jit(solution)/shard_map/project/pallas_call | solution.py:106
  26.6 1.9 %ask.1 = bf16[24,32,384]{2,1,0:T(8,128)(2,1)} custom-call(s32[24]{0:T(128)} %reshape.37.asked_ref, bf16[512,384]{1,0:T(8,128)(2,1)} %copy-done.6), custom_call_target="tpu_custom_call" | custom-call | tf_op jit(solution)/shard_map/ask/pallas_call | solution.py:297
  28.5 6.0 %all-to-all-start.1 = ((bf16[8,96,384]{2,1,0:T(8,128)(2,1)}), bf16[8,96,384]{2,1,0:T(8,128)(2,1)}, u32[]{:S(2)}, u32[]{:S(2)}) async-start(bf16[8,96,384]{2,1,0:T(8,128)(2,1)} %bitcast.24), calls=%async_computation.1 | async-start | bytes 1179648 | tf_op jit(solution)/shard_map/all_to_all | solution.py:477
  34.5 1.5 collective-permute-start.3
  36.0 1.5 copy.27.decay_ref
  37.5 12.4 %all-to-all-done.1 = bf16[8,96,384]{2,1,0:T(8,128)(2,1)} async-done(((bf16[8,96,384]{2,1,0:T(8,128)(2,1)}), bf16[8,96,384]{2,1,0:T(8,128)(2,1)}, u32[]{:S(2)}, u32[]{:S(2)}) %all-to-all-start.1) | async-done | bytes 589856 | tf_op jit(solution)/shard_map/all_to_all | solution.py:477
  50.0 2.3 %copy-done.1 = bf16[48,384,128]{2,1,0:T(8,128)(2,1)S(1)} copy-done((bf16[48,384,128]{2,1,0:T(8,128)(2,1)S(1)}, bf16[48,384,128]{2,1,0:T(8,128)(2,1)}, u32[]{:S(2)}) %copy-start.1) | copy-done | bytes 4718616
  52.3 2.3 %copy-done.3 = bf16[48,384,128]{2,1,0:T(8,128)(2,1)S(1)} copy-done((bf16[48,384,128]{2,1,0:T(8,128)(2,1)S(1)}, bf16[48,384,128]{2,1,0:T(8,128)(2,1)}, u32[]{:S(2)}) %copy-start.3) | copy-done | bytes 4718616
  55.5 7.5 %hosted_pages.1 = bf16[8,112,384]{2,1,0:T(8,128)(2,1)S(1)} custom-call(s32[48]{0:T(128)S(1)} %copy-done.26, s32[16]{0:T(128)S(1)} %copy-done.28, bf16[24,32,384]{2,1,0:T(8,128)(2,1)} %bitcast.4.q_ref, bf16[48,384,128]{2,1,0:T(8,128)(2,1)S(1)} %copy-done.1, bf16[48,384,128]{2,1,0:T(8,128)(2,1)S(1)} %copy-done.3, bf16[48,6,128]{2,1,0:T(8,128)(2,1)S(1)} %copy-done.10), custom_call_target="tpu_custom_call" | custom-call | flops 402653184 | bytes 3145728 | tf_op jit(solution)/shard_map/hosted_pages/pallas_call | solution.py:370
  63.9 4.2 %all-to-all-start.2 = ((bf16[8,112,384]{2,1,0:T(8,128)(2,1)}), bf16[8,112,384]{2,1,0:T(8,128)(2,1)}, u32[]{:S(2)}, u32[]{:S(2)}) async-start(bf16[8,112,384]{2,1,0:T(8,128)(2,1)} %copy-done.5), calls=%async_computation.2 | async-start | bytes 1376256 | tf_op jit(solution)/shard_map/all_to_all | solution.py:484
  68.8 2.3 %copy-done.2 = bf16[48,384,128]{2,1,0:T(8,128)(2,1)S(1)} copy-done((bf16[48,384,128]{2,1,0:T(8,128)(2,1)S(1)}, bf16[48,384,128]{2,1,0:T(8,128)(2,1)}, u32[]{:S(2)}) %copy-start.2) | copy-done | bytes 4718616
  71.1 2.3 %copy-done.4 = bf16[48,384,128]{2,1,0:T(8,128)(2,1)S(1)} copy-done((bf16[48,384,128]{2,1,0:T(8,128)(2,1)S(1)}, bf16[48,384,128]{2,1,0:T(8,128)(2,1)}, u32[]{:S(2)}) %copy-start.4) | copy-done | bytes 4718616
  77.3 16.2 %own_pages.1 = (f32[512,384]{1,0:T(8,128)S(1)}, f32[512,384]{1,0:T(8,128)S(1)}, f32[512,384]{1,0:T(8,128)S(1)}) custom-call(s32[48]{0:T(128)S(1)} %copy-done.27, s32[48]{0:T(128)S(1)} %copy-done.26, s32[3,128]{1,0:T(4,128)S(1)} %copy-done.25, bf16[512,384]{1,0:T(8,128)(2,1)S(1)} %copy-done.7, bf16[512,384]{1,0:T(8,128)(2,1)S(1)} %copy-done.19, ...), custom_call_target="tpu_custom_call" | custom-call | flops 805306368 | bytes 6291456 | tf_op jit(solution)/shard_map/own_pages/pallas_call | solution.py:275
  99.5 4.1 %merge.1 = bf16[4,128,384]{2,1,0:T(8,128)(2,1)S(1)} custom-call(s32[24]{0:T(128)S(1)} %copy-done.24, bf16[8,112,384]{2,1,0:T(8,128)(2,1)} %all-to-all-done.2.back_ref, f32[512,384]{1,0:T(8,128)S(1)} %copy-done.13, f32[512,384]{1,0:T(8,128)S(1)} %copy-done.15, f32[512,384]{1,0:T(8,128)S(1)} %copy-done.17), custom_call_target="tpu_custom_call" | custom-call | tf_op jit(solution)/shard_map/merge/pallas_call | solution.py:432
  103.6 1.6 collective-permute-start.2
  105.2 2.2 %fusion.5 = f32[512,1536]{1,0:T(8,128)S(1)} fusion(bf16[512,384]{1,0:T(8,128)(2,1)S(1)} %bitcast.21, bf16[384,1536]{1,0:T(8,128)(2,1)} %param.31), kind=kOutput, calls=%fused_computation.17 | convolution fusion | flops 603979776 | bytes 4718592 | tf_op jit(solution)/shard_map/dot_general | solution.py:28
  107.4 7.5 %collective-permute-done.2 = bf16[512,384]{1,0:T(8,128)(2,1)} collective-permute-done((bf16[512,384]{1,0:T(8,128)(2,1)S(1)}, bf16[512,384]{1,0:T(8,128)(2,1)}, u32[]{:S(2)}, u32[]{:S(2)}) %collective-permute-start.2) | collective-permute-done | bytes 393248 | tf_op jit(solution)/shard_map/ppermute | solution.py:455
  114.9 2.4 %fusion.6 = f32[512,1536]{1,0:T(8,128)S(1)} fusion(bf16[512,384]{1,0:T(8,128)(2,1)} %collective-permute-done.2, bf16[384,1536]{1,0:T(8,128)(2,1)} %collective-permute-done.3), kind=kOutput, calls=%fused_computation.18 | convolution fusion | flops 603979776 | bytes 4718592 | tf_op jit(solution)/shard_map/dot_general | solution.py:28
  117.3 2.4 %convolution_add_fusion.1 = f32[512,1536]{1,0:T(8,128)S(1)} fusion(f32[512,1536]{1,0:T(8,128)S(1)} %fusion.5, bf16[512,384]{1,0:T(8,128)(2,1)S(1)} %collective-permute-done, bf16[384,1536]{1,0:T(8,128)(2,1)} %collective-permute-done.1), kind=kOutput, calls=%fused_computation.3 | convolution fusion | flops 604766208 | bytes 7864320 | tf_op jit(solution)/shard_map/dot_general | solution.py:28
  119.8 4.3 %multiply_reduce_fusion = (f32[512]{0:T(512)S(1)}, f32[512,1536]{1,0:T(8,128)}) fusion(f32[512,1536]{1,0:T(8,128)S(1)} %convolution_add_fusion.1, f32[512,1536]{1,0:T(8,128)S(1)} %fusion.6, bf16[512,384]{1,0:T(8,128)(2,1)S(1)} %collective-permute-done.4, bf16[384,1536]{1,0:T(8,128)(2,1)} %collective-permute-done.5, bf16[512,1536]{1,0:T(8,128)(2,1)S(1)} %bitcast.22), kind=kOutput, calls=%fused_computation.5 | convolution fusion | flops 608697856 | bytes 12584960 | tf_op jit(solution)/shard_map/dot_general | solution.py:28
  124.0 5.2 %fusion.4 = f32[512,1024]{1,0:T(8,128)} fusion(bf16[1536,1024]{1,0:T(8,128)(2,1)S(1)} %copy-done.33, f32[512,1536]{1,0:T(8,128)} %get-tuple-element.26, f32[1536]{0:T(1024)S(1)} %copy-done.34, f32[512]{0:T(512)S(1)} %add_rsqrt_fusion), kind=kOutput, calls=%fused_computation.16 | convolution fusion | flops 1612972032 | bytes 8396800 | tf_op jit(solution)/shard_map/dot_general | solution.py:28
  129.2 8.6 %fusion.2 = f32[512,1536]{1,0:T(8,128)} fusion(bf16[1024,1536]{1,0:T(8,128)(2,1)S(1)} %copy-done, f32[512,1024]{1,0:T(8,128)} %fusion.4, bf16[1536,1024]{1,0:T(8,128)(2,1)} %param.34, f32[512,1536]{1,0:T(8,128)} %get-tuple-element.26, f32[1536]{0:T(1024)S(1)} %copy-done.34, f32[512]{0:T(512)S(1)} %add_rsqrt_fusion), kind=kOutput, calls=%fused_computation.11 | convolution fusion | flops 3226730496 | bytes 14688256 | tf_op jit(solution)/shard_map/dot_general | solution.py:28
  137.8 2.4 %dynamic-slice_convert_fusion = bf16[256,1536]{1,0:T(8,128)(2,1)} fusion(f32[512,1536]{1,0:T(8,128)} %fusion.2, s32[]{:T(128)S(6)} %select_n.29), kind=kLoop, calls=%fused_computation.10 | loop fusion | bytes 1572868 | tf_op jit(solution)/shard_map/convert_element_type | solution.py:504
  140.7 2.3 %collective-permute-done.6 = bf16[256,1536]{1,0:T(8,128)(2,1)} collective-permute-done((bf16[256,1536]{1,0:T(8,128)(2,1)}, bf16[256,1536]{1,0:T(8,128)(2,1)}, u32[]{:S(2)}, u32[]{:S(2)}) %collective-permute-start.6) | collective-permute-done | bytes 786464 | tf_op jit(solution)/shard_map/ppermute | solution.py:451
  143.0 1.8 %add_convert_fusion.1 = bf16[256,1536]{1,0:T(8,128)(2,1)S(1)} fusion(bf16[256,1536]{1,0:T(8,128)(2,1)} %collective-permute-done.6, f32[512,1536]{1,0:T(8,128)} %fusion.2, s32[]{:T(128)S(6)} %select_n.28), kind=kLoop, calls=%fused_computation.9 | loop fusion | flops 1179648 | bytes 3145732 | tf_op jit(solution)/shard_map/convert_element_type | solution.py:505
  144.8 1.6 collective-permute-start.7
  146.4 18.3 %collective-permute-done.7 = bf16[256,1536]{1,0:T(8,128)(2,1)S(1)} collective-permute-done((bf16[256,1536]{1,0:T(8,128)(2,1)S(1)}, bf16[256,1536]{1,0:T(8,128)(2,1)S(1)}, u32[]{:S(2)}, u32[]{:S(2)}) %collective-permute-start.7) | collective-permute-done | bytes 786464 | tf_op jit(solution)/shard_map/ppermute | solution.py:455
  164.7 2.6 %add_convert_fusion = bf16[256,1536]{1,0:T(8,128)(2,1)} fusion(bf16[256,1536]{1,0:T(8,128)(2,1)S(1)} %collective-permute-done.7, bf16[256,1536]{1,0:T(8,128)(2,1)S(1)} %add_convert_fusion.1, f32[512,1536]{1,0:T(8,128)} %get-tuple-element.26, s32[]{:T(128)S(6)} %select_n.28), kind=kLoop, calls=%fused_computation.8 | loop fusion | flops 1966080 | bytes 3932164 | tf_op jit(solution)/shard_map/convert_element_type | solution.py:507
  167.3 2.6 %collective-permute-done.8 = bf16[256,1536]{1,0:T(8,128)(2,1)} collective-permute-done((bf16[256,1536]{1,0:T(8,128)(2,1)}, bf16[256,1536]{1,0:T(8,128)(2,1)}, u32[]{:S(2)}, u32[]{:S(2)}) %collective-permute-start.8) | collective-permute-done | bytes 786464 | tf_op jit(solution)/shard_map/ppermute | solution.py:451
  169.9 1.5 broadcast_select_fusion.1
  (87 shorter events, 27.6 us)
Async XLA Ops:
  0.0 129.2 %copy-start = (bf16[1024,1536]{1,0:T(8,128)(2,1)S(1)}, bf16[1024,1536]{1,0:T(8,128)(2,1)}, u32[]{:S(2)}) copy-start(bf16[1024,1536]{1,0:T(8,128)(2,1)} %param.35) | copy-start | bytes 9437188
  2.7 22.0 %all-to-all-start = ((s32[8,1,3]{2,1,0:T(1,128)}), s32[8,1,3]{2,1,0:T(1,128)S(1)}, u32[]{:S(2)}, u32[]{:S(2)}) async-start(s32[8,1,3]{2,1,0:T(1,128)} %bitcast.1), calls=%async_computation | async-start | bytes 8192 | tf_op jit(solution)/shard_map/all_to_all | solution.py:472
  11.7 1.4 copy-start.8
  13.1 1.3 copy-start.29
  14.4 1.3 copy-start.30
  15.7 1.3 copy-start.31
  17.6 32.3 %copy-start.26 = (s32[48]{0:T(128)S(1)}, s32[48]{0:T(128)}, u32[]{:S(2)}) copy-start(s32[48]{0:T(128)} %fill_ref.3) | copy-start | bytes 580
  17.6 32.3 %copy-start.28 = (s32[16]{0:T(128)S(1)}, s32[16]{0:T(128)}, u32[]{:S(2)}) copy-start(s32[16]{0:T(128)} %get-tuple-element.15.slot_ref) | copy-start | bytes 196
  28.5 21.5 %all-to-all-start.1 = ((bf16[8,96,384]{2,1,0:T(8,128)(2,1)}), bf16[8,96,384]{2,1,0:T(8,128)(2,1)}, u32[]{:S(2)}, u32[]{:S(2)}) async-start(bf16[8,96,384]{2,1,0:T(8,128)(2,1)} %bitcast.24), calls=%async_computation.1 | async-start | bytes 1179648 | tf_op jit(solution)/shard_map/all_to_all | solution.py:477
  34.5 33.8 %collective-permute-start.3 = (bf16[384,1536]{1,0:T(8,128)(2,1)}, bf16[384,1536]{1,0:T(8,128)(2,1)}, u32[]{:S(2)}, u32[]{:S(2)}) collective-permute-start(bf16[384,1536]{1,0:T(8,128)(2,1)} %param.31), channel_id=1, source_target_pairs={{0,2},{1,3},{2,0},{3,1},{4,6},{5,7},{6,4},{7,5},{8,10},{9,11},{10,... | collective-permute-start | bytes 3538952 | tf_op jit(solution)/shard_map/ppermute | solution.py:455
  50.0 2.3 %copy-start.1 = (bf16[48,384,128]{2,1,0:T(8,128)(2,1)S(1)}, bf16[48,384,128]{2,1,0:T(8,128)(2,1)}, u32[]{:S(2)}) copy-start(bf16[48,384,128]{2,1,0:T(8,128)(2,1)} %keys_ref.3) | copy-start | bytes 14155780
  52.3 2.3 %copy-start.3 = (bf16[48,384,128]{2,1,0:T(8,128)(2,1)S(1)}, bf16[48,384,128]{2,1,0:T(8,128)(2,1)}, u32[]{:S(2)}) copy-start(bf16[48,384,128]{2,1,0:T(8,128)(2,1)} %values_ref.3) | copy-start | bytes 14155780
  55.5 13.2 %copy-start.7 = (bf16[512,384]{1,0:T(8,128)(2,1)S(1)}, bf16[512,384]{1,0:T(8,128)(2,1)}, u32[]{:S(2)}) copy-start(bf16[512,384]{1,0:T(8,128)(2,1)} %copy-done.6) | copy-start | bytes 1179652
  55.5 13.2 %copy-start.25 = (s32[3,128]{1,0:T(4,128)S(1)}, s32[3,128]{1,0:T(4,128)}, u32[]{:S(2)}) copy-start(s32[3,128]{1,0:T(4,128)} %parents_ref.1) | copy-start | bytes 4612
  55.5 13.2 %copy-start.27 = (s32[48]{0:T(128)S(1)}, s32[48]{0:T(128)}, u32[]{:S(2)}) copy-start(s32[48]{0:T(128)} %request_ref.3) | copy-start | bytes 580
  63.9 32.1 %all-to-all-start.2 = ((bf16[8,112,384]{2,1,0:T(8,128)(2,1)}), bf16[8,112,384]{2,1,0:T(8,128)(2,1)}, u32[]{:S(2)}, u32[]{:S(2)}) async-start(bf16[8,112,384]{2,1,0:T(8,128)(2,1)} %copy-done.5), calls=%async_computation.2 | async-start | bytes 1376256 | tf_op jit(solution)/shard_map/all_to_all | solution.py:484
  68.2 49.1 %collective-permute-start.1 = (bf16[384,1536]{1,0:T(8,128)(2,1)}, bf16[384,1536]{1,0:T(8,128)(2,1)}, u32[]{:S(2)}, u32[]{:S(2)}) collective-permute-start(bf16[384,1536]{1,0:T(8,128)(2,1)} %param.31), channel_id=1, source_target_pairs={{0,1},{1,0},{2,3},{3,2},{4,5},{5,4},{6,7},{7,6},{8,9},{9,8},{10,11... | collective-permute-start | bytes 3538952 | tf_op jit(solution)/shard_map/ppermute | solution.py:451
  68.3 51.4 %collective-permute-start.5 = (bf16[384,1536]{1,0:T(8,128)(2,1)}, bf16[384,1536]{1,0:T(8,128)(2,1)}, u32[]{:S(2)}, u32[]{:S(2)}) collective-permute-start(bf16[384,1536]{1,0:T(8,128)(2,1)} %collective-permute-done.3), channel_id=1, source_target_pairs={{0,1},{1,0},{2,3},{3,2},{4,5},{5,4},{6,7},{7,6},{8,9},{9,8},{10,11... | collective-permute-start | bytes 3538952 | tf_op jit(solution)/shard_map/ppermute | solution.py:451
  68.7 2.3 %copy-start.2 = (bf16[48,384,128]{2,1,0:T(8,128)(2,1)S(1)}, bf16[48,384,128]{2,1,0:T(8,128)(2,1)}, u32[]{:S(2)}) copy-start(bf16[48,384,128]{2,1,0:T(8,128)(2,1)} %keys_ref.3) | copy-start | bytes 14155780
  71.1 2.3 %copy-start.4 = (bf16[48,384,128]{2,1,0:T(8,128)(2,1)S(1)}, bf16[48,384,128]{2,1,0:T(8,128)(2,1)}, u32[]{:S(2)}) copy-start(bf16[48,384,128]{2,1,0:T(8,128)(2,1)} %values_ref.3) | copy-start | bytes 14155780
  77.3 18.8 %copy-start.24 = (s32[24]{0:T(128)S(1)}, s32[24]{0:T(128)}, u32[]{:S(2)}) copy-start(s32[24]{0:T(128)} %reshape.37.asked_ref) | copy-start | bytes 292
  96.1 1.1 copy-start.13
  97.2 1.1 copy-start.15
  103.6 11.3 %collective-permute-start.2 = (bf16[512,384]{1,0:T(8,128)(2,1)S(1)}, bf16[512,384]{1,0:T(8,128)(2,1)}, u32[]{:S(2)}, u32[]{:S(2)}) collective-permute-start(bf16[512,384]{1,0:T(8,128)(2,1)S(1)} %bitcast.19), channel_id=1, source_target_pairs={{0,2},{1,3},{2,0},{3,1},{4,6},{5,7},{6,4},{7,5},{8,10},{9,11},{10,... | collective-permute-start | bytes 1179656 | tf_op jit(solution)/shard_map/ppermute | solution.py:455
  105.2 12.1 %collective-permute-start = (bf16[512,384]{1,0:T(8,128)(2,1)S(1)}, bf16[512,384]{1,0:T(8,128)(2,1)S(1)}, u32[]{:S(2)}, u32[]{:S(2)}) collective-permute-start(bf16[512,384]{1,0:T(8,128)(2,1)S(1)} %bitcast.20), channel_id=1, source_target_pairs={{0,1},{1,0},{2,3},{3,2},{4,5},{5,4},{6,7},{7,6},{8,9},{9,8},{10,11... | collective-permute-start | bytes 1179656 | tf_op jit(solution)/shard_map/ppermute | solution.py:451
  114.9 4.8 %collective-permute-start.4 = (bf16[512,384]{1,0:T(8,128)(2,1)}, bf16[512,384]{1,0:T(8,128)(2,1)S(1)}, u32[]{:S(2)}, u32[]{:S(2)}) collective-permute-start(bf16[512,384]{1,0:T(8,128)(2,1)} %collective-permute-done.2), channel_id=1, source_target_pairs={{0,1},{1,0},{2,3},{3,2},{4,5},{5,4},{6,7},{7,6},{8,9},{9,8},{10,11... | collective-permute-start | bytes 1179656 | tf_op jit(solution)/shard_map/ppermute | solution.py:451
  117.3 2.4 %copy-start.9 = (bf16[4,128,1536]{2,1,0:T(8,128)(2,1)S(1)}, bf16[4,128,1536]{2,1,0:T(8,128)(2,1)}, u32[]{:S(2)}) copy-start(bf16[4,128,1536]{2,1,0:T(8,128)(2,1)} %tokens_ref.1) | copy-start | bytes 4718596
  119.7 4.3 %copy-start.33 = (bf16[1536,1024]{1,0:T(8,128)(2,1)S(1)}, bf16[1536,1024]{1,0:T(8,128)(2,1)}, u32[]{:S(2)}) copy-start(bf16[1536,1024]{1,0:T(8,128)(2,1)} %param.33) | copy-start | bytes 9437188
  119.7 4.3 %copy-start.34 = (f32[1536]{0:T(1024)S(1)}, f32[1536]{0:T(1024)}, u32[]{:S(2)}) copy-start(f32[1536]{0:T(1024)} %param.32) | copy-start | bytes 18436
  140.2 2.8 %collective-permute-start.6 = (bf16[256,1536]{1,0:T(8,128)(2,1)}, bf16[256,1536]{1,0:T(8,128)(2,1)}, u32[]{:S(2)}, u32[]{:S(2)}) collective-permute-start(bf16[256,1536]{1,0:T(8,128)(2,1)} %dynamic-slice_convert_fusion), channel_id=1, source_target_pairs={{0,1},{1,0},{2,3},{3,2},{4,5},{5,4},{6,7},{7,6},{8,9},{9,8},{10,11... | collective-permute-start | bytes 2359304 | tf_op jit(solution)/shard_map/ppermute | solution.py:451
  144.8 19.9 %collective-permute-start.7 = (bf16[256,1536]{1,0:T(8,128)(2,1)S(1)}, bf16[256,1536]{1,0:T(8,128)(2,1)S(1)}, u32[]{:S(2)}, u32[]{:S(2)}) collective-permute-start(bf16[256,1536]{1,0:T(8,128)(2,1)S(1)} %add_convert_fusion.1), channel_id=1, source_target_pairs={{0,2},{1,3},{2,0},{3,1},{4,6},{5,7},{6,4},{7,5},{8,10},{9,11},{10,... | collective-permute-start | bytes 2359304 | tf_op jit(solution)/shard_map/ppermute | solution.py:455
  167.3 2.6 %collective-permute-start.8 = (bf16[256,1536]{1,0:T(8,128)(2,1)}, bf16[256,1536]{1,0:T(8,128)(2,1)}, u32[]{:S(2)}, u32[]{:S(2)}) collective-permute-start(bf16[256,1536]{1,0:T(8,128)(2,1)} %add_convert_fusion), channel_id=1, source_target_pairs={{0,1},{1,0},{2,3},{3,2},{4,5},{5,4},{6,7},{7,6},{8,9},{9,8},{10,11... | collective-permute-start | bytes 2359304 | tf_op jit(solution)/shard_map/ppermute | solution.py:451
  (15 other events, 13.0 us)

commit v2 on v1

v2 whole, which is shorter than its diff:
```python
import functools

import jax
import jax.numpy as jnp
from jax import lax
from jax.experimental import pallas as pl
from jax.experimental.pallas import tpu as pltpu
from jax.sharding import PartitionSpec as P

BEAMS = 8
OWNED_SLOTS = 32
SPILL = 16
PAGE_BLOCK = 16
TAIL_ROWS = 16
MIB = 1 << 20

epsilon = 1e-05
masked_score = -1e30
f32 = jnp.float32
bf16 = jnp.bfloat16

NN = (((1,), (0,)), ((), ()))
NT = (((1,), (1,)), ((), ()))
SMEM = pl.BlockSpec(memory_space=pltpu.SMEM)


def dot(a, b, dims=NN):
    return lax.dot_general(a, b, dims, preferred_element_type=f32)


def lanes(shape):
    return lax.broadcasted_iota(jnp.int32, shape, len(shape) - 1)


def sublanes(shape):
    return lax.broadcasted_iota(jnp.int32, shape, len(shape) - 2)


def in_hbm(array):
    return pltpu.with_memory_space_constraint(array, pltpu.HBM)


def in_vmem(array):
    return pltpu.with_memory_space_constraint(array, pltpu.VMEM)


def start_all(pairs, sems):
    copies = [pltpu.make_async_copy(s, t, sems.at[i]) for i, (s, t) in enumerate(pairs)]
    for copy in copies:
        copy.start()
    return copies


def fill_table(local_count, capacity, first, ids_ref, table_ref):
    groups, _, spill = ids_ref.shape
    for slot in range(groups * capacity):
        table_ref[slot] = -1

    def group(index, carry):
        rank = jnp.int32(0)
        for page in range(spill):
            local = ids_ref[index, 0, page] - first
            mine = (local >= 0) & (local < local_count)

            @pl.when(mine)
            def _():
                table_ref[index * capacity + rank] = local

            rank = rank + mine.astype(jnp.int32)
        return carry

    lax.fori_loop(0, groups, group, 0)


def query_kernel(
    capacity, request_ref, ids_ref, tokens_hbm, gain_ref, wq_hbm,
    asked_ref, table_ref, q_hbm, normed_hbm,
    tokens_ref, wq_ref, normed_ref, q_ref, sems, out_sems,
):
    steps, rows, _ = tokens_ref.shape
    span = steps * BEAMS
    local_count = rows // BEAMS
    copies = start_all([(tokens_hbm, tokens_ref), (wq_hbm, wq_ref)], sems)
    first = request_ref[0] // local_count * local_count
    fill_table(local_count, capacity, first, ids_ref, table_ref)
    copies[0].wait()
    gain = gain_ref[...]

    def pair(index, carry):
        slabs = []
        for step in range(steps):
            x = tokens_ref[step, pl.ds(pl.multiple_of(index * 16, 16), 16), :].astype(f32)
            scale = lax.rsqrt(jnp.mean(x * x, axis=-1, keepdims=True) + epsilon)
            slabs.append(x * scale * gain)
        for half in range(2):
            part = jnp.concatenate([s[half * 8 : half * 8 + 8] for s in slabs], axis=0)
            start = pl.multiple_of((index * 2 + half) * span, span)
            normed_ref[pl.ds(start, span), :] = part.astype(bf16)
        return carry

    lax.fori_loop(0, rows // 16, pair, 0, unroll=2)
    leaving = start_all([(normed_ref, normed_hbm)], out_sems)
    copies[1].wait()
    query = dot(normed_ref[...], wq_ref[...], NT).astype(bf16)
    q_ref[...] = (query.astype(f32) * 0.125).astype(bf16)
    last = pltpu.make_async_copy(q_ref, q_hbm, out_sems.at[1])
    last.start()
    for slot in range(asked_ref.shape[0]):
        local = jnp.maximum(table_ref[slot], 0)
        asked_ref[slot] = q_ref[pl.ds(pl.multiple_of(local * span, span), span), :]
    leaving[0].wait()
    last.wait()


def queries_of(request, ids, tokens, gain, w_query, capacity):
    steps, rows, width = tokens.shape
    inner = w_query.shape[0]
    total = steps * rows
    slots = ids.shape[0] * capacity
    hbm = pl.BlockSpec(memory_space=pltpu.HBM)
    vmem = pl.BlockSpec(memory_space=pltpu.VMEM)
    return pl.pallas_call(
        functools.partial(query_kernel, capacity),
        in_specs=[SMEM, SMEM, hbm, vmem, hbm],
        out_specs=[vmem, SMEM, hbm, hbm],
        out_shape=[
            jax.ShapeDtypeStruct((slots, steps * BEAMS, inner), bf16),
            jax.ShapeDtypeStruct((slots,), jnp.int32),
            pltpu.HBM((total, inner), bf16),
            pltpu.HBM((total, width), bf16),
        ],
        scratch_shapes=[
            pltpu.VMEM(tokens.shape, bf16),
            pltpu.VMEM(w_query.shape, bf16),
            pltpu.VMEM((total, width), bf16),
            pltpu.VMEM((total, inner), bf16),
            pltpu.SemaphoreType.DMA((2,)),
            pltpu.SemaphoreType.DMA((2,)),
        ],
        compiler_params=pltpu.CompilerParams(vmem_limit_bytes=16 * MIB),
        cost_estimate=pl.CostEstimate(
            flops=2 * total * width * inner, bytes_accessed=6 * MIB, transcendentals=total
        ),
        name="queries",
    )(request, ids, in_hbm(tokens), gain.reshape(1, -1), in_hbm(w_query))


def half_masks(rows):
    low = lanes((rows, 128)) < 64
    return low.astype(f32).astype(bf16), jnp.logical_not(low).astype(f32).astype(bf16)


def stacked(pair_rows, masks):
    return jnp.concatenate([pair_rows * masks[0], pair_rows * masks[1]], axis=0)


def side_by_side(values, rows):
    low = lanes((rows, 128)) < 64
    top = jnp.broadcast_to(values[:rows], (rows, 128))
    bottom = jnp.broadcast_to(values[rows:], (rows, 128))
    return jnp.where(low, top, bottom)


def absorb(state, rows, columns, top, total, numer):
    top_ref, total_ref, numer_ref = state
    old = top_ref[rows, columns]
    new = jnp.maximum(old, top)
    keep = jnp.exp(old - new)
    add = jnp.exp(top - new)
    top_ref[rows, columns] = new
    total_ref[rows, columns] = total_ref[rows, columns] * keep + total * add
    numer_ref[rows, columns] = numer_ref[rows, columns] * keep + numer * add


def history(parents_ref, q_ref, k_ref, v_ref, forget_ref, state):
    top_ref, total_ref, numer_ref = state
    transitions, rows = parents_ref.shape
    span = (transitions + 1) * BEAMS
    pack = 128 // span
    square = (128, 128)
    down, across = sublanes(square), lanes(square)
    diagonal = down == across
    columns = []
    for step in range(transitions):
        row = parents_ref[step : step + 1, :].astype(f32)
        columns.append(
            jnp.sum(jnp.where(diagonal, jnp.broadcast_to(row, square), 0.0), axis=1, keepdims=True)
        )
    lane8 = lanes((8, 128)).astype(f32)
    masks = half_masks(128)
    for group in range(rows // BEAMS // pack):
        slabs = []
        for member in range(pack):
            first = (group * pack + member) * BEAMS
            slabs.append(jnp.zeros((8, 128), f32))
            for step in range(transitions):
                wanted = columns[step][first : first + 8] + float(member * span + step * 8)
                slabs.append(jnp.where(lane8 == wanted, 1.0, 0.0))
        parent = jnp.concatenate(slabs, axis=0)
        same = diagonal.astype(f32)
        parent16 = parent.astype(bf16)
        one = same + parent
        two = dot(parent16, parent16)
        ancestors = one + dot(two.astype(bf16), one.astype(bf16))
        here = pl.ds(group * 128, 128)
        running = lax.dot_general(
            ancestors, forget_ref[here, :], NN,
            precision=lax.Precision.HIGHEST, preferred_element_type=f32,
        ).T
        hidden = jnp.where(ancestors > 0.5, 0.0, masked_score)
        for pair in range(q_ref.shape[1] // 128):
            cols = pl.ds(pair * 128, 128)
            raw = dot(stacked(q_ref[here, cols], masks), k_ref[here, cols], NT)
            low = raw[:128] + (hidden - running[2 * pair : 2 * pair + 1])
            high = raw[128:] + (hidden - running[2 * pair + 1 : 2 * pair + 2])
            scores = jnp.concatenate([low, high], axis=0)
            top = jnp.max(scores, axis=-1, keepdims=True)
            weights = jnp.exp(scores - top)
            total = jnp.sum(weights, axis=-1, keepdims=True)
            numer = dot(weights.astype(bf16), v_ref[here, cols])
            top_ref[here, cols] = side_by_side(top, 128)
            total_ref[here, cols] = side_by_side(total, 128)
            numer_ref[here, cols] = side_by_side(numer, 128)


def fresh_kernel(
    parents_ref, bias_ref, normed_hbm, wk_hbm, wv_hbm, wf_hbm, q_hbm, top_hbm, total_hbm, numer_hbm,
    log_hbm, average_hbm,
    normed_ref, wk_ref, wv_ref, wf_ref, q_ref, top_own, total_own, numer_own,
    k_ref, v_ref, forget_ref, top_ref, total_ref, numer_ref, sems, out_sems,
):
    copies = start_all(
        [
            (normed_hbm, normed_ref), (wk_hbm, wk_ref), (wv_hbm, wv_ref), (wf_hbm, wf_ref),
            (q_hbm, q_ref), (top_hbm, top_own), (total_hbm, total_own), (numer_hbm, numer_own),
        ],
        sems,
    )
    copies[0].wait()
    copies[1].wait()
    k_ref[...] = dot(normed_ref[...], wk_ref[...], NT).astype(bf16)
    copies[2].wait()
    v_ref[...] = dot(normed_ref[...], wv_ref[...], NT).astype(bf16)
    copies[3].wait()
    gate = dot(normed_ref[...], wf_ref[...], NT) + bias_ref[...]
    forget = jnp.minimum(gate, 0.0) - jnp.log1p(jnp.exp(-jnp.abs(gate)))
    forget_ref[...] = jnp.zeros_like(forget_ref)
    forget_ref[:, : forget.shape[1]] = forget
    copies[4].wait()
    state = (top_ref, total_ref, numer_ref)
    history(parents_ref, q_ref, k_ref, v_ref, forget_ref, state)
    for copy in copies[5:]:
        copy.wait()

    def join(index, carry):
        rows = pl.ds(pl.multiple_of(index * 32, 32), 32)
        absorb(state, rows, slice(None), top_own[rows, :], total_own[rows, :], numer_own[rows, :])
        total = total_ref[rows, :]
        top_ref[rows, :] = top_ref[rows, :] + jnp.log(total)
        numer_ref[rows, :] = numer_ref[rows, :] / total
        return carry

    lax.fori_loop(0, top_ref.shape[0] // 32, join, 0, unroll=2)
    for copy in start_all([(top_ref, log_hbm), (numer_ref, average_hbm)], out_sems):
        copy.wait()


def fresh(parents, bias, normed, w_key, w_value, w_forget, q, own):
    rows, inner = q.shape
    vmem = pl.BlockSpec(memory_space=pltpu.VMEM)
    hbm = pl.BlockSpec(memory_space=pltpu.HBM)
    big = [normed, w_key, w_value, w_forget.T, q, *own]
    wide = pltpu.VMEM((rows, inner), f32)
    return pl.pallas_call(
        fresh_kernel,
        in_specs=[vmem, vmem] + [hbm] * len(big),
        out_specs=[hbm] * 2,
        out_shape=[pltpu.HBM((rows, inner), f32)] * 2,
        scratch_shapes=[pltpu.VMEM(x.shape, x.dtype) for x in big]
        + [pltpu.VMEM((rows, inner), bf16)] * 2
        + [pltpu.VMEM((rows, 128), f32), wide, wide, wide]
        + [pltpu.SemaphoreType.DMA((len(big),)), pltpu.SemaphoreType.DMA((2,))],
        compiler_params=pltpu.CompilerParams(vmem_limit_bytes=24 * MIB),
        cost_estimate=pl.CostEstimate(
            flops=4 * rows * normed.shape[1] * inner, bytes_accessed=12 * MIB,
            transcendentals=8 * rows * inner,
        ),
        name="fresh",
    )(parents, bias.reshape(1, -1), *[in_hbm(x) for x in big])


def page_weights(queries, fills, keys_ref, decay_ref, scores_ref, weights_ref, tops_ref):
    span = queries[0][0].shape[0]
    masks = half_masks(span)
    lane = lanes((1, 128))
    decay = [decay_ref[head].astype(f32) for head in range(decay_ref.shape[0])]
    for page, pairs in enumerate(queries):
        valid = lane < fills[page]
        for pair, query in enumerate(pairs):
            raw = dot(stacked(query, masks), keys_ref[page, pl.ds(pair * 128, 128), :])
            for half in range(2):
                head = pair * 2 + half
                bias = jnp.where(valid, decay[head][page : page + 1], masked_score)
                scores_ref[page, pl.ds(head * span, span), :] = (
                    raw[half * span : half * span + span] + bias
                )
    for page in range(len(queries)):
        for head in range(decay_ref.shape[0]):
            rows = pl.ds(head * span, span)
            scores = scores_ref[page, rows, :]
            top = jnp.broadcast_to(jnp.max(scores, axis=-1, keepdims=True), scores.shape)
            tops_ref[page, rows, :] = top
            weights = jnp.exp(scores - top)
            weights_ref[page, rows, :] = weights.astype(bf16)
            scores_ref[page, rows, :] = jnp.broadcast_to(
                jnp.sum(weights, axis=-1, keepdims=True), scores.shape
            )


def page_sums(page, pair, span, values_ref, scores_ref, weights_ref, tops_ref):
    low = lanes((span, 128)) < 64
    first, second = pl.ds(pair * 2 * span, span), pl.ds((pair * 2 + 1) * span, span)
    numer = dot(
        weights_ref[page, pl.ds(pair * 2 * span, 2 * span), :],
        values_ref[page, pl.ds(pair * 128, 128), :],
        NT,
    )
    top = jnp.where(low, tops_ref[page, first, :], tops_ref[page, second, :])
    total = jnp.where(low, scores_ref[page, first, :], scores_ref[page, second, :])
    return top, total, jnp.where(low, numer[:span], numer[span:])


def page_scratch(pages, span, heads):
    rows = span * heads
    return [
        pltpu.VMEM((pages, rows, 128), f32),
        pltpu.VMEM((pages, rows, 128), bf16),
        pltpu.VMEM((pages, rows, 128), f32),
    ]


def own_kernel(
    request_ref, fill_ref, q_ref, keys_ref, values_ref, decay_ref,
    top_ref, total_ref, numer_ref, *scratch,
):
    state = (top_ref, total_ref, numer_ref)
    block = pl.program_id(0)
    span = scratch[0].shape[1] // decay_ref.shape[0]
    local_count = q_ref.shape[0] // span
    pairs = q_ref.shape[1] // 128

    @pl.when(block == 0)
    def _():
        top_ref[...] = jnp.full_like(top_ref, masked_score)
        total_ref[...] = jnp.zeros_like(total_ref)
        numer_ref[...] = jnp.zeros_like(numer_ref)

    places, queries, fills = [], [], []
    for page in range(PAGE_BLOCK):
        index = block * PAGE_BLOCK + page
        local = lax.rem(request_ref[index], local_count)
        rows = pl.ds(pl.multiple_of(local * span, span), span)
        places.append(rows)
        queries.append([q_ref[rows, pl.ds(pair * 128, 128)] for pair in range(pairs)])
        fills.append(fill_ref[index])
    page_weights(queries, fills, keys_ref, decay_ref, *scratch)
    for page, rows in enumerate(places):
        for pair in range(pairs):
            sums = page_sums(page, pair, span, values_ref, *scratch)
            absorb(state, rows, pl.ds(pair * 128, 128), *sums)


def whole(array):
    return pl.BlockSpec(array.shape, lambda *_: (0,) * array.ndim)


def page_specs(keys, decay, first):
    shift = first // PAGE_BLOCK
    pool = pl.BlockSpec((PAGE_BLOCK,) + keys.shape[1:], lambda i: (i + shift, 0, 0))
    return [
        pool,
        pool,
        pl.BlockSpec((decay.shape[0], PAGE_BLOCK, decay.shape[2]), lambda i: (0, i + shift, 0)),
    ]


def page_cost(pages, keys, rows):
    inner, length = keys.shape[1:]
    return pl.CostEstimate(
        flops=pages * rows * inner * length * 8,
        bytes_accessed=pages * inner * length * 4,
        transcendentals=pages * rows * inner * length // 64,
    )


def own_pages(request, fill, q, keys, values, decay, span):
    out_spec = pl.BlockSpec(q.shape, lambda *_: (0, 0))
    return pl.pallas_call(
        own_kernel,
        grid=(OWNED_SLOTS // PAGE_BLOCK,),
        in_specs=[SMEM, SMEM, whole(q)] + page_specs(keys, decay, 0),
        out_specs=[out_spec] * 3,
        out_shape=[pltpu.HBM(q.shape, f32)] * 3,
        scratch_shapes=page_scratch(PAGE_BLOCK, span, decay.shape[0]),
        compiler_params=pltpu.CompilerParams(vmem_limit_bytes=24 * MIB),
        cost_estimate=page_cost(OWNED_SLOTS, keys, 64),
        name="own_pages",
    )(request, fill, in_hbm(q), in_hbm(keys), in_hbm(values), decay)


def hosted_kernel(
    local_count, capacity, request_ref, fill_ref, q_ref, keys_ref, values_ref, decay_ref,
    out_ref, tail_ref, count_ref, *scratch,
):
    span, inner = q_ref.shape[1:]
    pairs = inner // 128
    heads = decay_ref.shape[0]
    groups = out_ref.shape[0]
    out_ref[...] = jnp.zeros_like(out_ref)
    tail_ref[...] = jnp.zeros_like(tail_ref)
    for owner in range(groups):
        count_ref[owner] = 0
    places, queries, fills = [], [], []
    for page in range(SPILL):
        owner = request_ref[OWNED_SLOTS + page] // local_count
        rank = count_ref[owner]
        count_ref[owner] = rank + 1
        places.append((owner, rank))
        slot = owner * capacity + rank
        queries.append([q_ref[slot, :, pl.ds(pair * 128, 128)] for pair in range(pairs)])
        fills.append(fill_ref[OWNED_SLOTS + page])
    page_weights(queries, fills, keys_ref, decay_ref, *scratch)
    scores_ref, _, tops_ref = scratch
    lane = lanes((span, 128))
    for page, (owner, rank) in enumerate(places):
        here = pl.ds(pl.multiple_of(rank * span, span), span)
        for pair in range(pairs):
            _, total, numer = page_sums(page, pair, span, values_ref, *scratch)
            out_ref[owner, here, pl.ds(pair * 128, 128)] = (numer / total).astype(bf16)
        tail = tail_ref[owner]
        base = rank * (3 * heads)
        for head in range(heads):
            rows = pl.ds(head * span, span)
            rest = tops_ref[page, rows, :] + jnp.log(scores_ref[page, rows, :])
            for piece in range(3):
                part = rest.astype(bf16).astype(f32)
                rest = rest - part
                tail = jnp.where(lane == base + piece * heads + head, part, tail)
        tail_ref[owner] = tail
    first = capacity * span
    for owner in range(groups):
        tail = tail_ref[owner].astype(bf16)
        for part in range(span // TAIL_ROWS):
            out_ref[owner, first : first + TAIL_ROWS, part * 128 : part * 128 + 128] = tail[
                part * TAIL_ROWS : part * TAIL_ROWS + TAIL_ROWS
            ]


def hosted_pages(request, fill, asked_rows, keys, values, decay, groups, capacity, local_count):
    count, span, inner = asked_rows.shape
    out_shape = (groups, capacity * span + TAIL_ROWS, inner)
    return pl.pallas_call(
        functools.partial(hosted_kernel, local_count, capacity),
        grid=(1,),
        in_specs=[SMEM, SMEM, whole(asked_rows)] + page_specs(keys, decay, OWNED_SLOTS),
        out_specs=pl.BlockSpec(out_shape, lambda *_: (0, 0, 0)),
        out_shape=jax.ShapeDtypeStruct(out_shape, bf16),
        scratch_shapes=[pltpu.VMEM((groups, span, 128), f32), pltpu.SMEM((groups,), jnp.int32)]
        + page_scratch(SPILL, span, decay.shape[0]),
        compiler_params=pltpu.CompilerParams(vmem_limit_bytes=24 * MIB),
        cost_estimate=page_cost(SPILL, keys, 64),
        name="hosted_pages",
    )(request, fill, asked_rows, in_hbm(keys), in_hbm(values), decay)


def merge_kernel(
    capacity, steps, table_ref, back_ref, log_hbm, average_hbm, out_ref,
    top_ref, total_ref, numer_ref, sems,
):
    groups, _, inner = back_ref.shape
    span = steps * BEAMS
    heads = inner // 64
    state = (top_ref, total_ref, numer_ref)
    copies = start_all([(log_hbm, top_ref), (average_hbm, numer_ref)], sems)
    total_ref[...] = jnp.ones_like(total_ref)
    source, target = sublanes((128, inner)), lanes((128, inner)) // 64
    spread = []
    for rank in range(capacity):
        hit = source < 0
        for piece in range(3):
            hit = hit | (source == target + (rank * 3 + piece) * heads)
        spread.append(hit.astype(f32).astype(bf16))
    for copy in copies:
        copy.wait()

    for owner in range(groups):
        first = capacity * span
        for rank in range(capacity):
            local = table_ref[owner * capacity + rank]

            @pl.when(local >= 0)
            def _():
                tail = jnp.concatenate(
                    [
                        back_ref[owner, first : first + TAIL_ROWS, part * 128 : part * 128 + 128]
                        for part in range(span // TAIL_ROWS)
                    ],
                    axis=0,
                )
                top = dot(tail, spread[rank])
                average = back_ref[owner, rank * span : rank * span + span, :].astype(f32)
                rows = pl.ds(pl.multiple_of(local * span, span), span)
                absorb(state, rows, slice(None), top, 1.0, average)

    for index in range(top_ref.shape[0] // (2 * span)):
        parts = []
        for half in range(2):
            rows = slice((index * 2 + half) * span, (index * 2 + half + 1) * span)
            parts.append(numer_ref[rows, :] / total_ref[rows, :])
        for step in range(steps):
            both = jnp.concatenate([p[step * 8 : step * 8 + 8] for p in parts], axis=0)
            out_ref[step, index * 16 : index * 16 + 16, :] = both.astype(bf16)


def merge(table, back, logs, averages, steps, capacity):
    rows, inner = logs.shape
    vmem = pl.BlockSpec(memory_space=pltpu.VMEM)
    hbm = pl.BlockSpec(memory_space=pltpu.HBM)
    return pl.pallas_call(
        functools.partial(merge_kernel, capacity, steps),
        in_specs=[SMEM, vmem, hbm, hbm],
        out_shape=jax.ShapeDtypeStruct((steps, rows // steps, inner), bf16),
        scratch_shapes=[pltpu.VMEM((rows, inner), f32)] * 3 + [pltpu.SemaphoreType.DMA((2,))],
        compiler_params=pltpu.CompilerParams(vmem_limit_bytes=16 * MIB),
        cost_estimate=pl.CostEstimate(
            flops=40 * rows * inner, bytes_accessed=8 * MIB, transcendentals=4 * rows * inner
        ),
        name="merge",
    )(table, back, in_hbm(logs), in_hbm(averages))


def mix_kernel(
    first, att0, att1, att2, att3, w0, w1, w2, w3, tokens_hbm, gain_ref,
    residual_out, normed_ref, residual_ref, tokens_ref, sems,
):
    rows, width = residual_ref.shape
    half = rows // 2
    core = lax.axis_index("head") % 2
    near = pl.ds(pl.multiple_of(core * half, half), half)
    copies = start_all([(tokens_hbm.at[first : first + rows], tokens_ref)], sems)
    for start in range(0, width, 512):
        cols = slice(start, start + 512)
        mixed = (dot(att0[...], w0[:, cols]) + dot(att1[...], w1[:, cols])) + (
            dot(att2[...], w2[:, cols]) + dot(att3[...], w3[:, cols])
        )
        residual_ref[:, cols] = mixed
    copies[0].wait()
    gain = gain_ref[...]

    def norm(index, carry):
        here = pl.ds(pl.multiple_of(index * 32, 32), 32)
        x = tokens_ref[here, :].astype(f32) + residual_ref[here, :]
        residual_ref[here, :] = x
        scale = lax.rsqrt(jnp.mean(x * x, axis=-1, keepdims=True) + epsilon)
        normed_ref[here, :] = (x * scale * gain).astype(bf16)
        return carry

    lax.fori_loop(0, rows // 32, norm, 0, unroll=2)
    residual_out[...] = residual_ref[near, :]


def mix(first, attended, weights, tokens, gain):
    rows, inner = attended[0].shape
    width = tokens.shape[1]
    vmem = pl.BlockSpec(memory_space=pltpu.VMEM)
    return pl.pallas_call(
        functools.partial(mix_kernel, first),
        in_specs=[vmem] * 8 + [pl.BlockSpec(memory_space=pltpu.HBM), vmem],
        out_specs=[vmem] * 2,
        out_shape=[
            jax.ShapeDtypeStruct((rows // 2, width), f32),
            pltpu.VMEM((rows, width), bf16),
        ],
        scratch_shapes=[
            pltpu.VMEM((rows, width), f32),
            pltpu.VMEM((rows, width), bf16),
            pltpu.SemaphoreType.DMA((1,)),
        ],
        compiler_params=pltpu.CompilerParams(vmem_limit_bytes=10 * MIB),
        cost_estimate=pl.CostEstimate(
            flops=8 * rows * width * inner, bytes_accessed=8 * MIB, transcendentals=rows
        ),
        name="mix",
    )(*attended, *[in_vmem(w) for w in weights], in_hbm(tokens), gain.reshape(1, -1))


def ffn_kernel(normed_ref, gate_ref, up_ref, down_ref, mine_ref, other_ref, hidden_ref, sums_ref):
    rows, width = normed_ref.shape
    half = rows // 2
    core = lax.axis_index("head") % 2
    near = pl.ds(pl.multiple_of(core * half, half), half)
    away = pl.ds(pl.multiple_of((1 - core) * half, half), half)
    for first in range(0, gate_ref.shape[1], 256):
        cols = slice(first, first + 256)
        gate = dot(normed_ref[...], gate_ref[:, cols])
        up = dot(normed_ref[...], up_ref[:, cols])
        hidden_ref[:, cols] = (gate / (1.0 + jnp.exp(-gate)) * up).astype(bf16)
    for first in range(0, width, 512):
        cols = slice(first, first + 512)
        sums_ref[...] = dot(hidden_ref[...], down_ref[:, cols])
        mine_ref[:, cols] = sums_ref[near, :]
        other_ref[:, cols] = sums_ref[away, :].astype(bf16)


def ffn(normed, w_gate, w_up, w_down):
    rows, width = normed.shape
    hidden = w_gate.shape[1]
    vmem = pl.BlockSpec(memory_space=pltpu.VMEM)
    return pl.pallas_call(
        ffn_kernel,
        in_specs=[vmem] * 4,
        out_specs=[vmem] * 2,
        out_shape=[
            jax.ShapeDtypeStruct((rows // 2, width), f32),
            jax.ShapeDtypeStruct((rows // 2, width), bf16),
        ],
        scratch_shapes=[pltpu.VMEM((rows, hidden), bf16), pltpu.VMEM((rows, 512), f32)],
        compiler_params=pltpu.CompilerParams(vmem_limit_bytes=10 * MIB),
        cost_estimate=pl.CostEstimate(
            flops=6 * rows * width * hidden, bytes_accessed=10 * MIB, transcendentals=rows * hidden
        ),
        name="ffn",
    )(in_vmem(normed), in_vmem(w_gate), in_vmem(w_up), in_vmem(w_down))


def finish_kernel(*refs):
    parts, out_ref = refs[:-1], refs[-1]
    core = lax.axis_index("head") % 2
    for index, part in enumerate(parts):
        step = index // 2 * 2 + (core if index % 2 == 0 else 1 - core)
        out_ref[step] = part[...]


def finish(parts):
    vmem = pl.BlockSpec(memory_space=pltpu.VMEM)
    return pl.pallas_call(
        finish_kernel,
        in_specs=[vmem] * len(parts),
        out_specs=vmem,
        out_shape=jax.ShapeDtypeStruct((len(parts),) + parts[0].shape, parts[0].dtype),
        compiler_params=pltpu.CompilerParams(vmem_limit_bytes=12 * MIB),
        name="finish",
    )(*parts)


def swap_core(value):
    return lax.ppermute(value, "head", [(i, i ^ 1) for i in range(4)])


def swap_chip(value):
    return lax.ppermute(value, "head", [(i, i ^ 2) for i in range(4)])


def shards(
    tokens, parents, page_request, page_fill, keys_pool, values_pool, decay_pool,
    gain_attn, w_query, w_key, w_value, w_forget, forget_bias, w_out,
    gain_ffn, w_gate, w_up, w_down,
):
    steps, rows, width = tokens.shape
    inner = w_query.shape[0]
    local_count = rows // BEAMS
    span = steps * BEAMS
    groups = lax.axis_size("group")
    capacity = (SPILL + groups - 2) // (groups - 1)
    decay = decay_pool.transpose(1, 0, 2)

    hosted = page_request[OWNED_SLOTS:]
    ids = lax.all_to_all(
        jnp.broadcast_to(hosted, (groups, 1, SPILL)), "group", split_axis=0, concat_axis=0, tiled=True
    )
    w_out_far = swap_chip(w_out)
    asked, table, q, normed = queries_of(page_request, ids, tokens, gain_attn, w_query, capacity)
    asked_rows = lax.all_to_all(
        asked.reshape(groups, capacity * span, inner),
        "group", split_axis=0, concat_axis=0, tiled=True,
    ).reshape(groups * capacity, span, inner)
    own = own_pages(page_request, page_fill, q, keys_pool, values_pool, decay, span)
    asked_rows, own = lax.optimization_barrier((asked_rows, own))
    payload = hosted_pages(
        page_request, page_fill, asked_rows, keys_pool, values_pool, decay, groups, capacity, local_count
    )
    payload, normed = lax.optimization_barrier((payload, normed))
    back = lax.all_to_all(payload, "group", split_axis=0, concat_axis=0, tiled=True)
    logs, averages = fresh(parents, forget_bias, normed, w_key, w_value, w_forget, q, own)
    weights = [w_out, swap_core(w_out), w_out_far, swap_core(w_out_far)]
    attended = merge(table, back, logs, averages, steps, capacity)

    flat = tokens.reshape(steps * rows, width)
    heres = [attended[step : step + 2].reshape(2 * rows, inner) for step in range(0, steps, 2)]
    fars = [swap_chip(here) for here in heres]
    done = [None, None]
    residual, mine, other, chip = [[None, None] for _ in range(4)]
    for index, (here, far) in enumerate(zip(heres, fars)):
        gathered = [here, swap_core(here), far, swap_core(far)]
        if index:
            gathered, other[0] = lax.optimization_barrier((gathered, other[0]))
        residual[index], normed = mix(2 * index * rows, gathered, weights, flat, gain_ffn)
        if index:
            chip[0] = (mine[0] + swap_core(other[0]).astype(f32)).astype(bf16)
            chip[0], normed = lax.optimization_barrier((chip[0], normed))
        mine[index], other[index] = ffn(normed, w_gate, w_up, w_down)
    chip[1] = (mine[1] + swap_core(other[1]).astype(f32)).astype(bf16)
    parts = []
    for index in range(2):
        both = chip[index].astype(f32) + swap_chip(chip[index]).astype(f32)
        done = (residual[index] + both).astype(bf16)
        parts.extend([done, swap_core(done)])
    return finish(parts)


def solution(mesh):
    return jax.shard_map(
        shards,
        mesh=mesh,
        in_specs=(
            P(None, "group", None),
            P(None, "group"),
            P("group"),
            P("group"),
            P("group", "head", None),
            P("group", "head", None),
            P("group", "head", None),
            P(),
            P("head", None),
            P("head", None),
            P("head", None),
            P(None, "head"),
            P("head"),
            P("head", None),
            P(),
            P(None, "head"),
            P(None, "head"),
            P("head", None),
        ),
        out_specs=P(None, "group", None),
        check_vma=False,
    )
```

time: 174 us -> 119 us (0.68)
  local copies, waits for them, and re-layouts: 37.9 us -> 2.77 us
  matrix products: 25.1 us -> 0 us
  Pallas kernels: 35.4 us -> 49.7 us
  other arithmetic: 7.82 us -> 0.46 us
    unnamed x72 -> x22, local copies, waits for them, and re-layouts: 32.4 us -> 0.7 us
    dot_general x6 -> x0, matrix products: 25.1 us -> none  [dot(): return lax.dot_general(a, b, dims, preferred_element_type=f32)]
    pallas_call x4 -> x8, Pallas kernels: 15.1 us -> 37.5 us  [the longest x1 11 us: fresh(): pl.pallas_call(fresh_kernel, in_specs=[vmem, vmem] + [hbm] * len(big), ou...]
    pallas_call x1, Pallas kernels: 16.2 us -> 6.88 us  [own_pages(): pl.pallas_call(own_kernel, grid=(OWNED_SLOTS // PAGE_BLOCK,), in_specs=[S...]
    convert_element_type x2 -> x4, other arithmetic: 4.43 us -> 0.46 us  [the longest x2 0.29 us: shards(): done = (residual[index] + both).astype(bf16)]
    ppermute x6 -> x10, waiting for transfers between devices: 4.89 us -> 1.88 us  [swap_core(): return lax.ppermute(value, 'head', [(i, i ^ 1) for i in range(4)])]
    all_to_all x3, waiting for transfers between devices: 12.5 us -> 14.9 us  [the longest x1 6.21 us: shards(): lax.all_to_all(asked.reshape(groups, capacity * span, inner), 'group', sp...]
    all_to_all x3, starting transfers between devices: 17.5 us -> 15 us  [the longest x1 7.28 us: shards(): lax.all_to_all(jnp.broadcast_to(hosted, (groups, 1, SPILL)), 'group', spl...]
  transfers between devices with their start and end apart: 12 -> 18, of which waited for: 5 -> 10; matrix products, arithmetic and copies ran while one was open for 6% -> 1% of each run, Pallas kernels for 19% -> 34%
where the time goes in v2:
time: 119 us; the launch traced here: 118 us
  Pallas kernels  49.7 us (42%)
  waiting for transfers between devices  42 us (35%)
  starting transfers between devices  23.2 us (19%)
  local copies, waits for them, and re-layouts  2.77 us (2%)
    ppermute x5, waiting for transfers between devices, swap_chip(): return lax.ppermute(value, 'head', [(i, i ^ 2) for i in range(4)])  25.2 us
    pallas_call x1, Pallas kernels, fresh(): pl.pallas_call(fresh_kernel, in_specs=[vmem, vmem] + [hbm] * len(big), ou...  11 us
    pallas_call x2, Pallas kernels, mix(): pl.pallas_call(functools.partial(mix_kernel, first), in_specs=[vmem] * 8...  9.32 us
    all_to_all x1, starting transfers between devices, shards(): lax.all_to_all(jnp.broadcast_to(hosted, (groups, 1, SPILL)), 'group', spl...  7.28 us
    pallas_call x1, Pallas kernels, own_pages(): pl.pallas_call(own_kernel, grid=(OWNED_SLOTS // PAGE_BLOCK,), in_specs=[S...  6.88 us
    ppermute x5, starting transfers between devices, swap_chip(): return lax.ppermute(value, 'head', [(i, i ^ 2) for i in range(4)])  6.72 us
    all_to_all x1, waiting for transfers between devices, shards(): lax.all_to_all(asked.reshape(groups, capacity * span, inner), 'group', sp...  6.21 us
    all_to_all x1, waiting for transfers between devices, shards(): lax.all_to_all(jnp.broadcast_to(hosted, (groups, 1, SPILL)), 'group', spl...  5.68 us
  transfers between devices with their start and end apart: 18, of which 10 were waited for; matrix products, arithmetic and copies ran while one was open for 1% of the time, Pallas kernels for 34%

profile of v2, /device:TPU:0, one launch (start us, length us, event | category | flops | bytes accessed | tf_op | source)
XLA Modules:
  0.0 118.5 jit_solution(5327168918993231968)
XLA Ops:
  0.0 0.7 slice.9
  0.7 0.6 broadcast_in_dim.3
  1.3 7.3 %all-to-all-start = ((s32[8,1,16]{2,1,0:T(1,128)}), s32[8,1,16]{2,1,0:T(1,128)S(1)}, u32[]{:S(2)}, u32[]{:S(2)}) async-start(s32[8,1,16]{2,1,0:T(1,128)} %broadcast_in_dim.3), calls=%async_computation | async-start | bytes 8192 | tf_op jit(solution)/shard_map/all_to_all | solution.py:678
  8.6 0.7 reshape.25.gain_ref
  9.3 5.7 %all-to-all-done.ids_ref = s32[8,1,16]{2,1,0:T(1,128)S(1)} async-done(((s32[8,1,16]{2,1,0:T(1,128)}), s32[8,1,16]{2,1,0:T(1,128)S(1)}, u32[]{:S(2)}, u32[]{:S(2)}) %all-to-all-start) | async-done | bytes 544 | tf_op jit(solution)/shard_map/all_to_all | solution.py:678
  15.0 0.7 copy-done.5
  15.7 5.4 %queries.1 = (bf16[24,32,384]{2,1,0:T(8,128)(2,1)}, s32[24]{0:T(128)S(1)}, bf16[512,384]{1,0:T(8,128)(2,1)}, bf16[512,1536]{1,0:T(8,128)(2,1)}) custom-call(s32[48]{0:T(128)S(1)} %copy-done.5, s32[8,1,16]{2,1,0:T(1,128)S(1)} %all-to-all-done.ids_ref, bf16[4,128,1536]{2,1,0:T(8,128)(2,1)} %tokens_hbm.1, f32[1,1536]{1,0:T(1,128)S(1)} %reshape.25.gain_ref, ...), custom_call_target="tpu_custom_call" | custom-call | flops 603979776 | bytes 6291456 | tf_op jit(solution)/shard_map/queries/pallas_call | solution.py:122
  21.0 3.5 %all-to-all-start.1 = ((bf16[8,96,384]{2,1,0:T(8,128)(2,1)}), bf16[8,96,384]{2,1,0:T(8,128)(2,1)S(1)}, u32[]{:S(2)}, u32[]{:S(2)}) async-start(bf16[8,96,384]{2,1,0:T(8,128)(2,1)} %bitcast), calls=%async_computation.1 | async-start | bytes 1179648 | tf_op jit(solution)/shard_map/all_to_all | solution.py:683
  24.6 1.6 %collective-permute-start.4 = (bf16[384,1536]{1,0:T(8,128)(2,1)S(1)}, bf16[384,1536]{1,0:T(8,128)(2,1)S(1)}, u32[]{:S(2)}, u32[]{:S(2)}) collective-permute-start(bf16[384,1536]{1,0:T(8,128)(2,1)S(1)} %copy-done.3), channel_id=1, source_target_pairs={{0,2},{1,3},{2,0},{3,1},{4,6},{5,7},{6,4},{7,5},{8,10},{9,11},{10,... | collective-permute-start | bytes 3538952 | tf_op jit(solution)/shard_map/ppermute | solution.py:661
  26.2 6.9 %own_pages.1 = (f32[512,384]{1,0:T(8,128)}, f32[512,384]{1,0:T(8,128)}, f32[512,384]{1,0:T(8,128)}) custom-call(s32[48]{0:T(128)S(1)} %copy-done.6, s32[48]{0:T(128)S(1)} %copy-done.8, bf16[512,384]{1,0:T(8,128)(2,1)} %get-tuple-element.37.q_ref.q_hbm, bf16[48,384,128]{2,1,0:T(8,128)(2,1)} %keys_ref.3, bf16[48,384,128]{2,1,0:T(8,128)(2,1)} %values_ref.3, ...), custom_call_target="tpu_custom_call" | custom-call | flops 805306368 | bytes 6291456 | tf_op jit(solution)/shard_map/own_pages/pallas_call | solution.py:398
  33.1 6.2 %all-to-all-done.1 = bf16[8,96,384]{2,1,0:T(8,128)(2,1)S(1)} async-done(((bf16[8,96,384]{2,1,0:T(8,128)(2,1)}), bf16[8,96,384]{2,1,0:T(8,128)(2,1)S(1)}, u32[]{:S(2)}, u32[]{:S(2)}) %all-to-all-start.1) | async-done | bytes 589856 | tf_op jit(solution)/shard_map/all_to_all | solution.py:683
  39.3 4.8 %hosted_pages.1 = bf16[8,112,384]{2,1,0:T(8,128)(2,1)} custom-call(s32[48]{0:T(128)S(1)} %copy-done.6, s32[48]{0:T(128)S(1)} %copy-done.8, bf16[24,32,384]{2,1,0:T(8,128)(2,1)S(1)} %bitcast.8, bf16[48,384,128]{2,1,0:T(8,128)(2,1)} %keys_ref.3, bf16[48,384,128]{2,1,0:T(8,128)(2,1)} %values_ref.3, bf16[6,48,128]{2,1,0:T(8,128)(2,1)S(1)} %bitcast.16), custom_call_target="tpu_custom_call" | custom-call | flops 402653184 | bytes 3145728 | tf_op jit(solution)/shard_map/hosted_pages/pallas_call | solution.py:462
  44.1 4.2 %all-to-all-start.2 = ((bf16[8,112,384]{2,1,0:T(8,128)(2,1)}), bf16[8,112,384]{2,1,0:T(8,128)(2,1)}, u32[]{:S(2)}, u32[]{:S(2)}) async-start(bf16[8,112,384]{2,1,0:T(8,128)(2,1)} %hosted_pages.1), calls=%async_computation.2 | async-start | bytes 1376256 | tf_op jit(solution)/shard_map/all_to_all | solution.py:693
  48.4 2.6 %collective-permute-done.4.w2 = bf16[384,1536]{1,0:T(8,128)(2,1)S(1)} collective-permute-done((bf16[384,1536]{1,0:T(8,128)(2,1)S(1)}, bf16[384,1536]{1,0:T(8,128)(2,1)S(1)}, u32[]{:S(2)}, u32[]{:S(2)}) %collective-permute-start.4) | collective-permute-done | bytes 1179680 | tf_op jit(solution)/shard_map/ppermute | solution.py:661
  51.0 11.0 %fresh.1 = (f32[512,384]{1,0:T(8,128)}, f32[512,384]{1,0:T(8,128)}) custom-call(s32[3,128]{1,0:T(4,128)S(1)} %copy-done.7, f32[1,6]{1,0:T(1,128)S(1)} %bitcast.17, bf16[512,1536]{1,0:T(8,128)(2,1)} %get-tuple-element.44.normed_hbm, bf16[384,1536]{1,0:T(8,128)(2,1)} %wk_hbm.1, bf16[384,1536]{1,0:T(8,128)(2,1)} %wv_hbm.1, bf16[6,1536]{1,0:T(8,128)(2,1)} %bitcast.20, ...), custom_call_target="tpu_custom_call" | custom-call | flops 1207959552 | bytes 12582912 | tf_op jit(solution)/shard_map/fresh/pallas_call | solution.py:274
  62.0 3.1 %all-to-all-done.2.back_ref = bf16[8,112,384]{2,1,0:T(8,128)(2,1)} async-done(((bf16[8,112,384]{2,1,0:T(8,128)(2,1)}), bf16[8,112,384]{2,1,0:T(8,128)(2,1)}, u32[]{:S(2)}, u32[]{:S(2)}) %all-to-all-start.2) | async-done | bytes 688160 | tf_op jit(solution)/shard_map/all_to_all | solution.py:693
  65.1 5.4 %merge.1 = bf16[4,128,384]{2,1,0:T(8,128)(2,1)S(1)} custom-call(s32[24]{0:T(128)S(1)} %get-tuple-element.35.table_ref, bf16[8,112,384]{2,1,0:T(8,128)(2,1)} %all-to-all-done.2.back_ref, f32[512,384]{1,0:T(8,128)} %get-tuple-element.48.log_hbm, f32[512,384]{1,0:T(8,128)} %get-tuple-element.49.average_hbm), custom_call_target="tpu_custom_call" | custom-call | flops 7864320 | bytes 8388608 | tf_op jit(solution)/shard_map/merge/pallas_call | solution.py:529
  70.5 1.6 %collective-permute-start.1 = (bf16[256,384]{1,0:T(8,128)(2,1)S(1)}, bf16[256,384]{1,0:T(8,128)(2,1)S(1)}, u32[]{:S(2)}, u32[]{:S(2)}) collective-permute-start(bf16[256,384]{1,0:T(8,128)(2,1)S(1)} %bitcast.12), channel_id=1, source_target_pairs={{0,2},{1,3},{2,0},{3,1},{4,6},{5,7},{6,4},{7,5},{8,10},{9,11},{10,... | collective-permute-start | bytes 589832 | tf_op jit(solution)/shard_map/ppermute | solution.py:661
  72.6 4.7 %collective-permute-done.1.att2 = bf16[256,384]{1,0:T(8,128)(2,1)S(1)} collective-permute-done((bf16[256,384]{1,0:T(8,128)(2,1)S(1)}, bf16[256,384]{1,0:T(8,128)(2,1)S(1)}, u32[]{:S(2)}, u32[]{:S(2)}) %collective-permute-start.1) | collective-permute-done | bytes 196640 | tf_op jit(solution)/shard_map/ppermute | solution.py:661
  77.4 0.6 collective-permute-start.6
  77.9 1.5 %collective-permute-done.7.att2 = bf16[256,384]{1,0:T(8,128)(2,1)S(1)} collective-permute-done((bf16[256,384]{1,0:T(8,128)(2,1)S(1)}, bf16[256,384]{1,0:T(8,128)(2,1)S(1)}, u32[]{:S(2)}, u32[]{:S(2)}) %collective-permute-start.7) | collective-permute-done | bytes 196640 | tf_op jit(solution)/shard_map/ppermute | solution.py:661
  79.5 4.7 %mix.2 = (f32[128,1536]{1,0:T(8,128)S(1)}, bf16[256,1536]{1,0:T(8,128)(2,1)S(1)}) custom-call(bf16[256,384]{1,0:T(8,128)(2,1)S(1)} %bitcast.14, bf16[256,384]{1,0:T(8,128)(2,1)S(1)} %collective-permute-done.att1, bf16[256,384]{1,0:T(8,128)(2,1)S(1)} %collective-permute-done.1.att2, bf16[256,384]{1,0:T(8,128)(2,1)S(1)} %collective-permute-done.2.att3, ...), custom_call_target="tpu_custom_call" | custom-call | flops 1207959552 | bytes 8388608 | tf_op jit(solution)/shard_map/mix/pallas_call | solution.py:576
  84.3 2.8 %ffn.2 = (f32[128,1536]{1,0:T(8,128)S(1)}, bf16[128,1536]{1,0:T(8,128)(2,1)S(1)}) custom-call(bf16[256,1536]{1,0:T(8,128)(2,1)S(1)} %get-tuple-element.51.normed_ref, bf16[1536,1024]{1,0:T(8,128)(2,1)S(1)} %copy-done, bf16[1536,1024]{1,0:T(8,128)(2,1)S(1)} %copy-done.1, bf16[1024,1536]{1,0:T(8,128)(2,1)S(1)} %copy-done.2), custom_call_target="tpu_custom_call" | custom-call | flops 2415919104 | bytes 10485760 | tf_op jit(solution)/shard_map/ffn/pallas_call | solution.py:619
  87.1 0.6 collective-permute-start.9
  87.7 4.6 %mix.3 = (f32[128,1536]{1,0:T(8,128)S(1)}, bf16[256,1536]{1,0:T(8,128)(2,1)S(1)}) custom-call(bf16[256,384]{1,0:T(8,128)(2,1)S(1)} %bitcast.11, bf16[256,384]{1,0:T(8,128)(2,1)S(1)} %collective-permute-done.6.att1, bf16[256,384]{1,0:T(8,128)(2,1)S(1)} %collective-permute-done.7.att2, bf16[256,384]{1,0:T(8,128)(2,1)S(1)} %collective-permute-done.8.att3, ...), custom_call_target="tpu_custom_call" | custom-call | flops 1207959552 | bytes 8388608 | tf_op jit(solution)/shard_map/mix/pallas_call | solution.py:576
  92.4 2.8 %ffn.3 = (f32[128,1536]{1,0:T(8,128)S(1)}, bf16[128,1536]{1,0:T(8,128)(2,1)S(1)}) custom-call(bf16[256,1536]{1,0:T(8,128)(2,1)S(1)} %get-tuple-element.62.normed_ref, bf16[1536,1024]{1,0:T(8,128)(2,1)S(1)} %copy-done, bf16[1536,1024]{1,0:T(8,128)(2,1)S(1)} %copy-done.1, bf16[1024,1536]{1,0:T(8,128)(2,1)S(1)} %copy-done.2), custom_call_target="tpu_custom_call" | custom-call | flops 2415919104 | bytes 10485760 | tf_op jit(solution)/shard_map/ffn/pallas_call | solution.py:619
  95.3 1.5 %collective-permute-start.10 = (bf16[128,1536]{1,0:T(8,128)(2,1)S(1)}, bf16[128,1536]{1,0:T(8,128)(2,1)S(1)}, u32[]{:S(2)}, u32[]{:S(2)}) collective-permute-start(bf16[128,1536]{1,0:T(8,128)(2,1)S(1)} %add_convert_fusion.3), channel_id=1, source_target_pairs={{0,2},{1,3},{2,0},{3,1},{4,6},{5,7},{6,4},{7,5},{8,10},{9,11},{10,... | collective-permute-start | bytes 1179656 | tf_op jit(solution)/shard_map/ppermute | solution.py:661
  97.1 1.5 %collective-permute-start.13 = (bf16[128,1536]{1,0:T(8,128)(2,1)S(1)}, bf16[128,1536]{1,0:T(8,128)(2,1)S(1)}, u32[]{:S(2)}, u32[]{:S(2)}) collective-permute-start(bf16[128,1536]{1,0:T(8,128)(2,1)S(1)} %add_convert_fusion.1), channel_id=1, source_target_pairs={{0,2},{1,3},{2,0},{3,1},{4,6},{5,7},{6,4},{7,5},{8,10},{9,11},{10,... | collective-permute-start | bytes 1179656 | tf_op jit(solution)/shard_map/ppermute | solution.py:661
  98.6 8.6 %collective-permute-done.10 = bf16[128,1536]{1,0:T(8,128)(2,1)S(1)} collective-permute-done((bf16[128,1536]{1,0:T(8,128)(2,1)S(1)}, bf16[128,1536]{1,0:T(8,128)(2,1)S(1)}, u32[]{:S(2)}, u32[]{:S(2)}) %collective-permute-start.10) | collective-permute-done | bytes 393248 | tf_op jit(solution)/shard_map/ppermute | solution.py:661
  107.5 7.7 %collective-permute-done.13 = bf16[128,1536]{1,0:T(8,128)(2,1)S(1)} collective-permute-done((bf16[128,1536]{1,0:T(8,128)(2,1)S(1)}, bf16[128,1536]{1,0:T(8,128)(2,1)S(1)}, u32[]{:S(2)}, u32[]{:S(2)}) %collective-permute-start.13) | collective-permute-done | bytes 393248 | tf_op jit(solution)/shard_map/ppermute | solution.py:661
  115.5 1.7 %collective-permute-done.14.refs_3_ = bf16[128,1536]{1,0:T(8,128)(2,1)S(1)} collective-permute-done((bf16[128,1536]{1,0:T(8,128)(2,1)S(1)}, bf16[128,1536]{1,0:T(8,128)(2,1)S(1)}, u32[]{:S(2)}, u32[]{:S(2)}) %collective-permute-start.14) | collective-permute-done | bytes 393248 | tf_op jit(solution)/shard_map/ppermute | solution.py:657
  117.2 1.3 %finish.1 = bf16[4,128,1536]{2,1,0:T(8,128)(2,1)} custom-call(bf16[128,1536]{1,0:T(8,128)(2,1)S(1)} %add_convert_fusion.2.refs_0_, bf16[128,1536]{1,0:T(8,128)(2,1)S(1)} %collective-permute-done.11.refs_1_, bf16[128,1536]{1,0:T(8,128)(2,1)S(1)} %add_convert_fusion.refs_2_, bf16[128,1536]{1,0:T(8,128)(2,1)S(1)} %collective-permute-done.14.refs_3_), custom_call_target="tpu_custom_call" | custom-call | tf_op jit(solution)/shard_map/finish/pallas_call | solution.py:646
  (45 shorter events, 1.6 us)
Async XLA Ops:
  1.3 13.7 %all-to-all-start = ((s32[8,1,16]{2,1,0:T(1,128)}), s32[8,1,16]{2,1,0:T(1,128)S(1)}, u32[]{:S(2)}, u32[]{:S(2)}) async-start(s32[8,1,16]{2,1,0:T(1,128)} %broadcast_in_dim.3), calls=%async_computation | async-start | bytes 8192 | tf_op jit(solution)/shard_map/all_to_all | solution.py:678
  9.3 15.3 %copy-start.3 = (bf16[384,1536]{1,0:T(8,128)(2,1)S(1)}, bf16[384,1536]{1,0:T(8,128)(2,1)}, u32[]{:S(2)}) copy-start(bf16[384,1536]{1,0:T(8,128)(2,1)} %w0.3) | copy-start | bytes 3538948
  9.3 16.9 %copy-start.4 = (bf16[48,6,128]{2,0,1:T(8,128)(2,1)S(1)}, bf16[48,6,128]{2,0,1:T(8,128)(2,1)}, u32[]{:S(2)}) copy-start(bf16[48,6,128]{2,0,1:T(8,128)(2,1)} %param.24) | copy-start | bytes 221188
  15.0 0.7 copy-start.5
  15.7 10.5 %copy-start.6 = (s32[48]{0:T(128)S(1)}, s32[48]{0:T(128)}, u32[]{:S(2)}) copy-start(s32[48]{0:T(128)} %request_ref.5) | copy-start | bytes 580
  15.7 10.5 %copy-start.8 = (s32[48]{0:T(128)S(1)}, s32[48]{0:T(128)}, u32[]{:S(2)}) copy-start(s32[48]{0:T(128)} %fill_ref.3) | copy-start | bytes 580
  21.0 18.2 %all-to-all-start.1 = ((bf16[8,96,384]{2,1,0:T(8,128)(2,1)}), bf16[8,96,384]{2,1,0:T(8,128)(2,1)S(1)}, u32[]{:S(2)}, u32[]{:S(2)}) async-start(bf16[8,96,384]{2,1,0:T(8,128)(2,1)} %bitcast), calls=%async_computation.1 | async-start | bytes 1179648 | tf_op jit(solution)/shard_map/all_to_all | solution.py:683
  24.6 26.3 %collective-permute-start.4 = (bf16[384,1536]{1,0:T(8,128)(2,1)S(1)}, bf16[384,1536]{1,0:T(8,128)(2,1)S(1)}, u32[]{:S(2)}, u32[]{:S(2)}) collective-permute-start(bf16[384,1536]{1,0:T(8,128)(2,1)S(1)} %copy-done.3), channel_id=1, source_target_pairs={{0,2},{1,3},{2,0},{3,1},{4,6},{5,7},{6,4},{7,5},{8,10},{9,11},{10,... | collective-permute-start | bytes 3538952 | tf_op jit(solution)/shard_map/ppermute | solution.py:661
  39.3 11.7 %copy-start.7 = (s32[3,128]{1,0:T(4,128)S(1)}, s32[3,128]{1,0:T(4,128)}, u32[]{:S(2)}) copy-start(s32[3,128]{1,0:T(4,128)} %parents_ref.1) | copy-start | bytes 4612
  39.3 11.7 %copy-start.9 = (f32[6]{0:T(128)S(1)}, f32[6]{0:T(128)}, u32[]{:S(2)}) copy-start(f32[6]{0:T(128)} %param.30) | copy-start | bytes 76
  44.1 21.0 %all-to-all-start.2 = ((bf16[8,112,384]{2,1,0:T(8,128)(2,1)}), bf16[8,112,384]{2,1,0:T(8,128)(2,1)}, u32[]{:S(2)}, u32[]{:S(2)}) async-start(bf16[8,112,384]{2,1,0:T(8,128)(2,1)} %hosted_pages.1), calls=%async_computation.2 | async-start | bytes 1376256 | tf_op jit(solution)/shard_map/all_to_all | solution.py:693
  48.3 29.1 %collective-permute-start.3 = (bf16[384,1536]{1,0:T(8,128)(2,1)S(1)}, bf16[384,1536]{1,0:T(8,128)(2,1)S(1)}, u32[]{:S(2)}, u32[]{:S(2)}) collective-permute-start(bf16[384,1536]{1,0:T(8,128)(2,1)S(1)} %copy-done.3), channel_id=1, source_target_pairs={{0,1},{1,0},{2,3},{3,2},{4,5},{5,4},{6,7},{7,6},{8,9},{9,8},{10,11... | collective-permute-start | bytes 3538952 | tf_op jit(solution)/shard_map/ppermute | solution.py:657
  51.0 28.5 %collective-permute-start.5 = (bf16[384,1536]{1,0:T(8,128)(2,1)S(1)}, bf16[384,1536]{1,0:T(8,128)(2,1)}, u32[]{:S(2)}, u32[]{:S(2)}) collective-permute-start(bf16[384,1536]{1,0:T(8,128)(2,1)S(1)} %collective-permute-done.4.w2), channel_id=1, source_target_pairs={{0,1},{1,0},{2,3},{3,2},{4,5},{5,4},{6,7},{7,6},{8,9},{9,8},{10,11... | collective-permute-start | bytes 3538952 | tf_op jit(solution)/shard_map/ppermute | solution.py:657
  65.1 12.3 %copy-start.10 = (f32[1536]{0:T(1024)S(1)}, f32[1536]{0:T(1024)}, u32[]{:S(2)}) copy-start(f32[1536]{0:T(1024)} %param.32) | copy-start | bytes 18436
  65.1 19.2 %copy-start.2 = (bf16[1024,1536]{1,0:T(8,128)(2,1)S(1)}, bf16[1024,1536]{1,0:T(8,128)(2,1)}, u32[]{:S(2)}) copy-start(bf16[1024,1536]{1,0:T(8,128)(2,1)} %down_ref.3) | copy-start | bytes 9437188
  70.5 6.8 %collective-permute-start.1 = (bf16[256,384]{1,0:T(8,128)(2,1)S(1)}, bf16[256,384]{1,0:T(8,128)(2,1)S(1)}, u32[]{:S(2)}, u32[]{:S(2)}) collective-permute-start(bf16[256,384]{1,0:T(8,128)(2,1)S(1)} %bitcast.12), channel_id=1, source_target_pairs={{0,2},{1,3},{2,0},{3,1},{4,6},{5,7},{6,4},{7,5},{8,10},{9,11},{10,... | collective-permute-start | bytes 589832 | tf_op jit(solution)/shard_map/ppermute | solution.py:661
  72.1 7.4 %collective-permute-start.7 = (bf16[256,384]{1,0:T(8,128)(2,1)S(1)}, bf16[256,384]{1,0:T(8,128)(2,1)S(1)}, u32[]{:S(2)}, u32[]{:S(2)}) collective-permute-start(bf16[256,384]{1,0:T(8,128)(2,1)S(1)} %bitcast.9), channel_id=1, source_target_pairs={{0,2},{1,3},{2,0},{3,1},{4,6},{5,7},{6,4},{7,5},{8,10},{9,11},{10,... | collective-permute-start | bytes 589832 | tf_op jit(solution)/shard_map/ppermute | solution.py:661
  72.6 6.8 %collective-permute-start = (bf16[256,384]{1,0:T(8,128)(2,1)S(1)}, bf16[256,384]{1,0:T(8,128)(2,1)S(1)}, u32[]{:S(2)}, u32[]{:S(2)}) collective-permute-start(bf16[256,384]{1,0:T(8,128)(2,1)S(1)} %bitcast.13), channel_id=1, source_target_pairs={{0,1},{1,0},{2,3},{3,2},{4,5},{5,4},{6,7},{7,6},{8,9},{9,8},{10,11... | collective-permute-start | bytes 589832 | tf_op jit(solution)/shard_map/ppermute | solution.py:657
  77.3 2.1 %collective-permute-start.2 = (bf16[256,384]{1,0:T(8,128)(2,1)S(1)}, bf16[256,384]{1,0:T(8,128)(2,1)S(1)}, u32[]{:S(2)}, u32[]{:S(2)}) collective-permute-start(bf16[256,384]{1,0:T(8,128)(2,1)S(1)} %collective-permute-done.1.att2), channel_id=1, source_target_pairs={{0,1},{1,0},{2,3},{3,2},{4,5},{5,4},{6,7},{7,6},{8,9},{9,8},{10,11... | collective-permute-start | bytes 589832 | tf_op jit(solution)/shard_map/ppermute | solution.py:657
  77.4 9.7 %collective-permute-start.6 = (bf16[256,384]{1,0:T(8,128)(2,1)S(1)}, bf16[256,384]{1,0:T(8,128)(2,1)S(1)}, u32[]{:S(2)}, u32[]{:S(2)}) collective-permute-start(bf16[256,384]{1,0:T(8,128)(2,1)S(1)} %bitcast.10), channel_id=1, source_target_pairs={{0,1},{1,0},{2,3},{3,2},{4,5},{5,4},{6,7},{7,6},{8,9},{9,8},{10,11... | collective-permute-start | bytes 589832 | tf_op jit(solution)/shard_map/ppermute | solution.py:657
  79.5 7.7 %collective-permute-start.8 = (bf16[256,384]{1,0:T(8,128)(2,1)S(1)}, bf16[256,384]{1,0:T(8,128)(2,1)S(1)}, u32[]{:S(2)}, u32[]{:S(2)}) collective-permute-start(bf16[256,384]{1,0:T(8,128)(2,1)S(1)} %collective-permute-done.7.att2), channel_id=1, source_target_pairs={{0,1},{1,0},{2,3},{3,2},{4,5},{5,4},{6,7},{7,6},{8,9},{9,8},{10,11... | collective-permute-start | bytes 589832 | tf_op jit(solution)/shard_map/ppermute | solution.py:657
  79.5 4.8 %copy-start = (bf16[1536,1024]{1,0:T(8,128)(2,1)S(1)}, bf16[1536,1024]{1,0:T(8,128)(2,1)}, u32[]{:S(2)}) copy-start(bf16[1536,1024]{1,0:T(8,128)(2,1)} %gate_ref.3) | copy-start | bytes 9437188
  79.5 4.8 %copy-start.1 = (bf16[1536,1024]{1,0:T(8,128)(2,1)S(1)}, bf16[1536,1024]{1,0:T(8,128)(2,1)}, u32[]{:S(2)}) copy-start(bf16[1536,1024]{1,0:T(8,128)(2,1)} %up_ref.3) | copy-start | bytes 9437188
  87.1 5.1 %collective-permute-start.9 = (bf16[128,1536]{1,0:T(8,128)(2,1)S(1)}, bf16[128,1536]{1,0:T(8,128)(2,1)S(1)}, u32[]{:S(2)}, u32[]{:S(2)}) collective-permute-start(bf16[128,1536]{1,0:T(8,128)(2,1)S(1)} %get-tuple-element.54), channel_id=1, source_target_pairs={{0,1},{1,0},{2,3},{3,2},{4,5},{5,4},{6,7},{7,6},{8,9},{9,8},{10,11... | collective-permute-start | bytes 1179656 | tf_op jit(solution)/shard_map/ppermute | solution.py:657
  95.2 1.8 %collective-permute-start.12 = (bf16[128,1536]{1,0:T(8,128)(2,1)S(1)}, bf16[128,1536]{1,0:T(8,128)(2,1)S(1)}, u32[]{:S(2)}, u32[]{:S(2)}) collective-permute-start(bf16[128,1536]{1,0:T(8,128)(2,1)S(1)} %get-tuple-element.64), channel_id=1, source_target_pairs={{0,1},{1,0},{2,3},{3,2},{4,5},{5,4},{6,7},{7,6},{8,9},{9,8},{10,11... | collective-permute-start | bytes 1179656 | tf_op jit(solution)/shard_map/ppermute | solution.py:657
  95.3 12.0 %collective-permute-start.10 = (bf16[128,1536]{1,0:T(8,128)(2,1)S(1)}, bf16[128,1536]{1,0:T(8,128)(2,1)S(1)}, u32[]{:S(2)}, u32[]{:S(2)}) collective-permute-start(bf16[128,1536]{1,0:T(8,128)(2,1)S(1)} %add_convert_fusion.3), channel_id=1, source_target_pairs={{0,2},{1,3},{2,0},{3,1},{4,6},{5,7},{6,4},{7,5},{8,10},{9,11},{10,... | collective-permute-start | bytes 1179656 | tf_op jit(solution)/shard_map/ppermute | solution.py:661
  97.1 18.2 %collective-permute-start.13 = (bf16[128,1536]{1,0:T(8,128)(2,1)S(1)}, bf16[128,1536]{1,0:T(8,128)(2,1)S(1)}, u32[]{:S(2)}, u32[]{:S(2)}) collective-permute-start(bf16[128,1536]{1,0:T(8,128)(2,1)S(1)} %add_convert_fusion.1), channel_id=1, source_target_pairs={{0,2},{1,3},{2,0},{3,1},{4,6},{5,7},{6,4},{7,5},{8,10},{9,11},{10,... | collective-permute-start | bytes 1179656 | tf_op jit(solution)/shard_map/ppermute | solution.py:661
  107.4 8.1 %collective-permute-start.11 = (bf16[128,1536]{1,0:T(8,128)(2,1)S(1)}, bf16[128,1536]{1,0:T(8,128)(2,1)S(1)}, u32[]{:S(2)}, u32[]{:S(2)}) collective-permute-start(bf16[128,1536]{1,0:T(8,128)(2,1)S(1)} %add_convert_fusion.2.refs_0_), channel_id=1, source_target_pairs={{0,1},{1,0},{2,3},{3,2},{4,5},{5,4},{6,7},{7,6},{8,9},{9,8},{10,11... | collective-permute-start | bytes 1179656 | tf_op jit(solution)/shard_map/ppermute | solution.py:657
  115.4 1.8 %collective-permute-start.14 = (bf16[128,1536]{1,0:T(8,128)(2,1)S(1)}, bf16[128,1536]{1,0:T(8,128)(2,1)S(1)}, u32[]{:S(2)}, u32[]{:S(2)}) collective-permute-start(bf16[128,1536]{1,0:T(8,128)(2,1)S(1)} %add_convert_fusion.refs_2_), channel_id=1, source_target_pairs={{0,1},{1,0},{2,3},{3,2},{4,5},{5,4},{6,7},{7,6},{8,9},{9,8},{10,11... | collective-permute-start | bytes 1179656 | tf_op jit(solution)/shard_map/ppermute | solution.py:657

commit v3 on v2

--- a/solution.py
+++ b/solution.py
@@ -11,6 +11,7 @@
 OWNED_SLOTS = 32
 SPILL = 16
 PAGE_BLOCK = 16
+PARTS = 2
 TAIL_ROWS = 16
 MIB = 1 << 20
 
@@ -52,14 +53,14 @@
 
 
 def fill_table(local_count, capacity, first, ids_ref, table_ref):
-    groups, _, spill = ids_ref.shape
+    groups = ids_ref.shape[0]
     for slot in range(groups * capacity):
         table_ref[slot] = -1
 
     def group(index, carry):
         rank = jnp.int32(0)
-        for page in range(spill):
-            local = ids_ref[index, 0, page] - first
+        for page in range(SPILL):
+            local = ids_ref[index, 0, OWNED_SLOTS + page] - first
             mine = (local >= 0) & (local < local_count)
 
             @pl.when(mine)
@@ -73,17 +74,20 @@
 
 
 def query_kernel(
-    capacity, request_ref, ids_ref, tokens_hbm, gain_ref, wq_hbm,
-    asked_ref, table_ref, q_hbm, normed_hbm,
-    tokens_ref, wq_ref, normed_ref, q_ref, sems, out_sems,
+    tokens_hbm, gain_ref, wq_hbm, q_ref, q_hbm, normed_hbm,
+    tokens_ref, wq_ref, normed_ref, sems, out_sems,
 ):
     steps, rows, _ = tokens_ref.shape
     span = steps * BEAMS
-    local_count = rows // BEAMS
-    copies = start_all([(tokens_hbm, tokens_ref), (wq_hbm, wq_ref)], sems)
-    first = request_ref[0] // local_count * local_count
-    fill_table(local_count, capacity, first, ids_ref, table_ref)
-    copies[0].wait()
+    cut = rows // 2
+    copies = start_all(
+        [
+            (tokens_hbm.at[:, :cut], tokens_ref.at[:, :cut]),
+            (tokens_hbm.at[:, cut:], tokens_ref.at[:, cut:]),
+            (wq_hbm, wq_ref),
+        ],
+        sems,
+    )
     gain = gain_ref[...]
 
     def pair(index, carry):
@@ -98,34 +102,32 @@
             normed_ref[pl.ds(start, span), :] = part.astype(bf16)
         return carry
 
-    lax.fori_loop(0, rows // 16, pair, 0, unroll=2)
+    copies[0].wait()
+    lax.fori_loop(0, cut // 16, pair, 0, unroll=2)
+    copies[1].wait()
+    lax.fori_loop(cut // 16, rows // 16, pair, 0, unroll=2)
     leaving = start_all([(normed_ref, normed_hbm)], out_sems)
-    copies[1].wait()
+    copies[2].wait()
     query = dot(normed_ref[...], wq_ref[...], NT).astype(bf16)
     q_ref[...] = (query.astype(f32) * 0.125).astype(bf16)
     last = pltpu.make_async_copy(q_ref, q_hbm, out_sems.at[1])
     last.start()
-    for slot in range(asked_ref.shape[0]):
-        local = jnp.maximum(table_ref[slot], 0)
-        asked_ref[slot] = q_ref[pl.ds(pl.multiple_of(local * span, span), span), :]
     leaving[0].wait()
     last.wait()
 
 
-def queries_of(request, ids, tokens, gain, w_query, capacity):
+def queries_of(tokens, gain, w_query):
     steps, rows, width = tokens.shape
     inner = w_query.shape[0]
     total = steps * rows
-    slots = ids.shape[0] * capacity
     hbm = pl.BlockSpec(memory_space=pltpu.HBM)
     vmem = pl.BlockSpec(memory_space=pltpu.VMEM)
     return pl.pallas_call(
-        functools.partial(query_kernel, capacity),
-        in_specs=[SMEM, SMEM, hbm, vmem, hbm],
-        out_specs=[vmem, SMEM, hbm, hbm],
+        query_kernel,
+        in_specs=[hbm, vmem, hbm],
+        out_specs=[vmem, hbm, hbm],
         out_shape=[
-            jax.ShapeDtypeStruct((slots, steps * BEAMS, inner), bf16),
-            jax.ShapeDtypeStruct((slots,), jnp.int32),
+            pltpu.VMEM((total, inner), bf16),
             pltpu.HBM((total, inner), bf16),
             pltpu.HBM((total, width), bf16),
         ],
@@ -133,16 +135,41 @@
             pltpu.VMEM(tokens.shape, bf16),
             pltpu.VMEM(w_query.shape, bf16),
             pltpu.VMEM((total, width), bf16),
-            pltpu.VMEM((total, inner), bf16),
-            pltpu.SemaphoreType.DMA((2,)),
+            pltpu.SemaphoreType.DMA((3,)),
             pltpu.SemaphoreType.DMA((2,)),
         ],
-        compiler_params=pltpu.CompilerParams(vmem_limit_bytes=16 * MIB),
+        compiler_params=pltpu.CompilerParams(vmem_limit_bytes=12 * MIB),
         cost_estimate=pl.CostEstimate(
             flops=2 * total * width * inner, bytes_accessed=6 * MIB, transcendentals=total
         ),
         name="queries",
-    )(request, ids, in_hbm(tokens), gain.reshape(1, -1), in_hbm(w_query))
+    )(in_hbm(tokens), gain.reshape(1, -1), in_hbm(w_query))
+
+
+def ask_kernel(capacity, request_ref, ids_ref, q_ref, table_ref, *out_refs):
+    slots, part, _ = out_refs[0].shape
+    span = part * len(out_refs)
+    local_count = q_ref.shape[0] // span
+    first = request_ref[0] // local_count * local_count
+    fill_table(local_count, capacity, first, ids_ref, table_ref)
+    for slot in range(slots):
+        start = jnp.maximum(table_ref[slot], 0) * span
+        for index, out_ref in enumerate(out_refs):
+            out_ref[slot] = q_ref[pl.ds(pl.multiple_of(start + index * part, part), part), :]
+
+
+def ask(request, ids, q, span, capacity):
+    slots = ids.shape[0] * capacity
+    vmem = pl.BlockSpec(memory_space=pltpu.VMEM)
+    return pl.pallas_call(
+        functools.partial(ask_kernel, capacity),
+        in_specs=[SMEM, SMEM, vmem],
+        out_specs=[SMEM] + [vmem] * PARTS,
+        out_shape=[jax.ShapeDtypeStruct((slots,), jnp.int32)]
+        + [jax.ShapeDtypeStruct((slots, span // PARTS, q.shape[1]), bf16)] * PARTS,
+        compiler_params=pltpu.CompilerParams(vmem_limit_bytes=8 * MIB),
+        name="ask",
+    )(request, ids, in_vmem(q))
 
 
 def half_masks(rows):
@@ -172,14 +199,12 @@
     numer_ref[rows, columns] = numer_ref[rows, columns] * keep + numer * add
 
 
-def history(parents_ref, q_ref, k_ref, v_ref, forget_ref, state):
-    top_ref, total_ref, numer_ref = state
+def history(parents_ref, q_ref, k_ref, v_ref, forget_ref, state, scores_ref, weights_ref):
     transitions, rows = parents_ref.shape
     span = (transitions + 1) * BEAMS
     pack = 128 // span
     square = (128, 128)
-    down, across = sublanes(square), lanes(square)
-    diagonal = down == across
+    diagonal = sublanes(square) == lanes(square)
     columns = []
     for step in range(transitions):
         row = parents_ref[step : step + 1, :].astype(f32)
@@ -188,7 +213,11 @@
         )
     lane8 = lanes((8, 128)).astype(f32)
     masks = half_masks(128)
-    for group in range(rows // BEAMS // pack):
+    low = lanes(square) < 64
+    top_ref, total_ref, numer_ref = state
+    groups = rows // BEAMS // pack
+    pairs = q_ref.shape[1] // 128
+    for group in range(groups):
         slabs = []
         for member in range(pack):
             first = (group * pack + member) * BEAMS
@@ -197,9 +226,8 @@
                 wanted = columns[step][first : first + 8] + float(member * span + step * 8)
                 slabs.append(jnp.where(lane8 == wanted, 1.0, 0.0))
         parent = jnp.concatenate(slabs, axis=0)
-        same = diagonal.astype(f32)
         parent16 = parent.astype(bf16)
-        one = same + parent
+        one = diagonal.astype(f32) + parent
         two = dot(parent16, parent16)
         ancestors = one + dot(two.astype(bf16), one.astype(bf16))
         here = pl.ds(group * 128, 128)
@@ -208,26 +236,42 @@
             precision=lax.Precision.HIGHEST, preferred_element_type=f32,
         ).T
         hidden = jnp.where(ancestors > 0.5, 0.0, masked_score)
-        for pair in range(q_ref.shape[1] // 128):
+        for pair in range(pairs):
             cols = pl.ds(pair * 128, 128)
             raw = dot(stacked(q_ref[here, cols], masks), k_ref[here, cols], NT)
-            low = raw[:128] + (hidden - running[2 * pair : 2 * pair + 1])
-            high = raw[128:] + (hidden - running[2 * pair + 1 : 2 * pair + 2])
-            scores = jnp.concatenate([low, high], axis=0)
-            top = jnp.max(scores, axis=-1, keepdims=True)
-            weights = jnp.exp(scores - top)
-            total = jnp.sum(weights, axis=-1, keepdims=True)
-            numer = dot(weights.astype(bf16), v_ref[here, cols])
-            top_ref[here, cols] = side_by_side(top, 128)
-            total_ref[here, cols] = side_by_side(total, 128)
-            numer_ref[here, cols] = side_by_side(numer, 128)
+            for half in range(2):
+                head = pair * 2 + half
+                scores_ref[group * pairs + pair, half] = raw[half * 128 : half * 128 + 128] + (
+                    hidden - running[head : head + 1]
+                )
+    for group in range(groups):
+        here = pl.ds(group * 128, 128)
+        for pair in range(pairs):
+            cols = pl.ds(pair * 128, 128)
+            tops, totals = [], []
+            for half in range(2):
+                scores = scores_ref[group * pairs + pair, half]
+                top = jnp.broadcast_to(jnp.max(scores, axis=-1, keepdims=True), square)
+                weights = jnp.exp(scores - top)
+                weights_ref[group * pairs + pair, pl.ds(half * 128, 128), :] = weights.astype(bf16)
+                tops.append(top)
+                totals.append(jnp.broadcast_to(jnp.sum(weights, axis=-1, keepdims=True), square))
+            top_ref[here, cols] = jnp.where(low, *tops)
+            total_ref[here, cols] = jnp.where(low, *totals)
+    for group in range(groups):
+        here = pl.ds(group * 128, 128)
+        for pair in range(pairs):
+            cols = pl.ds(pair * 128, 128)
+            numer = dot(weights_ref[group * pairs + pair], v_ref[here, cols])
+            numer_ref[here, cols] = jnp.where(low, numer[:128], numer[128:])
 
 
 def fresh_kernel(
     parents_ref, bias_ref, normed_hbm, wk_hbm, wv_hbm, wf_hbm, q_hbm, top_hbm, total_hbm, numer_hbm,
-    log_hbm, average_hbm,
+    logs_hbm, averages_hbm,
     normed_ref, wk_ref, wv_ref, wf_ref, q_ref, top_own, total_own, numer_own,
-    k_ref, v_ref, forget_ref, top_ref, total_ref, numer_ref, sems, out_sems,
+    k_ref, v_ref, forget_ref, top_ref, total_ref, numer_ref, scores_ref, weights_ref,
+    logs_ref, averages_ref, sems, out_sems,
 ):
     copies = start_all(
         [
@@ -248,37 +292,48 @@
     forget_ref[:, : forget.shape[1]] = forget
     copies[4].wait()
     state = (top_ref, total_ref, numer_ref)
-    history(parents_ref, q_ref, k_ref, v_ref, forget_ref, state)
+    history(parents_ref, q_ref, k_ref, v_ref, forget_ref, state, scores_ref, weights_ref)
     for copy in copies[5:]:
         copy.wait()
 
+    parts, _, part = logs_ref.shape[:3]
+    span = parts * part
+
     def join(index, carry):
-        rows = pl.ds(pl.multiple_of(index * 32, 32), 32)
+        rows = pl.ds(pl.multiple_of(index * span, span), span)
         absorb(state, rows, slice(None), top_own[rows, :], total_own[rows, :], numer_own[rows, :])
         total = total_ref[rows, :]
-        top_ref[rows, :] = top_ref[rows, :] + jnp.log(total)
-        numer_ref[rows, :] = numer_ref[rows, :] / total
+        logs = top_ref[rows, :] + jnp.log(total)
+        averages = numer_ref[rows, :] / total
+        for number in range(parts):
+            logs_ref[number, index] = logs[number * part : number * part + part]
+            averages_ref[number, index] = averages[number * part : number * part + part]
         return carry
 
-    lax.fori_loop(0, top_ref.shape[0] // 32, join, 0, unroll=2)
-    for copy in start_all([(top_ref, log_hbm), (numer_ref, average_hbm)], out_sems):
+    lax.fori_loop(0, logs_ref.shape[1], join, 0, unroll=2)
+    for copy in start_all([(logs_ref, logs_hbm), (averages_ref, averages_hbm)], out_sems):
         copy.wait()
 
 
 def fresh(parents, bias, normed, w_key, w_value, w_forget, q, own):
     rows, inner = q.shape
+    span = (parents.shape[0] + 1) * BEAMS
     vmem = pl.BlockSpec(memory_space=pltpu.VMEM)
     hbm = pl.BlockSpec(memory_space=pltpu.HBM)
     big = [normed, w_key, w_value, w_forget.T, q, *own]
     wide = pltpu.VMEM((rows, inner), f32)
+    out = (PARTS, rows // span, span // PARTS, inner)
+    tiles = rows * inner // (128 * 128)
     return pl.pallas_call(
         fresh_kernel,
         in_specs=[vmem, vmem] + [hbm] * len(big),
         out_specs=[hbm] * 2,
-        out_shape=[pltpu.HBM((rows, inner), f32)] * 2,
+        out_shape=[pltpu.HBM(out, f32)] * 2,
         scratch_shapes=[pltpu.VMEM(x.shape, x.dtype) for x in big]
         + [pltpu.VMEM((rows, inner), bf16)] * 2
         + [pltpu.VMEM((rows, 128), f32), wide, wide, wide]
+        + [pltpu.VMEM((tiles, 2, 128, 128), f32), pltpu.VMEM((tiles, 256, 128), bf16)]
+        + [pltpu.VMEM(out, f32)] * 2
         + [pltpu.SemaphoreType.DMA((len(big),)), pltpu.SemaphoreType.DMA((2,))],
         compiler_params=pltpu.CompilerParams(vmem_limit_bytes=24 * MIB),
         cost_estimate=pl.CostEstimate(
@@ -344,44 +399,33 @@
     top_ref, total_ref, numer_ref, *scratch,
 ):
     state = (top_ref, total_ref, numer_ref)
-    block = pl.program_id(0)
     span = scratch[0].shape[1] // decay_ref.shape[0]
     local_count = q_ref.shape[0] // span
     pairs = q_ref.shape[1] // 128
 
-    @pl.when(block == 0)
-    def _():
-        top_ref[...] = jnp.full_like(top_ref, masked_score)
-        total_ref[...] = jnp.zeros_like(total_ref)
-        numer_ref[...] = jnp.zeros_like(numer_ref)
-
-    places, queries, fills = [], [], []
-    for page in range(PAGE_BLOCK):
-        index = block * PAGE_BLOCK + page
-        local = lax.rem(request_ref[index], local_count)
-        rows = pl.ds(pl.multiple_of(local * span, span), span)
-        places.append(rows)
-        queries.append([q_ref[rows, pl.ds(pair * 128, 128)] for pair in range(pairs)])
-        fills.append(fill_ref[index])
-    page_weights(queries, fills, keys_ref, decay_ref, *scratch)
-    for page, rows in enumerate(places):
-        for pair in range(pairs):
-            sums = page_sums(page, pair, span, values_ref, *scratch)
-            absorb(state, rows, pl.ds(pair * 128, 128), *sums)
-
-
-def whole(array):
-    return pl.BlockSpec(array.shape, lambda *_: (0,) * array.ndim)
-
-
-def page_specs(keys, decay, first):
-    shift = first // PAGE_BLOCK
-    pool = pl.BlockSpec((PAGE_BLOCK,) + keys.shape[1:], lambda i: (i + shift, 0, 0))
-    return [
-        pool,
-        pool,
-        pl.BlockSpec((decay.shape[0], PAGE_BLOCK, decay.shape[2]), lambda i: (0, i + shift, 0)),
-    ]
+    top_ref[...] = jnp.full_like(top_ref, masked_score)
+    total_ref[...] = jnp.zeros_like(total_ref)
+    numer_ref[...] = jnp.zeros_like(numer_ref)
+
+    def block(number, carry):
+        start = pl.multiple_of(number * PAGE_BLOCK, PAGE_BLOCK)
+        pages = pl.ds(start, PAGE_BLOCK)
+        places, queries, fills = [], [], []
+        for page in range(PAGE_BLOCK):
+            local = lax.rem(request_ref[start + page], local_count)
+            rows = pl.ds(pl.multiple_of(local * span, span), span)
+            places.append(rows)
+            queries.append([q_ref[rows, pl.ds(pair * 128, 128)] for pair in range(pairs)])
+            fills.append(fill_ref[start + page])
+        values = values_ref.at[pages]
+        page_weights(queries, fills, keys_ref.at[pages], decay_ref.at[:, pages], *scratch)
+        for page, rows in enumerate(places):
+            for pair in range(pairs):
+                sums = page_sums(page, pair, span, values, *scratch)
+                absorb(state, rows, pl.ds(pair * 128, 128), *sums)
+        return carry
+
+    lax.fori_loop(0, OWNED_SLOTS // PAGE_BLOCK, block, 0)
 
 
 def page_cost(pages, keys, rows):
@@ -394,18 +438,17 @@
 
 
 def own_pages(request, fill, q, keys, values, decay, span):
-    out_spec = pl.BlockSpec(q.shape, lambda *_: (0, 0))
+    vmem = pl.BlockSpec(memory_space=pltpu.VMEM)
     return pl.pallas_call(
         own_kernel,
-        grid=(OWNED_SLOTS // PAGE_BLOCK,),
-        in_specs=[SMEM, SMEM, whole(q)] + page_specs(keys, decay, 0),
-        out_specs=[out_spec] * 3,
-        out_shape=[pltpu.HBM(q.shape, f32)] * 3,
+        in_specs=[SMEM, SMEM, vmem, vmem, vmem, vmem],
+        out_specs=[vmem] * 3,
+        out_shape=[jax.ShapeDtypeStruct(q.shape, f32)] * 3,
         scratch_shapes=page_scratch(PAGE_BLOCK, span, decay.shape[0]),
-        compiler_params=pltpu.CompilerParams(vmem_limit_bytes=24 * MIB),
+        compiler_params=pltpu.CompilerParams(vmem_limit_bytes=12 * MIB),
         cost_estimate=page_cost(OWNED_SLOTS, keys, 64),
         name="own_pages",
-    )(request, fill, in_hbm(q), in_hbm(keys), in_hbm(values), decay)
+    )(request, fill, in_vmem(q), in_vmem(keys), in_vmem(values), decay)
 
 
 def hosted_kernel(
@@ -429,13 +472,15 @@
         slot = owner * capacity + rank
         queries.append([q_ref[slot, :, pl.ds(pair * 128, 128)] for pair in range(pairs)])
         fills.append(fill_ref[OWNED_SLOTS + page])
-    page_weights(queries, fills, keys_ref, decay_ref, *scratch)
+    hosted = pl.ds(OWNED_SLOTS, SPILL)
+    values = values_ref.at[hosted]
+    page_weights(queries, fills, keys_ref.at[hosted], decay_ref.at[:, hosted], *scratch)
     scores_ref, _, tops_ref = scratch
     lane = lanes((span, 128))
     for page, (owner, rank) in enumerate(places):
         here = pl.ds(pl.multiple_of(rank * span, span), span)
         for pair in range(pairs):
-            _, total, numer = page_sums(page, pair, span, values_ref, *scratch)
+            _, total, numer = page_sums(page, pair, span, values, *scratch)
             out_ref[owner, here, pl.ds(pair * 128, 128)] = (numer / total).astype(bf16)
         tail = tail_ref[owner]
         base = rank * (3 * heads)
@@ -458,30 +503,29 @@
 
 def hosted_pages(request, fill, asked_rows, keys, values, decay, groups, capacity, local_count):
     count, span, inner = asked_rows.shape
-    out_shape = (groups, capacity * span + TAIL_ROWS, inner)
+    vmem = pl.BlockSpec(memory_space=pltpu.VMEM)
     return pl.pallas_call(
         functools.partial(hosted_kernel, local_count, capacity),
-        grid=(1,),
-        in_specs=[SMEM, SMEM, whole(asked_rows)] + page_specs(keys, decay, OWNED_SLOTS),
-        out_specs=pl.BlockSpec(out_shape, lambda *_: (0, 0, 0)),
-        out_shape=jax.ShapeDtypeStruct(out_shape, bf16),
+        in_specs=[SMEM, SMEM, vmem, vmem, vmem, vmem],
+        out_specs=vmem,
+        out_shape=jax.ShapeDtypeStruct((groups, capacity * span + TAIL_ROWS, inner), bf16),
         scratch_shapes=[pltpu.VMEM((groups, span, 128), f32), pltpu.SMEM((groups,), jnp.int32)]
         + page_scratch(SPILL, span, decay.shape[0]),
-        compiler_params=pltpu.CompilerParams(vmem_limit_bytes=24 * MIB),
+        compiler_params=pltpu.CompilerParams(vmem_limit_bytes=12 * MIB),
         cost_estimate=page_cost(SPILL, keys, 64),
         name="hosted_pages",
-    )(request, fill, asked_rows, in_hbm(keys), in_hbm(values), decay)
+    )(request, fill, asked_rows, in_vmem(keys), in_vmem(values), decay)
 
 
 def merge_kernel(
-    capacity, steps, table_ref, back_ref, log_hbm, average_hbm, out_ref,
+    capacity, steps, part, table_ref, back_ref, log_hbm, average_hbm, out_ref,
     top_ref, total_ref, numer_ref, sems,
 ):
     groups, _, inner = back_ref.shape
     span = steps * BEAMS
     heads = inner // 64
     state = (top_ref, total_ref, numer_ref)
-    copies = start_all([(log_hbm, top_ref), (average_hbm, numer_ref)], sems)
+    copies = start_all([(log_hbm.at[part], top_ref), (average_hbm.at[part], numer_ref)], sems)
     total_ref[...] = jnp.ones_like(total_ref)
     source, target = sublanes((128, inner)), lanes((128, inner)) // 64
     spread = []
@@ -522,16 +566,18 @@
             out_ref[step, index * 16 : index * 16 + 16, :] = both.astype(bf16)
 
 
-def merge(table, back, logs, averages, steps, capacity):
-    rows, inner = logs.shape
+def merge(part, table, back, logs, averages, steps, capacity):
+    _, requests, span, inner = logs.shape
+    rows = requests * span
+    logs, averages = (x.reshape(PARTS, rows, inner) for x in (logs, averages))
     vmem = pl.BlockSpec(memory_space=pltpu.VMEM)
     hbm = pl.BlockSpec(memory_space=pltpu.HBM)
     return pl.pallas_call(
-        functools.partial(merge_kernel, capacity, steps),
+        functools.partial(merge_kernel, capacity, steps, part),
         in_specs=[SMEM, vmem, hbm, hbm],
         out_shape=jax.ShapeDtypeStruct((steps, rows // steps, inner), bf16),
         scratch_shapes=[pltpu.VMEM((rows, inner), f32)] * 3 + [pltpu.SemaphoreType.DMA((2,))],
-        compiler_params=pltpu.CompilerParams(vmem_limit_bytes=16 * MIB),
+        compiler_params=pltpu.CompilerParams(vmem_limit_bytes=10 * MIB),
         cost_estimate=pl.CostEstimate(
             flops=40 * rows * inner, bytes_accessed=8 * MIB, transcendentals=4 * rows * inner
         ),
@@ -545,15 +591,20 @@
 ):
     rows, width = residual_ref.shape
     half = rows // 2
-    core = lax.axis_index("head") % 2
-    near = pl.ds(pl.multiple_of(core * half, half), half)
+    head = lax.axis_index("head")
+    near = pl.ds(pl.multiple_of(head % 2 * half, half), half)
     copies = start_all([(tokens_hbm.at[first : first + rows], tokens_ref)], sems)
-    for start in range(0, width, 512):
-        cols = slice(start, start + 512)
-        mixed = (dot(att0[...], w0[:, cols]) + dot(att1[...], w1[:, cols])) + (
-            dot(att2[...], w2[:, cols]) + dot(att3[...], w3[:, cols])
-        )
-        residual_ref[:, cols] = mixed
+    for own in range(4):
+
+        @pl.when(head == own)
+        def _():
+            order = [own ^ other for other in range(4)]
+            attended = jnp.concatenate([(att0, att1, att2, att3)[k][...] for k in order], axis=1)
+            for start in range(0, width, 512):
+                cols = slice(start, start + 512)
+                weight = jnp.concatenate([(w0, w1, w2, w3)[k][:, cols] for k in order], axis=0)
+                residual_ref[:, cols] = dot(attended, weight)
+
     copies[0].wait()
     gain = gain_ref[...]
 
@@ -674,45 +725,57 @@
     capacity = (SPILL + groups - 2) // (groups - 1)
     decay = decay_pool.transpose(1, 0, 2)
 
-    hosted = page_request[OWNED_SLOTS:]
-    ids = lax.all_to_all(
-        jnp.broadcast_to(hosted, (groups, 1, SPILL)), "group", split_axis=0, concat_axis=0, tiled=True
-    )
+    def exchange(value):
+        return lax.all_to_all(value, "group", split_axis=0, concat_axis=0, tiled=True)
+
+    ids = exchange(jnp.broadcast_to(page_request, (groups, 1, page_request.shape[0])))
     w_out_far = swap_chip(w_out)
-    asked, table, q, normed = queries_of(page_request, ids, tokens, gain_attn, w_query, capacity)
-    asked_rows = lax.all_to_all(
-        asked.reshape(groups, capacity * span, inner),
-        "group", split_axis=0, concat_axis=0, tiled=True,
-    ).reshape(groups * capacity, span, inner)
+    q_near, q, normed = queries_of(tokens, gain_attn, w_query)
+    table, *asked = ask(page_request, ids, q_near, span, capacity)
+    part = span // PARTS
+    asked_rows = [
+        exchange(x.reshape(groups, capacity * part, inner)).reshape(groups * capacity, part, inner)
+        for x in asked
+    ]
     own = own_pages(page_request, page_fill, q, keys_pool, values_pool, decay, span)
-    asked_rows, own = lax.optimization_barrier((asked_rows, own))
-    payload = hosted_pages(
-        page_request, page_fill, asked_rows, keys_pool, values_pool, decay, groups, capacity, local_count
-    )
+    asked_rows[0], own = lax.optimization_barrier((asked_rows[0], own))
+    back = []
+    for index in range(PARTS):
+        if index:
+            asked_rows[index], payload = lax.optimization_barrier((asked_rows[index], payload))
+        payload = hosted_pages(
+            page_request, page_fill, asked_rows[index], keys_pool, values_pool, decay,
+            groups, capacity, local_count,
+        )
+        back.append(exchange(payload))
     payload, normed = lax.optimization_barrier((payload, normed))
-    back = lax.all_to_all(payload, "group", split_axis=0, concat_axis=0, tiled=True)
     logs, averages = fresh(parents, forget_bias, normed, w_key, w_value, w_forget, q, own)
     weights = [w_out, swap_core(w_out), w_out_far, swap_core(w_out_far)]
-    attended = merge(table, back, logs, averages, steps, capacity)
 
     flat = tokens.reshape(steps * rows, width)
-    heres = [attended[step : step + 2].reshape(2 * rows, inner) for step in range(0, steps, 2)]
+    each = steps // PARTS
+    heres = [
+        merge(index, table, back[index], logs, averages, each, capacity).reshape(each * rows, inner)
+        for index in range(PARTS)
+    ]
     fars = [swap_chip(here) for here in heres]
-    done = [None, None]
-    residual, mine, other, chip = [[None, None] for _ in range(4)]
+    residual, mine, other, chip, far_chip = [[None] * PARTS for _ in range(5)]
     for index, (here, far) in enumerate(zip(heres, fars)):
         gathered = [here, swap_core(here), far, swap_core(far)]
         if index:
             gathered, other[0] = lax.optimization_barrier((gathered, other[0]))
-        residual[index], normed = mix(2 * index * rows, gathered, weights, flat, gain_ffn)
+        residual[index], normed = mix(index * each * rows, gathered, weights, flat, gain_ffn)
         if index:
             chip[0] = (mine[0] + swap_core(other[0]).astype(f32)).astype(bf16)
             chip[0], normed = lax.optimization_barrier((chip[0], normed))
         mine[index], other[index] = ffn(normed, w_gate, w_up, w_down)
+    far_chip[0] = swap_chip(chip[0])
     chip[1] = (mine[1] + swap_core(other[1]).astype(f32)).astype(bf16)
+    chip[1], far_chip[0] = lax.optimization_barrier((chip[1], far_chip[0]))
+    far_chip[1] = swap_chip(chip[1])
     parts = []
-    for index in range(2):
-        both = chip[index].astype(f32) + swap_chip(chip[index]).astype(f32)
+    for index in range(PARTS):
+        both = chip[index].astype(f32) + far_chip[index].astype(f32)
         done = (residual[index] + both).astype(bf16)
         parts.extend([done, swap_core(done)])
     return finish(parts)

time: 119 us -> 138 us (1.16)
  local copies, waits for them, and re-layouts: 2.77 us -> 14.1 us
  starting transfers between devices: 23.2 us -> 31.8 us
  waiting for transfers between devices: 42 us -> 39.1 us
  Pallas kernels: 49.7 us -> 51.1 us
    unnamed x22 -> x40, local copies, waits for them, and re-layouts: 0.7 us -> 12.1 us
    all_to_all x3 -> x5, starting transfers between devices: 15 us -> 25.2 us  [exchange(): lax.all_to_all(value, 'group', split_axis=0, concat_axis=0, tiled=True)]
    pallas_call x4 -> x7, Pallas kernels: 22.5 us -> 25.5 us  [the longest x2 9.8 us: merge(): pl.pallas_call(functools.partial(merge_kernel, capacity, steps, part), in...]
    all_to_all x3 -> x5, waiting for transfers between devices: 14.9 us -> 12 us  [exchange(): lax.all_to_all(value, 'group', split_axis=0, concat_axis=0, tiled=True)]
    pallas_call x1, Pallas kernels: 11 us -> 8.9 us  [fresh(): pl.pallas_call(fresh_kernel, in_specs=[vmem, vmem] + [hbm] * len(big), ou...]
    ppermute x5, starting transfers between devices: 6.72 us -> 4.78 us  [swap_chip(): return lax.ppermute(value, 'head', [(i, i ^ 2) for i in range(4)])]
  transfers between devices with their start and end apart: 18 -> 20, of which waited for: 10 -> 8; matrix products, arithmetic and copies ran while one was open for 1% -> 1% of each run, Pallas kernels for 34% -> 33%
where the time goes in v3:
time: 138 us; the launch traced here: 137 us
  Pallas kernels  51.1 us (37%)
  waiting for transfers between devices  39.1 us (28%)
  starting transfers between devices  31.8 us (23%)
  local copies, waits for them, and re-layouts  14.1 us (10%)
    all_to_all x5, starting transfers between devices, exchange(): lax.all_to_all(value, 'group', split_axis=0, concat_axis=0, tiled=True)  25.2 us
    ppermute x5, waiting for transfers between devices, swap_chip(): return lax.ppermute(value, 'head', [(i, i ^ 2) for i in range(4)])  24.2 us
    unnamed x40, local copies, waits for them, and re-layouts  12.1 us
    all_to_all x5, waiting for transfers between devices, exchange(): lax.all_to_all(value, 'group', split_axis=0, concat_axis=0, tiled=True)  12 us
    pallas_call x2, Pallas kernels, merge(): pl.pallas_call(functools.partial(merge_kernel, capacity, steps, part), in...  9.8 us
    pallas_call x2, Pallas kernels, mix(): pl.pallas_call(functools.partial(mix_kernel, first), in_specs=[vmem] * 8...  9.73 us
    pallas_call x1, Pallas kernels, fresh(): pl.pallas_call(fresh_kernel, in_specs=[vmem, vmem] + [hbm] * len(big), ou...  8.9 us
    pallas_call x2, Pallas kernels, hosted_pages(): pl.pallas_call(functools.partial(hosted_kernel, local_count, capacity), i...  5.67 us
  transfers between devices with their start and end apart: 20, of which 8 were waited for; matrix products, arithmetic and copies ran while one was open for 1% of the time, Pallas kernels for 33%

profile of v3, /device:TPU:0, one launch (start us, length us, event | category | flops | bytes accessed | tf_op | source)
XLA Modules:
  0.0 136.9 jit_solution(17496121071318724015)
XLA Ops:
  0.0 1.3 broadcast_in_dim.3
  1.3 7.3 %all-to-all-start = ((s32[8,1,48]{2,1,0:T(1,128)}), s32[8,1,48]{2,1,0:T(1,128)S(1)}, u32[]{:S(2)}, u32[]{:S(2)}) async-start(s32[8,1,48]{2,1,0:T(1,128)} %broadcast_in_dim.3), calls=%async_computation | async-start | bytes 8192 | tf_op jit(solution)/shard_map/all_to_all | solution.py:729
  9.3 3.7 %queries.1 = (bf16[512,384]{1,0:T(8,128)(2,1)S(1)}, bf16[512,384]{1,0:T(8,128)(2,1)}, bf16[512,1536]{1,0:T(8,128)(2,1)}) custom-call(bf16[4,128,1536]{2,1,0:T(8,128)(2,1)} %tokens_hbm.1, f32[1,1536]{1,0:T(1,128)S(1)} %reshape.39.gain_ref, bf16[384,1536]{1,0:T(8,128)(2,1)} %wq_hbm.1), custom_call_target="tpu_custom_call" | custom-call | flops 603979776 | bytes 6291456 | tf_op jit(solution)/shard_map/queries/pallas_call | solution.py:125
  13.1 2.0 %all-to-all-done.ids_ref = s32[8,1,48]{2,1,0:T(1,128)S(1)} async-done(((s32[8,1,48]{2,1,0:T(1,128)}), s32[8,1,48]{2,1,0:T(1,128)S(1)}, u32[]{:S(2)}, u32[]{:S(2)}) %all-to-all-start) | async-done | bytes 1568 | tf_op jit(solution)/shard_map/all_to_all | solution.py:729
  15.1 2.0 %ask.1 = (s32[24]{0:T(128)S(1)}, bf16[24,16,384]{2,1,0:T(8,128)(2,1)}, bf16[24,16,384]{2,1,0:T(8,128)(2,1)}) custom-call(s32[48]{0:T(128)S(1)} %copy-done.13, s32[8,1,48]{2,1,0:T(1,128)S(1)} %all-to-all-done.ids_ref, bf16[512,384]{1,0:T(8,128)(2,1)S(1)} %get-tuple-element.39.q_ref), custom_call_target="tpu_custom_call" | custom-call | tf_op jit(solution)/shard_map/ask/pallas_call | solution.py:164
  17.1 4.2 %all-to-all-start.1 = ((bf16[8,48,384]{2,1,0:T(8,128)(2,1)}), bf16[8,48,384]{2,1,0:T(8,128)(2,1)S(1)}, u32[]{:S(2)}, u32[]{:S(2)}) async-start(bf16[8,48,384]{2,1,0:T(8,128)(2,1)} %bitcast), calls=%async_computation.1 | async-start | bytes 589824 | tf_op jit(solution)/shard_map/all_to_all | solution.py:729
  21.3 1.5 %collective-permute-start.4 = (bf16[384,1536]{1,0:T(8,128)(2,1)}, bf16[384,1536]{1,0:T(8,128)(2,1)}, u32[]{:S(2)}, u32[]{:S(2)}) collective-permute-start(bf16[384,1536]{1,0:T(8,128)(2,1)} %w0.3), channel_id=1, source_target_pairs={{0,2},{1,3},{2,0},{3,1},{4,6},{5,7},{6,4},{7,5},{8,10},{9,11},{10,... | collective-permute-start | bytes 3538952 | tf_op jit(solution)/shard_map/ppermute | solution.py:712
  22.7 7.5 %all-to-all-done.1 = bf16[8,48,384]{2,1,0:T(8,128)(2,1)S(1)} async-done(((bf16[8,48,384]{2,1,0:T(8,128)(2,1)}), bf16[8,48,384]{2,1,0:T(8,128)(2,1)S(1)}, u32[]{:S(2)}, u32[]{:S(2)}) %all-to-all-start.1) | async-done | bytes 294944 | tf_op jit(solution)/shard_map/all_to_all | solution.py:729
  30.3 3.6 %all-to-all-start.3 = ((bf16[8,48,384]{2,1,0:T(8,128)(2,1)}), bf16[8,48,384]{2,1,0:T(8,128)(2,1)S(1)}, u32[]{:S(2)}, u32[]{:S(2)}) async-start(bf16[8,48,384]{2,1,0:T(8,128)(2,1)} %bitcast.4), calls=%async_computation.3 | async-start | bytes 589824 | tf_op jit(solution)/shard_map/all_to_all | solution.py:729
  33.9 2.3 %copy-done = bf16[48,384,128]{2,1,0:T(8,128)(2,1)S(1)} copy-done((bf16[48,384,128]{2,1,0:T(8,128)(2,1)S(1)}, bf16[48,384,128]{2,1,0:T(8,128)(2,1)}, u32[]{:S(2)}) %copy-start) | copy-done | bytes 4718616
  36.3 2.3 %copy-done.2 = bf16[48,384,128]{2,1,0:T(8,128)(2,1)S(1)} copy-done((bf16[48,384,128]{2,1,0:T(8,128)(2,1)S(1)}, bf16[48,384,128]{2,1,0:T(8,128)(2,1)}, u32[]{:S(2)}) %copy-start.2) | copy-done | bytes 4718616
  38.6 4.3 %own_pages.1 = (f32[512,384]{1,0:T(8,128)S(1)}, f32[512,384]{1,0:T(8,128)S(1)}, f32[512,384]{1,0:T(8,128)S(1)}) custom-call(s32[48]{0:T(128)S(1)} %copy-done.13, s32[48]{0:T(128)S(1)} %copy-done.14, bf16[512,384]{1,0:T(8,128)(2,1)S(1)} %copy-done.8, bf16[48,384,128]{2,1,0:T(8,128)(2,1)S(1)} %copy-done, bf16[48,384,128]{2,1,0:T(8,128)(2,1)S(1)} %copy-done.2, ...), custom_call_target="tpu_custom_call" | custom-call | flops 805306368 | bytes 6291456 | tf_op jit(solution)/shard_map/own_pages/pallas_call | solution.py:442
  45.7 2.8 %hosted_pages.2 = bf16[8,64,384]{2,1,0:T(8,128)(2,1)} custom-call(s32[48]{0:T(128)S(1)} %copy-done.13, s32[48]{0:T(128)S(1)} %copy-done.14, bf16[24,16,384]{2,1,0:T(8,128)(2,1)S(1)} %bitcast.15, bf16[48,384,128]{2,1,0:T(8,128)(2,1)S(1)} %bitcast.13, bf16[48,384,128]{2,1,0:T(8,128)(2,1)S(1)} %copy-done.3, bf16[6,48,128]{2,1,0:T(8,128)(2,1)S(1)} %bitcast.20), custom_call_target="tpu_custom_call" | custom-call | flops 402653184 | bytes 3145728 | tf_op jit(solution)/shard_map/hosted_pages/pallas_call | solution.py:507
  48.5 6.0 %all-to-all-start.2 = ((bf16[8,64,384]{2,1,0:T(8,128)(2,1)}), bf16[8,64,384]{2,1,0:T(8,128)(2,1)S(1)}, u32[]{:S(2)}, u32[]{:S(2)}) async-start(bf16[8,64,384]{2,1,0:T(8,128)(2,1)} %hosted_pages.2), calls=%async_computation.2 | async-start | bytes 786432 | tf_op jit(solution)/shard_map/all_to_all | solution.py:729
  55.0 2.3 %copy-done.1 = bf16[48,384,128]{2,1,0:T(8,128)(2,1)S(1)} copy-done((bf16[48,384,128]{2,1,0:T(8,128)(2,1)S(1)}, bf16[48,384,128]{2,1,0:T(8,128)(2,1)}, u32[]{:S(2)}) %copy-start.1) | copy-done | bytes 4718616
  57.4 2.3 %copy-done.4 = bf16[48,384,128]{2,1,0:T(8,128)(2,1)S(1)} copy-done((bf16[48,384,128]{2,1,0:T(8,128)(2,1)S(1)}, bf16[48,384,128]{2,1,0:T(8,128)(2,1)}, u32[]{:S(2)}) %copy-start.4) | copy-done | bytes 4718616
  59.7 2.9 %hosted_pages.3 = bf16[8,64,384]{2,1,0:T(8,128)(2,1)} custom-call(s32[48]{0:T(128)S(1)} %copy-done.13, s32[48]{0:T(128)S(1)} %copy-done.14, bf16[24,16,384]{2,1,0:T(8,128)(2,1)S(1)} %bitcast.14, bf16[48,384,128]{2,1,0:T(8,128)(2,1)S(1)} %copy-done.1, bf16[48,384,128]{2,1,0:T(8,128)(2,1)S(1)} %copy-done.4, bf16[6,48,128]{2,1,0:T(8,128)(2,1)S(1)} %bitcast.21), custom_call_target="tpu_custom_call" | custom-call | flops 402653184 | bytes 3145728 | tf_op jit(solution)/shard_map/hosted_pages/pallas_call | solution.py:507
  62.5 2.5 %all-to-all-done.2.back_ref = bf16[8,64,384]{2,1,0:T(8,128)(2,1)S(1)} async-done(((bf16[8,64,384]{2,1,0:T(8,128)(2,1)}), bf16[8,64,384]{2,1,0:T(8,128)(2,1)S(1)}, u32[]{:S(2)}, u32[]{:S(2)}) %all-to-all-start.2) | async-done | bytes 393248 | tf_op jit(solution)/shard_map/all_to_all | solution.py:729
  65.0 4.1 %all-to-all-start.4 = ((bf16[8,64,384]{2,1,0:T(8,128)(2,1)}), bf16[8,64,384]{2,1,0:T(8,128)(2,1)}, u32[]{:S(2)}, u32[]{:S(2)}) async-start(bf16[8,64,384]{2,1,0:T(8,128)(2,1)} %hosted_pages.3), calls=%async_computation.4 | async-start | bytes 786432 | tf_op jit(solution)/shard_map/all_to_all | solution.py:729
  69.2 8.9 %fresh.1 = (f32[2,16,16,384]{3,2,1,0:T(8,128)}, f32[2,16,16,384]{3,2,1,0:T(8,128)}) custom-call(s32[3,128]{1,0:T(4,128)S(1)} %copy-done.15, f32[1,6]{1,0:T(1,128)S(1)} %bitcast.22, bf16[512,1536]{1,0:T(8,128)(2,1)} %get-tuple-element.50.normed_hbm, bf16[384,1536]{1,0:T(8,128)(2,1)} %wk_hbm.1, bf16[384,1536]{1,0:T(8,128)(2,1)} %wv_hbm.1, ...), custom_call_target="tpu_custom_call" | custom-call | flops 1207959552 | bytes 12582912 | tf_op jit(solution)/shard_map/fresh/pallas_call | solution.py:327
  78.1 5.1 %merge.2 = bf16[2,128,384]{2,1,0:T(8,128)(2,1)} custom-call(s32[24]{0:T(128)S(1)} %get-tuple-element.40.table_ref, bf16[8,64,384]{2,1,0:T(8,128)(2,1)S(1)} %all-to-all-done.2.back_ref, f32[2,256,384]{2,1,0:T(8,128)} %bitcast.25, f32[2,256,384]{2,1,0:T(8,128)} %bitcast.27), custom_call_target="tpu_custom_call" | custom-call | flops 3932160 | bytes 8388608 | tf_op jit(solution)/shard_map/merge/pallas_call | solution.py:575
  83.2 1.6 %collective-permute-start.1 = (bf16[256,384]{1,0:T(8,128)(2,1)}, bf16[256,384]{1,0:T(8,128)(2,1)S(1)}, u32[]{:S(2)}, u32[]{:S(2)}) collective-permute-start(bf16[256,384]{1,0:T(8,128)(2,1)} %bitcast.9.att0), channel_id=1, source_target_pairs={{0,2},{1,3},{2,0},{3,1},{4,6},{5,7},{6,4},{7,5},{8,10},{9,11},{10,... | collective-permute-start | bytes 589832 | tf_op jit(solution)/shard_map/ppermute | solution.py:712
  84.7 4.7 %merge.3 = bf16[2,128,384]{2,1,0:T(8,128)(2,1)S(1)} custom-call(s32[24]{0:T(128)S(1)} %get-tuple-element.40.table_ref, bf16[8,64,384]{2,1,0:T(8,128)(2,1)} %all-to-all-done.4.back_ref, f32[2,256,384]{2,1,0:T(8,128)} %bitcast.26, f32[2,256,384]{2,1,0:T(8,128)} %bitcast.28), custom_call_target="tpu_custom_call" | custom-call | flops 3932160 | bytes 8388608 | tf_op jit(solution)/shard_map/merge/pallas_call | solution.py:575
  90.7 4.6 %collective-permute-done.7.att2 = bf16[256,384]{1,0:T(8,128)(2,1)S(1)} collective-permute-done((bf16[256,384]{1,0:T(8,128)(2,1)S(1)}, bf16[256,384]{1,0:T(8,128)(2,1)S(1)}, u32[]{:S(2)}, u32[]{:S(2)}) %collective-permute-start.7) | collective-permute-done | bytes 196640 | tf_op jit(solution)/shard_map/ppermute | solution.py:712
  95.3 5.1 %mix.2 = (f32[128,1536]{1,0:T(8,128)S(1)}, bf16[256,1536]{1,0:T(8,128)(2,1)S(1)}) custom-call(bf16[256,384]{1,0:T(8,128)(2,1)} %bitcast.9.att0, bf16[256,384]{1,0:T(8,128)(2,1)S(1)} %collective-permute-done.att1, bf16[256,384]{1,0:T(8,128)(2,1)S(1)} %collective-permute-done.1.att2, bf16[256,384]{1,0:T(8,128)(2,1)S(1)} %collective-permute-done.2.att3, ...), custom_call_target="tpu_custom_call" | custom-call | flops 1207959552 | bytes 8388608 | tf_op jit(solution)/shard_map/mix/pallas_call | solution.py:627
  100.4 2.8 %ffn.2 = (f32[128,1536]{1,0:T(8,128)S(1)}, bf16[128,1536]{1,0:T(8,128)(2,1)S(1)}) custom-call(bf16[256,1536]{1,0:T(8,128)(2,1)S(1)} %get-tuple-element.57.normed_ref, bf16[1536,1024]{1,0:T(8,128)(2,1)S(1)} %copy-done.5, bf16[1536,1024]{1,0:T(8,128)(2,1)S(1)} %copy-done.6, bf16[1024,1536]{1,0:T(8,128)(2,1)S(1)} %copy-done.7), custom_call_target="tpu_custom_call" | custom-call | flops 2415919104 | bytes 10485760 | tf_op jit(solution)/shard_map/ffn/pallas_call | solution.py:670
  103.9 4.6 %mix.3 = (f32[128,1536]{1,0:T(8,128)S(1)}, bf16[256,1536]{1,0:T(8,128)(2,1)S(1)}) custom-call(bf16[256,384]{1,0:T(8,128)(2,1)S(1)} %bitcast.18, bf16[256,384]{1,0:T(8,128)(2,1)S(1)} %collective-permute-done.6.att1, bf16[256,384]{1,0:T(8,128)(2,1)S(1)} %collective-permute-done.7.att2, bf16[256,384]{1,0:T(8,128)(2,1)S(1)} %collective-permute-done.8.att3, ...), custom_call_target="tpu_custom_call" | custom-call | flops 1207959552 | bytes 8388608 | tf_op jit(solution)/shard_map/mix/pallas_call | solution.py:627
  108.6 2.8 %ffn.3 = (f32[128,1536]{1,0:T(8,128)S(1)}, bf16[128,1536]{1,0:T(8,128)(2,1)S(1)}) custom-call(bf16[256,1536]{1,0:T(8,128)(2,1)S(1)} %get-tuple-element.67.normed_ref, bf16[1536,1024]{1,0:T(8,128)(2,1)S(1)} %copy-done.5, bf16[1536,1024]{1,0:T(8,128)(2,1)S(1)} %copy-done.6, bf16[1024,1536]{1,0:T(8,128)(2,1)S(1)} %copy-done.7), custom_call_target="tpu_custom_call" | custom-call | flops 2415919104 | bytes 10485760 | tf_op jit(solution)/shard_map/ffn/pallas_call | solution.py:670
  113.3 9.7 %collective-permute-done.11 = bf16[128,1536]{1,0:T(8,128)(2,1)S(1)} collective-permute-done((bf16[128,1536]{1,0:T(8,128)(2,1)S(1)}, bf16[128,1536]{1,0:T(8,128)(2,1)S(1)}, u32[]{:S(2)}, u32[]{:S(2)}) %collective-permute-start.11) | collective-permute-done | bytes 393248 | tf_op jit(solution)/shard_map/ppermute | solution.py:712
  123.8 9.9 %collective-permute-done.13 = bf16[128,1536]{1,0:T(8,128)(2,1)S(1)} collective-permute-done((bf16[128,1536]{1,0:T(8,128)(2,1)S(1)}, bf16[128,1536]{1,0:T(8,128)(2,1)S(1)}, u32[]{:S(2)}, u32[]{:S(2)}) %collective-permute-start.13) | collective-permute-done | bytes 393248 | tf_op jit(solution)/shard_map/ppermute | solution.py:712
  133.9 1.7 %collective-permute-done.14.refs_3_ = bf16[128,1536]{1,0:T(8,128)(2,1)S(1)} collective-permute-done((bf16[128,1536]{1,0:T(8,128)(2,1)S(1)}, bf16[128,1536]{1,0:T(8,128)(2,1)S(1)}, u32[]{:S(2)}, u32[]{:S(2)}) %collective-permute-start.14) | collective-permute-done | bytes 393248 | tf_op jit(solution)/shard_map/ppermute | solution.py:708
  135.6 1.3 finish.1
  (69 shorter events, 8.6 us)
Async XLA Ops:
  0.0 15.1 %copy-start.13 = (s32[48]{0:T(128)S(1)}, s32[48]{0:T(128)}, u32[]{:S(2)}) copy-start(s32[48]{0:T(128)} %request_ref.7) | copy-start | bytes 580
  1.3 13.7 %all-to-all-start = ((s32[8,1,48]{2,1,0:T(1,128)}), s32[8,1,48]{2,1,0:T(1,128)S(1)}, u32[]{:S(2)}, u32[]{:S(2)}) async-start(s32[8,1,48]{2,1,0:T(1,128)} %broadcast_in_dim.3), calls=%async_computation | async-start | bytes 8192 | tf_op jit(solution)/shard_map/all_to_all | solution.py:729
  9.3 24.6 %copy-start.12 = (bf16[48,6,128]{2,0,1:T(8,128)(2,1)S(1)}, bf16[48,6,128]{2,0,1:T(8,128)(2,1)}, u32[]{:S(2)}) copy-start(bf16[48,6,128]{2,0,1:T(8,128)(2,1)} %param.24) | copy-start | bytes 221188
  9.3 24.6 %copy-start.14 = (s32[48]{0:T(128)S(1)}, s32[48]{0:T(128)}, u32[]{:S(2)}) copy-start(s32[48]{0:T(128)} %fill_ref.5) | copy-start | bytes 580
  13.1 20.9 %copy-start.8 = (bf16[512,384]{1,0:T(8,128)(2,1)S(1)}, bf16[512,384]{1,0:T(8,128)(2,1)}, u32[]{:S(2)}) copy-start(bf16[512,384]{1,0:T(8,128)(2,1)} %get-tuple-element.42.q_ref.q_hbm) | copy-start | bytes 1179652
  17.1 28.6 %slice-start = ((s8[4718592]{0:T(1024)(128)(4,1)}), s8[524288]{0:T(1024)(128)(4,1)S(1)}, s32[]{:S(2)}) async-start(s8[4718592]{0:T(1024)(128)(4,1)} %bitcast.12), calls=%async_computation.5 | async-start | bytes 1048576
  17.1 13.2 %all-to-all-start.1 = ((bf16[8,48,384]{2,1,0:T(8,128)(2,1)}), bf16[8,48,384]{2,1,0:T(8,128)(2,1)S(1)}, u32[]{:S(2)}, u32[]{:S(2)}) async-start(bf16[8,48,384]{2,1,0:T(8,128)(2,1)} %bitcast), calls=%async_computation.1 | async-start | bytes 589824 | tf_op jit(solution)/shard_map/all_to_all | solution.py:729
  21.3 33.3 %collective-permute-start.4 = (bf16[384,1536]{1,0:T(8,128)(2,1)}, bf16[384,1536]{1,0:T(8,128)(2,1)}, u32[]{:S(2)}, u32[]{:S(2)}) collective-permute-start(bf16[384,1536]{1,0:T(8,128)(2,1)} %w0.3), channel_id=1, source_target_pairs={{0,2},{1,3},{2,0},{3,1},{4,6},{5,7},{6,4},{7,5},{8,10},{9,11},{10,... | collective-permute-start | bytes 3538952 | tf_op jit(solution)/shard_map/ppermute | solution.py:712
  30.3 18.2 %all-to-all-start.3 = ((bf16[8,48,384]{2,1,0:T(8,128)(2,1)}), bf16[8,48,384]{2,1,0:T(8,128)(2,1)S(1)}, u32[]{:S(2)}, u32[]{:S(2)}) async-start(bf16[8,48,384]{2,1,0:T(8,128)(2,1)} %bitcast.4), calls=%async_computation.3 | async-start | bytes 589824 | tf_op jit(solution)/shard_map/all_to_all | solution.py:729
  38.6 7.1 %slice-start.1 = ((s8[4718592]{0:T(1024)(128)(4,1)}), s8[4194304]{0:T(1024)(128)(4,1)S(1)}, s32[]{:S(2)}) async-start(s8[4718592]{0:T(1024)(128)(4,1)} %bitcast.12), calls=%async_computation.6 | async-start | bytes 8388608
  38.6 7.1 %copy-start.3 = (bf16[48,384,128]{2,1,0:T(8,128)(2,1)S(1)}, bf16[48,384,128]{2,1,0:T(8,128)(2,1)}, u32[]{:S(2)}) copy-start(bf16[48,384,128]{2,1,0:T(8,128)(2,1)} %values_ref.5) | copy-start | bytes 14155780
  48.5 16.5 %all-to-all-start.2 = ((bf16[8,64,384]{2,1,0:T(8,128)(2,1)}), bf16[8,64,384]{2,1,0:T(8,128)(2,1)S(1)}, u32[]{:S(2)}, u32[]{:S(2)}) async-start(bf16[8,64,384]{2,1,0:T(8,128)(2,1)} %hosted_pages.2), calls=%async_computation.2 | async-start | bytes 786432 | tf_op jit(solution)/shard_map/all_to_all | solution.py:729
  54.5 36.1 %collective-permute-start.3 = (bf16[384,1536]{1,0:T(8,128)(2,1)}, bf16[384,1536]{1,0:T(8,128)(2,1)}, u32[]{:S(2)}, u32[]{:S(2)}) collective-permute-start(bf16[384,1536]{1,0:T(8,128)(2,1)} %w0.3), channel_id=1, source_target_pairs={{0,1},{1,0},{2,3},{3,2},{4,5},{5,4},{6,7},{7,6},{8,9},{9,8},{10,11... | collective-permute-start | bytes 3538952 | tf_op jit(solution)/shard_map/ppermute | solution.py:708
  54.5 40.7 %collective-permute-start.5 = (bf16[384,1536]{1,0:T(8,128)(2,1)}, bf16[384,1536]{1,0:T(8,128)(2,1)}, u32[]{:S(2)}, u32[]{:S(2)}) collective-permute-start(bf16[384,1536]{1,0:T(8,128)(2,1)} %collective-permute-done.4.w2), channel_id=1, source_target_pairs={{0,1},{1,0},{2,3},{3,2},{4,5},{5,4},{6,7},{7,6},{8,9},{9,8},{10,11... | collective-permute-start | bytes 3538952 | tf_op jit(solution)/shard_map/ppermute | solution.py:708
  59.7 9.5 %copy-start.15 = (s32[3,128]{1,0:T(4,128)S(1)}, s32[3,128]{1,0:T(4,128)}, u32[]{:S(2)}) copy-start(s32[3,128]{1,0:T(4,128)} %parents_ref.1) | copy-start | bytes 4612
  59.7 9.5 %copy-start.16 = (f32[6]{0:T(128)S(1)}, f32[6]{0:T(128)}, u32[]{:S(2)}) copy-start(f32[6]{0:T(128)} %param.30) | copy-start | bytes 76
  65.0 19.7 %all-to-all-start.4 = ((bf16[8,64,384]{2,1,0:T(8,128)(2,1)}), bf16[8,64,384]{2,1,0:T(8,128)(2,1)}, u32[]{:S(2)}, u32[]{:S(2)}) async-start(bf16[8,64,384]{2,1,0:T(8,128)(2,1)} %hosted_pages.3), calls=%async_computation.4 | async-start | bytes 786432 | tf_op jit(solution)/shard_map/all_to_all | solution.py:729
  78.1 22.3 %copy-start.7 = (bf16[1024,1536]{1,0:T(8,128)(2,1)S(1)}, bf16[1024,1536]{1,0:T(8,128)(2,1)}, u32[]{:S(2)}) copy-start(bf16[1024,1536]{1,0:T(8,128)(2,1)} %down_ref.3) | copy-start | bytes 9437188
  83.1 7.4 %copy-start.17 = (f32[1536]{0:T(1024)S(1)}, f32[1536]{0:T(1024)}, u32[]{:S(2)}) copy-start(f32[1536]{0:T(1024)} %param.32) | copy-start | bytes 18436
  83.2 6.9 %collective-permute-start.1 = (bf16[256,384]{1,0:T(8,128)(2,1)}, bf16[256,384]{1,0:T(8,128)(2,1)S(1)}, u32[]{:S(2)}, u32[]{:S(2)}) collective-permute-start(bf16[256,384]{1,0:T(8,128)(2,1)} %bitcast.9.att0), channel_id=1, source_target_pairs={{0,2},{1,3},{2,0},{3,1},{4,6},{5,7},{6,4},{7,5},{8,10},{9,11},{10,... | collective-permute-start | bytes 589832 | tf_op jit(solution)/shard_map/ppermute | solution.py:712
  89.5 5.8 %collective-permute-start.7 = (bf16[256,384]{1,0:T(8,128)(2,1)S(1)}, bf16[256,384]{1,0:T(8,128)(2,1)S(1)}, u32[]{:S(2)}, u32[]{:S(2)}) collective-permute-start(bf16[256,384]{1,0:T(8,128)(2,1)S(1)} %bitcast.16), channel_id=1, source_target_pairs={{0,2},{1,3},{2,0},{3,1},{4,6},{5,7},{6,4},{7,5},{8,10},{9,11},{10,... | collective-permute-start | bytes 589832 | tf_op jit(solution)/shard_map/ppermute | solution.py:712
  90.1 5.2 %collective-permute-start = (bf16[256,384]{1,0:T(8,128)(2,1)}, bf16[256,384]{1,0:T(8,128)(2,1)S(1)}, u32[]{:S(2)}, u32[]{:S(2)}) collective-permute-start(bf16[256,384]{1,0:T(8,128)(2,1)} %bitcast.9.att0), channel_id=1, source_target_pairs={{0,1},{1,0},{2,3},{3,2},{4,5},{5,4},{6,7},{7,6},{8,9},{9,8},{10,11... | collective-permute-start | bytes 589832 | tf_op jit(solution)/shard_map/ppermute | solution.py:708
  90.1 5.2 %collective-permute-start.2 = (bf16[256,384]{1,0:T(8,128)(2,1)S(1)}, bf16[256,384]{1,0:T(8,128)(2,1)S(1)}, u32[]{:S(2)}, u32[]{:S(2)}) collective-permute-start(bf16[256,384]{1,0:T(8,128)(2,1)S(1)} %collective-permute-done.1.att2), channel_id=1, source_target_pairs={{0,1},{1,0},{2,3},{3,2},{4,5},{5,4},{6,7},{7,6},{8,9},{9,8},{10,11... | collective-permute-start | bytes 589832 | tf_op jit(solution)/shard_map/ppermute | solution.py:708
  90.6 12.7 %collective-permute-start.6 = (bf16[256,384]{1,0:T(8,128)(2,1)S(1)}, bf16[256,384]{1,0:T(8,128)(2,1)S(1)}, u32[]{:S(2)}, u32[]{:S(2)}) collective-permute-start(bf16[256,384]{1,0:T(8,128)(2,1)S(1)} %bitcast.17), channel_id=1, source_target_pairs={{0,1},{1,0},{2,3},{3,2},{4,5},{5,4},{6,7},{7,6},{8,9},{9,8},{10,11... | collective-permute-start | bytes 589832 | tf_op jit(solution)/shard_map/ppermute | solution.py:708
  95.2 8.0 %collective-permute-start.8 = (bf16[256,384]{1,0:T(8,128)(2,1)S(1)}, bf16[256,384]{1,0:T(8,128)(2,1)S(1)}, u32[]{:S(2)}, u32[]{:S(2)}) collective-permute-start(bf16[256,384]{1,0:T(8,128)(2,1)S(1)} %collective-permute-done.7.att2), channel_id=1, source_target_pairs={{0,1},{1,0},{2,3},{3,2},{4,5},{5,4},{6,7},{7,6},{8,9},{9,8},{10,11... | collective-permute-start | bytes 589832 | tf_op jit(solution)/shard_map/ppermute | solution.py:708
  95.3 5.2 %copy-start.5 = (bf16[1536,1024]{1,0:T(8,128)(2,1)S(1)}, bf16[1536,1024]{1,0:T(8,128)(2,1)}, u32[]{:S(2)}) copy-start(bf16[1536,1024]{1,0:T(8,128)(2,1)} %gate_ref.3) | copy-start | bytes 9437188
  103.3 5.2 %collective-permute-start.9 = (bf16[128,1536]{1,0:T(8,128)(2,1)S(1)}, bf16[128,1536]{1,0:T(8,128)(2,1)S(1)}, u32[]{:S(2)}, u32[]{:S(2)}) collective-permute-start(bf16[128,1536]{1,0:T(8,128)(2,1)S(1)} %get-tuple-element.60), channel_id=1, source_target_pairs={{0,1},{1,0},{2,3},{3,2},{4,5},{5,4},{6,7},{7,6},{8,9},{9,8},{10,11... | collective-permute-start | bytes 1179656 | tf_op jit(solution)/shard_map/ppermute | solution.py:708
  111.4 1.8 %collective-permute-start.10 = (bf16[128,1536]{1,0:T(8,128)(2,1)S(1)}, bf16[128,1536]{1,0:T(8,128)(2,1)S(1)}, u32[]{:S(2)}, u32[]{:S(2)}) collective-permute-start(bf16[128,1536]{1,0:T(8,128)(2,1)S(1)} %get-tuple-element.69), channel_id=1, source_target_pairs={{0,1},{1,0},{2,3},{3,2},{4,5},{5,4},{6,7},{7,6},{8,9},{9,8},{10,11... | collective-permute-start | bytes 1179656 | tf_op jit(solution)/shard_map/ppermute | solution.py:708
  111.5 11.5 %collective-permute-start.11 = (bf16[128,1536]{1,0:T(8,128)(2,1)S(1)}, bf16[128,1536]{1,0:T(8,128)(2,1)S(1)}, u32[]{:S(2)}, u32[]{:S(2)}) collective-permute-start(bf16[128,1536]{1,0:T(8,128)(2,1)S(1)} %add_convert_fusion.3), channel_id=1, source_target_pairs={{0,2},{1,3},{2,0},{3,1},{4,6},{5,7},{6,4},{7,5},{8,10},{9,11},{10,... | collective-permute-start | bytes 1179656 | tf_op jit(solution)/shard_map/ppermute | solution.py:712
  123.0 10.7 %collective-permute-start.13 = (bf16[128,1536]{1,0:T(8,128)(2,1)S(1)}, bf16[128,1536]{1,0:T(8,128)(2,1)S(1)}, u32[]{:S(2)}, u32[]{:S(2)}) collective-permute-start(bf16[128,1536]{1,0:T(8,128)(2,1)S(1)} %add_convert_fusion.2), channel_id=1, source_target_pairs={{0,2},{1,3},{2,0},{3,1},{4,6},{5,7},{6,4},{7,5},{8,10},{9,11},{10,... | collective-permute-start | bytes 1179656 | tf_op jit(solution)/shard_map/ppermute | solution.py:712
  123.7 10.2 %collective-permute-start.12 = (bf16[128,1536]{1,0:T(8,128)(2,1)S(1)}, bf16[128,1536]{1,0:T(8,128)(2,1)S(1)}, u32[]{:S(2)}, u32[]{:S(2)}) collective-permute-start(bf16[128,1536]{1,0:T(8,128)(2,1)S(1)} %add_convert_fusion.1.refs_0_), channel_id=1, source_target_pairs={{0,1},{1,0},{2,3},{3,2},{4,5},{5,4},{6,7},{7,6},{8,9},{9,8},{10,11... | collective-permute-start | bytes 1179656 | tf_op jit(solution)/shard_map/ppermute | solution.py:708
  133.8 1.8 %collective-permute-start.14 = (bf16[128,1536]{1,0:T(8,128)(2,1)S(1)}, bf16[128,1536]{1,0:T(8,128)(2,1)S(1)}, u32[]{:S(2)}, u32[]{:S(2)}) collective-permute-start(bf16[128,1536]{1,0:T(8,128)(2,1)S(1)} %add_convert_fusion.refs_2_), channel_id=1, source_target_pairs={{0,1},{1,0},{2,3},{3,2},{4,5},{5,4},{6,7},{7,6},{8,9},{9,8},{10,11... | collective-permute-start | bytes 1179656 | tf_op jit(solution)/shard_map/ppermute | solution.py:708
  (8 other events, 17.2 us)

commit v4 on v3

--- a/solution.py
+++ b/solution.py
@@ -146,16 +146,14 @@
     )(in_hbm(tokens), gain.reshape(1, -1), in_hbm(w_query))
 
 
-def ask_kernel(capacity, request_ref, ids_ref, q_ref, table_ref, *out_refs):
-    slots, part, _ = out_refs[0].shape
-    span = part * len(out_refs)
+def ask_kernel(capacity, request_ref, ids_ref, q_ref, table_ref, out_ref):
+    slots, span, _ = out_ref.shape
     local_count = q_ref.shape[0] // span
     first = request_ref[0] // local_count * local_count
     fill_table(local_count, capacity, first, ids_ref, table_ref)
     for slot in range(slots):
         start = jnp.maximum(table_ref[slot], 0) * span
-        for index, out_ref in enumerate(out_refs):
-            out_ref[slot] = q_ref[pl.ds(pl.multiple_of(start + index * part, part), part), :]
+        out_ref[slot] = q_ref[pl.ds(pl.multiple_of(start, span), span), :]
 
 
 def ask(request, ids, q, span, capacity):
@@ -164,9 +162,11 @@
     return pl.pallas_call(
         functools.partial(ask_kernel, capacity),
         in_specs=[SMEM, SMEM, vmem],
-        out_specs=[SMEM] + [vmem] * PARTS,
-        out_shape=[jax.ShapeDtypeStruct((slots,), jnp.int32)]
-        + [jax.ShapeDtypeStruct((slots, span // PARTS, q.shape[1]), bf16)] * PARTS,
+        out_specs=[SMEM, vmem],
+        out_shape=[
+            jax.ShapeDtypeStruct((slots,), jnp.int32),
+            jax.ShapeDtypeStruct((slots, span, q.shape[1]), bf16),
+        ],
         compiler_params=pltpu.CompilerParams(vmem_limit_bytes=8 * MIB),
         name="ask",
     )(request, ids, in_vmem(q))
@@ -344,12 +344,15 @@
     )(parents, bias.reshape(1, -1), *[in_hbm(x) for x in big])
 
 
-def page_weights(queries, fills, keys_ref, decay_ref, scores_ref, weights_ref, tops_ref):
+def page_weights(
+    queries, fills, keys_ref, decay_ref, scores_ref, weights_ref, tops_ref, arrival=lambda page: None
+):
     span = queries[0][0].shape[0]
     masks = half_masks(span)
     lane = lanes((1, 128))
     decay = [decay_ref[head].astype(f32) for head in range(decay_ref.shape[0])]
     for page, pairs in enumerate(queries):
+        arrival(page)
         valid = lane < fills[page]
         for pair, query in enumerate(pairs):
             raw = dot(stacked(query, masks), keys_ref[page, pl.ds(pair * 128, 128), :])
@@ -403,29 +406,27 @@
     local_count = q_ref.shape[0] // span
     pairs = q_ref.shape[1] // 128
 
-    top_ref[...] = jnp.full_like(top_ref, masked_score)
-    total_ref[...] = jnp.zeros_like(total_ref)
-    numer_ref[...] = jnp.zeros_like(numer_ref)
-
-    def block(number, carry):
-        start = pl.multiple_of(number * PAGE_BLOCK, PAGE_BLOCK)
-        pages = pl.ds(start, PAGE_BLOCK)
-        places, queries, fills = [], [], []
-        for page in range(PAGE_BLOCK):
-            local = lax.rem(request_ref[start + page], local_count)
-            rows = pl.ds(pl.multiple_of(local * span, span), span)
-            places.append(rows)
-            queries.append([q_ref[rows, pl.ds(pair * 128, 128)] for pair in range(pairs)])
-            fills.append(fill_ref[start + page])
-        values = values_ref.at[pages]
-        page_weights(queries, fills, keys_ref.at[pages], decay_ref.at[:, pages], *scratch)
-        for page, rows in enumerate(places):
-            for pair in range(pairs):
-                sums = page_sums(page, pair, span, values, *scratch)
-                absorb(state, rows, pl.ds(pair * 128, 128), *sums)
-        return carry
-
-    lax.fori_loop(0, OWNED_SLOTS // PAGE_BLOCK, block, 0)
+    block = pl.program_id(0)
+
+    @pl.when(block == 0)
+    def _():
+        top_ref[...] = jnp.full_like(top_ref, masked_score)
+        total_ref[...] = jnp.zeros_like(total_ref)
+        numer_ref[...] = jnp.zeros_like(numer_ref)
+
+    places, queries, fills = [], [], []
+    for page in range(PAGE_BLOCK):
+        index = block * PAGE_BLOCK + page
+        local = lax.rem(request_ref[index], local_count)
+        rows = pl.ds(pl.multiple_of(local * span, span), span)
+        places.append(rows)
+        queries.append([q_ref[rows, pl.ds(pair * 128, 128)] for pair in range(pairs)])
+        fills.append(fill_ref[index])
+    page_weights(queries, fills, keys_ref, decay_ref, *scratch)
+    for page, rows in enumerate(places):
+        for pair in range(pairs):
+            sums = page_sums(page, pair, span, values_ref, *scratch)
+            absorb(state, rows, pl.ds(pair * 128, 128), *sums)
 
 
 def page_cost(pages, keys, rows):
@@ -438,23 +439,36 @@
 
 
 def own_pages(request, fill, q, keys, values, decay, span):
-    vmem = pl.BlockSpec(memory_space=pltpu.VMEM)
+    pool = pl.BlockSpec((PAGE_BLOCK,) + keys.shape[1:], lambda i: (i, 0, 0))
+    decay_spec = pl.BlockSpec((decay.shape[0], PAGE_BLOCK, decay.shape[2]), lambda i: (0, i, 0))
+    rows = pl.BlockSpec(q.shape, lambda i: (0, 0))
     return pl.pallas_call(
         own_kernel,
-        in_specs=[SMEM, SMEM, vmem, vmem, vmem, vmem],
-        out_specs=[vmem] * 3,
-        out_shape=[jax.ShapeDtypeStruct(q.shape, f32)] * 3,
+        grid=(OWNED_SLOTS // PAGE_BLOCK,),
+        in_specs=[SMEM, SMEM, rows, pool, pool, decay_spec],
+        out_specs=[rows] * 3,
+        out_shape=[pltpu.HBM(q.shape, f32)] * 3,
         scratch_shapes=page_scratch(PAGE_BLOCK, span, decay.shape[0]),
-        compiler_params=pltpu.CompilerParams(vmem_limit_bytes=12 * MIB),
+        compiler_params=pltpu.CompilerParams(vmem_limit_bytes=20 * MIB),
         cost_estimate=page_cost(OWNED_SLOTS, keys, 64),
         name="own_pages",
-    )(request, fill, in_vmem(q), in_vmem(keys), in_vmem(values), decay)
+    )(request, fill, in_hbm(q), in_hbm(keys), in_hbm(values), decay)
 
 
 def hosted_kernel(
-    local_count, capacity, request_ref, fill_ref, q_ref, keys_ref, values_ref, decay_ref,
-    out_ref, tail_ref, count_ref, *scratch,
+    local_count, capacity, request_ref, fill_ref, q_ref, keys_hbm, values_hbm, decay_ref,
+    out_ref, keys_ref, values_ref, sems, tail_ref, count_ref, *scratch,
 ):
+    pieces = sems.shape[0] // 2
+    chunk = SPILL // pieces
+    copies = start_all(
+        [
+            (pool.at[pl.ds(OWNED_SLOTS + piece * chunk, chunk)], target.at[pl.ds(piece * chunk, chunk)])
+            for pool, target in ((keys_hbm, keys_ref), (values_hbm, values_ref))
+            for piece in range(pieces)
+        ],
+        sems,
+    )
     span, inner = q_ref.shape[1:]
     pairs = inner // 128
     heads = decay_ref.shape[0]
@@ -472,15 +486,21 @@
         slot = owner * capacity + rank
         queries.append([q_ref[slot, :, pl.ds(pair * 128, 128)] for pair in range(pairs)])
         fills.append(fill_ref[OWNED_SLOTS + page])
-    hosted = pl.ds(OWNED_SLOTS, SPILL)
-    values = values_ref.at[hosted]
-    page_weights(queries, fills, keys_ref.at[hosted], decay_ref.at[:, hosted], *scratch)
+
+    def arrival(page):
+        if page % chunk == 0:
+            copies[page // chunk].wait()
+
+    hosted = decay_ref.at[:, pl.ds(OWNED_SLOTS, SPILL)]
+    page_weights(queries, fills, keys_ref, hosted, *scratch, arrival=arrival)
+    for copy in copies[pieces:]:
+        copy.wait()
     scores_ref, _, tops_ref = scratch
     lane = lanes((span, 128))
     for page, (owner, rank) in enumerate(places):
         here = pl.ds(pl.multiple_of(rank * span, span), span)
         for pair in range(pairs):
-            _, total, numer = page_sums(page, pair, span, values, *scratch)
+            _, total, numer = page_sums(page, pair, span, values_ref, *scratch)
             out_ref[owner, here, pl.ds(pair * 128, 128)] = (numer / total).astype(bf16)
         tail = tail_ref[owner]
         base = rank * (3 * heads)
@@ -504,63 +524,63 @@
 def hosted_pages(request, fill, asked_rows, keys, values, decay, groups, capacity, local_count):
     count, span, inner = asked_rows.shape
     vmem = pl.BlockSpec(memory_space=pltpu.VMEM)
+    hbm = pl.BlockSpec(memory_space=pltpu.HBM)
+    pages = pltpu.VMEM((SPILL,) + keys.shape[1:], bf16)
     return pl.pallas_call(
         functools.partial(hosted_kernel, local_count, capacity),
-        in_specs=[SMEM, SMEM, vmem, vmem, vmem, vmem],
+        in_specs=[SMEM, SMEM, vmem, hbm, hbm, vmem],
         out_specs=vmem,
         out_shape=jax.ShapeDtypeStruct((groups, capacity * span + TAIL_ROWS, inner), bf16),
-        scratch_shapes=[pltpu.VMEM((groups, span, 128), f32), pltpu.SMEM((groups,), jnp.int32)]
+        scratch_shapes=[pages, pages, pltpu.SemaphoreType.DMA((8,))]
+        + [pltpu.VMEM((groups, span, 128), f32), pltpu.SMEM((groups,), jnp.int32)]
         + page_scratch(SPILL, span, decay.shape[0]),
-        compiler_params=pltpu.CompilerParams(vmem_limit_bytes=12 * MIB),
+        compiler_params=pltpu.CompilerParams(vmem_limit_bytes=14 * MIB),
         cost_estimate=page_cost(SPILL, keys, 64),
         name="hosted_pages",
-    )(request, fill, asked_rows, in_vmem(keys), in_vmem(values), decay)
+    )(request, fill, asked_rows, in_hbm(keys), in_hbm(values), decay)
 
 
 def merge_kernel(
     capacity, steps, part, table_ref, back_ref, log_hbm, average_hbm, out_ref,
-    top_ref, total_ref, numer_ref, sems,
+    top_ref, total_ref, numer_ref, tops_ref, sems,
 ):
     groups, _, inner = back_ref.shape
-    span = steps * BEAMS
+    rows = steps * BEAMS
+    span = PARTS * rows
     heads = inner // 64
     state = (top_ref, total_ref, numer_ref)
     copies = start_all([(log_hbm.at[part], top_ref), (average_hbm.at[part], numer_ref)], sems)
     total_ref[...] = jnp.ones_like(total_ref)
+    first = capacity * span
+    tails = jnp.concatenate(
+        [
+            back_ref[owner, first : first + TAIL_ROWS, part * 128 : part * 128 + 128]
+            for owner in range(groups)
+        ],
+        axis=0,
+    )
     source, target = sublanes((128, inner)), lanes((128, inner)) // 64
-    spread = []
     for rank in range(capacity):
         hit = source < 0
         for piece in range(3):
             hit = hit | (source == target + (rank * 3 + piece) * heads)
-        spread.append(hit.astype(f32).astype(bf16))
+        tops_ref[:, rank * inner : rank * inner + inner] = dot(tails, hit.astype(f32).astype(bf16))
     for copy in copies:
         copy.wait()
-
     for owner in range(groups):
-        first = capacity * span
         for rank in range(capacity):
             local = table_ref[owner * capacity + rank]
-
-            @pl.when(local >= 0)
-            def _():
-                tail = jnp.concatenate(
-                    [
-                        back_ref[owner, first : first + TAIL_ROWS, part * 128 : part * 128 + 128]
-                        for part in range(span // TAIL_ROWS)
-                    ],
-                    axis=0,
-                )
-                top = dot(tail, spread[rank])
-                average = back_ref[owner, rank * span : rank * span + span, :].astype(f32)
-                rows = pl.ds(pl.multiple_of(local * span, span), span)
-                absorb(state, rows, slice(None), top, 1.0, average)
-
-    for index in range(top_ref.shape[0] // (2 * span)):
+            bias = jnp.where(local >= 0, 0.0, masked_score)
+            top = tops_ref[owner * rows : owner * rows + rows, rank * inner : rank * inner + inner]
+            start = rank * span + part * rows
+            average = back_ref[owner, start : start + rows, :].astype(f32)
+            here = pl.ds(pl.multiple_of(jnp.maximum(local, 0) * rows, rows), rows)
+            absorb(state, here, slice(None), top + bias, 1.0, average)
+    for index in range(top_ref.shape[0] // (2 * rows)):
         parts = []
         for half in range(2):
-            rows = slice((index * 2 + half) * span, (index * 2 + half + 1) * span)
-            parts.append(numer_ref[rows, :] / total_ref[rows, :])
+            here = slice((index * 2 + half) * rows, (index * 2 + half + 1) * rows)
+            parts.append(numer_ref[here, :] / total_ref[here, :])
         for step in range(steps):
             both = jnp.concatenate([p[step * 8 : step * 8 + 8] for p in parts], axis=0)
             out_ref[step, index * 16 : index * 16 + 16, :] = both.astype(bf16)
@@ -576,7 +596,8 @@
         functools.partial(merge_kernel, capacity, steps, part),
         in_specs=[SMEM, vmem, hbm, hbm],
         out_shape=jax.ShapeDtypeStruct((steps, rows // steps, inner), bf16),
-        scratch_shapes=[pltpu.VMEM((rows, inner), f32)] * 3 + [pltpu.SemaphoreType.DMA((2,))],
+        scratch_shapes=[pltpu.VMEM((rows, inner), f32)] * 3
+        + [pltpu.VMEM((back.shape[0] * span, capacity * inner), f32), pltpu.SemaphoreType.DMA((2,))],
         compiler_params=pltpu.CompilerParams(vmem_limit_bytes=10 * MIB),
         cost_estimate=pl.CostEstimate(
             flops=40 * rows * inner, bytes_accessed=8 * MIB, transcendentals=4 * rows * inner
@@ -587,25 +608,29 @@
 
 def mix_kernel(
     first, att0, att1, att2, att3, w0, w1, w2, w3, tokens_hbm, gain_ref,
-    residual_out, normed_ref, residual_ref, tokens_ref, sems,
+    residual_out, normed_ref, residual_ref, tokens_ref, attended_ref, weight_ref, sems,
 ):
     rows, width = residual_ref.shape
+    inner = att0.shape[1]
     half = rows // 2
     head = lax.axis_index("head")
     near = pl.ds(pl.multiple_of(head % 2 * half, half), half)
-    copies = start_all([(tokens_hbm.at[first : first + rows], tokens_ref)], sems)
-    for own in range(4):
-
-        @pl.when(head == own)
-        def _():
-            order = [own ^ other for other in range(4)]
-            attended = jnp.concatenate([(att0, att1, att2, att3)[k][...] for k in order], axis=1)
-            for start in range(0, width, 512):
-                cols = slice(start, start + 512)
-                weight = jnp.concatenate([(w0, w1, w2, w3)[k][:, cols] for k in order], axis=0)
-                residual_ref[:, cols] = dot(attended, weight)
-
-    copies[0].wait()
+    places = [pl.ds(pl.multiple_of((head ^ other) * inner, inner), inner) for other in range(4)]
+    step = width // 3
+    columns = [slice(start, start + step) for start in range(0, width, step)]
+    pairs = [
+        (weight.at[:, cols], weight_ref.at[place, cols])
+        for cols in columns
+        for weight, place in zip((w0, w1, w2, w3), places)
+    ]
+    copies = start_all(pairs + [(tokens_hbm.at[first : first + rows], tokens_ref)], sems)
+    for att, place in zip((att0, att1, att2, att3), places):
+        attended_ref[:, place] = att[...]
+    for index, cols in enumerate(columns):
+        for copy in copies[index * 4 : index * 4 + 4]:
+            copy.wait()
+        residual_ref[:, cols] = dot(attended_ref[...], weight_ref[:, cols])
+    copies[-1].wait()
     gain = gain_ref[...]
 
     def norm(index, carry):
@@ -624,25 +649,28 @@
     rows, inner = attended[0].shape
     width = tokens.shape[1]
     vmem = pl.BlockSpec(memory_space=pltpu.VMEM)
+    hbm = pl.BlockSpec(memory_space=pltpu.HBM)
     return pl.pallas_call(
         functools.partial(mix_kernel, first),
-        in_specs=[vmem] * 8 + [pl.BlockSpec(memory_space=pltpu.HBM), vmem],
+        in_specs=[vmem] * 4 + [hbm] * 5 + [vmem],
         out_specs=[vmem] * 2,
         out_shape=[
             jax.ShapeDtypeStruct((rows // 2, width), f32),
-            pltpu.VMEM((rows, width), bf16),
+            jax.ShapeDtypeStruct((rows, width), bf16),
         ],
         scratch_shapes=[
             pltpu.VMEM((rows, width), f32),
             pltpu.VMEM((rows, width), bf16),
-            pltpu.SemaphoreType.DMA((1,)),
-        ],
-        compiler_params=pltpu.CompilerParams(vmem_limit_bytes=10 * MIB),
+            pltpu.VMEM((rows, 4 * inner), bf16),
+            pltpu.VMEM((4 * inner, width), bf16),
+            pltpu.SemaphoreType.DMA((13,)),
+        ],
+        compiler_params=pltpu.CompilerParams(vmem_limit_bytes=14 * MIB),
         cost_estimate=pl.CostEstimate(
             flops=8 * rows * width * inner, bytes_accessed=8 * MIB, transcendentals=rows
         ),
         name="mix",
-    )(*attended, *[in_vmem(w) for w in weights], in_hbm(tokens), gain.reshape(1, -1))
+    )(*attended, *[in_hbm(w) for w in weights], in_hbm(tokens), gain.reshape(1, -1))
 
 
 def ffn_kernel(normed_ref, gate_ref, up_ref, down_ref, mine_ref, other_ref, hidden_ref, sums_ref):
@@ -731,31 +759,22 @@
     ids = exchange(jnp.broadcast_to(page_request, (groups, 1, page_request.shape[0])))
     w_out_far = swap_chip(w_out)
     q_near, q, normed = queries_of(tokens, gain_attn, w_query)
-    table, *asked = ask(page_request, ids, q_near, span, capacity)
-    part = span // PARTS
-    asked_rows = [
-        exchange(x.reshape(groups, capacity * part, inner)).reshape(groups * capacity, part, inner)
-        for x in asked
-    ]
+    table, asked = ask(page_request, ids, q_near, span, capacity)
+    asked_rows = exchange(asked.reshape(groups, capacity * span, inner)).reshape(asked.shape)
     own = own_pages(page_request, page_fill, q, keys_pool, values_pool, decay, span)
-    asked_rows[0], own = lax.optimization_barrier((asked_rows[0], own))
-    back = []
-    for index in range(PARTS):
-        if index:
-            asked_rows[index], payload = lax.optimization_barrier((asked_rows[index], payload))
-        payload = hosted_pages(
-            page_request, page_fill, asked_rows[index], keys_pool, values_pool, decay,
-            groups, capacity, local_count,
-        )
-        back.append(exchange(payload))
+    asked_rows, own = lax.optimization_barrier((asked_rows, own))
+    payload = hosted_pages(
+        page_request, page_fill, asked_rows, keys_pool, values_pool, decay, groups, capacity, local_count
+    )
     payload, normed = lax.optimization_barrier((payload, normed))
+    back = exchange(payload)
     logs, averages = fresh(parents, forget_bias, normed, w_key, w_value, w_forget, q, own)
     weights = [w_out, swap_core(w_out), w_out_far, swap_core(w_out_far)]
 
     flat = tokens.reshape(steps * rows, width)
     each = steps // PARTS
     heres = [
-        merge(index, table, back[index], logs, averages, each, capacity).reshape(each * rows, inner)
+        merge(index, table, back, logs, averages, each, capacity).reshape(each * rows, inner)
         for index in range(PARTS)
     ]
     fars = [swap_chip(here) for here in heres]
@@ -770,8 +789,8 @@
             chip[0], normed = lax.optimization_barrier((chip[0], normed))
         mine[index], other[index] = ffn(normed, w_gate, w_up, w_down)
     far_chip[0] = swap_chip(chip[0])
+    other[1], far_chip[0] = lax.optimization_barrier((other[1], far_chip[0]))
     chip[1] = (mine[1] + swap_core(other[1]).astype(f32)).astype(bf16)
-    chip[1], far_chip[0] = lax.optimization_barrier((chip[1], far_chip[0]))
     far_chip[1] = swap_chip(chip[1])
     parts = []
     for index in range(PARTS):

time: 138 us -> 122 us (0.88)
  local copies, waits for them, and re-layouts: 14.1 us -> 2.51 us
  starting transfers between devices: 31.8 us -> 23.6 us
  waiting for transfers between devices: 39.1 us -> 41.8 us
  Pallas kernels: 51.1 us -> 52.8 us
    unnamed x40 -> x22, local copies, waits for them, and re-layouts: 12.1 us -> 0.5 us
    all_to_all x5 -> x3, starting transfers between devices: 25.2 us -> 15.1 us  [exchange(): lax.all_to_all(value, 'group', split_axis=0, concat_axis=0, tiled=True)]
    pallas_call x2 -> x1, Pallas kernels: 5.67 us -> 11.9 us  [hosted_pages(): pl.pallas_call(functools.partial(hosted_kernel, local_count, capacity), i...]
    pallas_call x2, Pallas kernels: 9.8 us -> 4.37 us  [merge(): pl.pallas_call(functools.partial(merge_kernel, capacity, steps, part), in...]
    all_to_all x5 -> x3, waiting for transfers between devices: 12 us -> 17.1 us  [exchange(): lax.all_to_all(value, 'group', split_axis=0, concat_axis=0, tiled=True)]
    ppermute x5, waiting for transfers between devices: 24.2 us -> 21.3 us  [swap_chip(): return lax.ppermute(value, 'head', [(i, i ^ 2) for i in range(4)])]
    ppermute x5, starting transfers between devices: 4.78 us -> 6.6 us  [swap_chip(): return lax.ppermute(value, 'head', [(i, i ^ 2) for i in range(4)])]
  transfers between devices with their start and end apart: 20 -> 18, of which waited for: 8 -> 9; matrix products, arithmetic and copies ran while one was open for 1% -> 1% of each run, Pallas kernels for 33% -> 41%
where the time goes in v4:
time: 122 us; the launch traced here: 121 us
  Pallas kernels  52.8 us (43%)
  waiting for transfers between devices  41.8 us (34%)
  starting transfers between devices  23.6 us (19%)
  local copies, waits for them, and re-layouts  2.51 us (2%)
    ppermute x5, waiting for transfers between devices, swap_chip(): return lax.ppermute(value, 'head', [(i, i ^ 2) for i in range(4)])  21.3 us
    all_to_all x3, waiting for transfers between devices, exchange(): lax.all_to_all(value, 'group', split_axis=0, concat_axis=0, tiled=True)  17.1 us
    all_to_all x3, starting transfers between devices, exchange(): lax.all_to_all(value, 'group', split_axis=0, concat_axis=0, tiled=True)  15.1 us
    pallas_call x1, Pallas kernels, hosted_pages(): pl.pallas_call(functools.partial(hosted_kernel, local_count, capacity), i...  11.9 us
    pallas_call x1, Pallas kernels, fresh(): pl.pallas_call(fresh_kernel, in_specs=[vmem, vmem] + [hbm] * len(big), ou...  8.89 us
    pallas_call x2, Pallas kernels, mix(): pl.pallas_call(functools.partial(mix_kernel, first), in_specs=[vmem] * 4...  8.13 us
    pallas_call x1, Pallas kernels, own_pages(): pl.pallas_call(own_kernel, grid=(OWNED_SLOTS // PAGE_BLOCK,), in_specs=[S...  6.89 us
    ppermute x5, starting transfers between devices, swap_chip(): return lax.ppermute(value, 'head', [(i, i ^ 2) for i in range(4)])  6.6 us
  transfers between devices with their start and end apart: 18, of which 9 were waited for; matrix products, arithmetic and copies ran while one was open for 1% of the time, Pallas kernels for 41%

profile of v4, /device:TPU:0, one launch (start us, length us, event | category | flops | bytes accessed | tf_op | source)
XLA Modules:
  0.0 121.4 jit_solution(16646395285892503447)
XLA Ops:
  0.0 1.3 %broadcast_in_dim.3 = s32[8,1,48]{2,1,0:T(1,128)} broadcast(s32[48]{0:T(128)} %request_ref.5), dimensions={2} | broadcast | bytes 1728 | tf_op jit(solution)/shard_map/broadcast_in_dim | solution.py:759
  1.3 7.3 %all-to-all-start = ((s32[8,1,48]{2,1,0:T(1,128)}), s32[8,1,48]{2,1,0:T(1,128)S(1)}, u32[]{:S(2)}, u32[]{:S(2)}) async-start(s32[8,1,48]{2,1,0:T(1,128)} %broadcast_in_dim.3), calls=%async_computation | async-start | bytes 8192 | tf_op jit(solution)/shard_map/all_to_all | solution.py:757
  8.6 0.7 reshape.33.gain_ref
  9.3 3.8 %queries.1 = (bf16[512,384]{1,0:T(8,128)(2,1)S(1)}, bf16[512,384]{1,0:T(8,128)(2,1)}, bf16[512,1536]{1,0:T(8,128)(2,1)}) custom-call(bf16[4,128,1536]{2,1,0:T(8,128)(2,1)} %tokens_hbm.1, f32[1,1536]{1,0:T(1,128)S(1)} %reshape.33.gain_ref, bf16[384,1536]{1,0:T(8,128)(2,1)} %wq_hbm.1), custom_call_target="tpu_custom_call" | custom-call | flops 603979776 | bytes 6291456 | tf_op jit(solution)/shard_map/queries/pallas_call | solution.py:125
  13.1 1.9 %all-to-all-done.ids_ref = s32[8,1,48]{2,1,0:T(1,128)S(1)} async-done(((s32[8,1,48]{2,1,0:T(1,128)}), s32[8,1,48]{2,1,0:T(1,128)S(1)}, u32[]{:S(2)}, u32[]{:S(2)}) %all-to-all-start) | async-done | bytes 1568 | tf_op jit(solution)/shard_map/all_to_all | solution.py:757
  15.1 2.0 %ask.1 = (s32[24]{0:T(128)S(1)}, bf16[24,32,384]{2,1,0:T(8,128)(2,1)}) custom-call(s32[48]{0:T(128)S(1)} %copy-done.4, s32[8,1,48]{2,1,0:T(1,128)S(1)} %all-to-all-done.ids_ref, bf16[512,384]{1,0:T(8,128)(2,1)S(1)} %get-tuple-element.38.q_ref), custom_call_target="tpu_custom_call" | custom-call | tf_op jit(solution)/shard_map/ask/pallas_call | solution.py:162
  17.0 4.1 %all-to-all-start.1 = ((bf16[8,96,384]{2,1,0:T(8,128)(2,1)}), bf16[8,96,384]{2,1,0:T(8,128)(2,1)S(1)}, u32[]{:S(2)}, u32[]{:S(2)}) async-start(bf16[8,96,384]{2,1,0:T(8,128)(2,1)} %bitcast), calls=%async_computation.1 | async-start | bytes 1179648 | tf_op jit(solution)/shard_map/all_to_all | solution.py:757
  21.1 1.6 %collective-permute-start.4 = (bf16[384,1536]{1,0:T(8,128)(2,1)S(1)}, bf16[384,1536]{1,0:T(8,128)(2,1)S(1)}, u32[]{:S(2)}, u32[]{:S(2)}) collective-permute-start(bf16[384,1536]{1,0:T(8,128)(2,1)S(1)} %copy-done.8), channel_id=1, source_target_pairs={{0,2},{1,3},{2,0},{3,1},{4,6},{5,7},{6,4},{7,5},{8,10},{9,11},{10,... | collective-permute-start | bytes 3538952 | tf_op jit(solution)/shard_map/ppermute | solution.py:740
  22.7 6.9 %own_pages.1 = (f32[512,384]{1,0:T(8,128)}, f32[512,384]{1,0:T(8,128)}, f32[512,384]{1,0:T(8,128)}) custom-call(s32[48]{0:T(128)S(1)} %copy-done.4, s32[48]{0:T(128)S(1)} %copy-done.6, bf16[512,384]{1,0:T(8,128)(2,1)} %get-tuple-element.41.q_ref.q_hbm, bf16[48,384,128]{2,1,0:T(8,128)(2,1)} %keys_hbm.1, bf16[48,384,128]{2,1,0:T(8,128)(2,1)} %values_hbm.1, ...), custom_call_target="tpu_custom_call" | custom-call | flops 805306368 | bytes 6291456 | tf_op jit(solution)/shard_map/own_pages/pallas_call | solution.py:445
  29.6 6.9 %all-to-all-done.1 = bf16[8,96,384]{2,1,0:T(8,128)(2,1)S(1)} async-done(((bf16[8,96,384]{2,1,0:T(8,128)(2,1)}), bf16[8,96,384]{2,1,0:T(8,128)(2,1)S(1)}, u32[]{:S(2)}, u32[]{:S(2)}) %all-to-all-start.1) | async-done | bytes 589856 | tf_op jit(solution)/shard_map/all_to_all | solution.py:757
  36.5 11.9 %hosted_pages.1 = bf16[8,112,384]{2,1,0:T(8,128)(2,1)} custom-call(s32[48]{0:T(128)S(1)} %copy-done.4, s32[48]{0:T(128)S(1)} %copy-done.6, bf16[24,32,384]{2,1,0:T(8,128)(2,1)S(1)} %bitcast.10, bf16[48,384,128]{2,1,0:T(8,128)(2,1)} %keys_hbm.1, bf16[48,384,128]{2,1,0:T(8,128)(2,1)} %values_hbm.1, bf16[6,48,128]{2,1,0:T(8,128)(2,1)S(1)} %bitcast.18), custom_call_target="tpu_custom_call" | custom-call | flops 402653184 | bytes 3145728 | tf_op jit(solution)/shard_map/hosted_pages/pallas_call | solution.py:529
  48.4 3.7 %all-to-all-start.2 = ((bf16[8,112,384]{2,1,0:T(8,128)(2,1)}), bf16[8,112,384]{2,1,0:T(8,128)(2,1)S(1)}, u32[]{:S(2)}, u32[]{:S(2)}) async-start(bf16[8,112,384]{2,1,0:T(8,128)(2,1)} %hosted_pages.1), calls=%async_computation.2 | async-start | bytes 1376256 | tf_op jit(solution)/shard_map/all_to_all | solution.py:757
  52.7 8.9 %fresh.1 = (f32[2,16,16,384]{3,2,1,0:T(8,128)}, f32[2,16,16,384]{3,2,1,0:T(8,128)}) custom-call(s32[3,128]{1,0:T(4,128)S(1)} %copy-done.5, f32[1,6]{1,0:T(1,128)S(1)} %bitcast.19, bf16[512,1536]{1,0:T(8,128)(2,1)} %get-tuple-element.48.normed_hbm, bf16[384,1536]{1,0:T(8,128)(2,1)} %wk_hbm.1, bf16[384,1536]{1,0:T(8,128)(2,1)} %wv_hbm.1, ...), custom_call_target="tpu_custom_call" | custom-call | flops 1207959552 | bytes 12582912 | tf_op jit(solution)/shard_map/fresh/pallas_call | solution.py:327
  61.6 8.3 %all-to-all-done.2.back_ref = bf16[8,112,384]{2,1,0:T(8,128)(2,1)S(1)} async-done(((bf16[8,112,384]{2,1,0:T(8,128)(2,1)}), bf16[8,112,384]{2,1,0:T(8,128)(2,1)S(1)}, u32[]{:S(2)}, u32[]{:S(2)}) %all-to-all-start.2) | async-done | bytes 688160 | tf_op jit(solution)/shard_map/all_to_all | solution.py:757
  69.9 2.0 %merge.2 = bf16[2,128,384]{2,1,0:T(8,128)(2,1)S(1)} custom-call(s32[24]{0:T(128)S(1)} %get-tuple-element.39.table_ref, bf16[8,112,384]{2,1,0:T(8,128)(2,1)S(1)} %all-to-all-done.2.back_ref, f32[2,256,384]{2,1,0:T(8,128)} %bitcast.22, f32[2,256,384]{2,1,0:T(8,128)} %bitcast.24), custom_call_target="tpu_custom_call" | custom-call | flops 3932160 | bytes 8388608 | tf_op jit(solution)/shard_map/merge/pallas_call | solution.py:595
  72.0 1.6 %collective-permute-start.1 = (bf16[256,384]{1,0:T(8,128)(2,1)S(1)}, bf16[256,384]{1,0:T(8,128)(2,1)S(1)}, u32[]{:S(2)}, u32[]{:S(2)}) collective-permute-start(bf16[256,384]{1,0:T(8,128)(2,1)S(1)} %bitcast.14), channel_id=1, source_target_pairs={{0,2},{1,3},{2,0},{3,1},{4,6},{5,7},{6,4},{7,5},{8,10},{9,11},{10,... | collective-permute-start | bytes 589832 | tf_op jit(solution)/shard_map/ppermute | solution.py:740
  73.6 2.3 %merge.3 = bf16[2,128,384]{2,1,0:T(8,128)(2,1)S(1)} custom-call(s32[24]{0:T(128)S(1)} %get-tuple-element.39.table_ref, bf16[8,112,384]{2,1,0:T(8,128)(2,1)S(1)} %all-to-all-done.2.back_ref, f32[2,256,384]{2,1,0:T(8,128)} %bitcast.23, f32[2,256,384]{2,1,0:T(8,128)} %bitcast.25), custom_call_target="tpu_custom_call" | custom-call | flops 3932160 | bytes 8388608 | tf_op jit(solution)/shard_map/merge/pallas_call | solution.py:595
  76.4 2.4 %collective-permute-done.1.att2 = bf16[256,384]{1,0:T(8,128)(2,1)S(1)} collective-permute-done((bf16[256,384]{1,0:T(8,128)(2,1)S(1)}, bf16[256,384]{1,0:T(8,128)(2,1)S(1)}, u32[]{:S(2)}, u32[]{:S(2)}) %collective-permute-start.1) | collective-permute-done | bytes 196640 | tf_op jit(solution)/shard_map/ppermute | solution.py:740
  78.8 0.6 collective-permute-start.6
  79.4 2.5 %collective-permute-done.7.att2 = bf16[256,384]{1,0:T(8,128)(2,1)S(1)} collective-permute-done((bf16[256,384]{1,0:T(8,128)(2,1)S(1)}, bf16[256,384]{1,0:T(8,128)(2,1)S(1)}, u32[]{:S(2)}, u32[]{:S(2)}) %collective-permute-start.7) | collective-permute-done | bytes 196640 | tf_op jit(solution)/shard_map/ppermute | solution.py:740
  82.0 4.0 %mix.2 = (f32[128,1536]{1,0:T(8,128)S(1)}, bf16[256,1536]{1,0:T(8,128)(2,1)S(1)}) custom-call(bf16[256,384]{1,0:T(8,128)(2,1)S(1)} %bitcast.16, bf16[256,384]{1,0:T(8,128)(2,1)S(1)} %collective-permute-done.att1, bf16[256,384]{1,0:T(8,128)(2,1)S(1)} %collective-permute-done.1.att2, bf16[256,384]{1,0:T(8,128)(2,1)S(1)} %collective-permute-done.2.att3, ...), custom_call_target="tpu_custom_call" | custom-call | flops 1207959552 | bytes 8388608 | tf_op jit(solution)/shard_map/mix/pallas_call | solution.py:653
  86.5 2.8 %ffn.2 = (f32[128,1536]{1,0:T(8,128)S(1)}, bf16[128,1536]{1,0:T(8,128)(2,1)S(1)}) custom-call(bf16[256,1536]{1,0:T(8,128)(2,1)S(1)} %get-tuple-element.55.normed_ref, bf16[1536,1024]{1,0:T(8,128)(2,1)S(1)} %copy-done, bf16[1536,1024]{1,0:T(8,128)(2,1)S(1)} %copy-done.1, bf16[1024,1536]{1,0:T(8,128)(2,1)S(1)} %copy-done.2), custom_call_target="tpu_custom_call" | custom-call | flops 2415919104 | bytes 10485760 | tf_op jit(solution)/shard_map/ffn/pallas_call | solution.py:698
  89.3 0.6 collective-permute-start.9
  89.9 4.1 %mix.3 = (f32[128,1536]{1,0:T(8,128)S(1)}, bf16[256,1536]{1,0:T(8,128)(2,1)S(1)}) custom-call(bf16[256,384]{1,0:T(8,128)(2,1)S(1)} %bitcast.13, bf16[256,384]{1,0:T(8,128)(2,1)S(1)} %collective-permute-done.6.att1, bf16[256,384]{1,0:T(8,128)(2,1)S(1)} %collective-permute-done.7.att2, bf16[256,384]{1,0:T(8,128)(2,1)S(1)} %collective-permute-done.8.att3, ...), custom_call_target="tpu_custom_call" | custom-call | flops 1207959552 | bytes 8388608 | tf_op jit(solution)/shard_map/mix/pallas_call | solution.py:653
  94.1 1.4 %collective-permute-start.10 = (bf16[128,1536]{1,0:T(8,128)(2,1)S(1)}, bf16[128,1536]{1,0:T(8,128)(2,1)S(1)}, u32[]{:S(2)}, u32[]{:S(2)}) collective-permute-start(bf16[128,1536]{1,0:T(8,128)(2,1)S(1)} %add_convert_fusion.3), channel_id=1, source_target_pairs={{0,2},{1,3},{2,0},{3,1},{4,6},{5,7},{6,4},{7,5},{8,10},{9,11},{10,... | collective-permute-start | bytes 1179656 | tf_op jit(solution)/shard_map/ppermute | solution.py:740
  95.5 2.8 %ffn.3 = (f32[128,1536]{1,0:T(8,128)S(1)}, bf16[128,1536]{1,0:T(8,128)(2,1)S(1)}) custom-call(bf16[256,1536]{1,0:T(8,128)(2,1)S(1)} %get-tuple-element.65.normed_ref, bf16[1536,1024]{1,0:T(8,128)(2,1)S(1)} %copy-done, bf16[1536,1024]{1,0:T(8,128)(2,1)S(1)} %copy-done.1, bf16[1024,1536]{1,0:T(8,128)(2,1)S(1)} %copy-done.2), custom_call_target="tpu_custom_call" | custom-call | flops 2415919104 | bytes 10485760 | tf_op jit(solution)/shard_map/ffn/pallas_call | solution.py:698
  98.3 6.8 %collective-permute-done.10 = bf16[128,1536]{1,0:T(8,128)(2,1)S(1)} collective-permute-done((bf16[128,1536]{1,0:T(8,128)(2,1)S(1)}, bf16[128,1536]{1,0:T(8,128)(2,1)S(1)}, u32[]{:S(2)}, u32[]{:S(2)}) %collective-permute-start.10) | collective-permute-done | bytes 393248 | tf_op jit(solution)/shard_map/ppermute | solution.py:740
  105.2 1.7 %collective-permute-done.12 = bf16[128,1536]{1,0:T(8,128)(2,1)S(1)} collective-permute-done((bf16[128,1536]{1,0:T(8,128)(2,1)S(1)}, bf16[128,1536]{1,0:T(8,128)(2,1)S(1)}, u32[]{:S(2)}, u32[]{:S(2)}) %collective-permute-start.12) | collective-permute-done | bytes 393248 | tf_op jit(solution)/shard_map/ppermute | solution.py:736
  107.0 1.4 %collective-permute-start.13 = (bf16[128,1536]{1,0:T(8,128)(2,1)S(1)}, bf16[128,1536]{1,0:T(8,128)(2,1)S(1)}, u32[]{:S(2)}, u32[]{:S(2)}) collective-permute-start(bf16[128,1536]{1,0:T(8,128)(2,1)S(1)} %add_convert_fusion.1), channel_id=1, source_target_pairs={{0,2},{1,3},{2,0},{3,1},{4,6},{5,7},{6,4},{7,5},{8,10},{9,11},{10,... | collective-permute-start | bytes 1179656 | tf_op jit(solution)/shard_map/ppermute | solution.py:740
  108.6 9.6 %collective-permute-done.13 = bf16[128,1536]{1,0:T(8,128)(2,1)S(1)} collective-permute-done((bf16[128,1536]{1,0:T(8,128)(2,1)S(1)}, bf16[128,1536]{1,0:T(8,128)(2,1)S(1)}, u32[]{:S(2)}, u32[]{:S(2)}) %collective-permute-start.13) | collective-permute-done | bytes 393248 | tf_op jit(solution)/shard_map/ppermute | solution.py:740
  118.4 1.7 %collective-permute-done.14.refs_3_ = bf16[128,1536]{1,0:T(8,128)(2,1)S(1)} collective-permute-done((bf16[128,1536]{1,0:T(8,128)(2,1)S(1)}, bf16[128,1536]{1,0:T(8,128)(2,1)S(1)}, u32[]{:S(2)}, u32[]{:S(2)}) %collective-permute-start.14) | collective-permute-done | bytes 393248 | tf_op jit(solution)/shard_map/ppermute | solution.py:736
  120.1 1.3 %finish.1 = bf16[4,128,1536]{2,1,0:T(8,128)(2,1)} custom-call(bf16[128,1536]{1,0:T(8,128)(2,1)S(1)} %add_convert_fusion.2.refs_0_, bf16[128,1536]{1,0:T(8,128)(2,1)S(1)} %collective-permute-done.11.refs_1_, bf16[128,1536]{1,0:T(8,128)(2,1)S(1)} %add_convert_fusion.refs_2_, bf16[128,1536]{1,0:T(8,128)(2,1)S(1)} %collective-permute-done.14.refs_3_), custom_call_target="tpu_custom_call" | custom-call | tf_op jit(solution)/shard_map/finish/pallas_call | solution.py:725
  (45 shorter events, 2.2 us)
Async XLA Ops:
  0.0 15.0 %copy-start.4 = (s32[48]{0:T(128)S(1)}, s32[48]{0:T(128)}, u32[]{:S(2)}) copy-start(s32[48]{0:T(128)} %request_ref.5) | copy-start | bytes 580
  1.3 13.7 %all-to-all-start = ((s32[8,1,48]{2,1,0:T(1,128)}), s32[8,1,48]{2,1,0:T(1,128)S(1)}, u32[]{:S(2)}, u32[]{:S(2)}) async-start(s32[8,1,48]{2,1,0:T(1,128)} %broadcast_in_dim.3), calls=%async_computation | async-start | bytes 8192 | tf_op jit(solution)/shard_map/all_to_all | solution.py:757
  9.3 11.8 %copy-start.8 = (bf16[384,1536]{1,0:T(8,128)(2,1)S(1)}, bf16[384,1536]{1,0:T(8,128)(2,1)}, u32[]{:S(2)}) copy-start(bf16[384,1536]{1,0:T(8,128)(2,1)} %w0.3) | copy-start | bytes 3538948
  9.3 13.4 %copy-start.3 = (bf16[48,6,128]{2,0,1:T(8,128)(2,1)S(1)}, bf16[48,6,128]{2,0,1:T(8,128)(2,1)}, u32[]{:S(2)}) copy-start(bf16[48,6,128]{2,0,1:T(8,128)(2,1)} %param.24) | copy-start | bytes 221188
  9.3 13.4 %copy-start.6 = (s32[48]{0:T(128)S(1)}, s32[48]{0:T(128)}, u32[]{:S(2)}) copy-start(s32[48]{0:T(128)} %fill_ref.3) | copy-start | bytes 580
  17.0 19.5 %all-to-all-start.1 = ((bf16[8,96,384]{2,1,0:T(8,128)(2,1)}), bf16[8,96,384]{2,1,0:T(8,128)(2,1)S(1)}, u32[]{:S(2)}, u32[]{:S(2)}) async-start(bf16[8,96,384]{2,1,0:T(8,128)(2,1)} %bitcast), calls=%async_computation.1 | async-start | bytes 1179648 | tf_op jit(solution)/shard_map/all_to_all | solution.py:757
  21.1 31.1 %collective-permute-start.4 = (bf16[384,1536]{1,0:T(8,128)(2,1)S(1)}, bf16[384,1536]{1,0:T(8,128)(2,1)S(1)}, u32[]{:S(2)}, u32[]{:S(2)}) collective-permute-start(bf16[384,1536]{1,0:T(8,128)(2,1)S(1)} %copy-done.8), channel_id=1, source_target_pairs={{0,2},{1,3},{2,0},{3,1},{4,6},{5,7},{6,4},{7,5},{8,10},{9,11},{10,... | collective-permute-start | bytes 3538952 | tf_op jit(solution)/shard_map/ppermute | solution.py:740
  36.5 16.2 %copy-start.5 = (s32[3,128]{1,0:T(4,128)S(1)}, s32[3,128]{1,0:T(4,128)}, u32[]{:S(2)}) copy-start(s32[3,128]{1,0:T(4,128)} %parents_ref.1) | copy-start | bytes 4612
  36.5 16.2 %copy-start.7 = (f32[6]{0:T(128)S(1)}, f32[6]{0:T(128)}, u32[]{:S(2)}) copy-start(f32[6]{0:T(128)} %param.30) | copy-start | bytes 76
  48.4 21.5 %all-to-all-start.2 = ((bf16[8,112,384]{2,1,0:T(8,128)(2,1)}), bf16[8,112,384]{2,1,0:T(8,128)(2,1)S(1)}, u32[]{:S(2)}, u32[]{:S(2)}) async-start(bf16[8,112,384]{2,1,0:T(8,128)(2,1)} %hosted_pages.1), calls=%async_computation.2 | async-start | bytes 1376256 | tf_op jit(solution)/shard_map/all_to_all | solution.py:757
  52.1 26.7 %collective-permute-start.3 = (bf16[384,1536]{1,0:T(8,128)(2,1)S(1)}, bf16[384,1536]{1,0:T(8,128)(2,1)}, u32[]{:S(2)}, u32[]{:S(2)}) collective-permute-start(bf16[384,1536]{1,0:T(8,128)(2,1)S(1)} %copy-done.8), channel_id=1, source_target_pairs={{0,1},{1,0},{2,3},{3,2},{4,5},{5,4},{6,7},{7,6},{8,9},{9,8},{10,11... | collective-permute-start | bytes 3538952 | tf_op jit(solution)/shard_map/ppermute | solution.py:736
  52.2 9.4 %copy-start.9 = (bf16[384,1536]{1,0:T(8,128)(2,1)}, bf16[384,1536]{1,0:T(8,128)(2,1)S(1)}, u32[]{:S(2)}) copy-start(bf16[384,1536]{1,0:T(8,128)(2,1)S(1)} %collective-permute-done.4.w2) | copy-start | bytes 3538948
  52.2 29.7 %collective-permute-start.5 = (bf16[384,1536]{1,0:T(8,128)(2,1)S(1)}, bf16[384,1536]{1,0:T(8,128)(2,1)}, u32[]{:S(2)}, u32[]{:S(2)}) collective-permute-start(bf16[384,1536]{1,0:T(8,128)(2,1)S(1)} %collective-permute-done.4.w2), channel_id=1, source_target_pairs={{0,1},{1,0},{2,3},{3,2},{4,5},{5,4},{6,7},{7,6},{8,9},{9,8},{10,11... | collective-permute-start | bytes 3538952 | tf_op jit(solution)/shard_map/ppermute | solution.py:736
  71.9 6.9 %copy-start.10 = (f32[1536]{0:T(1024)S(1)}, f32[1536]{0:T(1024)}, u32[]{:S(2)}) copy-start(f32[1536]{0:T(1024)} %param.32) | copy-start | bytes 18436
  72.0 6.9 %collective-permute-start.1 = (bf16[256,384]{1,0:T(8,128)(2,1)S(1)}, bf16[256,384]{1,0:T(8,128)(2,1)S(1)}, u32[]{:S(2)}, u32[]{:S(2)}) collective-permute-start(bf16[256,384]{1,0:T(8,128)(2,1)S(1)} %bitcast.14), channel_id=1, source_target_pairs={{0,2},{1,3},{2,0},{3,1},{4,6},{5,7},{6,4},{7,5},{8,10},{9,11},{10,... | collective-permute-start | bytes 589832 | tf_op jit(solution)/shard_map/ppermute | solution.py:740
  73.6 12.4 %copy-start.2 = (bf16[1024,1536]{1,0:T(8,128)(2,1)S(1)}, bf16[1024,1536]{1,0:T(8,128)(2,1)}, u32[]{:S(2)}) copy-start(bf16[1024,1536]{1,0:T(8,128)(2,1)} %down_ref.3) | copy-start | bytes 9437188
  75.9 6.0 %collective-permute-start.7 = (bf16[256,384]{1,0:T(8,128)(2,1)S(1)}, bf16[256,384]{1,0:T(8,128)(2,1)S(1)}, u32[]{:S(2)}, u32[]{:S(2)}) collective-permute-start(bf16[256,384]{1,0:T(8,128)(2,1)S(1)} %bitcast.11), channel_id=1, source_target_pairs={{0,2},{1,3},{2,0},{3,1},{4,6},{5,7},{6,4},{7,5},{8,10},{9,11},{10,... | collective-permute-start | bytes 589832 | tf_op jit(solution)/shard_map/ppermute | solution.py:740
  76.4 5.5 %collective-permute-start = (bf16[256,384]{1,0:T(8,128)(2,1)S(1)}, bf16[256,384]{1,0:T(8,128)(2,1)S(1)}, u32[]{:S(2)}, u32[]{:S(2)}) collective-permute-start(bf16[256,384]{1,0:T(8,128)(2,1)S(1)} %bitcast.15), channel_id=1, source_target_pairs={{0,1},{1,0},{2,3},{3,2},{4,5},{5,4},{6,7},{7,6},{8,9},{9,8},{10,11... | collective-permute-start | bytes 589832 | tf_op jit(solution)/shard_map/ppermute | solution.py:736
  78.8 3.1 %collective-permute-start.2 = (bf16[256,384]{1,0:T(8,128)(2,1)S(1)}, bf16[256,384]{1,0:T(8,128)(2,1)S(1)}, u32[]{:S(2)}, u32[]{:S(2)}) collective-permute-start(bf16[256,384]{1,0:T(8,128)(2,1)S(1)} %collective-permute-done.1.att2), channel_id=1, source_target_pairs={{0,1},{1,0},{2,3},{3,2},{4,5},{5,4},{6,7},{7,6},{8,9},{9,8},{10,11... | collective-permute-start | bytes 589832 | tf_op jit(solution)/shard_map/ppermute | solution.py:736
  78.8 10.4 %collective-permute-start.6 = (bf16[256,384]{1,0:T(8,128)(2,1)S(1)}, bf16[256,384]{1,0:T(8,128)(2,1)S(1)}, u32[]{:S(2)}, u32[]{:S(2)}) collective-permute-start(bf16[256,384]{1,0:T(8,128)(2,1)S(1)} %bitcast.12), channel_id=1, source_target_pairs={{0,1},{1,0},{2,3},{3,2},{4,5},{5,4},{6,7},{7,6},{8,9},{9,8},{10,11... | collective-permute-start | bytes 589832 | tf_op jit(solution)/shard_map/ppermute | solution.py:736
  81.9 7.4 %collective-permute-start.8 = (bf16[256,384]{1,0:T(8,128)(2,1)S(1)}, bf16[256,384]{1,0:T(8,128)(2,1)S(1)}, u32[]{:S(2)}, u32[]{:S(2)}) collective-permute-start(bf16[256,384]{1,0:T(8,128)(2,1)S(1)} %collective-permute-done.7.att2), channel_id=1, source_target_pairs={{0,1},{1,0},{2,3},{3,2},{4,5},{5,4},{6,7},{7,6},{8,9},{9,8},{10,11... | collective-permute-start | bytes 589832 | tf_op jit(solution)/shard_map/ppermute | solution.py:736
  81.9 4.1 %copy-start = (bf16[1536,1024]{1,0:T(8,128)(2,1)S(1)}, bf16[1536,1024]{1,0:T(8,128)(2,1)}, u32[]{:S(2)}) copy-start(bf16[1536,1024]{1,0:T(8,128)(2,1)} %gate_ref.3) | copy-start | bytes 9437188
  81.9 4.5 %copy-start.1 = (bf16[1536,1024]{1,0:T(8,128)(2,1)S(1)}, bf16[1536,1024]{1,0:T(8,128)(2,1)}, u32[]{:S(2)}) copy-start(bf16[1536,1024]{1,0:T(8,128)(2,1)} %up_ref.3) | copy-start | bytes 9437188
  89.3 4.7 %collective-permute-start.9 = (bf16[128,1536]{1,0:T(8,128)(2,1)S(1)}, bf16[128,1536]{1,0:T(8,128)(2,1)S(1)}, u32[]{:S(2)}, u32[]{:S(2)}) collective-permute-start(bf16[128,1536]{1,0:T(8,128)(2,1)S(1)} %get-tuple-element.58), channel_id=1, source_target_pairs={{0,1},{1,0},{2,3},{3,2},{4,5},{5,4},{6,7},{7,6},{8,9},{9,8},{10,11... | collective-permute-start | bytes 1179656 | tf_op jit(solution)/shard_map/ppermute | solution.py:736
  94.1 11.1 %collective-permute-start.10 = (bf16[128,1536]{1,0:T(8,128)(2,1)S(1)}, bf16[128,1536]{1,0:T(8,128)(2,1)S(1)}, u32[]{:S(2)}, u32[]{:S(2)}) collective-permute-start(bf16[128,1536]{1,0:T(8,128)(2,1)S(1)} %add_convert_fusion.3), channel_id=1, source_target_pairs={{0,2},{1,3},{2,0},{3,1},{4,6},{5,7},{6,4},{7,5},{8,10},{9,11},{10,... | collective-permute-start | bytes 1179656 | tf_op jit(solution)/shard_map/ppermute | solution.py:740
  105.2 1.7 %collective-permute-start.12 = (bf16[128,1536]{1,0:T(8,128)(2,1)S(1)}, bf16[128,1536]{1,0:T(8,128)(2,1)S(1)}, u32[]{:S(2)}, u32[]{:S(2)}) collective-permute-start(bf16[128,1536]{1,0:T(8,128)(2,1)S(1)} %get-tuple-element.70), channel_id=1, source_target_pairs={{0,1},{1,0},{2,3},{3,2},{4,5},{5,4},{6,7},{7,6},{8,9},{9,8},{10,11... | collective-permute-start | bytes 1179656 | tf_op jit(solution)/shard_map/ppermute | solution.py:736
  107.0 11.2 %collective-permute-start.13 = (bf16[128,1536]{1,0:T(8,128)(2,1)S(1)}, bf16[128,1536]{1,0:T(8,128)(2,1)S(1)}, u32[]{:S(2)}, u32[]{:S(2)}) collective-permute-start(bf16[128,1536]{1,0:T(8,128)(2,1)S(1)} %add_convert_fusion.1), channel_id=1, source_target_pairs={{0,2},{1,3},{2,0},{3,1},{4,6},{5,7},{6,4},{7,5},{8,10},{9,11},{10,... | collective-permute-start | bytes 1179656 | tf_op jit(solution)/shard_map/ppermute | solution.py:740
  108.5 9.9 %collective-permute-start.11 = (bf16[128,1536]{1,0:T(8,128)(2,1)S(1)}, bf16[128,1536]{1,0:T(8,128)(2,1)S(1)}, u32[]{:S(2)}, u32[]{:S(2)}) collective-permute-start(bf16[128,1536]{1,0:T(8,128)(2,1)S(1)} %add_convert_fusion.2.refs_0_), channel_id=1, source_target_pairs={{0,1},{1,0},{2,3},{3,2},{4,5},{5,4},{6,7},{7,6},{8,9},{9,8},{10,11... | collective-permute-start | bytes 1179656 | tf_op jit(solution)/shard_map/ppermute | solution.py:736
  118.3 1.8 %collective-permute-start.14 = (bf16[128,1536]{1,0:T(8,128)(2,1)S(1)}, bf16[128,1536]{1,0:T(8,128)(2,1)S(1)}, u32[]{:S(2)}, u32[]{:S(2)}) collective-permute-start(bf16[128,1536]{1,0:T(8,128)(2,1)S(1)} %add_convert_fusion.refs_2_), channel_id=1, source_target_pairs={{0,1},{1,0},{2,3},{3,2},{4,5},{5,4},{6,7},{7,6},{8,9},{9,8},{10,11... | collective-permute-start | bytes 1179656 | tf_op jit(solution)/shard_map/ppermute | solution.py:736

commit v5 on v4

--- a/solution.py
+++ b/solution.py
@@ -88,7 +88,7 @@
         ],
         sems,
     )
-    gain = gain_ref[...]
+    gain = gain_ref[...].reshape(1, -1)
 
     def pair(index, carry):
         slabs = []
@@ -143,7 +143,7 @@
             flops=2 * total * width * inner, bytes_accessed=6 * MIB, transcendentals=total
         ),
         name="queries",
-    )(in_hbm(tokens), gain.reshape(1, -1), in_hbm(w_query))
+    )(in_hbm(tokens), gain, in_hbm(w_query))
 
 
 def ask_kernel(capacity, request_ref, ids_ref, q_ref, table_ref, out_ref):
@@ -344,15 +344,12 @@
     )(parents, bias.reshape(1, -1), *[in_hbm(x) for x in big])
 
 
-def page_weights(
-    queries, fills, keys_ref, decay_ref, scores_ref, weights_ref, tops_ref, arrival=lambda page: None
-):
+def page_weights(queries, fills, keys_ref, decay_ref, scores_ref, weights_ref, tops_ref):
     span = queries[0][0].shape[0]
     masks = half_masks(span)
     lane = lanes((1, 128))
     decay = [decay_ref[head].astype(f32) for head in range(decay_ref.shape[0])]
     for page, pairs in enumerate(queries):
-        arrival(page)
         valid = lane < fills[page]
         for pair, query in enumerate(pairs):
             raw = dot(stacked(query, masks), keys_ref[page, pl.ds(pair * 128, 128), :])
@@ -456,19 +453,9 @@
 
 
 def hosted_kernel(
-    local_count, capacity, request_ref, fill_ref, q_ref, keys_hbm, values_hbm, decay_ref,
-    out_ref, keys_ref, values_ref, sems, tail_ref, count_ref, *scratch,
+    local_count, capacity, request_ref, fill_ref, q_ref, keys_ref, values_ref, decay_ref,
+    out_ref, tail_ref, count_ref, *scratch,
 ):
-    pieces = sems.shape[0] // 2
-    chunk = SPILL // pieces
-    copies = start_all(
-        [
-            (pool.at[pl.ds(OWNED_SLOTS + piece * chunk, chunk)], target.at[pl.ds(piece * chunk, chunk)])
-            for pool, target in ((keys_hbm, keys_ref), (values_hbm, values_ref))
-            for piece in range(pieces)
-        ],
-        sems,
-    )
     span, inner = q_ref.shape[1:]
     pairs = inner // 128
     heads = decay_ref.shape[0]
@@ -486,15 +473,7 @@
         slot = owner * capacity + rank
         queries.append([q_ref[slot, :, pl.ds(pair * 128, 128)] for pair in range(pairs)])
         fills.append(fill_ref[OWNED_SLOTS + page])
-
-    def arrival(page):
-        if page % chunk == 0:
-            copies[page // chunk].wait()
-
-    hosted = decay_ref.at[:, pl.ds(OWNED_SLOTS, SPILL)]
-    page_weights(queries, fills, keys_ref, hosted, *scratch, arrival=arrival)
-    for copy in copies[pieces:]:
-        copy.wait()
+    page_weights(queries, fills, keys_ref, decay_ref, *scratch)
     scores_ref, _, tops_ref = scratch
     lane = lanes((span, 128))
     for page, (owner, rank) in enumerate(places):
@@ -523,27 +502,30 @@
 
 def hosted_pages(request, fill, asked_rows, keys, values, decay, groups, capacity, local_count):
     count, span, inner = asked_rows.shape
-    vmem = pl.BlockSpec(memory_space=pltpu.VMEM)
-    hbm = pl.BlockSpec(memory_space=pltpu.HBM)
-    pages = pltpu.VMEM((SPILL,) + keys.shape[1:], bf16)
+    shift = OWNED_SLOTS // SPILL
+    pool = pl.BlockSpec((SPILL,) + keys.shape[1:], lambda i: (shift, 0, 0))
+    decay_spec = pl.BlockSpec((decay.shape[0], SPILL, decay.shape[2]), lambda i: (0, shift, 0))
+    out_shape = (groups, capacity * span + TAIL_ROWS, inner)
     return pl.pallas_call(
         functools.partial(hosted_kernel, local_count, capacity),
-        in_specs=[SMEM, SMEM, vmem, hbm, hbm, vmem],
-        out_specs=vmem,
-        out_shape=jax.ShapeDtypeStruct((groups, capacity * span + TAIL_ROWS, inner), bf16),
-        scratch_shapes=[pages, pages, pltpu.SemaphoreType.DMA((8,))]
-        + [pltpu.VMEM((groups, span, 128), f32), pltpu.SMEM((groups,), jnp.int32)]
+        grid=(1,),
+        in_specs=[
+            SMEM, SMEM, pl.BlockSpec(asked_rows.shape, lambda i: (0, 0, 0)), pool, pool, decay_spec
+        ],
+        out_specs=pl.BlockSpec(out_shape, lambda i: (0, 0, 0)),
+        out_shape=jax.ShapeDtypeStruct(out_shape, bf16),
+        scratch_shapes=[pltpu.VMEM((groups, span, 128), f32), pltpu.SMEM((groups,), jnp.int32)]
         + page_scratch(SPILL, span, decay.shape[0]),
-        compiler_params=pltpu.CompilerParams(vmem_limit_bytes=14 * MIB),
+        compiler_params=pltpu.CompilerParams(vmem_limit_bytes=24 * MIB),
         cost_estimate=page_cost(SPILL, keys, 64),
         name="hosted_pages",
     )(request, fill, asked_rows, in_hbm(keys), in_hbm(values), decay)
 
 
 def merge_kernel(
-    capacity, steps, part, table_ref, back_ref, log_hbm, average_hbm, out_ref,
-    top_ref, total_ref, numer_ref, tops_ref, sems,
+    capacity, steps, part, table_ref, back_ref, log_hbm, average_hbm, *refs
 ):
+    out_refs, (top_ref, total_ref, numer_ref, tops_ref, sems) = refs[:steps], refs[steps:]
     groups, _, inner = back_ref.shape
     rows = steps * BEAMS
     span = PARTS * rows
@@ -583,7 +565,7 @@
             parts.append(numer_ref[here, :] / total_ref[here, :])
         for step in range(steps):
             both = jnp.concatenate([p[step * 8 : step * 8 + 8] for p in parts], axis=0)
-            out_ref[step, index * 16 : index * 16 + 16, :] = both.astype(bf16)
+            out_refs[step][index * 16 : index * 16 + 16, :] = both.astype(bf16)
 
 
 def merge(part, table, back, logs, averages, steps, capacity):
@@ -595,7 +577,7 @@
     return pl.pallas_call(
         functools.partial(merge_kernel, capacity, steps, part),
         in_specs=[SMEM, vmem, hbm, hbm],
-        out_shape=jax.ShapeDtypeStruct((steps, rows // steps, inner), bf16),
+        out_shape=[jax.ShapeDtypeStruct((rows // steps, inner), bf16)] * steps,
         scratch_shapes=[pltpu.VMEM((rows, inner), f32)] * 3
         + [pltpu.VMEM((back.shape[0] * span, capacity * inner), f32), pltpu.SemaphoreType.DMA((2,))],
         compiler_params=pltpu.CompilerParams(vmem_limit_bytes=10 * MIB),
@@ -606,32 +588,53 @@
     )(table, back, in_hbm(logs), in_hbm(averages))
 
 
-def mix_kernel(
-    first, att0, att1, att2, att3, w0, w1, w2, w3, tokens_hbm, gain_ref,
-    residual_out, normed_ref, residual_ref, tokens_ref, attended_ref, weight_ref, sems,
+def arrange_kernel(w0, w1, w2, w3, out_ref, sems):
+    inner = w0.shape[0]
+    head = lax.axis_index("head")
+    pairs = [
+        (weight, out_ref.at[pl.ds(pl.multiple_of((head ^ other) * inner, inner), inner)])
+        for other, weight in enumerate((w0, w1, w2, w3))
+    ]
+    for copy in start_all(pairs, sems):
+        copy.wait()
+
+
+def arrange(weights):
+    inner, width = weights[0].shape
+    anywhere = pl.BlockSpec(memory_space=pl.ANY)
+    return pl.pallas_call(
+        arrange_kernel,
+        in_specs=[anywhere] * 4,
+        out_specs=pl.BlockSpec(memory_space=pltpu.VMEM),
+        out_shape=jax.ShapeDtypeStruct((4 * inner, width), bf16),
+        scratch_shapes=[pltpu.SemaphoreType.DMA((4,))],
+        compiler_params=pltpu.CompilerParams(vmem_limit_bytes=10 * MIB),
+        cost_estimate=pl.CostEstimate(flops=0, bytes_accessed=8 * MIB, transcendentals=0),
+        name="arrange",
+    )(*weights)
+
+
+def block_kernel(
+    first, att0, att1, att2, att3, weight_ref, tokens_hbm, gain_ref, gate_ref, up_ref, down_ref,
+    residual_out, mine_ref, other_ref,
+    residual_ref, tokens_ref, attended_ref, normed_ref, hidden_ref, sums_ref, sems,
 ):
     rows, width = residual_ref.shape
     inner = att0.shape[1]
     half = rows // 2
     head = lax.axis_index("head")
-    near = pl.ds(pl.multiple_of(head % 2 * half, half), half)
-    places = [pl.ds(pl.multiple_of((head ^ other) * inner, inner), inner) for other in range(4)]
-    step = width // 3
-    columns = [slice(start, start + step) for start in range(0, width, step)]
-    pairs = [
-        (weight.at[:, cols], weight_ref.at[place, cols])
-        for cols in columns
-        for weight, place in zip((w0, w1, w2, w3), places)
-    ]
-    copies = start_all(pairs + [(tokens_hbm.at[first : first + rows], tokens_ref)], sems)
-    for att, place in zip((att0, att1, att2, att3), places):
+    core = lax.rem(head, 2)
+    near = pl.ds(pl.multiple_of(core * half, half), half)
+    away = pl.ds(pl.multiple_of((1 - core) * half, half), half)
+    copies = start_all([(tokens_hbm.at[first : first + rows], tokens_ref)], sems)
+    for other, att in enumerate((att0, att1, att2, att3)):
+        place = pl.ds(pl.multiple_of((head ^ other) * inner, inner), inner)
         attended_ref[:, place] = att[...]
-    for index, cols in enumerate(columns):
-        for copy in copies[index * 4 : index * 4 + 4]:
-            copy.wait()
+    for start in range(0, width, 512):
+        cols = slice(start, start + 512)
         residual_ref[:, cols] = dot(attended_ref[...], weight_ref[:, cols])
-    copies[-1].wait()
-    gain = gain_ref[...]
+    copies[0].wait()
+    gain = gain_ref[...].reshape(1, -1)
 
     def norm(index, carry):
         here = pl.ds(pl.multiple_of(index * 32, 32), 32)
@@ -642,91 +645,69 @@
         return carry
 
     lax.fori_loop(0, rows // 32, norm, 0, unroll=2)
+    for start in range(0, gate_ref.shape[1], 256):
+        cols = slice(start, start + 256)
+        gate = dot(normed_ref[...], gate_ref[:, cols])
+        up = dot(normed_ref[...], up_ref[:, cols])
+        hidden_ref[:, cols] = (gate / (1.0 + jnp.exp(-gate)) * up).astype(bf16)
+    for start in range(0, width, 512):
+        cols = slice(start, start + 512)
+        sums_ref[:, cols] = dot(hidden_ref[...], down_ref[:, cols])
     residual_out[...] = residual_ref[near, :]
-
-
-def mix(first, attended, weights, tokens, gain):
+    mine_ref[...] = sums_ref[near, :]
+    other_ref[...] = sums_ref[away, :].astype(bf16)
+
+
+def block(first, attended, weight, tokens, gain, w_gate, w_up, w_down):
     rows, inner = attended[0].shape
     width = tokens.shape[1]
+    hidden = w_gate.shape[1]
     vmem = pl.BlockSpec(memory_space=pltpu.VMEM)
     hbm = pl.BlockSpec(memory_space=pltpu.HBM)
+    half = jax.ShapeDtypeStruct((rows // 2, width), f32)
     return pl.pallas_call(
-        functools.partial(mix_kernel, first),
-        in_specs=[vmem] * 4 + [hbm] * 5 + [vmem],
-        out_specs=[vmem] * 2,
-        out_shape=[
-            jax.ShapeDtypeStruct((rows // 2, width), f32),
-            jax.ShapeDtypeStruct((rows, width), bf16),
-        ],
+        functools.partial(block_kernel, first),
+        in_specs=[vmem] * 5 + [hbm] + [vmem] * 4,
+        out_specs=[vmem] * 3,
+        out_shape=[half, half, jax.ShapeDtypeStruct((rows // 2, width), bf16)],
         scratch_shapes=[
             pltpu.VMEM((rows, width), f32),
             pltpu.VMEM((rows, width), bf16),
             pltpu.VMEM((rows, 4 * inner), bf16),
-            pltpu.VMEM((4 * inner, width), bf16),
-            pltpu.SemaphoreType.DMA((13,)),
+            pltpu.VMEM((rows, width), bf16),
+            pltpu.VMEM((rows, hidden), bf16),
+            pltpu.VMEM((rows, width), f32),
+            pltpu.SemaphoreType.DMA((1,)),
         ],
-        compiler_params=pltpu.CompilerParams(vmem_limit_bytes=14 * MIB),
+        compiler_params=pltpu.CompilerParams(vmem_limit_bytes=20 * MIB),
         cost_estimate=pl.CostEstimate(
-            flops=8 * rows * width * inner, bytes_accessed=8 * MIB, transcendentals=rows
+            flops=2 * rows * width * (4 * inner + 3 * hidden), bytes_accessed=16 * MIB,
+            transcendentals=rows * hidden,
         ),
-        name="mix",
-    )(*attended, *[in_hbm(w) for w in weights], in_hbm(tokens), gain.reshape(1, -1))
-
-
-def ffn_kernel(normed_ref, gate_ref, up_ref, down_ref, mine_ref, other_ref, hidden_ref, sums_ref):
-    rows, width = normed_ref.shape
-    half = rows // 2
-    core = lax.axis_index("head") % 2
-    near = pl.ds(pl.multiple_of(core * half, half), half)
-    away = pl.ds(pl.multiple_of((1 - core) * half, half), half)
-    for first in range(0, gate_ref.shape[1], 256):
-        cols = slice(first, first + 256)
-        gate = dot(normed_ref[...], gate_ref[:, cols])
-        up = dot(normed_ref[...], up_ref[:, cols])
-        hidden_ref[:, cols] = (gate / (1.0 + jnp.exp(-gate)) * up).astype(bf16)
-    for first in range(0, width, 512):
-        cols = slice(first, first + 512)
-        sums_ref[...] = dot(hidden_ref[...], down_ref[:, cols])
-        mine_ref[:, cols] = sums_ref[near, :]
-        other_ref[:, cols] = sums_ref[away, :].astype(bf16)
-
-
-def ffn(normed, w_gate, w_up, w_down):
-    rows, width = normed.shape
-    hidden = w_gate.shape[1]
-    vmem = pl.BlockSpec(memory_space=pltpu.VMEM)
-    return pl.pallas_call(
-        ffn_kernel,
-        in_specs=[vmem] * 4,
-        out_specs=[vmem] * 2,
-        out_shape=[
-            jax.ShapeDtypeStruct((rows // 2, width), f32),
-            jax.ShapeDtypeStruct((rows // 2, width), bf16),
-        ],
-        scratch_shapes=[pltpu.VMEM((rows, hidden), bf16), pltpu.VMEM((rows, 512), f32)],
-        compiler_params=pltpu.CompilerParams(vmem_limit_bytes=10 * MIB),
-        cost_estimate=pl.CostEstimate(
-            flops=6 * rows * width * hidden, bytes_accessed=10 * MIB, transcendentals=rows * hidden
-        ),
-        name="ffn",
-    )(in_vmem(normed), in_vmem(w_gate), in_vmem(w_up), in_vmem(w_down))
+        name="block",
+    )(*attended, weight, in_hbm(tokens), gain, w_gate, w_up, w_down)
 
 
 def finish_kernel(*refs):
     parts, out_ref = refs[:-1], refs[-1]
     core = lax.axis_index("head") % 2
-    for index, part in enumerate(parts):
-        step = index // 2 * 2 + (core if index % 2 == 0 else 1 - core)
-        out_ref[step] = part[...]
+    first = 0
+    for index in range(0, len(parts), 2):
+        half = parts[index].shape[0]
+        for part, place in ((parts[index], core), (parts[index + 1], 1 - core)):
+            rows = pl.ds(pl.multiple_of(first + place * half, half), half)
+            out_ref[rows, :] = part[...]
+        first += 2 * half
 
 
 def finish(parts):
     vmem = pl.BlockSpec(memory_space=pltpu.VMEM)
+    rows, width = sum(part.shape[0] for part in parts), parts[0].shape[1]
     return pl.pallas_call(
         finish_kernel,
         in_specs=[vmem] * len(parts),
         out_specs=vmem,
-        out_shape=jax.ShapeDtypeStruct((len(parts),) + parts[0].shape, parts[0].dtype),
+        out_shape=jax.ShapeDtypeStruct((rows, width), parts[0].dtype),
         compiler_params=pltpu.CompilerParams(vmem_limit_bytes=12 * MIB),
         name="finish",
     )(*parts)
@@ -769,35 +750,41 @@
     payload, normed = lax.optimization_barrier((payload, normed))
     back = exchange(payload)
     logs, averages = fresh(parents, forget_bias, normed, w_key, w_value, w_forget, q, own)
-    weights = [w_out, swap_core(w_out), w_out_far, swap_core(w_out_far)]
+    weight = arrange([w_out, swap_core(w_out), w_out_far, swap_core(w_out_far)])
+    logs, weight = lax.optimization_barrier((logs, weight))
 
     flat = tokens.reshape(steps * rows, width)
     each = steps // PARTS
-    heres = [
-        merge(index, table, back, logs, averages, each, capacity).reshape(each * rows, inner)
-        for index in range(PARTS)
-    ]
+    attended = []
+    for index in range(PARTS):
+        attended.extend(merge(index, table, back, logs, averages, each, capacity))
+    heres = [attended[0], attended[1], jnp.concatenate(attended[2:], axis=0)]
     fars = [swap_chip(here) for here in heres]
-    residual, mine, other, chip, far_chip = [[None] * PARTS for _ in range(5)]
+    residual, mine, other, chip, far_chip = [], [], [], [], []
+    first = 0
     for index, (here, far) in enumerate(zip(heres, fars)):
         gathered = [here, swap_core(here), far, swap_core(far)]
         if index:
-            gathered, other[0] = lax.optimization_barrier((gathered, other[0]))
-        residual[index], normed = mix(index * each * rows, gathered, weights, flat, gain_ffn)
+            gathered, other[-1] = lax.optimization_barrier((gathered, other[-1]))
+        if index > 1:
+            gathered, chip[0] = lax.optimization_barrier((gathered, chip[0]))
+        outs = block(first, gathered, weight, flat, gain_ffn, w_gate, w_up, w_down)
+        for values, out in zip((residual, mine, other), outs):
+            values.append(out)
+        first += here.shape[0]
         if index:
-            chip[0] = (mine[0] + swap_core(other[0]).astype(f32)).astype(bf16)
-            chip[0], normed = lax.optimization_barrier((chip[0], normed))
-        mine[index], other[index] = ffn(normed, w_gate, w_up, w_down)
-    far_chip[0] = swap_chip(chip[0])
-    other[1], far_chip[0] = lax.optimization_barrier((other[1], far_chip[0]))
-    chip[1] = (mine[1] + swap_core(other[1]).astype(f32)).astype(bf16)
-    far_chip[1] = swap_chip(chip[1])
+            chip.append((mine[-2] + swap_core(other[-2]).astype(f32)).astype(bf16))
+    chip.append((mine[-1] + swap_core(other[-1]).astype(f32)).astype(bf16))
     parts = []
-    for index in range(PARTS):
+    for index in range(len(chip)):
+        if index:
+            chip[index], far_chip[-1] = lax.optimization_barrier((chip[index], far_chip[-1]))
+        far_chip.append(swap_chip(chip[index]))
+    for index in range(len(chip)):
         both = chip[index].astype(f32) + far_chip[index].astype(f32)
         done = (residual[index] + both).astype(bf16)
         parts.extend([done, swap_core(done)])
-    return finish(parts)
+    return finish(parts).reshape(steps, rows, width)
 
 
 def solution(mesh):

time: 122 us -> 119 us (0.975)
  local copies, waits for them, and re-layouts: 2.51 us -> 9.19 us
  waiting for transfers between devices: 41.8 us -> 35.3 us
  Pallas kernels: 52.8 us -> 47.4 us
  starting transfers between devices: 23.6 us -> 25.6 us
    unnamed x22 -> x33, local copies, waits for them, and re-layouts: 0.5 us -> 7.93 us
    pallas_call x5, Pallas kernels: 25.6 us -> 18.9 us  [the longest x3 13 us: block(): pl.pallas_call(functools.partial(block_kernel, first), in_specs=[vmem] *...]
    all_to_all x3, waiting for transfers between devices: 17.1 us -> 13.1 us  [exchange(): lax.all_to_all(value, 'group', split_axis=0, concat_axis=0, tiled=True)]
    ppermute x5 -> x7, starting transfers between devices: 6.6 us -> 8.39 us  [swap_chip(): return lax.ppermute(value, 'head', [(i, i ^ 2) for i in range(4)])]
    ppermute x5 -> x7, waiting for transfers between devices: 21.3 us -> 19.8 us  [swap_chip(): return lax.ppermute(value, 'head', [(i, i ^ 2) for i in range(4)])]
    pallas_call x2, Pallas kernels: 4.37 us -> 5.68 us  [merge(): pl.pallas_call(functools.partial(merge_kernel, capacity, steps, part), in...]
    ppermute x10 -> x14, starting transfers between devices: 1.85 us -> 2.99 us  [swap_core(): return lax.ppermute(value, 'head', [(i, i ^ 1) for i in range(4)])]
    ppermute x10 -> x14, waiting for transfers between devices: 3.44 us -> 2.37 us  [swap_core(): return lax.ppermute(value, 'head', [(i, i ^ 1) for i in range(4)])]
  transfers between devices with their start and end apart: 18 -> 24, of which waited for: 9 -> 9; matrix products, arithmetic and copies ran while one was open for 1% -> 1% of each run, Pallas kernels for 41% -> 36%
where the time goes in v5:
time: 119 us; the launch traced here: 118 us
  Pallas kernels  47.4 us (40%)
  waiting for transfers between devices  35.3 us (30%)
  starting transfers between devices  25.6 us (22%)
  local copies, waits for them, and re-layouts  9.19 us (8%)
    ppermute x7, waiting for transfers between devices, swap_chip(): return lax.ppermute(value, 'head', [(i, i ^ 2) for i in range(4)])  19.8 us
    all_to_all x3, starting transfers between devices, exchange(): lax.all_to_all(value, 'group', split_axis=0, concat_axis=0, tiled=True)  14.2 us
    all_to_all x3, waiting for transfers between devices, exchange(): lax.all_to_all(value, 'group', split_axis=0, concat_axis=0, tiled=True)  13.1 us
    pallas_call x3, Pallas kernels, block(): pl.pallas_call(functools.partial(block_kernel, first), in_specs=[vmem] *...  13 us
    pallas_call x1, Pallas kernels, fresh(): pl.pallas_call(fresh_kernel, in_specs=[vmem, vmem] + [hbm] * len(big), ou...  9 us
    ppermute x7, starting transfers between devices, swap_chip(): return lax.ppermute(value, 'head', [(i, i ^ 2) for i in range(4)])  8.39 us
    unnamed x33, local copies, waits for them, and re-layouts  7.93 us
    pallas_call x1, Pallas kernels, own_pages(): pl.pallas_call(own_kernel, grid=(OWNED_SLOTS // PAGE_BLOCK,), in_specs=[S...  6.9 us
  transfers between devices with their start and end apart: 24, of which 9 were waited for; matrix products, arithmetic and copies ran while one was open for 1% of the time, Pallas kernels for 36%

profile of v5, /device:TPU:0, one launch (start us, length us, event | category | flops | bytes accessed | tf_op | source)
XLA Modules:
  0.0 118.2 jit_solution(2234144529446499748)
XLA Ops:
  0.0 2.9 %collective-permute-start.1 = (bf16[384,1536]{1,0:T(8,128)(2,1)}, bf16[384,1536]{1,0:T(8,128)(2,1)S(1)}, u32[]{:S(2)}, u32[]{:S(2)}) collective-permute-start(bf16[384,1536]{1,0:T(8,128)(2,1)} %w0.1), channel_id=1, source_target_pairs={{0,2},{1,3},{2,0},{3,1},{4,6},{5,7},{6,4},{7,5},{8,10},{9,11},{10,... | collective-permute-start | bytes 3538952 | tf_op jit(solution)/shard_map/ppermute | solution.py:721
  2.9 1.2 %broadcast_in_dim.3 = s32[8,1,48]{2,1,0:T(1,128)} broadcast(s32[48]{0:T(128)} %request_ref.5), dimensions={2} | broadcast | bytes 1728 | tf_op jit(solution)/shard_map/broadcast_in_dim | solution.py:740
  4.2 5.8 %all-to-all-start = ((s32[8,1,48]{2,1,0:T(1,128)}), s32[8,1,48]{2,1,0:T(1,128)S(1)}, u32[]{:S(2)}, u32[]{:S(2)}) async-start(s32[8,1,48]{2,1,0:T(1,128)} %broadcast_in_dim.3), calls=%async_computation | async-start | bytes 8192 | tf_op jit(solution)/shard_map/all_to_all | solution.py:738
  10.7 3.7 %queries.1 = (bf16[512,384]{1,0:T(8,128)(2,1)S(1)}, bf16[512,384]{1,0:T(8,128)(2,1)}, bf16[512,1536]{1,0:T(8,128)(2,1)}) custom-call(bf16[4,128,1536]{2,1,0:T(8,128)(2,1)} %tokens_hbm.1, f32[1536]{0:T(1024)S(1)} %copy-done.11, bf16[384,1536]{1,0:T(8,128)(2,1)} %wq_hbm.1), custom_call_target="tpu_custom_call" | custom-call | flops 603979776 | bytes 6291456 | tf_op jit(solution)/shard_map/queries/pallas_call | solution.py:125
  14.4 2.0 %all-to-all-done.ids_ref = s32[8,1,48]{2,1,0:T(1,128)S(1)} async-done(((s32[8,1,48]{2,1,0:T(1,128)}), s32[8,1,48]{2,1,0:T(1,128)S(1)}, u32[]{:S(2)}, u32[]{:S(2)}) %all-to-all-start) | async-done | bytes 1568 | tf_op jit(solution)/shard_map/all_to_all | solution.py:738
  16.5 2.0 %ask.1 = (s32[24]{0:T(128)S(1)}, bf16[24,32,384]{2,1,0:T(8,128)(2,1)}) custom-call(s32[48]{0:T(128)S(1)} %copy-done.12, s32[8,1,48]{2,1,0:T(1,128)S(1)} %all-to-all-done.ids_ref, bf16[512,384]{1,0:T(8,128)(2,1)S(1)} %get-tuple-element.55.q_ref), custom_call_target="tpu_custom_call" | custom-call | tf_op jit(solution)/shard_map/ask/pallas_call | solution.py:162
  18.4 4.0 %all-to-all-start.1 = ((bf16[8,96,384]{2,1,0:T(8,128)(2,1)}), bf16[8,96,384]{2,1,0:T(8,128)(2,1)S(1)}, u32[]{:S(2)}, u32[]{:S(2)}) async-start(bf16[8,96,384]{2,1,0:T(8,128)(2,1)} %bitcast), calls=%async_computation.1 | async-start | bytes 1179648 | tf_op jit(solution)/shard_map/all_to_all | solution.py:738
  22.4 6.9 %own_pages.1 = (f32[512,384]{1,0:T(8,128)}, f32[512,384]{1,0:T(8,128)}, f32[512,384]{1,0:T(8,128)}) custom-call(s32[48]{0:T(128)S(1)} %copy-done.12, s32[48]{0:T(128)S(1)} %copy-done.14, bf16[512,384]{1,0:T(8,128)(2,1)} %get-tuple-element.58.q_ref.q_hbm, bf16[48,384,128]{2,1,0:T(8,128)(2,1)} %keys_ref.3, bf16[48,384,128]{2,1,0:T(8,128)(2,1)} %values_ref.3, ...), custom_call_target="tpu_custom_call" | custom-call | flops 805306368 | bytes 6291456 | tf_op jit(solution)/shard_map/own_pages/pallas_call | solution.py:442
  29.3 8.2 %all-to-all-done.1 = bf16[8,96,384]{2,1,0:T(8,128)(2,1)S(1)} async-done(((bf16[8,96,384]{2,1,0:T(8,128)(2,1)}), bf16[8,96,384]{2,1,0:T(8,128)(2,1)S(1)}, u32[]{:S(2)}, u32[]{:S(2)}) %all-to-all-start.1) | async-done | bytes 589856 | tf_op jit(solution)/shard_map/all_to_all | solution.py:738
  37.5 4.9 %hosted_pages.1 = bf16[8,112,384]{2,1,0:T(8,128)(2,1)} custom-call(s32[48]{0:T(128)S(1)} %copy-done.12, s32[48]{0:T(128)S(1)} %copy-done.14, bf16[24,32,384]{2,1,0:T(8,128)(2,1)S(1)} %bitcast.9, bf16[48,384,128]{2,1,0:T(8,128)(2,1)} %keys_ref.3, bf16[48,384,128]{2,1,0:T(8,128)(2,1)} %values_ref.3, bf16[6,48,128]{2,1,0:T(8,128)(2,1)S(1)} %bitcast.11), custom_call_target="tpu_custom_call" | custom-call | flops 402653184 | bytes 3145728 | tf_op jit(solution)/shard_map/hosted_pages/pallas_call | solution.py:509
  42.4 4.4 %all-to-all-start.2 = ((bf16[8,112,384]{2,1,0:T(8,128)(2,1)}), bf16[8,112,384]{2,1,0:T(8,128)(2,1)}, u32[]{:S(2)}, u32[]{:S(2)}) async-start(bf16[8,112,384]{2,1,0:T(8,128)(2,1)} %hosted_pages.1), calls=%async_computation.2 | async-start | bytes 1376256 | tf_op jit(solution)/shard_map/all_to_all | solution.py:738
  47.4 9.0 %fresh.1 = (f32[2,16,16,384]{3,2,1,0:T(8,128)}, f32[2,16,16,384]{3,2,1,0:T(8,128)}) custom-call(s32[3,128]{1,0:T(4,128)S(1)} %copy-done.13, f32[1,6]{1,0:T(1,128)S(1)} %bitcast.12, bf16[512,1536]{1,0:T(8,128)(2,1)} %get-tuple-element.65.normed_hbm, bf16[384,1536]{1,0:T(8,128)(2,1)} %wk_hbm.1, bf16[384,1536]{1,0:T(8,128)(2,1)} %wv_hbm.1, ...), custom_call_target="tpu_custom_call" | custom-call | flops 1207959552 | bytes 12582912 | tf_op jit(solution)/shard_map/fresh/pallas_call | solution.py:327
  56.5 1.3 %copy-done.8 = bf16[384,1536]{1,0:T(8,128)(2,1)S(1)} copy-done((bf16[384,1536]{1,0:T(8,128)(2,1)S(1)}, bf16[384,1536]{1,0:T(8,128)(2,1)}, u32[]{:S(2)}) %copy-start.8) | copy-done | bytes 1179672
  57.8 1.0 arrange.1.weight_ref
  58.8 2.1 %copy-done = bf16[1536,1536]{1,0:T(8,128)(2,1)} copy-done((bf16[1536,1536]{1,0:T(8,128)(2,1)}, bf16[1536,1536]{1,0:T(8,128)(2,1)S(1)}, u32[]{:S(2)}) %copy-start) | copy-done | bytes 4718616
  60.9 2.9 %all-to-all-done.2.back_ref = bf16[8,112,384]{2,1,0:T(8,128)(2,1)} async-done(((bf16[8,112,384]{2,1,0:T(8,128)(2,1)}), bf16[8,112,384]{2,1,0:T(8,128)(2,1)}, u32[]{:S(2)}, u32[]{:S(2)}) %all-to-all-start.2) | async-done | bytes 688160 | tf_op jit(solution)/shard_map/all_to_all | solution.py:738
  63.8 3.1 %merge.3 = (bf16[128,384]{1,0:T(8,128)(2,1)S(1)}, bf16[128,384]{1,0:T(8,128)(2,1)S(1)}) custom-call(s32[24]{0:T(128)S(1)} %get-tuple-element.56.table_ref, bf16[8,112,384]{2,1,0:T(8,128)(2,1)} %all-to-all-done.2.back_ref, f32[2,256,384]{2,1,0:T(8,128)} %bitcast.16, f32[2,256,384]{2,1,0:T(8,128)} %bitcast.18), custom_call_target="tpu_custom_call" | custom-call | flops 3932160 | bytes 8388608 | tf_op jit(solution)/shard_map/merge/pallas_call | solution.py:577
  67.5 2.6 %merge.2 = (bf16[128,384]{1,0:T(8,128)(2,1)S(1)}, bf16[128,384]{1,0:T(8,128)(2,1)S(1)}) custom-call(s32[24]{0:T(128)S(1)} %get-tuple-element.56.table_ref, bf16[8,112,384]{2,1,0:T(8,128)(2,1)} %all-to-all-done.2.back_ref, f32[2,256,384]{2,1,0:T(8,128)} %bitcast.17, f32[2,256,384]{2,1,0:T(8,128)} %bitcast.19), custom_call_target="tpu_custom_call" | custom-call | flops 3932160 | bytes 8388608 | tf_op jit(solution)/shard_map/merge/pallas_call | solution.py:577
  70.2 1.5 %collective-permute-start.4 = (bf16[128,384]{1,0:T(8,128)(2,1)S(1)}, bf16[128,384]{1,0:T(8,128)(2,1)S(1)}, u32[]{:S(2)}, u32[]{:S(2)}) collective-permute-start(bf16[128,384]{1,0:T(8,128)(2,1)S(1)} %get-tuple-element.72.att0), channel_id=1, source_target_pairs={{0,2},{1,3},{2,0},{3,1},{4,6},{5,7},{6,4},{7,5},{8,10},{9,11},{10,... | collective-permute-start | bytes 294920 | tf_op jit(solution)/shard_map/ppermute | solution.py:721
  72.2 2.6 %collective-permute-done.4.att2 = bf16[128,384]{1,0:T(8,128)(2,1)S(1)} collective-permute-done((bf16[128,384]{1,0:T(8,128)(2,1)S(1)}, bf16[128,384]{1,0:T(8,128)(2,1)S(1)}, u32[]{:S(2)}, u32[]{:S(2)}) %collective-permute-start.4) | collective-permute-done | bytes 98336 | tf_op jit(solution)/shard_map/ppermute | solution.py:721
  75.4 1.6 %collective-permute-done.10.att2 = bf16[128,384]{1,0:T(8,128)(2,1)S(1)} collective-permute-done((bf16[128,384]{1,0:T(8,128)(2,1)S(1)}, bf16[128,384]{1,0:T(8,128)(2,1)S(1)}, u32[]{:S(2)}, u32[]{:S(2)}) %collective-permute-start.10) | collective-permute-done | bytes 98336 | tf_op jit(solution)/shard_map/ppermute | solution.py:721
  77.5 1.9 %copy-done.3 = bf16[1536,1024]{1,0:T(8,128)(2,1)S(1)} copy-done((bf16[1536,1024]{1,0:T(8,128)(2,1)S(1)}, bf16[1536,1024]{1,0:T(8,128)(2,1)}, u32[]{:S(2)}) %copy-start.3) | copy-done | bytes 3145752
  79.4 1.9 %copy-done.4 = bf16[1024,1536]{1,0:T(8,128)(2,1)S(1)} copy-done((bf16[1024,1536]{1,0:T(8,128)(2,1)S(1)}, bf16[1024,1536]{1,0:T(8,128)(2,1)}, u32[]{:S(2)}) %copy-start.4) | copy-done | bytes 3145752
  81.3 3.5 %block.3 = (f32[64,1536]{1,0:T(8,128)S(1)}, f32[64,1536]{1,0:T(8,128)S(1)}, bf16[64,1536]{1,0:T(8,128)(2,1)S(1)}) custom-call(bf16[128,384]{1,0:T(8,128)(2,1)S(1)} %get-tuple-element.72.att0, bf16[128,384]{1,0:T(8,128)(2,1)S(1)} %collective-permute-done.3.att1, bf16[128,384]{1,0:T(8,128)(2,1)S(1)} %collective-permute-done.4.att2, ...), custom_call_target="tpu_custom_call" | custom-call | flops 1811939328 | bytes 16777216 | tf_op jit(solution)/shard_map/block/pallas_call | solution.py:668
  84.8 3.5 %block.4 = (f32[64,1536]{1,0:T(8,128)S(1)}, f32[64,1536]{1,0:T(8,128)S(1)}, bf16[64,1536]{1,0:T(8,128)(2,1)S(1)}) custom-call(bf16[128,384]{1,0:T(8,128)(2,1)S(1)} %get-tuple-element.79.att0, bf16[128,384]{1,0:T(8,128)(2,1)S(1)} %collective-permute-done.9.att1, bf16[128,384]{1,0:T(8,128)(2,1)S(1)} %collective-permute-done.10.att2, ...), custom_call_target="tpu_custom_call" | custom-call | flops 1811939328 | bytes 16777216 | tf_op jit(solution)/shard_map/block/pallas_call | solution.py:668
  89.0 1.5 %collective-permute-start.14 = (bf16[64,1536]{1,0:T(8,128)(2,1)S(1)}, bf16[64,1536]{1,0:T(8,128)(2,1)S(1)}, u32[]{:S(2)}, u32[]{:S(2)}) collective-permute-start(bf16[64,1536]{1,0:T(8,128)(2,1)S(1)} %add_convert_fusion.5), channel_id=1, source_target_pairs={{0,2},{1,3},{2,0},{3,1},{4,6},{5,7},{6,4},{7,5},{8,10},{9,11},{10,... | collective-permute-start | bytes 589832 | tf_op jit(solution)/shard_map/ppermute | solution.py:721
  90.5 6.0 %block.5 = (f32[128,1536]{1,0:T(8,128)S(1)}, f32[128,1536]{1,0:T(8,128)S(1)}, bf16[128,1536]{1,0:T(8,128)(2,1)S(1)}) custom-call(bf16[256,384]{1,0:T(8,128)(2,1)S(1)} %constant_dynamic-update-slice_fusion.att0, bf16[256,384]{1,0:T(8,128)(2,1)S(1)} %collective-permute-done.6.att1, bf16[256,384]{1,0:T(8,128)(2,1)S(1)} %collective-permute-done.7.att2, ...), custom_call_target="tpu_custom_call" | custom-call | flops 3623878656 | bytes 16777216 | tf_op jit(solution)/shard_map/block/pallas_call | solution.py:668
  97.3 1.0 collective-permute-done.16
  98.4 5.6 %collective-permute-done.17 = bf16[64,1536]{1,0:T(8,128)(2,1)S(1)} collective-permute-done((bf16[64,1536]{1,0:T(8,128)(2,1)S(1)}, bf16[64,1536]{1,0:T(8,128)(2,1)S(1)}, u32[]{:S(2)}, u32[]{:S(2)}) %collective-permute-start.17) | collective-permute-done | bytes 196640 | tf_op jit(solution)/shard_map/ppermute | solution.py:721
  104.7 10.0 %collective-permute-done.19 = bf16[128,1536]{1,0:T(8,128)(2,1)S(1)} collective-permute-done((bf16[128,1536]{1,0:T(8,128)(2,1)S(1)}, bf16[128,1536]{1,0:T(8,128)(2,1)S(1)}, u32[]{:S(2)}, u32[]{:S(2)}) %collective-permute-start.19) | collective-permute-done | bytes 393248 | tf_op jit(solution)/shard_map/ppermute | solution.py:721
  115.6 1.4 %collective-permute-done.18.refs_3_ = bf16[64,1536]{1,0:T(8,128)(2,1)S(1)} collective-permute-done((bf16[64,1536]{1,0:T(8,128)(2,1)S(1)}, bf16[64,1536]{1,0:T(8,128)(2,1)S(1)}, u32[]{:S(2)}, u32[]{:S(2)}) %collective-permute-start.18) | collective-permute-done | bytes 196640 | tf_op jit(solution)/shard_map/ppermute | solution.py:717
  117.0 1.3 %finish.1 = bf16[512,1536]{1,0:T(8,128)(2,1)} custom-call(bf16[64,1536]{1,0:T(8,128)(2,1)S(1)} %add_convert_fusion.3.refs_0_, bf16[64,1536]{1,0:T(8,128)(2,1)S(1)} %collective-permute-done.15.refs_1_, bf16[64,1536]{1,0:T(8,128)(2,1)S(1)} %add_convert_fusion.2.refs_2_, bf16[64,1536]{1,0:T(8,128)(2,1)S(1)} %collective-permute-done.18.refs_3_, ...), custom_call_target="tpu_custom_call" | custom-call | tf_op jit(solution)/shard_map/finish/pallas_call | solution.py:706
  (69 shorter events, 6.6 us)
Async XLA Ops:
  0.0 16.5 %copy-start.12 = (s32[48]{0:T(128)S(1)}, s32[48]{0:T(128)}, u32[]{:S(2)}) copy-start(s32[48]{0:T(128)} %request_ref.5) | copy-start | bytes 580
  0.0 46.9 %collective-permute-start.1 = (bf16[384,1536]{1,0:T(8,128)(2,1)}, bf16[384,1536]{1,0:T(8,128)(2,1)S(1)}, u32[]{:S(2)}, u32[]{:S(2)}) collective-permute-start(bf16[384,1536]{1,0:T(8,128)(2,1)} %w0.1), channel_id=1, source_target_pairs={{0,2},{1,3},{2,0},{3,1},{4,6},{5,7},{6,4},{7,5},{8,10},{9,11},{10,... | collective-permute-start | bytes 3538952 | tf_op jit(solution)/shard_map/ppermute | solution.py:721
  4.2 12.3 %all-to-all-start = ((s32[8,1,48]{2,1,0:T(1,128)}), s32[8,1,48]{2,1,0:T(1,128)S(1)}, u32[]{:S(2)}, u32[]{:S(2)}) async-start(s32[8,1,48]{2,1,0:T(1,128)} %broadcast_in_dim.3), calls=%async_computation | async-start | bytes 8192 | tf_op jit(solution)/shard_map/all_to_all | solution.py:738
  10.7 11.7 %copy-start.9 = (bf16[48,6,128]{2,0,1:T(8,128)(2,1)S(1)}, bf16[48,6,128]{2,0,1:T(8,128)(2,1)}, u32[]{:S(2)}) copy-start(bf16[48,6,128]{2,0,1:T(8,128)(2,1)} %param.24) | copy-start | bytes 221188
  10.7 11.7 %copy-start.14 = (s32[48]{0:T(128)S(1)}, s32[48]{0:T(128)}, u32[]{:S(2)}) copy-start(s32[48]{0:T(128)} %fill_ref.3) | copy-start | bytes 580
  18.4 19.1 %all-to-all-start.1 = ((bf16[8,96,384]{2,1,0:T(8,128)(2,1)}), bf16[8,96,384]{2,1,0:T(8,128)(2,1)S(1)}, u32[]{:S(2)}, u32[]{:S(2)}) async-start(bf16[8,96,384]{2,1,0:T(8,128)(2,1)} %bitcast), calls=%async_computation.1 | async-start | bytes 1179648 | tf_op jit(solution)/shard_map/all_to_all | solution.py:738
  37.5 9.9 %copy-start.13 = (s32[3,128]{1,0:T(4,128)S(1)}, s32[3,128]{1,0:T(4,128)}, u32[]{:S(2)}) copy-start(s32[3,128]{1,0:T(4,128)} %parents_ref.1) | copy-start | bytes 4612
  37.5 9.9 %copy-start.15 = (f32[6]{0:T(128)S(1)}, f32[6]{0:T(128)}, u32[]{:S(2)}) copy-start(f32[6]{0:T(128)} %param.30) | copy-start | bytes 76
  42.4 21.3 %all-to-all-start.2 = ((bf16[8,112,384]{2,1,0:T(8,128)(2,1)}), bf16[8,112,384]{2,1,0:T(8,128)(2,1)}, u32[]{:S(2)}, u32[]{:S(2)}) async-start(bf16[8,112,384]{2,1,0:T(8,128)(2,1)} %hosted_pages.1), calls=%async_computation.2 | async-start | bytes 1376256 | tf_op jit(solution)/shard_map/all_to_all | solution.py:738
  46.8 9.6 %collective-permute-start = (bf16[384,1536]{1,0:T(8,128)(2,1)S(1)}, bf16[384,1536]{1,0:T(8,128)(2,1)S(1)}, u32[]{:S(2)}, u32[]{:S(2)}) collective-permute-start(bf16[384,1536]{1,0:T(8,128)(2,1)S(1)} %copy-done.5), channel_id=1, source_target_pairs={{0,1},{1,0},{2,3},{3,2},{4,5},{5,4},{6,7},{7,6},{8,9},{9,8},{10,11... | collective-permute-start | bytes 3538952 | tf_op jit(solution)/shard_map/ppermute | solution.py:717
  46.9 9.5 %collective-permute-start.2 = (bf16[384,1536]{1,0:T(8,128)(2,1)S(1)}, bf16[384,1536]{1,0:T(8,128)(2,1)S(1)}, u32[]{:S(2)}, u32[]{:S(2)}) collective-permute-start(bf16[384,1536]{1,0:T(8,128)(2,1)S(1)} %collective-permute-done.1.w2), channel_id=1, source_target_pairs={{0,1},{1,0},{2,3},{3,2},{4,5},{5,4},{6,7},{7,6},{8,9},{9,8},{10,11... | collective-permute-start | bytes 3538952 | tf_op jit(solution)/shard_map/ppermute | solution.py:717
  57.8 19.7 %copy-start.2 = (bf16[1536,1024]{1,0:T(8,128)(2,1)S(1)}, bf16[1536,1024]{1,0:T(8,128)(2,1)}, u32[]{:S(2)}) copy-start(bf16[1536,1024]{1,0:T(8,128)(2,1)} %gate_ref.5) | copy-start | bytes 9437188
  63.8 13.7 %copy-start.1 = (bf16[1536,1536]{1,0:T(8,128)(2,1)S(1)}, bf16[1536,1536]{1,0:T(8,128)(2,1)}, u32[]{:S(2)}) copy-start(bf16[1536,1536]{1,0:T(8,128)(2,1)} %copy-done) | copy-start | bytes 14155780
  66.9 10.6 %copy-start.10 = (f32[1536]{0:T(1024)S(1)}, f32[1536]{0:T(1024)}, u32[]{:S(2)}) copy-start(f32[1536]{0:T(1024)} %gain_ref.7) | copy-start | bytes 18436
  66.9 10.0 %collective-permute-start.7 = (bf16[256,384]{1,0:T(8,128)(2,1)S(1)}, bf16[256,384]{1,0:T(8,128)(2,1)S(1)}, u32[]{:S(2)}, u32[]{:S(2)}) collective-permute-start(bf16[256,384]{1,0:T(8,128)(2,1)S(1)} %constant_dynamic-update-slice_fusion.att0), channel_id=1, source_target_pairs={{0,2},{1,3},{2,0},{3,1},{4,6},{5,7},{6,4},{7,5},{8,10},{9,11},{10,... | collective-permute-start | bytes 589832 | tf_op jit(solution)/shard_map/ppermute | solution.py:721
  70.2 4.7 %collective-permute-start.4 = (bf16[128,384]{1,0:T(8,128)(2,1)S(1)}, bf16[128,384]{1,0:T(8,128)(2,1)S(1)}, u32[]{:S(2)}, u32[]{:S(2)}) collective-permute-start(bf16[128,384]{1,0:T(8,128)(2,1)S(1)} %get-tuple-element.72.att0), channel_id=1, source_target_pairs={{0,2},{1,3},{2,0},{3,1},{4,6},{5,7},{6,4},{7,5},{8,10},{9,11},{10,... | collective-permute-start | bytes 294920 | tf_op jit(solution)/shard_map/ppermute | solution.py:721
  71.7 3.7 %collective-permute-start.3 = (bf16[128,384]{1,0:T(8,128)(2,1)S(1)}, bf16[128,384]{1,0:T(8,128)(2,1)S(1)}, u32[]{:S(2)}, u32[]{:S(2)}) collective-permute-start(bf16[128,384]{1,0:T(8,128)(2,1)S(1)} %get-tuple-element.72.att0), channel_id=1, source_target_pairs={{0,1},{1,0},{2,3},{3,2},{4,5},{5,4},{6,7},{7,6},{8,9},{9,8},{10,11... | collective-permute-start | bytes 294920 | tf_op jit(solution)/shard_map/ppermute | solution.py:717
  71.7 5.2 %collective-permute-start.10 = (bf16[128,384]{1,0:T(8,128)(2,1)S(1)}, bf16[128,384]{1,0:T(8,128)(2,1)S(1)}, u32[]{:S(2)}, u32[]{:S(2)}) collective-permute-start(bf16[128,384]{1,0:T(8,128)(2,1)S(1)} %get-tuple-element.79.att0), channel_id=1, source_target_pairs={{0,2},{1,3},{2,0},{3,1},{4,6},{5,7},{6,4},{7,5},{8,10},{9,11},{10,... | collective-permute-start | bytes 294920 | tf_op jit(solution)/shard_map/ppermute | solution.py:721
  74.9 2.6 %collective-permute-start.5 = (bf16[128,384]{1,0:T(8,128)(2,1)S(1)}, bf16[128,384]{1,0:T(8,128)(2,1)S(1)}, u32[]{:S(2)}, u32[]{:S(2)}) collective-permute-start(bf16[128,384]{1,0:T(8,128)(2,1)S(1)} %collective-permute-done.4.att2), channel_id=1, source_target_pairs={{0,1},{1,0},{2,3},{3,2},{4,5},{5,4},{6,7},{7,6},{8,9},{9,8},{10,11... | collective-permute-start | bytes 294920 | tf_op jit(solution)/shard_map/ppermute | solution.py:717
  74.9 9.9 %collective-permute-start.9 = (bf16[128,384]{1,0:T(8,128)(2,1)S(1)}, bf16[128,384]{1,0:T(8,128)(2,1)S(1)}, u32[]{:S(2)}, u32[]{:S(2)}) collective-permute-start(bf16[128,384]{1,0:T(8,128)(2,1)S(1)} %get-tuple-element.79.att0), channel_id=1, source_target_pairs={{0,1},{1,0},{2,3},{3,2},{4,5},{5,4},{6,7},{7,6},{8,9},{9,8},{10,11... | collective-permute-start | bytes 294920 | tf_op jit(solution)/shard_map/ppermute | solution.py:717
  75.4 13.0 %collective-permute-start.6 = (bf16[256,384]{1,0:T(8,128)(2,1)S(1)}, bf16[256,384]{1,0:T(8,128)(2,1)S(1)}, u32[]{:S(2)}, u32[]{:S(2)}) collective-permute-start(bf16[256,384]{1,0:T(8,128)(2,1)S(1)} %constant_dynamic-update-slice_fusion.att0), channel_id=1, source_target_pairs={{0,1},{1,0},{2,3},{3,2},{4,5},{5,4},{6,7},{7,6},{8,9},{9,8},{10,11... | collective-permute-start | bytes 589832 | tf_op jit(solution)/shard_map/ppermute | solution.py:717
  76.9 7.8 %collective-permute-start.11 = (bf16[128,384]{1,0:T(8,128)(2,1)S(1)}, bf16[128,384]{1,0:T(8,128)(2,1)S(1)}, u32[]{:S(2)}, u32[]{:S(2)}) collective-permute-start(bf16[128,384]{1,0:T(8,128)(2,1)S(1)} %collective-permute-done.10.att2), channel_id=1, source_target_pairs={{0,1},{1,0},{2,3},{3,2},{4,5},{5,4},{6,7},{7,6},{8,9},{9,8},{10,11... | collective-permute-start | bytes 294920 | tf_op jit(solution)/shard_map/ppermute | solution.py:717
  76.9 11.4 %collective-permute-start.8 = (bf16[256,384]{1,0:T(8,128)(2,1)S(1)}, bf16[256,384]{1,0:T(8,128)(2,1)S(1)}, u32[]{:S(2)}, u32[]{:S(2)}) collective-permute-start(bf16[256,384]{1,0:T(8,128)(2,1)S(1)} %collective-permute-done.7.att2), channel_id=1, source_target_pairs={{0,1},{1,0},{2,3},{3,2},{4,5},{5,4},{6,7},{7,6},{8,9},{9,8},{10,11... | collective-permute-start | bytes 589832 | tf_op jit(solution)/shard_map/ppermute | solution.py:717
  84.8 4.1 %collective-permute-start.12 = (bf16[64,1536]{1,0:T(8,128)(2,1)S(1)}, bf16[64,1536]{1,0:T(8,128)(2,1)S(1)}, u32[]{:S(2)}, u32[]{:S(2)}) collective-permute-start(bf16[64,1536]{1,0:T(8,128)(2,1)S(1)} %get-tuple-element.89), channel_id=1, source_target_pairs={{0,1},{1,0},{2,3},{3,2},{4,5},{5,4},{6,7},{7,6},{8,9},{9,8},{10,11... | collective-permute-start | bytes 589832 | tf_op jit(solution)/shard_map/ppermute | solution.py:717
  88.4 8.2 %collective-permute-start.13 = (bf16[64,1536]{1,0:T(8,128)(2,1)S(1)}, bf16[64,1536]{1,0:T(8,128)(2,1)S(1)}, u32[]{:S(2)}, u32[]{:S(2)}) collective-permute-start(bf16[64,1536]{1,0:T(8,128)(2,1)S(1)} %get-tuple-element.92), channel_id=1, source_target_pairs={{0,1},{1,0},{2,3},{3,2},{4,5},{5,4},{6,7},{7,6},{8,9},{9,8},{10,11... | collective-permute-start | bytes 589832 | tf_op jit(solution)/shard_map/ppermute | solution.py:717
  89.0 7.7 %collective-permute-start.14 = (bf16[64,1536]{1,0:T(8,128)(2,1)S(1)}, bf16[64,1536]{1,0:T(8,128)(2,1)S(1)}, u32[]{:S(2)}, u32[]{:S(2)}) collective-permute-start(bf16[64,1536]{1,0:T(8,128)(2,1)S(1)} %add_convert_fusion.5), channel_id=1, source_target_pairs={{0,2},{1,3},{2,0},{3,1},{4,6},{5,7},{6,4},{7,5},{8,10},{9,11},{10,... | collective-permute-start | bytes 589832 | tf_op jit(solution)/shard_map/ppermute | solution.py:721
  96.5 1.8 %collective-permute-start.16 = (bf16[128,1536]{1,0:T(8,128)(2,1)S(1)}, bf16[128,1536]{1,0:T(8,128)(2,1)S(1)}, u32[]{:S(2)}, u32[]{:S(2)}) collective-permute-start(bf16[128,1536]{1,0:T(8,128)(2,1)S(1)} %get-tuple-element.101), channel_id=1, source_target_pairs={{0,1},{1,0},{2,3},{3,2},{4,5},{5,4},{6,7},{7,6},{8,9},{9,8},{10,11... | collective-permute-start | bytes 1179656 | tf_op jit(solution)/shard_map/ppermute | solution.py:717
  96.7 7.4 %collective-permute-start.17 = (bf16[64,1536]{1,0:T(8,128)(2,1)S(1)}, bf16[64,1536]{1,0:T(8,128)(2,1)S(1)}, u32[]{:S(2)}, u32[]{:S(2)}) collective-permute-start(bf16[64,1536]{1,0:T(8,128)(2,1)S(1)} %add_convert_fusion.4), channel_id=1, source_target_pairs={{0,2},{1,3},{2,0},{3,1},{4,6},{5,7},{6,4},{7,5},{8,10},{9,11},{10,... | collective-permute-start | bytes 589832 | tf_op jit(solution)/shard_map/ppermute | solution.py:721
  104.0 10.7 %collective-permute-start.19 = (bf16[128,1536]{1,0:T(8,128)(2,1)S(1)}, bf16[128,1536]{1,0:T(8,128)(2,1)S(1)}, u32[]{:S(2)}, u32[]{:S(2)}) collective-permute-start(bf16[128,1536]{1,0:T(8,128)(2,1)S(1)} %add_convert_fusion.1), channel_id=1, source_target_pairs={{0,2},{1,3},{2,0},{3,1},{4,6},{5,7},{6,4},{7,5},{8,10},{9,11},{10,... | collective-permute-start | bytes 1179656 | tf_op jit(solution)/shard_map/ppermute | solution.py:721
  104.7 10.9 %collective-permute-start.15 = (bf16[64,1536]{1,0:T(8,128)(2,1)S(1)}, bf16[64,1536]{1,0:T(8,128)(2,1)S(1)}, u32[]{:S(2)}, u32[]{:S(2)}) collective-permute-start(bf16[64,1536]{1,0:T(8,128)(2,1)S(1)} %add_convert_fusion.3.refs_0_), channel_id=1, source_target_pairs={{0,1},{1,0},{2,3},{3,2},{4,5},{5,4},{6,7},{7,6},{8,9},{9,8},{10,11... | collective-permute-start | bytes 589832 | tf_op jit(solution)/shard_map/ppermute | solution.py:717
  114.9 2.1 %collective-permute-start.20 = (bf16[128,1536]{1,0:T(8,128)(2,1)S(1)}, bf16[128,1536]{1,0:T(8,128)(2,1)S(1)}, u32[]{:S(2)}, u32[]{:S(2)}) collective-permute-start(bf16[128,1536]{1,0:T(8,128)(2,1)S(1)} %add_convert_fusion.refs_4_), channel_id=1, source_target_pairs={{0,1},{1,0},{2,3},{3,2},{4,5},{5,4},{6,7},{7,6},{8,9},{9,8},{10,11... | collective-permute-start | bytes 1179656 | tf_op jit(solution)/shard_map/ppermute | solution.py:717
  115.0 1.9 %collective-permute-start.18 = (bf16[64,1536]{1,0:T(8,128)(2,1)S(1)}, bf16[64,1536]{1,0:T(8,128)(2,1)S(1)}, u32[]{:S(2)}, u32[]{:S(2)}) collective-permute-start(bf16[64,1536]{1,0:T(8,128)(2,1)S(1)} %add_convert_fusion.2.refs_2_), channel_id=1, source_target_pairs={{0,1},{1,0},{2,3},{3,2},{4,5},{5,4},{6,7},{7,6},{8,9},{9,8},{10,11... | collective-permute-start | bytes 589832 | tf_op jit(solution)/shard_map/ppermute | solution.py:717
  (8 other events, 35.8 us)

commit v6 on v5

--- a/solution.py
+++ b/solution.py
@@ -522,16 +522,31 @@
     )(request, fill, asked_rows, in_hbm(keys), in_hbm(values), decay)
 
 
-def merge_kernel(
-    capacity, steps, part, table_ref, back_ref, log_hbm, average_hbm, *refs
-):
-    out_refs, (top_ref, total_ref, numer_ref, tops_ref, sems) = refs[:steps], refs[steps:]
+def merge_kernel(capacity, steps, part, table_ref, back_ref, log_hbm, average_hbm, *refs):
+    loads = []
+    if part == PARTS - 1:
+        mixes, others, refs = refs[:4], refs[4:7], refs[7:]
+        *refs, load_sems = refs
+        out_ref, weight_ref, *targets = refs[:5]
+        scratch = refs[5:]
+        height = mixes[0].shape[0]
+        head = lax.axis_index("head")
+        pairs = [
+            (mix, weight_ref.at[pl.ds(pl.multiple_of((head ^ other) * height, height), height)])
+            for other, mix in enumerate(mixes)
+        ]
+        pairs.extend(zip(others, targets))
+    else:
+        out_ref, *scratch = refs
+    top_ref, total_ref, numer_ref, tops_ref, sems = scratch
     groups, _, inner = back_ref.shape
     rows = steps * BEAMS
     span = PARTS * rows
     heads = inner // 64
     state = (top_ref, total_ref, numer_ref)
     copies = start_all([(log_hbm.at[part], top_ref), (average_hbm.at[part], numer_ref)], sems)
+    if part == PARTS - 1:
+        loads = start_all(pairs, load_sems)
     total_ref[...] = jnp.ones_like(total_ref)
     first = capacity * span
     tails = jnp.concatenate(
@@ -565,53 +580,37 @@
             parts.append(numer_ref[here, :] / total_ref[here, :])
         for step in range(steps):
             both = jnp.concatenate([p[step * 8 : step * 8 + 8] for p in parts], axis=0)
-            out_refs[step][index * 16 : index * 16 + 16, :] = both.astype(bf16)
-
-
-def merge(part, table, back, logs, averages, steps, capacity):
+            start = step * (top_ref.shape[0] // steps) + index * 16
+            out_ref[start : start + 16, :] = both.astype(bf16)
+    for copy in loads:
+        copy.wait()
+
+
+def merge(part, table, back, logs, averages, steps, capacity, mixes=(), others=()):
     _, requests, span, inner = logs.shape
     rows = requests * span
     logs, averages = (x.reshape(PARTS, rows, inner) for x in (logs, averages))
     vmem = pl.BlockSpec(memory_space=pltpu.VMEM)
     hbm = pl.BlockSpec(memory_space=pltpu.HBM)
+    loads = [*mixes, *others]
+    kept = [jax.ShapeDtypeStruct(x.shape, x.dtype) for x in others]
+    if mixes:
+        kept = [jax.ShapeDtypeStruct((4 * inner, mixes[0].shape[1]), bf16)] + kept
     return pl.pallas_call(
         functools.partial(merge_kernel, capacity, steps, part),
-        in_specs=[SMEM, vmem, hbm, hbm],
-        out_shape=[jax.ShapeDtypeStruct((rows // steps, inner), bf16)] * steps,
+        in_specs=[SMEM, vmem, hbm, hbm]
+        + [pl.BlockSpec(memory_space=pl.ANY)] * len(mixes)
+        + [hbm] * len(others),
+        out_shape=[jax.ShapeDtypeStruct((rows, inner), bf16)] + kept,
         scratch_shapes=[pltpu.VMEM((rows, inner), f32)] * 3
-        + [pltpu.VMEM((back.shape[0] * span, capacity * inner), f32), pltpu.SemaphoreType.DMA((2,))],
+        + [pltpu.VMEM((back.shape[0] * span, capacity * inner), f32), pltpu.SemaphoreType.DMA((2,))]
+        + [pltpu.SemaphoreType.DMA((len(loads),))] * bool(loads),
         compiler_params=pltpu.CompilerParams(vmem_limit_bytes=10 * MIB),
         cost_estimate=pl.CostEstimate(
             flops=40 * rows * inner, bytes_accessed=8 * MIB, transcendentals=4 * rows * inner
         ),
         name="merge",
-    )(table, back, in_hbm(logs), in_hbm(averages))
-
-
-def arrange_kernel(w0, w1, w2, w3, out_ref, sems):
-    inner = w0.shape[0]
-    head = lax.axis_index("head")
-    pairs = [
-        (weight, out_ref.at[pl.ds(pl.multiple_of((head ^ other) * inner, inner), inner)])
-        for other, weight in enumerate((w0, w1, w2, w3))
-    ]
-    for copy in start_all(pairs, sems):
-        copy.wait()
-
-
-def arrange(weights):
-    inner, width = weights[0].shape
-    anywhere = pl.BlockSpec(memory_space=pl.ANY)
-    return pl.pallas_call(
-        arrange_kernel,
-        in_specs=[anywhere] * 4,
-        out_specs=pl.BlockSpec(memory_space=pltpu.VMEM),
-        out_shape=jax.ShapeDtypeStruct((4 * inner, width), bf16),
-        scratch_shapes=[pltpu.SemaphoreType.DMA((4,))],
-        compiler_params=pltpu.CompilerParams(vmem_limit_bytes=10 * MIB),
-        cost_estimate=pl.CostEstimate(flops=0, bytes_accessed=8 * MIB, transcendentals=0),
-        name="arrange",
-    )(*weights)
+    )(table, back, in_hbm(logs), in_hbm(averages), *mixes, *[in_hbm(x) for x in others])
 
 
 def block_kernel(
@@ -738,9 +737,10 @@
         return lax.all_to_all(value, "group", split_axis=0, concat_axis=0, tiled=True)
 
     ids = exchange(jnp.broadcast_to(page_request, (groups, 1, page_request.shape[0])))
-    w_out_far = swap_chip(w_out)
     q_near, q, normed = queries_of(tokens, gain_attn, w_query)
     table, asked = ask(page_request, ids, q_near, span, capacity)
+    asked, w_out = lax.optimization_barrier((asked, w_out))
+    w_out_far = swap_chip(w_out)
     asked_rows = exchange(asked.reshape(groups, capacity * span, inner)).reshape(asked.shape)
     own = own_pages(page_request, page_fill, q, keys_pool, values_pool, decay, span)
     asked_rows, own = lax.optimization_barrier((asked_rows, own))
@@ -750,37 +750,46 @@
     payload, normed = lax.optimization_barrier((payload, normed))
     back = exchange(payload)
     logs, averages = fresh(parents, forget_bias, normed, w_key, w_value, w_forget, q, own)
-    weight = arrange([w_out, swap_core(w_out), w_out_far, swap_core(w_out_far)])
-    logs, weight = lax.optimization_barrier((logs, weight))
+    mixes = [w_out, swap_core(w_out), w_out_far, swap_core(w_out_far)]
+    logs, mixes = lax.optimization_barrier((logs, mixes))
 
     flat = tokens.reshape(steps * rows, width)
     each = steps // PARTS
-    attended = []
-    for index in range(PARTS):
-        attended.extend(merge(index, table, back, logs, averages, each, capacity))
-    heres = [attended[0], attended[1], jnp.concatenate(attended[2:], axis=0)]
+    heres = list(merge(0, table, back, logs, averages, each, capacity))
+    back, heres[0] = lax.optimization_barrier((back, heres[0]))
+    here, *weights = merge(
+        1, table, back, logs, averages, each, capacity, mixes, [w_gate, w_up, w_down]
+    )
+    heres.append(here)
     fars = [swap_chip(here) for here in heres]
-    residual, mine, other, chip, far_chip = [], [], [], [], []
-    first = 0
-    for index, (here, far) in enumerate(zip(heres, fars)):
+    fars[0], heres[1] = lax.optimization_barrier((fars[0], heres[1]))
+
+    def block_of(index):
+        here, far = heres[index], fars[index]
         gathered = [here, swap_core(here), far, swap_core(far)]
         if index:
-            gathered, other[-1] = lax.optimization_barrier((gathered, other[-1]))
-        if index > 1:
             gathered, chip[0] = lax.optimization_barrier((gathered, chip[0]))
-        outs = block(first, gathered, weight, flat, gain_ffn, w_gate, w_up, w_down)
-        for values, out in zip((residual, mine, other), outs):
-            values.append(out)
-        first += here.shape[0]
-        if index:
-            chip.append((mine[-2] + swap_core(other[-2]).astype(f32)).astype(bf16))
-    chip.append((mine[-1] + swap_core(other[-1]).astype(f32)).astype(bf16))
+        return block(
+            index * here.shape[0], gathered, weights[0], flat, gain_ffn, *weights[1:]
+        )
+
+    def chip_sum(mine, other):
+        return (mine + swap_core(other).astype(f32)).astype(bf16)
+
+    chip, residual = [None] * PARTS, [None] * PARTS
+    residual[0], mine, other = block_of(0)
+    other, fars[1] = lax.optimization_barrier((other, fars[1]))
+    chip[0] = chip_sum(mine, other)
+    most = chip[0].shape[0] // 4 * 3
+    chip_most, chip_rest = chip[0][:most], chip[0][most:]
+    far_most, far_rest = swap_chip(chip_most), swap_chip(chip_rest)
+    residual[1], mine, other = block_of(1)
+    other, far_most = lax.optimization_barrier((other, far_most))
+    chip[1] = chip_sum(mine, other)
+    chip[1], far_rest = lax.optimization_barrier((chip[1], far_rest))
+    far_chip = [jnp.concatenate([far_most, far_rest], axis=0), swap_chip(chip[1])]
     parts = []
-    for index in range(len(chip)):
-        if index:
-            chip[index], far_chip[-1] = lax.optimization_barrier((chip[index], far_chip[-1]))
-        far_chip.append(swap_chip(chip[index]))
-    for index in range(len(chip)):
+    for index in range(PARTS):
         both = chip[index].astype(f32) + far_chip[index].astype(f32)
         done = (residual[index] + both).astype(bf16)
         parts.extend([done, swap_core(done)])

time: 119 us -> 111 us (0.933)
  local copies, waits for them, and re-layouts: 9.19 us -> 4.11 us
  starting transfers between devices: 25.6 us -> 24.4 us
    ppermute x7 -> x6, waiting for transfers between devices: 19.8 us -> 14.6 us  [swap_chip(): return lax.ppermute(value, 'head', [(i, i ^ 2) for i in range(4)])]
    unnamed x33 -> x24, local copies, waits for them, and re-layouts: 7.93 us -> 2.76 us
    all_to_all x3, waiting for transfers between devices: 13.1 us -> 16 us  [exchange(): lax.all_to_all(value, 'group', split_axis=0, concat_axis=0, tiled=True)]
    pallas_call x2, Pallas kernels: 5.68 us -> 7.68 us  [merge(): pl.pallas_call(functools.partial(merge_kernel, capacity, steps, part), in...]
    ppermute x14 -> x10, waiting for transfers between devices: 2.37 us -> 3.64 us  [swap_core(): return lax.ppermute(value, 'head', [(i, i ^ 1) for i in range(4)])]
    pallas_call x3 -> x2, Pallas kernels: 13 us -> 11.8 us  [block(): pl.pallas_call(functools.partial(block_kernel, first), in_specs=[vmem] *...]
    ppermute x14 -> x10, starting transfers between devices: 2.99 us -> 1.92 us  [swap_core(): return lax.ppermute(value, 'head', [(i, i ^ 1) for i in range(4)])]
    ppermute x7 -> x6, starting transfers between devices: 8.39 us -> 7.41 us  [swap_chip(): return lax.ppermute(value, 'head', [(i, i ^ 2) for i in range(4)])]
  transfers between devices with their start and end apart: 24 -> 19, of which waited for: 9 -> 11; matrix products, arithmetic and copies ran while one was open for 1% -> 0% of each run, Pallas kernels for 36% -> 38%
where the time goes in v6:
time: 111 us
  Pallas kernels  47.2 us (43%)
  waiting for transfers between devices  34.3 us (31%)
  starting transfers between devices  24.4 us (22%)
  local copies, waits for them, and re-layouts  4.11 us (4%)
    all_to_all x3, waiting for transfers between devices, exchange(): lax.all_to_all(value, 'group', split_axis=0, concat_axis=0, tiled=True)  16 us
    all_to_all x3, starting transfers between devices, exchange(): lax.all_to_all(value, 'group', split_axis=0, concat_axis=0, tiled=True)  15 us
    ppermute x6, waiting for transfers between devices, swap_chip(): return lax.ppermute(value, 'head', [(i, i ^ 2) for i in range(4)])  14.6 us
    pallas_call x2, Pallas kernels, block(): pl.pallas_call(functools.partial(block_kernel, first), in_specs=[vmem] *...  11.8 us
    pallas_call x1, Pallas kernels, fresh(): pl.pallas_call(fresh_kernel, in_specs=[vmem, vmem] + [hbm] * len(big), ou...  8.94 us
    pallas_call x2, Pallas kernels, merge(): pl.pallas_call(functools.partial(merge_kernel, capacity, steps, part), in...  7.68 us
    ppermute x6, starting transfers between devices, swap_chip(): return lax.ppermute(value, 'head', [(i, i ^ 2) for i in range(4)])  7.41 us
    pallas_call x1, Pallas kernels, own_pages(): pl.pallas_call(own_kernel, grid=(OWNED_SLOTS // PAGE_BLOCK,), in_specs=[S...  6.91 us
  transfers between devices with their start and end apart: 19, of which 11 were waited for; matrix products, arithmetic and copies ran while one was open for 0% of the time, Pallas kernels for 38%

profile of v6, /device:TPU:0, one launch (start us, length us, event | category | flops | bytes accessed | tf_op | source)
XLA Modules:
  0.0 110.6 jit_solution(13323111717469857220)
XLA Ops:
  0.0 1.3 %broadcast_in_dim.3 = s32[8,1,48]{2,1,0:T(1,128)} broadcast(s32[48]{0:T(128)} %request_ref.5), dimensions={2} | broadcast | bytes 1728 | tf_op jit(solution)/shard_map/broadcast_in_dim | solution.py:739
  1.3 7.3 %all-to-all-start = ((s32[8,1,48]{2,1,0:T(1,128)}), s32[8,1,48]{2,1,0:T(1,128)S(1)}, u32[]{:S(2)}, u32[]{:S(2)}) async-start(s32[8,1,48]{2,1,0:T(1,128)} %broadcast_in_dim.3), calls=%async_computation | async-start | bytes 8192 | tf_op jit(solution)/shard_map/all_to_all | solution.py:737
  8.6 0.7 copy-done.7
  9.3 3.8 %queries.1 = (bf16[512,384]{1,0:T(8,128)(2,1)S(1)}, bf16[512,384]{1,0:T(8,128)(2,1)}, bf16[512,1536]{1,0:T(8,128)(2,1)}) custom-call(bf16[4,128,1536]{2,1,0:T(8,128)(2,1)} %tokens_hbm.1, f32[1536]{0:T(1024)S(1)} %copy-done.7, bf16[384,1536]{1,0:T(8,128)(2,1)} %wq_hbm.1), custom_call_target="tpu_custom_call" | custom-call | flops 603979776 | bytes 6291456 | tf_op jit(solution)/shard_map/queries/pallas_call | solution.py:125
  13.1 2.0 %all-to-all-done.ids_ref = s32[8,1,48]{2,1,0:T(1,128)S(1)} async-done(((s32[8,1,48]{2,1,0:T(1,128)}), s32[8,1,48]{2,1,0:T(1,128)S(1)}, u32[]{:S(2)}, u32[]{:S(2)}) %all-to-all-start) | async-done | bytes 1568 | tf_op jit(solution)/shard_map/all_to_all | solution.py:737
  15.1 2.0 %ask.1 = (s32[24]{0:T(128)S(1)}, bf16[24,32,384]{2,1,0:T(8,128)(2,1)}) custom-call(s32[48]{0:T(128)S(1)} %copy-done.8, s32[8,1,48]{2,1,0:T(1,128)S(1)} %all-to-all-done.ids_ref, bf16[512,384]{1,0:T(8,128)(2,1)S(1)} %get-tuple-element.54.q_ref), custom_call_target="tpu_custom_call" | custom-call | tf_op jit(solution)/shard_map/ask/pallas_call | solution.py:162
  17.1 1.6 %collective-permute-start.1 = (bf16[384,1536]{1,0:T(8,128)(2,1)S(1)}, bf16[384,1536]{1,0:T(8,128)(2,1)S(1)}, u32[]{:S(2)}, u32[]{:S(2)}) collective-permute-start(bf16[384,1536]{1,0:T(8,128)(2,1)S(1)} %copy-done), channel_id=1, source_target_pairs={{0,2},{1,3},{2,0},{3,1},{4,6},{5,7},{6,4},{7,5},{8,10},{9,11},{10,... | collective-permute-start | bytes 3538952 | tf_op jit(solution)/shard_map/ppermute | solution.py:720
  18.6 4.0 %all-to-all-start.1 = ((bf16[8,96,384]{2,1,0:T(8,128)(2,1)}), bf16[8,96,384]{2,1,0:T(8,128)(2,1)S(1)}, u32[]{:S(2)}, u32[]{:S(2)}) async-start(bf16[8,96,384]{2,1,0:T(8,128)(2,1)} %bitcast), calls=%async_computation.1 | async-start | bytes 1179648 | tf_op jit(solution)/shard_map/all_to_all | solution.py:737
  22.7 6.9 %own_pages.1 = (f32[512,384]{1,0:T(8,128)}, f32[512,384]{1,0:T(8,128)}, f32[512,384]{1,0:T(8,128)}) custom-call(s32[48]{0:T(128)S(1)} %copy-done.8, s32[48]{0:T(128)S(1)} %copy-done.10, bf16[512,384]{1,0:T(8,128)(2,1)} %get-tuple-element.57.q_ref.q_hbm, bf16[48,384,128]{2,1,0:T(8,128)(2,1)} %keys_ref.3, bf16[48,384,128]{2,1,0:T(8,128)(2,1)} %values_ref.3, ...), custom_call_target="tpu_custom_call" | custom-call | flops 805306368 | bytes 6291456 | tf_op jit(solution)/shard_map/own_pages/pallas_call | solution.py:442
  29.6 8.2 %all-to-all-done.1 = bf16[8,96,384]{2,1,0:T(8,128)(2,1)S(1)} async-done(((bf16[8,96,384]{2,1,0:T(8,128)(2,1)}), bf16[8,96,384]{2,1,0:T(8,128)(2,1)S(1)}, u32[]{:S(2)}, u32[]{:S(2)}) %all-to-all-start.1) | async-done | bytes 589856 | tf_op jit(solution)/shard_map/all_to_all | solution.py:737
  37.8 4.8 %hosted_pages.1 = bf16[8,112,384]{2,1,0:T(8,128)(2,1)} custom-call(s32[48]{0:T(128)S(1)} %copy-done.8, s32[48]{0:T(128)S(1)} %copy-done.10, bf16[24,32,384]{2,1,0:T(8,128)(2,1)S(1)} %bitcast.9, bf16[48,384,128]{2,1,0:T(8,128)(2,1)} %keys_ref.3, bf16[48,384,128]{2,1,0:T(8,128)(2,1)} %values_ref.3, bf16[6,48,128]{2,1,0:T(8,128)(2,1)S(1)} %bitcast.11), custom_call_target="tpu_custom_call" | custom-call | flops 402653184 | bytes 3145728 | tf_op jit(solution)/shard_map/hosted_pages/pallas_call | solution.py:509
  42.6 3.7 %all-to-all-start.2 = ((bf16[8,112,384]{2,1,0:T(8,128)(2,1)}), bf16[8,112,384]{2,1,0:T(8,128)(2,1)S(1)}, u32[]{:S(2)}, u32[]{:S(2)}) async-start(bf16[8,112,384]{2,1,0:T(8,128)(2,1)} %hosted_pages.1), calls=%async_computation.2 | async-start | bytes 1376256 | tf_op jit(solution)/shard_map/all_to_all | solution.py:737
  46.9 8.9 %fresh.1 = (f32[2,16,16,384]{3,2,1,0:T(8,128)}, f32[2,16,16,384]{3,2,1,0:T(8,128)}) custom-call(s32[3,128]{1,0:T(4,128)S(1)} %copy-done.9, f32[1,6]{1,0:T(1,128)S(1)} %bitcast.12, bf16[512,1536]{1,0:T(8,128)(2,1)} %get-tuple-element.65.normed_hbm, bf16[384,1536]{1,0:T(8,128)(2,1)} %wk_hbm.1, bf16[384,1536]{1,0:T(8,128)(2,1)} %wv_hbm.1, ...), custom_call_target="tpu_custom_call" | custom-call | flops 1207959552 | bytes 12582912 | tf_op jit(solution)/shard_map/fresh/pallas_call | solution.py:327
  55.9 1.0 copy-done.1
  56.9 1.0 copy-done.3
  57.9 5.9 %all-to-all-done.2.back_ref = bf16[8,112,384]{2,1,0:T(8,128)(2,1)S(1)} async-done(((bf16[8,112,384]{2,1,0:T(8,128)(2,1)}), bf16[8,112,384]{2,1,0:T(8,128)(2,1)S(1)}, u32[]{:S(2)}, u32[]{:S(2)}) %all-to-all-start.2) | async-done | bytes 688160 | tf_op jit(solution)/shard_map/all_to_all | solution.py:737
  63.8 2.2 %merge.2.att0 = bf16[256,384]{1,0:T(8,128)(2,1)S(1)} custom-call(s32[24]{0:T(128)S(1)} %get-tuple-element.64.table_ref, bf16[8,112,384]{2,1,0:T(8,128)(2,1)S(1)} %all-to-all-done.2.back_ref, f32[2,256,384]{2,1,0:T(8,128)} %bitcast.15, f32[2,256,384]{2,1,0:T(8,128)} %bitcast.17), custom_call_target="tpu_custom_call" | custom-call | flops 3932160 | bytes 8388608 | tf_op jit(solution)/shard_map/merge/pallas_call | solution.py:599
  66.0 0.6 collective-permute-start.4
  66.6 5.5 %merge.3 = (bf16[256,384]{1,0:T(8,128)(2,1)S(1)}, bf16[1536,1536]{1,0:T(8,128)(2,1)S(1)}, bf16[1536,1024]{1,0:T(8,128)(2,1)S(1)}, bf16[1536,1024]{1,0:T(8,128)(2,1)S(1)}, bf16[1024,1536]{1,0:T(8,128)(2,1)S(1)}) custom-call(s32[24]{0:T(128)S(1)} %get-tuple-element.64.table_ref, bf16[8,112,384]{2,1,0:T(8,128)(2,1)S(1)} %all-to-all-done.2.back_ref, ...), custom_call_target="tpu_custom_call" | custom-call | flops 3932160 | bytes 8388608 | tf_op jit(solution)/shard_map/merge/pallas_call | solution.py:599
  72.1 0.6 collective-permute-start.5
  72.7 1.5 %collective-permute-start.7 = (bf16[256,384]{1,0:T(8,128)(2,1)S(1)}, bf16[256,384]{1,0:T(8,128)(2,1)S(1)}, u32[]{:S(2)}, u32[]{:S(2)}) collective-permute-start(bf16[256,384]{1,0:T(8,128)(2,1)S(1)} %get-tuple-element.92.att0), channel_id=1, source_target_pairs={{0,2},{1,3},{2,0},{3,1},{4,6},{5,7},{6,4},{7,5},{8,10},{9,11},{10,... | collective-permute-start | bytes 589832 | tf_op jit(solution)/shard_map/ppermute | solution.py:720
  74.2 5.8 %block.2 = (f32[128,1536]{1,0:T(8,128)S(1)}, f32[128,1536]{1,0:T(8,128)S(1)}, bf16[128,1536]{1,0:T(8,128)(2,1)S(1)}) custom-call(bf16[256,384]{1,0:T(8,128)(2,1)S(1)} %merge.2.att0, bf16[256,384]{1,0:T(8,128)(2,1)S(1)} %collective-permute-done.3.att1, bf16[256,384]{1,0:T(8,128)(2,1)S(1)} %collective-permute-done.4.att2, ...), custom_call_target="tpu_custom_call" | custom-call | flops 3623878656 | bytes 16777216 | tf_op jit(solution)/shard_map/block/pallas_call | solution.py:667
  80.7 1.1 %collective-permute-done.9 = bf16[128,1536]{1,0:T(8,128)(2,1)S(1)} collective-permute-done((bf16[128,1536]{1,0:T(8,128)(2,1)S(1)}, bf16[128,1536]{1,0:T(8,128)(2,1)S(1)}, u32[]{:S(2)}, u32[]{:S(2)}) %collective-permute-start.9) | collective-permute-done | bytes 393248 | tf_op jit(solution)/shard_map/ppermute | solution.py:716
  82.4 1.1 collective-permute-start.10
  83.4 6.0 %block.3 = (f32[128,1536]{1,0:T(8,128)S(1)}, f32[128,1536]{1,0:T(8,128)S(1)}, bf16[128,1536]{1,0:T(8,128)(2,1)S(1)}) custom-call(bf16[256,384]{1,0:T(8,128)(2,1)S(1)} %get-tuple-element.92.att0, bf16[256,384]{1,0:T(8,128)(2,1)S(1)} %collective-permute-done.6.att1, bf16[256,384]{1,0:T(8,128)(2,1)S(1)} %collective-permute-done.7.att2, ...), custom_call_target="tpu_custom_call" | custom-call | flops 3623878656 | bytes 16777216 | tf_op jit(solution)/shard_map/block/pallas_call | solution.py:667
  89.5 1.9 %collective-permute-done.10 = bf16[96,1536]{1,0:T(8,128)(2,1)S(1)} collective-permute-done((bf16[96,1536]{1,0:T(8,128)(2,1)S(1)}, bf16[96,1536]{1,0:T(8,128)(2,1)S(1)}, u32[]{:S(2)}, u32[]{:S(2)}) %collective-permute-start.10) | collective-permute-done | bytes 294944 | tf_op jit(solution)/shard_map/ppermute | solution.py:720
  91.4 1.4 %collective-permute-start.12 = (bf16[32,1536]{1,0:T(8,128)(2,1)S(1)}, bf16[32,1536]{1,0:T(8,128)(2,1)S(1)}, u32[]{:S(2)}, u32[]{:S(2)}) collective-permute-start(bf16[32,1536]{1,0:T(8,128)(2,1)S(1)} %slice.9), channel_id=1, source_target_pairs={{0,2},{1,3},{2,0},{3,1},{4,6},{5,7},{6,4},{7,5},{8,10},{9,11},{10,... | collective-permute-start | bytes 294920 | tf_op jit(solution)/shard_map/ppermute | solution.py:720
  93.2 3.5 %collective-permute-done.12 = bf16[32,1536]{1,0:T(8,128)(2,1)S(1)} collective-permute-done((bf16[32,1536]{1,0:T(8,128)(2,1)S(1)}, bf16[32,1536]{1,0:T(8,128)(2,1)S(1)}, u32[]{:S(2)}, u32[]{:S(2)}) %collective-permute-start.12) | collective-permute-done | bytes 98336 | tf_op jit(solution)/shard_map/ppermute | solution.py:720
  96.7 1.3 %collective-permute-start.14 = (bf16[128,1536]{1,0:T(8,128)(2,1)S(1)}, bf16[128,1536]{1,0:T(8,128)(2,1)S(1)}, u32[]{:S(2)}, u32[]{:S(2)}) collective-permute-start(bf16[128,1536]{1,0:T(8,128)(2,1)S(1)} %add_convert_fusion.2), channel_id=1, source_target_pairs={{0,2},{1,3},{2,0},{3,1},{4,6},{5,7},{6,4},{7,5},{8,10},{9,11},{10,... | collective-permute-start | bytes 1179656 | tf_op jit(solution)/shard_map/ppermute | solution.py:720
  98.2 9.2 %collective-permute-done.14 = bf16[128,1536]{1,0:T(8,128)(2,1)S(1)} collective-permute-done((bf16[128,1536]{1,0:T(8,128)(2,1)S(1)}, bf16[128,1536]{1,0:T(8,128)(2,1)S(1)}, u32[]{:S(2)}, u32[]{:S(2)}) %collective-permute-start.14) | collective-permute-done | bytes 393248 | tf_op jit(solution)/shard_map/ppermute | solution.py:720
  107.6 1.7 %collective-permute-done.15.refs_3_ = bf16[128,1536]{1,0:T(8,128)(2,1)S(1)} collective-permute-done((bf16[128,1536]{1,0:T(8,128)(2,1)S(1)}, bf16[128,1536]{1,0:T(8,128)(2,1)S(1)}, u32[]{:S(2)}, u32[]{:S(2)}) %collective-permute-start.15) | collective-permute-done | bytes 393248 | tf_op jit(solution)/shard_map/ppermute | solution.py:716
  109.3 1.3 %finish.1 = bf16[512,1536]{1,0:T(8,128)(2,1)} custom-call(bf16[128,1536]{1,0:T(8,128)(2,1)S(1)} %add_convert_fusion.1.refs_0_, bf16[128,1536]{1,0:T(8,128)(2,1)S(1)} %collective-permute-done.13.refs_1_, bf16[128,1536]{1,0:T(8,128)(2,1)S(1)} %add_convert_fusion.refs_2_, bf16[128,1536]{1,0:T(8,128)(2,1)S(1)} %collective-permute-done.15.refs_3_), custom_call_target="tpu_custom_call" | custom-call | tf_op jit(solution)/shard_map/finish/pallas_call | solution.py:705
  (47 shorter events, 2.6 us)
Async XLA Ops:
  0.0 15.1 %copy-start.8 = (s32[48]{0:T(128)S(1)}, s32[48]{0:T(128)}, u32[]{:S(2)}) copy-start(s32[48]{0:T(128)} %request_ref.5) | copy-start | bytes 580
  1.3 13.7 %all-to-all-start = ((s32[8,1,48]{2,1,0:T(1,128)}), s32[8,1,48]{2,1,0:T(1,128)S(1)}, u32[]{:S(2)}, u32[]{:S(2)}) async-start(s32[8,1,48]{2,1,0:T(1,128)} %broadcast_in_dim.3), calls=%async_computation | async-start | bytes 8192 | tf_op jit(solution)/shard_map/all_to_all | solution.py:737
  8.6 0.7 copy-start.7
  9.3 7.7 %copy-start = (bf16[384,1536]{1,0:T(8,128)(2,1)S(1)}, bf16[384,1536]{1,0:T(8,128)(2,1)}, u32[]{:S(2)}) copy-start(bf16[384,1536]{1,0:T(8,128)(2,1)} %refs_0_) | copy-start | bytes 3538948
  9.3 13.4 %copy-start.5 = (bf16[48,6,128]{2,0,1:T(8,128)(2,1)S(1)}, bf16[48,6,128]{2,0,1:T(8,128)(2,1)}, u32[]{:S(2)}) copy-start(bf16[48,6,128]{2,0,1:T(8,128)(2,1)} %param.24) | copy-start | bytes 221188
  9.3 13.4 %copy-start.10 = (s32[48]{0:T(128)S(1)}, s32[48]{0:T(128)}, u32[]{:S(2)}) copy-start(s32[48]{0:T(128)} %fill_ref.3) | copy-start | bytes 580
  17.1 29.3 %collective-permute-start.1 = (bf16[384,1536]{1,0:T(8,128)(2,1)S(1)}, bf16[384,1536]{1,0:T(8,128)(2,1)S(1)}, u32[]{:S(2)}, u32[]{:S(2)}) collective-permute-start(bf16[384,1536]{1,0:T(8,128)(2,1)S(1)} %copy-done), channel_id=1, source_target_pairs={{0,2},{1,3},{2,0},{3,1},{4,6},{5,7},{6,4},{7,5},{8,10},{9,11},{10,... | collective-permute-start | bytes 3538952 | tf_op jit(solution)/shard_map/ppermute | solution.py:720
  18.6 19.1 %all-to-all-start.1 = ((bf16[8,96,384]{2,1,0:T(8,128)(2,1)}), bf16[8,96,384]{2,1,0:T(8,128)(2,1)S(1)}, u32[]{:S(2)}, u32[]{:S(2)}) async-start(bf16[8,96,384]{2,1,0:T(8,128)(2,1)} %bitcast), calls=%async_computation.1 | async-start | bytes 1179648 | tf_op jit(solution)/shard_map/all_to_all | solution.py:737
  37.8 9.1 %copy-start.9 = (s32[3,128]{1,0:T(4,128)S(1)}, s32[3,128]{1,0:T(4,128)}, u32[]{:S(2)}) copy-start(s32[3,128]{1,0:T(4,128)} %parents_ref.1) | copy-start | bytes 4612
  37.8 9.1 %copy-start.11 = (f32[6]{0:T(128)S(1)}, f32[6]{0:T(128)}, u32[]{:S(2)}) copy-start(f32[6]{0:T(128)} %param.30) | copy-start | bytes 76
  42.6 21.2 %all-to-all-start.2 = ((bf16[8,112,384]{2,1,0:T(8,128)(2,1)}), bf16[8,112,384]{2,1,0:T(8,128)(2,1)S(1)}, u32[]{:S(2)}, u32[]{:S(2)}) async-start(bf16[8,112,384]{2,1,0:T(8,128)(2,1)} %hosted_pages.1), calls=%async_computation.2 | async-start | bytes 1376256 | tf_op jit(solution)/shard_map/all_to_all | solution.py:737
  46.3 9.5 %collective-permute-start = (bf16[384,1536]{1,0:T(8,128)(2,1)S(1)}, bf16[384,1536]{1,0:T(8,128)(2,1)S(1)}, u32[]{:S(2)}, u32[]{:S(2)}) collective-permute-start(bf16[384,1536]{1,0:T(8,128)(2,1)S(1)} %copy-done), channel_id=1, source_target_pairs={{0,1},{1,0},{2,3},{3,2},{4,5},{5,4},{6,7},{7,6},{8,9},{9,8},{10,11... | collective-permute-start | bytes 3538952 | tf_op jit(solution)/shard_map/ppermute | solution.py:716
  46.4 10.5 %collective-permute-start.2 = (bf16[384,1536]{1,0:T(8,128)(2,1)S(1)}, bf16[384,1536]{1,0:T(8,128)(2,1)S(1)}, u32[]{:S(2)}, u32[]{:S(2)}) collective-permute-start(bf16[384,1536]{1,0:T(8,128)(2,1)S(1)} %collective-permute-done.1.refs_2_), channel_id=1, source_target_pairs={{0,1},{1,0},{2,3},{3,2},{4,5},{5,4},{6,7},{7,6},{8,9},{9,8},{10,11... | collective-permute-start | bytes 3538952 | tf_op jit(solution)/shard_map/ppermute | solution.py:716
  55.8 1.0 copy-start.1
  56.9 1.0 copy-start.3
  63.8 2.8 %copy-start.2 = (bf16[384,1536]{1,0:T(8,128)(2,1)S(1)}, bf16[384,1536]{1,0:T(8,128)(2,1)}, u32[]{:S(2)}) copy-start(bf16[384,1536]{1,0:T(8,128)(2,1)} %copy-done.1) | copy-start | bytes 3538948
  63.8 2.8 %copy-start.4 = (bf16[384,1536]{1,0:T(8,128)(2,1)S(1)}, bf16[384,1536]{1,0:T(8,128)(2,1)}, u32[]{:S(2)}) copy-start(bf16[384,1536]{1,0:T(8,128)(2,1)} %copy-done.3) | copy-start | bytes 3538948
  66.0 8.2 %copy-start.6 = (f32[1536]{0:T(1024)S(1)}, f32[1536]{0:T(1024)}, u32[]{:S(2)}) copy-start(f32[1536]{0:T(1024)} %gain_ref.5) | copy-start | bytes 18436
  66.0 6.1 %collective-permute-start.4 = (bf16[256,384]{1,0:T(8,128)(2,1)S(1)}, bf16[256,384]{1,0:T(8,128)(2,1)S(1)}, u32[]{:S(2)}, u32[]{:S(2)}) collective-permute-start(bf16[256,384]{1,0:T(8,128)(2,1)S(1)} %merge.2.att0), channel_id=1, source_target_pairs={{0,2},{1,3},{2,0},{3,1},{4,6},{5,7},{6,4},{7,5},{8,10},{9,11},{10,... | collective-permute-start | bytes 589832 | tf_op jit(solution)/shard_map/ppermute | solution.py:720
  66.6 7.6 %collective-permute-start.3 = (bf16[256,384]{1,0:T(8,128)(2,1)S(1)}, bf16[256,384]{1,0:T(8,128)(2,1)S(1)}, u32[]{:S(2)}, u32[]{:S(2)}) collective-permute-start(bf16[256,384]{1,0:T(8,128)(2,1)S(1)} %merge.2.att0), channel_id=1, source_target_pairs={{0,1},{1,0},{2,3},{3,2},{4,5},{5,4},{6,7},{7,6},{8,9},{9,8},{10,11... | collective-permute-start | bytes 589832 | tf_op jit(solution)/shard_map/ppermute | solution.py:716
  72.1 2.1 %collective-permute-start.5 = (bf16[256,384]{1,0:T(8,128)(2,1)S(1)}, bf16[256,384]{1,0:T(8,128)(2,1)S(1)}, u32[]{:S(2)}, u32[]{:S(2)}) collective-permute-start(bf16[256,384]{1,0:T(8,128)(2,1)S(1)} %collective-permute-done.4.att2), channel_id=1, source_target_pairs={{0,1},{1,0},{2,3},{3,2},{4,5},{5,4},{6,7},{7,6},{8,9},{9,8},{10,11... | collective-permute-start | bytes 589832 | tf_op jit(solution)/shard_map/ppermute | solution.py:716
  72.7 7.3 %collective-permute-start.7 = (bf16[256,384]{1,0:T(8,128)(2,1)S(1)}, bf16[256,384]{1,0:T(8,128)(2,1)S(1)}, u32[]{:S(2)}, u32[]{:S(2)}) collective-permute-start(bf16[256,384]{1,0:T(8,128)(2,1)S(1)} %get-tuple-element.92.att0), channel_id=1, source_target_pairs={{0,2},{1,3},{2,0},{3,1},{4,6},{5,7},{6,4},{7,5},{8,10},{9,11},{10,... | collective-permute-start | bytes 589832 | tf_op jit(solution)/shard_map/ppermute | solution.py:720
  80.0 1.8 %collective-permute-start.9 = (bf16[128,1536]{1,0:T(8,128)(2,1)S(1)}, bf16[128,1536]{1,0:T(8,128)(2,1)S(1)}, u32[]{:S(2)}, u32[]{:S(2)}) collective-permute-start(bf16[128,1536]{1,0:T(8,128)(2,1)S(1)} %get-tuple-element.90), channel_id=1, source_target_pairs={{0,1},{1,0},{2,3},{3,2},{4,5},{5,4},{6,7},{7,6},{8,9},{9,8},{10,11... | collective-permute-start | bytes 1179656 | tf_op jit(solution)/shard_map/ppermute | solution.py:716
  80.1 2.0 %collective-permute-start.6 = (bf16[256,384]{1,0:T(8,128)(2,1)S(1)}, bf16[256,384]{1,0:T(8,128)(2,1)S(1)}, u32[]{:S(2)}, u32[]{:S(2)}) collective-permute-start(bf16[256,384]{1,0:T(8,128)(2,1)S(1)} %get-tuple-element.92.att0), channel_id=1, source_target_pairs={{0,1},{1,0},{2,3},{3,2},{4,5},{5,4},{6,7},{7,6},{8,9},{9,8},{10,11... | collective-permute-start | bytes 589832 | tf_op jit(solution)/shard_map/ppermute | solution.py:716
  80.6 1.8 %collective-permute-start.8 = (bf16[256,384]{1,0:T(8,128)(2,1)S(1)}, bf16[256,384]{1,0:T(8,128)(2,1)S(1)}, u32[]{:S(2)}, u32[]{:S(2)}) collective-permute-start(bf16[256,384]{1,0:T(8,128)(2,1)S(1)} %collective-permute-done.7.att2), channel_id=1, source_target_pairs={{0,1},{1,0},{2,3},{3,2},{4,5},{5,4},{6,7},{7,6},{8,9},{9,8},{10,11... | collective-permute-start | bytes 589832 | tf_op jit(solution)/shard_map/ppermute | solution.py:716
  82.4 9.1 %collective-permute-start.10 = (bf16[96,1536]{1,0:T(8,128)(2,1)S(1)}, bf16[96,1536]{1,0:T(8,128)(2,1)S(1)}, u32[]{:S(2)}, u32[]{:S(2)}) collective-permute-start(bf16[96,1536]{1,0:T(8,128)(2,1)S(1)} %slice.8), channel_id=1, source_target_pairs={{0,2},{1,3},{2,0},{3,1},{4,6},{5,7},{6,4},{7,5},{8,10},{9,11},{10,... | collective-permute-start | bytes 884744 | tf_op jit(solution)/shard_map/ppermute | solution.py:720
  91.4 1.7 %collective-permute-start.11 = (bf16[128,1536]{1,0:T(8,128)(2,1)S(1)}, bf16[128,1536]{1,0:T(8,128)(2,1)S(1)}, u32[]{:S(2)}, u32[]{:S(2)}) collective-permute-start(bf16[128,1536]{1,0:T(8,128)(2,1)S(1)} %get-tuple-element.99), channel_id=1, source_target_pairs={{0,1},{1,0},{2,3},{3,2},{4,5},{5,4},{6,7},{7,6},{8,9},{9,8},{10,11... | collective-permute-start | bytes 1179656 | tf_op jit(solution)/shard_map/ppermute | solution.py:716
  91.4 5.3 %collective-permute-start.12 = (bf16[32,1536]{1,0:T(8,128)(2,1)S(1)}, bf16[32,1536]{1,0:T(8,128)(2,1)S(1)}, u32[]{:S(2)}, u32[]{:S(2)}) collective-permute-start(bf16[32,1536]{1,0:T(8,128)(2,1)S(1)} %slice.9), channel_id=1, source_target_pairs={{0,2},{1,3},{2,0},{3,1},{4,6},{5,7},{6,4},{7,5},{8,10},{9,11},{10,... | collective-permute-start | bytes 294920 | tf_op jit(solution)/shard_map/ppermute | solution.py:720
  96.7 10.7 %collective-permute-start.14 = (bf16[128,1536]{1,0:T(8,128)(2,1)S(1)}, bf16[128,1536]{1,0:T(8,128)(2,1)S(1)}, u32[]{:S(2)}, u32[]{:S(2)}) collective-permute-start(bf16[128,1536]{1,0:T(8,128)(2,1)S(1)} %add_convert_fusion.2), channel_id=1, source_target_pairs={{0,2},{1,3},{2,0},{3,1},{4,6},{5,7},{6,4},{7,5},{8,10},{9,11},{10,... | collective-permute-start | bytes 1179656 | tf_op jit(solution)/shard_map/ppermute | solution.py:720
  98.1 9.5 %collective-permute-start.13 = (bf16[128,1536]{1,0:T(8,128)(2,1)S(1)}, bf16[128,1536]{1,0:T(8,128)(2,1)S(1)}, u32[]{:S(2)}, u32[]{:S(2)}) collective-permute-start(bf16[128,1536]{1,0:T(8,128)(2,1)S(1)} %add_convert_fusion.1.refs_0_), channel_id=1, source_target_pairs={{0,1},{1,0},{2,3},{3,2},{4,5},{5,4},{6,7},{7,6},{8,9},{9,8},{10,11... | collective-permute-start | bytes 1179656 | tf_op jit(solution)/shard_map/ppermute | solution.py:716
  107.6 1.8 %collective-permute-start.15 = (bf16[128,1536]{1,0:T(8,128)(2,1)S(1)}, bf16[128,1536]{1,0:T(8,128)(2,1)S(1)}, u32[]{:S(2)}, u32[]{:S(2)}) collective-permute-start(bf16[128,1536]{1,0:T(8,128)(2,1)S(1)} %add_convert_fusion.refs_2_), channel_id=1, source_target_pairs={{0,1},{1,0},{2,3},{3,2},{4,5},{5,4},{6,7},{7,6},{8,9},{9,8},{10,11... | collective-permute-start | bytes 1179656 | tf_op jit(solution)/shard_map/ppermute | solution.py:716

commit v7 on v6

--- a/solution.py
+++ b/solution.py
@@ -12,7 +12,6 @@
 SPILL = 16
 PAGE_BLOCK = 16
 PARTS = 2
-TAIL_ROWS = 16
 MIB = 1 << 20
 
 epsilon = 1e-05
@@ -460,6 +459,8 @@
     pairs = inner // 128
     heads = decay_ref.shape[0]
     groups = out_ref.shape[0]
+    half = span // PARTS
+    slot_rows = pairs * span
     out_ref[...] = jnp.zeros_like(out_ref)
     tail_ref[...] = jnp.zeros_like(tail_ref)
     for owner in range(groups):
@@ -475,29 +476,26 @@
         fills.append(fill_ref[OWNED_SLOTS + page])
     page_weights(queries, fills, keys_ref, decay_ref, *scratch)
     scores_ref, _, tops_ref = scratch
-    lane = lanes((span, 128))
+    lane = lanes((half, 128))
     for page, (owner, rank) in enumerate(places):
-        here = pl.ds(pl.multiple_of(rank * span, span), span)
         for pair in range(pairs):
             _, total, numer = page_sums(page, pair, span, values_ref, *scratch)
-            out_ref[owner, here, pl.ds(pair * 128, 128)] = (numer / total).astype(bf16)
+            here = pl.ds(pl.multiple_of(rank * slot_rows + pair * span, span), span)
+            out_ref[owner, here, :] = (numer / total).astype(bf16)
         tail = tail_ref[owner]
         base = rank * (3 * heads)
         for head in range(heads):
             rows = pl.ds(head * span, span)
             rest = tops_ref[page, rows, :] + jnp.log(scores_ref[page, rows, :])
+            rest = jnp.where(lane < 64, rest[:half], rest[half:])
             for piece in range(3):
                 part = rest.astype(bf16).astype(f32)
                 rest = rest - part
-                tail = jnp.where(lane == base + piece * heads + head, part, tail)
+                tail = jnp.where(lane % 64 == base + piece * heads + head, part, tail)
         tail_ref[owner] = tail
-    first = capacity * span
+    first = capacity * slot_rows
     for owner in range(groups):
-        tail = tail_ref[owner].astype(bf16)
-        for part in range(span // TAIL_ROWS):
-            out_ref[owner, first : first + TAIL_ROWS, part * 128 : part * 128 + 128] = tail[
-                part * TAIL_ROWS : part * TAIL_ROWS + TAIL_ROWS
-            ]
+        out_ref[owner, first : first + half, :] = tail_ref[owner].astype(bf16)
 
 
 def hosted_pages(request, fill, asked_rows, keys, values, decay, groups, capacity, local_count):
@@ -505,7 +503,7 @@
     shift = OWNED_SLOTS // SPILL
     pool = pl.BlockSpec((SPILL,) + keys.shape[1:], lambda i: (shift, 0, 0))
     decay_spec = pl.BlockSpec((decay.shape[0], SPILL, decay.shape[2]), lambda i: (0, shift, 0))
-    out_shape = (groups, capacity * span + TAIL_ROWS, inner)
+    out_shape = (groups, capacity * span * inner // 128 + span // PARTS, 128)
     return pl.pallas_call(
         functools.partial(hosted_kernel, local_count, capacity),
         grid=(1,),
@@ -514,7 +512,7 @@
         ],
         out_specs=pl.BlockSpec(out_shape, lambda i: (0, 0, 0)),
         out_shape=jax.ShapeDtypeStruct(out_shape, bf16),
-        scratch_shapes=[pltpu.VMEM((groups, span, 128), f32), pltpu.SMEM((groups,), jnp.int32)]
+        scratch_shapes=[pltpu.VMEM((groups, span // PARTS, 128), f32), pltpu.SMEM((groups,), jnp.int32)]
         + page_scratch(SPILL, span, decay.shape[0]),
         compiler_params=pltpu.CompilerParams(vmem_limit_bytes=24 * MIB),
         cost_estimate=page_cost(SPILL, keys, 64),
@@ -522,45 +520,38 @@
     )(request, fill, asked_rows, in_hbm(keys), in_hbm(values), decay)
 
 
-def merge_kernel(capacity, steps, part, table_ref, back_ref, log_hbm, average_hbm, *refs):
-    loads = []
-    if part == PARTS - 1:
-        mixes, others, refs = refs[:4], refs[4:7], refs[7:]
-        *refs, load_sems = refs
-        out_ref, weight_ref, *targets = refs[:5]
-        scratch = refs[5:]
-        height = mixes[0].shape[0]
-        head = lax.axis_index("head")
-        pairs = [
-            (mix, weight_ref.at[pl.ds(pl.multiple_of((head ^ other) * height, height), height)])
-            for other, mix in enumerate(mixes)
-        ]
-        pairs.extend(zip(others, targets))
-    else:
-        out_ref, *scratch = refs
-    top_ref, total_ref, numer_ref, tops_ref, sems = scratch
-    groups, _, inner = back_ref.shape
+def merge_kernel(capacity, steps, part, heads, table_ref, back_ref, log_hbm, average_hbm, *refs):
+    top_ref, total_ref, numer_ref, tops_ref, sems, load_sems = refs[-6:]
+    count = load_sems.shape[0]
+    sources, (out_ref, *targets) = refs[:count], refs[count:-6]
+    groups = back_ref.shape[0]
+    inner = heads * 64
     rows = steps * BEAMS
     span = PARTS * rows
-    heads = inner // 64
     state = (top_ref, total_ref, numer_ref)
     copies = start_all([(log_hbm.at[part], top_ref), (average_hbm.at[part], numer_ref)], sems)
-    if part == PARTS - 1:
-        loads = start_all(pairs, load_sems)
+    pairs = []
+    if part == 0:
+        weight_ref, *targets = targets
+        height = sources[0].shape[0]
+        head = lax.axis_index("head")
+        for other in range(4):
+            place = pl.ds(pl.multiple_of((head ^ other) * height, height), height)
+            pairs.append((sources[other], weight_ref.at[place]))
+        sources = sources[4:]
+    pairs.extend(zip(sources, targets))
+    loads = start_all(pairs, load_sems)
     total_ref[...] = jnp.ones_like(total_ref)
-    first = capacity * span
+    slot_rows = (inner // 128) * span
+    first = capacity * slot_rows
     tails = jnp.concatenate(
-        [
-            back_ref[owner, first : first + TAIL_ROWS, part * 128 : part * 128 + 128]
-            for owner in range(groups)
-        ],
-        axis=0,
+        [back_ref[owner, first : first + rows, :] for owner in range(groups)], axis=0
     )
     source, target = sublanes((128, inner)), lanes((128, inner)) // 64
     for rank in range(capacity):
         hit = source < 0
         for piece in range(3):
-            hit = hit | (source == target + (rank * 3 + piece) * heads)
+            hit = hit | (source == target + part * 64 + (rank * 3 + piece) * heads)
         tops_ref[:, rank * inner : rank * inner + inner] = dot(tails, hit.astype(f32).astype(bf16))
     for copy in copies:
         copy.wait()
@@ -569,8 +560,10 @@
             local = table_ref[owner * capacity + rank]
             bias = jnp.where(local >= 0, 0.0, masked_score)
             top = tops_ref[owner * rows : owner * rows + rows, rank * inner : rank * inner + inner]
-            start = rank * span + part * rows
-            average = back_ref[owner, start : start + rows, :].astype(f32)
+            starts = [rank * slot_rows + pair * span + part * rows for pair in range(inner // 128)]
+            average = jnp.concatenate(
+                [back_ref[owner, start : start + rows, :].astype(f32) for start in starts], axis=1
+            )
             here = pl.ds(pl.multiple_of(jnp.maximum(local, 0) * rows, rows), rows)
             absorb(state, here, slice(None), top + bias, 1.0, average)
     for index in range(top_ref.shape[0] // (2 * rows)):
@@ -586,25 +579,28 @@
         copy.wait()
 
 
-def merge(part, table, back, logs, averages, steps, capacity, mixes=(), others=()):
+def merge(part, table, back, logs, averages, steps, capacity, sources):
     _, requests, span, inner = logs.shape
     rows = requests * span
     logs, averages = (x.reshape(PARTS, rows, inner) for x in (logs, averages))
     vmem = pl.BlockSpec(memory_space=pltpu.VMEM)
     hbm = pl.BlockSpec(memory_space=pltpu.HBM)
-    loads = [*mixes, *others]
+    anywhere = pl.BlockSpec(memory_space=pl.ANY)
+    mixes = sources[:4] if part == 0 else []
+    others = sources[len(mixes) :]
     kept = [jax.ShapeDtypeStruct(x.shape, x.dtype) for x in others]
     if mixes:
         kept = [jax.ShapeDtypeStruct((4 * inner, mixes[0].shape[1]), bf16)] + kept
     return pl.pallas_call(
-        functools.partial(merge_kernel, capacity, steps, part),
-        in_specs=[SMEM, vmem, hbm, hbm]
-        + [pl.BlockSpec(memory_space=pl.ANY)] * len(mixes)
-        + [hbm] * len(others),
+        functools.partial(merge_kernel, capacity, steps, part, inner // 64),
+        in_specs=[SMEM, vmem, hbm, hbm] + [anywhere] * len(mixes) + [hbm] * len(others),
         out_shape=[jax.ShapeDtypeStruct((rows, inner), bf16)] + kept,
         scratch_shapes=[pltpu.VMEM((rows, inner), f32)] * 3
-        + [pltpu.VMEM((back.shape[0] * span, capacity * inner), f32), pltpu.SemaphoreType.DMA((2,))]
-        + [pltpu.SemaphoreType.DMA((len(loads),))] * bool(loads),
+        + [
+            pltpu.VMEM((back.shape[0] * span, capacity * inner), f32),
+            pltpu.SemaphoreType.DMA((2,)),
+            pltpu.SemaphoreType.DMA((len(sources),)),
+        ],
         compiler_params=pltpu.CompilerParams(vmem_limit_bytes=10 * MIB),
         cost_estimate=pl.CostEstimate(
             flops=40 * rows * inner, bytes_accessed=8 * MIB, transcendentals=4 * rows * inner
@@ -614,9 +610,9 @@
 
 
 def block_kernel(
-    first, att0, att1, att2, att3, weight_ref, tokens_hbm, gain_ref, gate_ref, up_ref, down_ref,
+    first, att0, att1, att2, att3, weight_ref, tokens_ref, gain_ref, gate_ref, up_ref, down_ref,
     residual_out, mine_ref, other_ref,
-    residual_ref, tokens_ref, attended_ref, normed_ref, hidden_ref, sums_ref, sems,
+    residual_ref, attended_ref, scaled_ref, hidden_ref, sums_ref,
 ):
     rows, width = residual_ref.shape
     inner = att0.shape[1]
@@ -625,34 +621,27 @@
     core = lax.rem(head, 2)
     near = pl.ds(pl.multiple_of(core * half, half), half)
     away = pl.ds(pl.multiple_of((1 - core) * half, half), half)
-    copies = start_all([(tokens_hbm.at[first : first + rows], tokens_ref)], sems)
     for other, att in enumerate((att0, att1, att2, att3)):
         place = pl.ds(pl.multiple_of((head ^ other) * inner, inner), inner)
         attended_ref[:, place] = att[...]
+    gain = gain_ref[...].reshape(1, -1)
+    squares = jnp.zeros((rows, 1), f32)
     for start in range(0, width, 512):
         cols = slice(start, start + 512)
-        residual_ref[:, cols] = dot(attended_ref[...], weight_ref[:, cols])
-    copies[0].wait()
-    gain = gain_ref[...].reshape(1, -1)
-
-    def norm(index, carry):
-        here = pl.ds(pl.multiple_of(index * 32, 32), 32)
-        x = tokens_ref[here, :].astype(f32) + residual_ref[here, :]
-        residual_ref[here, :] = x
-        scale = lax.rsqrt(jnp.mean(x * x, axis=-1, keepdims=True) + epsilon)
-        normed_ref[here, :] = (x * scale * gain).astype(bf16)
-        return carry
-
-    lax.fori_loop(0, rows // 32, norm, 0, unroll=2)
+        x = tokens_ref[first : first + rows, cols].astype(f32) + dot(attended_ref[...], weight_ref[:, cols])
+        residual_ref[:, cols] = x
+        scaled_ref[:, cols] = (x * gain[:, cols]).astype(bf16)
+        squares = squares + jnp.sum(x * x, axis=-1, keepdims=True)
+    scale = lax.rsqrt(squares / width + epsilon)
     for start in range(0, gate_ref.shape[1], 256):
         cols = slice(start, start + 256)
-        gate = dot(normed_ref[...], gate_ref[:, cols])
-        up = dot(normed_ref[...], up_ref[:, cols])
+        gate = dot(scaled_ref[...], gate_ref[:, cols]) * scale
+        up = dot(scaled_ref[...], up_ref[:, cols]) * scale
         hidden_ref[:, cols] = (gate / (1.0 + jnp.exp(-gate)) * up).astype(bf16)
+    residual_out[...] = residual_ref[near, :]
     for start in range(0, width, 512):
         cols = slice(start, start + 512)
         sums_ref[:, cols] = dot(hidden_ref[...], down_ref[:, cols])
-    residual_out[...] = residual_ref[near, :]
     mine_ref[...] = sums_ref[near, :]
     other_ref[...] = sums_ref[away, :].astype(bf16)
 
@@ -662,21 +651,18 @@
     width = tokens.shape[1]
     hidden = w_gate.shape[1]
     vmem = pl.BlockSpec(memory_space=pltpu.VMEM)
-    hbm = pl.BlockSpec(memory_space=pltpu.HBM)
     half = jax.ShapeDtypeStruct((rows // 2, width), f32)
     return pl.pallas_call(
         functools.partial(block_kernel, first),
-        in_specs=[vmem] * 5 + [hbm] + [vmem] * 4,
+        in_specs=[vmem] * 10,
         out_specs=[vmem] * 3,
         out_shape=[half, half, jax.ShapeDtypeStruct((rows // 2, width), bf16)],
         scratch_shapes=[
             pltpu.VMEM((rows, width), f32),
-            pltpu.VMEM((rows, width), bf16),
             pltpu.VMEM((rows, 4 * inner), bf16),
             pltpu.VMEM((rows, width), bf16),
             pltpu.VMEM((rows, hidden), bf16),
             pltpu.VMEM((rows, width), f32),
-            pltpu.SemaphoreType.DMA((1,)),
         ],
         compiler_params=pltpu.CompilerParams(vmem_limit_bytes=20 * MIB),
         cost_estimate=pl.CostEstimate(
@@ -684,7 +670,7 @@
             transcendentals=rows * hidden,
         ),
         name="block",
-    )(*attended, weight, in_hbm(tokens), gain, w_gate, w_up, w_down)
+    )(*attended, weight, tokens, gain, w_gate, w_up, w_down)
 
 
 def finish_kernel(*refs):
@@ -755,11 +741,12 @@
 
     flat = tokens.reshape(steps * rows, width)
     each = steps // PARTS
-    heres = list(merge(0, table, back, logs, averages, each, capacity))
+    sums = (table, back, logs, averages, each, capacity)
+    here, weight = merge(0, *sums, mixes)
+    heres = [here]
     back, heres[0] = lax.optimization_barrier((back, heres[0]))
-    here, *weights = merge(
-        1, table, back, logs, averages, each, capacity, mixes, [w_gate, w_up, w_down]
-    )
+    sums = (table, back, logs, averages, each, capacity)
+    here, w_gate, w_up, w_down, flat = merge(1, *sums, [w_gate, w_up, w_down, flat])
     heres.append(here)
     fars = [swap_chip(here) for here in heres]
     fars[0], heres[1] = lax.optimization_barrier((fars[0], heres[1]))
@@ -769,9 +756,8 @@
         gathered = [here, swap_core(here), far, swap_core(far)]
         if index:
             gathered, chip[0] = lax.optimization_barrier((gathered, chip[0]))
-        return block(
-            index * here.shape[0], gathered, weights[0], flat, gain_ffn, *weights[1:]
-        )
+        first = index * here.shape[0]
+        return block(first, gathered, weight, flat, gain_ffn, w_gate, w_up, w_down)
 
     def chip_sum(mine, other):
         return (mine + swap_core(other).astype(f32)).astype(bf16)
@@ -780,13 +766,12 @@
     residual[0], mine, other = block_of(0)
     other, fars[1] = lax.optimization_barrier((other, fars[1]))
     chip[0] = chip_sum(mine, other)
-    most = chip[0].shape[0] // 4 * 3
+    most = chip[0].shape[0] // 8 * 5
     chip_most, chip_rest = chip[0][:most], chip[0][most:]
     far_most, far_rest = swap_chip(chip_most), swap_chip(chip_rest)
     residual[1], mine, other = block_of(1)
     other, far_most = lax.optimization_barrier((other, far_most))
     chip[1] = chip_sum(mine, other)
-    chip[1], far_rest = lax.optimization_barrier((chip[1], far_rest))
     far_chip = [jnp.concatenate([far_most, far_rest], axis=0), swap_chip(chip[1])]
     parts = []
     for index in range(PARTS):

time: 111 us -> 122 us (1.099)
  waiting for transfers between devices: 34.3 us -> 51.1 us
  Pallas kernels: 47.2 us -> 43.8 us
  local copies, waits for them, and re-layouts: 4.11 us -> 2.06 us
    ppermute x6, waiting for transfers between devices: 14.6 us -> 36.4 us  [swap_chip(): return lax.ppermute(value, 'head', [(i, i ^ 2) for i in range(4)])]
    all_to_all x3, waiting for transfers between devices: 16 us -> 10.3 us  [exchange(): lax.all_to_all(value, 'group', split_axis=0, concat_axis=0, tiled=True)]
    pallas_call x2, Pallas kernels: 11.8 us -> 8.71 us  [block(): pl.pallas_call(functools.partial(block_kernel, first), in_specs=[vmem] *...]
    unnamed x24 -> x16, local copies, waits for them, and re-layouts: 2.76 us -> 0.72 us
  transfers between devices with their start and end apart: 19 -> 19, of which waited for: 11 -> 13; matrix products, arithmetic and copies ran while one was open for 0% -> 0% of each run, Pallas kernels for 38% -> 31%
where the time goes in v7:
time: 122 us
  waiting for transfers between devices  51.1 us (42%)
  Pallas kernels  43.8 us (36%)
  starting transfers between devices  24.5 us (20%)
  local copies, waits for them, and re-layouts  2.06 us (2%)
    ppermute x6, waiting for transfers between devices, swap_chip(): return lax.ppermute(value, 'head', [(i, i ^ 2) for i in range(4)])  36.4 us
    all_to_all x3, starting transfers between devices, exchange(): lax.all_to_all(value, 'group', split_axis=0, concat_axis=0, tiled=True)  16.2 us
    all_to_all x3, waiting for transfers between devices, exchange(): lax.all_to_all(value, 'group', split_axis=0, concat_axis=0, tiled=True)  10.3 us
    pallas_call x1, Pallas kernels, fresh(): pl.pallas_call(fresh_kernel, in_specs=[vmem, vmem] + [hbm] * len(big), ou...  8.9 us
    pallas_call x2, Pallas kernels, block(): pl.pallas_call(functools.partial(block_kernel, first), in_specs=[vmem] *...  8.71 us
    pallas_call x2, Pallas kernels, merge(): pl.pallas_call(functools.partial(merge_kernel, capacity, steps, part, inn...  7.8 us
    ppermute x6, starting transfers between devices, swap_chip(): return lax.ppermute(value, 'head', [(i, i ^ 2) for i in range(4)])  7.05 us
    pallas_call x1, Pallas kernels, own_pages(): pl.pallas_call(own_kernel, grid=(OWNED_SLOTS // PAGE_BLOCK,), in_specs=[S...  6.91 us
  transfers between devices with their start and end apart: 19, of which 13 were waited for; matrix products, arithmetic and copies ran while one was open for 0% of the time, Pallas kernels for 31%

profile of v7, /device:TPU:0, one launch (start us, length us, event | category | flops | bytes accessed | tf_op | source)
XLA Modules:
  0.0 122.1 jit_solution(3739733523371973990)
XLA Ops:
  0.0 1.3 %broadcast_in_dim.3 = s32[8,1,48]{2,1,0:T(1,128)} broadcast(s32[48]{0:T(128)} %request_ref.5), dimensions={2} | broadcast | bytes 1728 | tf_op jit(solution)/shard_map/broadcast_in_dim | solution.py:725
  1.3 7.3 %all-to-all-start = ((s32[8,1,48]{2,1,0:T(1,128)}), s32[8,1,48]{2,1,0:T(1,128)S(1)}, u32[]{:S(2)}, u32[]{:S(2)}) async-start(s32[8,1,48]{2,1,0:T(1,128)} %broadcast_in_dim.3), calls=%async_computation | async-start | bytes 8192 | tf_op jit(solution)/shard_map/all_to_all | solution.py:723
  8.6 0.7 copy-done.3
  9.3 3.8 %queries.1 = (bf16[512,384]{1,0:T(8,128)(2,1)S(1)}, bf16[512,384]{1,0:T(8,128)(2,1)}, bf16[512,1536]{1,0:T(8,128)(2,1)}) custom-call(bf16[4,128,1536]{2,1,0:T(8,128)(2,1)} %tokens_hbm.1, f32[1536]{0:T(1024)S(1)} %copy-done.3, bf16[384,1536]{1,0:T(8,128)(2,1)} %wq_hbm.1), custom_call_target="tpu_custom_call" | custom-call | flops 603979776 | bytes 6291456 | tf_op jit(solution)/shard_map/queries/pallas_call | solution.py:124
  13.1 2.0 %all-to-all-done.ids_ref = s32[8,1,48]{2,1,0:T(1,128)S(1)} async-done(((s32[8,1,48]{2,1,0:T(1,128)}), s32[8,1,48]{2,1,0:T(1,128)S(1)}, u32[]{:S(2)}, u32[]{:S(2)}) %all-to-all-start) | async-done | bytes 1568 | tf_op jit(solution)/shard_map/all_to_all | solution.py:723
  15.1 2.0 %ask.1 = (s32[24]{0:T(128)S(1)}, bf16[24,32,384]{2,1,0:T(8,128)(2,1)}) custom-call(s32[48]{0:T(128)S(1)} %copy-done.4, s32[8,1,48]{2,1,0:T(1,128)S(1)} %all-to-all-done.ids_ref, bf16[512,384]{1,0:T(8,128)(2,1)S(1)} %get-tuple-element.54.q_ref), custom_call_target="tpu_custom_call" | custom-call | tf_op jit(solution)/shard_map/ask/pallas_call | solution.py:161
  17.0 1.6 %collective-permute-start.1 = (bf16[384,1536]{1,0:T(8,128)(2,1)S(1)}, bf16[384,1536]{1,0:T(8,128)(2,1)S(1)}, u32[]{:S(2)}, u32[]{:S(2)}) collective-permute-start(bf16[384,1536]{1,0:T(8,128)(2,1)S(1)} %copy-done), channel_id=1, source_target_pairs={{0,2},{1,3},{2,0},{3,1},{4,6},{5,7},{6,4},{7,5},{8,10},{9,11},{10,... | collective-permute-start | bytes 3538952 | tf_op jit(solution)/shard_map/ppermute | solution.py:706
  18.6 4.0 %all-to-all-start.1 = ((bf16[8,96,384]{2,1,0:T(8,128)(2,1)}), bf16[8,96,384]{2,1,0:T(8,128)(2,1)S(1)}, u32[]{:S(2)}, u32[]{:S(2)}) async-start(bf16[8,96,384]{2,1,0:T(8,128)(2,1)} %bitcast), calls=%async_computation.1 | async-start | bytes 1179648 | tf_op jit(solution)/shard_map/all_to_all | solution.py:723
  22.6 20.7 %collective-permute-done.1.refs_2_ = bf16[384,1536]{1,0:T(8,128)(2,1)S(1)} collective-permute-done((bf16[384,1536]{1,0:T(8,128)(2,1)S(1)}, bf16[384,1536]{1,0:T(8,128)(2,1)S(1)}, u32[]{:S(2)}, u32[]{:S(2)}) %collective-permute-start.1) | collective-permute-done | bytes 1179680 | tf_op jit(solution)/shard_map/ppermute | solution.py:706
  43.4 6.9 %own_pages.1 = (f32[512,384]{1,0:T(8,128)}, f32[512,384]{1,0:T(8,128)}, f32[512,384]{1,0:T(8,128)}) custom-call(s32[48]{0:T(128)S(1)} %copy-done.4, s32[48]{0:T(128)S(1)} %copy-done.6, bf16[512,384]{1,0:T(8,128)(2,1)} %get-tuple-element.57.q_ref.q_hbm, bf16[48,384,128]{2,1,0:T(8,128)(2,1)} %keys_ref.3, bf16[48,384,128]{2,1,0:T(8,128)(2,1)} %values_ref.3, ...), custom_call_target="tpu_custom_call" | custom-call | flops 805306368 | bytes 6291456 | tf_op jit(solution)/shard_map/own_pages/pallas_call | solution.py:441
  50.3 4.5 %hosted_pages.1 = bf16[8,304,128]{2,1,0:T(8,128)(2,1)} custom-call(s32[48]{0:T(128)S(1)} %copy-done.4, s32[48]{0:T(128)S(1)} %copy-done.6, bf16[24,32,384]{2,1,0:T(8,128)(2,1)S(1)} %bitcast.9, bf16[48,384,128]{2,1,0:T(8,128)(2,1)} %keys_ref.3, bf16[48,384,128]{2,1,0:T(8,128)(2,1)} %values_ref.3, bf16[6,48,128]{2,1,0:T(8,128)(2,1)S(1)} %bitcast.11), custom_call_target="tpu_custom_call" | custom-call | flops 402653184 | bytes 3145728 | tf_op jit(solution)/shard_map/hosted_pages/pallas_call | solution.py:507
  54.8 4.9 %all-to-all-start.2 = ((bf16[8,304,128]{2,1,0:T(8,128)(2,1)}), bf16[8,304,128]{2,1,0:T(8,128)(2,1)S(1)}, u32[]{:S(2)}, u32[]{:S(2)}) async-start(bf16[8,304,128]{2,1,0:T(8,128)(2,1)} %hosted_pages.1), calls=%async_computation.2 | async-start | bytes 1245184 | tf_op jit(solution)/shard_map/all_to_all | solution.py:723
  59.8 8.9 %fresh.1 = (f32[2,16,16,384]{3,2,1,0:T(8,128)}, f32[2,16,16,384]{3,2,1,0:T(8,128)}) custom-call(s32[3,128]{1,0:T(4,128)S(1)} %copy-done.5, f32[1,6]{1,0:T(1,128)S(1)} %bitcast.12, bf16[512,1536]{1,0:T(8,128)(2,1)} %get-tuple-element.65.normed_hbm, bf16[384,1536]{1,0:T(8,128)(2,1)} %wk_hbm.1, bf16[384,1536]{1,0:T(8,128)(2,1)} %wv_hbm.1, ...), custom_call_target="tpu_custom_call" | custom-call | flops 1207959552 | bytes 12582912 | tf_op jit(solution)/shard_map/fresh/pallas_call | solution.py:326
  68.7 8.3 %all-to-all-done.2.back_ref = bf16[8,304,128]{2,1,0:T(8,128)(2,1)S(1)} async-done(((bf16[8,304,128]{2,1,0:T(8,128)(2,1)}), bf16[8,304,128]{2,1,0:T(8,128)(2,1)S(1)}, u32[]{:S(2)}, u32[]{:S(2)}) %all-to-all-start.2) | async-done | bytes 622624 | tf_op jit(solution)/shard_map/all_to_all | solution.py:723
  77.0 2.8 %merge.2 = (bf16[256,384]{1,0:T(8,128)(2,1)S(1)}, bf16[1536,1536]{1,0:T(8,128)(2,1)S(1)}) custom-call(s32[24]{0:T(128)S(1)} %get-tuple-element.64.table_ref, bf16[8,304,128]{2,1,0:T(8,128)(2,1)S(1)} %all-to-all-done.2.back_ref, f32[2,256,384]{2,1,0:T(8,128)} %bitcast.14, f32[2,256,384]{2,1,0:T(8,128)} %bitcast.16, bf16[384,1536]{1,0:T(8,128)(2,1)S(1)} %copy-done, ...), custom_call_target="tpu_custom_call" | custom-call | flops 3932160 | bytes 8388608 | tf_op jit(solution)/shard_map/merge/pallas_call | solution.py:594
  79.8 1.6 %collective-permute-start.4 = (bf16[256,384]{1,0:T(8,128)(2,1)S(1)}, bf16[256,384]{1,0:T(8,128)(2,1)S(1)}, u32[]{:S(2)}, u32[]{:S(2)}) collective-permute-start(bf16[256,384]{1,0:T(8,128)(2,1)S(1)} %get-tuple-element.78.att0), channel_id=1, source_target_pairs={{0,2},{1,3},{2,0},{3,1},{4,6},{5,7},{6,4},{7,5},{8,10},{9,11},{10,... | collective-permute-start | bytes 589832 | tf_op jit(solution)/shard_map/ppermute | solution.py:706
  81.4 5.0 %merge.3 = (bf16[256,384]{1,0:T(8,128)(2,1)S(1)}, bf16[1536,1024]{1,0:T(8,128)(2,1)S(1)}, bf16[1536,1024]{1,0:T(8,128)(2,1)S(1)}, bf16[1024,1536]{1,0:T(8,128)(2,1)S(1)}, bf16[512,1536]{1,0:T(8,128)(2,1)S(1)}) custom-call(s32[24]{0:T(128)S(1)} %get-tuple-element.64.table_ref, bf16[8,304,128]{2,1,0:T(8,128)(2,1)S(1)} %all-to-all-done.2.back_ref, ...), custom_call_target="tpu_custom_call" | custom-call | flops 3932160 | bytes 8388608 | tf_op jit(solution)/shard_map/merge/pallas_call | solution.py:594
  86.4 0.6 collective-permute-start.5
  87.0 0.6 collective-permute-start.7
  88.0 4.4 %block.2 = (f32[128,1536]{1,0:T(8,128)S(1)}, f32[128,1536]{1,0:T(8,128)S(1)}, bf16[128,1536]{1,0:T(8,128)(2,1)S(1)}) custom-call(bf16[256,384]{1,0:T(8,128)(2,1)S(1)} %get-tuple-element.78.att0, bf16[256,384]{1,0:T(8,128)(2,1)S(1)} %collective-permute-done.3.att1, bf16[256,384]{1,0:T(8,128)(2,1)S(1)} %collective-permute-done.4.att2, ...), custom_call_target="tpu_custom_call" | custom-call | flops 3623878656 | bytes 16777216 | tf_op jit(solution)/shard_map/block/pallas_call | solution.py:655
  92.4 1.4 %collective-permute-done.7.att2 = bf16[256,384]{1,0:T(8,128)(2,1)S(1)} collective-permute-done((bf16[256,384]{1,0:T(8,128)(2,1)S(1)}, bf16[256,384]{1,0:T(8,128)(2,1)S(1)}, u32[]{:S(2)}, u32[]{:S(2)}) %collective-permute-start.7) | collective-permute-done | bytes 196640 | tf_op jit(solution)/shard_map/ppermute | solution.py:706
  94.4 1.2 collective-permute-done.9
  96.1 1.1 collective-permute-start.10
  97.2 4.4 %block.3 = (f32[128,1536]{1,0:T(8,128)S(1)}, f32[128,1536]{1,0:T(8,128)S(1)}, bf16[128,1536]{1,0:T(8,128)(2,1)S(1)}) custom-call(bf16[256,384]{1,0:T(8,128)(2,1)S(1)} %get-tuple-element.94.att0, bf16[256,384]{1,0:T(8,128)(2,1)S(1)} %collective-permute-done.6.att1, bf16[256,384]{1,0:T(8,128)(2,1)S(1)} %collective-permute-done.7.att2, ...), custom_call_target="tpu_custom_call" | custom-call | flops 3623878656 | bytes 16777216 | tf_op jit(solution)/shard_map/block/pallas_call | solution.py:655
  101.6 2.6 %collective-permute-done.10 = bf16[80,1536]{1,0:T(8,128)(2,1)S(1)} collective-permute-done((bf16[80,1536]{1,0:T(8,128)(2,1)S(1)}, bf16[80,1536]{1,0:T(8,128)(2,1)S(1)}, u32[]{:S(2)}, u32[]{:S(2)}) %collective-permute-start.10) | collective-permute-done | bytes 245792 | tf_op jit(solution)/shard_map/ppermute | solution.py:706
  104.2 1.1 collective-permute-start.11
  105.3 0.6 collective-permute-done.13
  105.9 1.1 collective-permute-start.14
  107.1 3.8 %collective-permute-done.11 = bf16[48,1536]{1,0:T(8,128)(2,1)S(1)} collective-permute-done((bf16[48,1536]{1,0:T(8,128)(2,1)S(1)}, bf16[48,1536]{1,0:T(8,128)(2,1)S(1)}, u32[]{:S(2)}, u32[]{:S(2)}) %collective-permute-start.11) | collective-permute-done | bytes 147488 | tf_op jit(solution)/shard_map/ppermute | solution.py:706
  111.1 7.8 %collective-permute-done.14 = bf16[128,1536]{1,0:T(8,128)(2,1)S(1)} collective-permute-done((bf16[128,1536]{1,0:T(8,128)(2,1)S(1)}, bf16[128,1536]{1,0:T(8,128)(2,1)S(1)}, u32[]{:S(2)}, u32[]{:S(2)}) %collective-permute-start.14) | collective-permute-done | bytes 393248 | tf_op jit(solution)/shard_map/ppermute | solution.py:706
  119.1 1.7 %collective-permute-done.15.refs_3_ = bf16[128,1536]{1,0:T(8,128)(2,1)S(1)} collective-permute-done((bf16[128,1536]{1,0:T(8,128)(2,1)S(1)}, bf16[128,1536]{1,0:T(8,128)(2,1)S(1)}, u32[]{:S(2)}, u32[]{:S(2)}) %collective-permute-start.15) | collective-permute-done | bytes 393248 | tf_op jit(solution)/shard_map/ppermute | solution.py:702
  120.8 1.3 %finish.1 = bf16[512,1536]{1,0:T(8,128)(2,1)} custom-call(bf16[128,1536]{1,0:T(8,128)(2,1)S(1)} %add_convert_fusion.2.refs_0_, bf16[128,1536]{1,0:T(8,128)(2,1)S(1)} %collective-permute-done.12.refs_1_, bf16[128,1536]{1,0:T(8,128)(2,1)S(1)} %add_convert_fusion.refs_2_, bf16[128,1536]{1,0:T(8,128)(2,1)S(1)} %collective-permute-done.15.refs_3_), custom_call_target="tpu_custom_call" | custom-call | tf_op jit(solution)/shard_map/finish/pallas_call | solution.py:691
  (39 shorter events, 2.0 us)
Async XLA Ops:
  0.0 15.1 %copy-start.4 = (s32[48]{0:T(128)S(1)}, s32[48]{0:T(128)}, u32[]{:S(2)}) copy-start(s32[48]{0:T(128)} %request_ref.5) | copy-start | bytes 580
  1.3 13.7 %all-to-all-start = ((s32[8,1,48]{2,1,0:T(1,128)}), s32[8,1,48]{2,1,0:T(1,128)S(1)}, u32[]{:S(2)}, u32[]{:S(2)}) async-start(s32[8,1,48]{2,1,0:T(1,128)} %broadcast_in_dim.3), calls=%async_computation | async-start | bytes 8192 | tf_op jit(solution)/shard_map/all_to_all | solution.py:723
  8.6 0.7 copy-start.3
  9.3 7.7 %copy-start = (bf16[384,1536]{1,0:T(8,128)(2,1)S(1)}, bf16[384,1536]{1,0:T(8,128)(2,1)}, u32[]{:S(2)}) copy-start(bf16[384,1536]{1,0:T(8,128)(2,1)} %refs_0_.1) | copy-start | bytes 3538948
  9.3 34.1 %copy-start.1 = (bf16[48,6,128]{2,0,1:T(8,128)(2,1)S(1)}, bf16[48,6,128]{2,0,1:T(8,128)(2,1)}, u32[]{:S(2)}) copy-start(bf16[48,6,128]{2,0,1:T(8,128)(2,1)} %param.24) | copy-start | bytes 221188
  9.3 34.1 %copy-start.6 = (s32[48]{0:T(128)S(1)}, s32[48]{0:T(128)}, u32[]{:S(2)}) copy-start(s32[48]{0:T(128)} %fill_ref.3) | copy-start | bytes 580
  17.0 26.3 %collective-permute-start.1 = (bf16[384,1536]{1,0:T(8,128)(2,1)S(1)}, bf16[384,1536]{1,0:T(8,128)(2,1)S(1)}, u32[]{:S(2)}, u32[]{:S(2)}) collective-permute-start(bf16[384,1536]{1,0:T(8,128)(2,1)S(1)} %copy-done), channel_id=1, source_target_pairs={{0,2},{1,3},{2,0},{3,1},{4,6},{5,7},{6,4},{7,5},{8,10},{9,11},{10,... | collective-permute-start | bytes 3538952 | tf_op jit(solution)/shard_map/ppermute | solution.py:706
  18.6 31.7 %all-to-all-start.1 = ((bf16[8,96,384]{2,1,0:T(8,128)(2,1)}), bf16[8,96,384]{2,1,0:T(8,128)(2,1)S(1)}, u32[]{:S(2)}, u32[]{:S(2)}) async-start(bf16[8,96,384]{2,1,0:T(8,128)(2,1)} %bitcast), calls=%async_computation.1 | async-start | bytes 1179648 | tf_op jit(solution)/shard_map/all_to_all | solution.py:723
  22.6 46.0 %collective-permute-start = (bf16[384,1536]{1,0:T(8,128)(2,1)S(1)}, bf16[384,1536]{1,0:T(8,128)(2,1)}, u32[]{:S(2)}, u32[]{:S(2)}) collective-permute-start(bf16[384,1536]{1,0:T(8,128)(2,1)S(1)} %copy-done), channel_id=1, source_target_pairs={{0,1},{1,0},{2,3},{3,2},{4,5},{5,4},{6,7},{7,6},{8,9},{9,8},{10,11... | collective-permute-start | bytes 3538952 | tf_op jit(solution)/shard_map/ppermute | solution.py:702
  43.4 25.3 %collective-permute-start.2 = (bf16[384,1536]{1,0:T(8,128)(2,1)S(1)}, bf16[384,1536]{1,0:T(8,128)(2,1)}, u32[]{:S(2)}, u32[]{:S(2)}) collective-permute-start(bf16[384,1536]{1,0:T(8,128)(2,1)S(1)} %collective-permute-done.1.refs_2_), channel_id=1, source_target_pairs={{0,1},{1,0},{2,3},{3,2},{4,5},{5,4},{6,7},{7,6},{8,9},{9,8},{10,11... | collective-permute-start | bytes 3538952 | tf_op jit(solution)/shard_map/ppermute | solution.py:702
  50.3 9.5 %copy-start.5 = (s32[3,128]{1,0:T(4,128)S(1)}, s32[3,128]{1,0:T(4,128)}, u32[]{:S(2)}) copy-start(s32[3,128]{1,0:T(4,128)} %parents_ref.1) | copy-start | bytes 4612
  50.3 9.5 %copy-start.7 = (f32[6]{0:T(128)S(1)}, f32[6]{0:T(128)}, u32[]{:S(2)}) copy-start(f32[6]{0:T(128)} %param.30) | copy-start | bytes 76
  54.8 22.2 %all-to-all-start.2 = ((bf16[8,304,128]{2,1,0:T(8,128)(2,1)}), bf16[8,304,128]{2,1,0:T(8,128)(2,1)S(1)}, u32[]{:S(2)}, u32[]{:S(2)}) async-start(bf16[8,304,128]{2,1,0:T(8,128)(2,1)} %hosted_pages.1), calls=%async_computation.2 | async-start | bytes 1245184 | tf_op jit(solution)/shard_map/all_to_all | solution.py:723
  79.8 6.5 %collective-permute-start.4 = (bf16[256,384]{1,0:T(8,128)(2,1)S(1)}, bf16[256,384]{1,0:T(8,128)(2,1)S(1)}, u32[]{:S(2)}, u32[]{:S(2)}) collective-permute-start(bf16[256,384]{1,0:T(8,128)(2,1)S(1)} %get-tuple-element.78.att0), channel_id=1, source_target_pairs={{0,2},{1,3},{2,0},{3,1},{4,6},{5,7},{6,4},{7,5},{8,10},{9,11},{10,... | collective-permute-start | bytes 589832 | tf_op jit(solution)/shard_map/ppermute | solution.py:706
  81.4 6.2 %collective-permute-start.3 = (bf16[256,384]{1,0:T(8,128)(2,1)S(1)}, bf16[256,384]{1,0:T(8,128)(2,1)S(1)}, u32[]{:S(2)}, u32[]{:S(2)}) collective-permute-start(bf16[256,384]{1,0:T(8,128)(2,1)S(1)} %get-tuple-element.78.att0), channel_id=1, source_target_pairs={{0,1},{1,0},{2,3},{3,2},{4,5},{5,4},{6,7},{7,6},{8,9},{9,8},{10,11... | collective-permute-start | bytes 589832 | tf_op jit(solution)/shard_map/ppermute | solution.py:702
  81.4 6.6 %copy-start.2 = (f32[1536]{0:T(1024)S(1)}, f32[1536]{0:T(1024)}, u32[]{:S(2)}) copy-start(f32[1536]{0:T(1024)} %gain_ref.5) | copy-start | bytes 18436
  86.4 1.6 %collective-permute-start.5 = (bf16[256,384]{1,0:T(8,128)(2,1)S(1)}, bf16[256,384]{1,0:T(8,128)(2,1)S(1)}, u32[]{:S(2)}, u32[]{:S(2)}) collective-permute-start(bf16[256,384]{1,0:T(8,128)(2,1)S(1)} %collective-permute-done.4.att2), channel_id=1, source_target_pairs={{0,1},{1,0},{2,3},{3,2},{4,5},{5,4},{6,7},{7,6},{8,9},{9,8},{10,11... | collective-permute-start | bytes 589832 | tf_op jit(solution)/shard_map/ppermute | solution.py:702
  87.0 6.9 %collective-permute-start.7 = (bf16[256,384]{1,0:T(8,128)(2,1)S(1)}, bf16[256,384]{1,0:T(8,128)(2,1)S(1)}, u32[]{:S(2)}, u32[]{:S(2)}) collective-permute-start(bf16[256,384]{1,0:T(8,128)(2,1)S(1)} %get-tuple-element.94.att0), channel_id=1, source_target_pairs={{0,2},{1,3},{2,0},{3,1},{4,6},{5,7},{6,4},{7,5},{8,10},{9,11},{10,... | collective-permute-start | bytes 589832 | tf_op jit(solution)/shard_map/ppermute | solution.py:706
  93.9 1.7 %collective-permute-start.9 = (bf16[128,1536]{1,0:T(8,128)(2,1)S(1)}, bf16[128,1536]{1,0:T(8,128)(2,1)S(1)}, u32[]{:S(2)}, u32[]{:S(2)}) collective-permute-start(bf16[128,1536]{1,0:T(8,128)(2,1)S(1)} %get-tuple-element.92), channel_id=1, source_target_pairs={{0,1},{1,0},{2,3},{3,2},{4,5},{5,4},{6,7},{7,6},{8,9},{9,8},{10,11... | collective-permute-start | bytes 1179656 | tf_op jit(solution)/shard_map/ppermute | solution.py:702
  93.9 2.0 %collective-permute-start.6 = (bf16[256,384]{1,0:T(8,128)(2,1)S(1)}, bf16[256,384]{1,0:T(8,128)(2,1)S(1)}, u32[]{:S(2)}, u32[]{:S(2)}) collective-permute-start(bf16[256,384]{1,0:T(8,128)(2,1)S(1)} %get-tuple-element.94.att0), channel_id=1, source_target_pairs={{0,1},{1,0},{2,3},{3,2},{4,5},{5,4},{6,7},{7,6},{8,9},{9,8},{10,11... | collective-permute-start | bytes 589832 | tf_op jit(solution)/shard_map/ppermute | solution.py:702
  94.4 1.8 %collective-permute-start.8 = (bf16[256,384]{1,0:T(8,128)(2,1)S(1)}, bf16[256,384]{1,0:T(8,128)(2,1)S(1)}, u32[]{:S(2)}, u32[]{:S(2)}) collective-permute-start(bf16[256,384]{1,0:T(8,128)(2,1)S(1)} %collective-permute-done.7.att2), channel_id=1, source_target_pairs={{0,1},{1,0},{2,3},{3,2},{4,5},{5,4},{6,7},{7,6},{8,9},{9,8},{10,11... | collective-permute-start | bytes 589832 | tf_op jit(solution)/shard_map/ppermute | solution.py:702
  96.1 8.0 %collective-permute-start.10 = (bf16[80,1536]{1,0:T(8,128)(2,1)S(1)}, bf16[80,1536]{1,0:T(8,128)(2,1)S(1)}, u32[]{:S(2)}, u32[]{:S(2)}) collective-permute-start(bf16[80,1536]{1,0:T(8,128)(2,1)S(1)} %slice.8), channel_id=1, source_target_pairs={{0,2},{1,3},{2,0},{3,1},{4,6},{5,7},{6,4},{7,5},{8,10},{9,11},{10,... | collective-permute-start | bytes 737288 | tf_op jit(solution)/shard_map/ppermute | solution.py:706
  104.1 1.7 %collective-permute-start.13 = (bf16[128,1536]{1,0:T(8,128)(2,1)S(1)}, bf16[128,1536]{1,0:T(8,128)(2,1)S(1)}, u32[]{:S(2)}, u32[]{:S(2)}) collective-permute-start(bf16[128,1536]{1,0:T(8,128)(2,1)S(1)} %get-tuple-element.102), channel_id=1, source_target_pairs={{0,1},{1,0},{2,3},{3,2},{4,5},{5,4},{6,7},{7,6},{8,9},{9,8},{10,11... | collective-permute-start | bytes 1179656 | tf_op jit(solution)/shard_map/ppermute | solution.py:702
  104.2 6.7 %collective-permute-start.11 = (bf16[48,1536]{1,0:T(8,128)(2,1)S(1)}, bf16[48,1536]{1,0:T(8,128)(2,1)S(1)}, u32[]{:S(2)}, u32[]{:S(2)}) collective-permute-start(bf16[48,1536]{1,0:T(8,128)(2,1)S(1)} %slice.9), channel_id=1, source_target_pairs={{0,2},{1,3},{2,0},{3,1},{4,6},{5,7},{6,4},{7,5},{8,10},{9,11},{10,... | collective-permute-start | bytes 442376 | tf_op jit(solution)/shard_map/ppermute | solution.py:706
  105.9 13.0 %collective-permute-start.14 = (bf16[128,1536]{1,0:T(8,128)(2,1)S(1)}, bf16[128,1536]{1,0:T(8,128)(2,1)S(1)}, u32[]{:S(2)}, u32[]{:S(2)}) collective-permute-start(bf16[128,1536]{1,0:T(8,128)(2,1)S(1)} %add_convert_fusion.1), channel_id=1, source_target_pairs={{0,2},{1,3},{2,0},{3,1},{4,6},{5,7},{6,4},{7,5},{8,10},{9,11},{10,... | collective-permute-start | bytes 1179656 | tf_op jit(solution)/shard_map/ppermute | solution.py:706
  111.0 8.1 %collective-permute-start.12 = (bf16[128,1536]{1,0:T(8,128)(2,1)S(1)}, bf16[128,1536]{1,0:T(8,128)(2,1)S(1)}, u32[]{:S(2)}, u32[]{:S(2)}) collective-permute-start(bf16[128,1536]{1,0:T(8,128)(2,1)S(1)} %add_convert_fusion.2.refs_0_), channel_id=1, source_target_pairs={{0,1},{1,0},{2,3},{3,2},{4,5},{5,4},{6,7},{7,6},{8,9},{9,8},{10,11... | collective-permute-start | bytes 1179656 | tf_op jit(solution)/shard_map/ppermute | solution.py:702
  119.0 1.8 %collective-permute-start.15 = (bf16[128,1536]{1,0:T(8,128)(2,1)S(1)}, bf16[128,1536]{1,0:T(8,128)(2,1)S(1)}, u32[]{:S(2)}, u32[]{:S(2)}) collective-permute-start(bf16[128,1536]{1,0:T(8,128)(2,1)S(1)} %add_convert_fusion.refs_2_), channel_id=1, source_target_pairs={{0,1},{1,0},{2,3},{3,2},{4,5},{5,4},{6,7},{7,6},{8,9},{9,8},{10,11... | collective-permute-start | bytes 1179656 | tf_op jit(solution)/shard_map/ppermute | solution.py:702

commit v8 on v7

--- a/solution.py
+++ b/solution.py
@@ -733,7 +733,7 @@
     payload = hosted_pages(
         page_request, page_fill, asked_rows, keys_pool, values_pool, decay, groups, capacity, local_count
     )
-    payload, normed = lax.optimization_barrier((payload, normed))
+    payload, normed, w_out_far = lax.optimization_barrier((payload, normed, w_out_far))
     back = exchange(payload)
     logs, averages = fresh(parents, forget_bias, normed, w_key, w_value, w_forget, q, own)
     mixes = [w_out, swap_core(w_out), w_out_far, swap_core(w_out_far)]

time: 122 us -> 111 us (0.910)
  waiting for transfers between devices: 51.1 us -> 39.6 us
    ppermute x6, waiting for transfers between devices: 36.4 us -> 16.7 us  [swap_chip(): return lax.ppermute(value, 'head', [(i, i ^ 2) for i in range(4)])]
    all_to_all x3, waiting for transfers between devices: 10.3 us -> 18.5 us  [exchange(): lax.all_to_all(value, 'group', split_axis=0, concat_axis=0, tiled=True)]
  transfers between devices with their start and end apart: 19 -> 19, of which waited for: 13 -> 14; matrix products, arithmetic and copies ran while one was open for 0% -> 0% of each run, Pallas kernels for 31% -> 34%
where the time goes in v8:
time: 111 us
  Pallas kernels  43.9 us (40%)
  waiting for transfers between devices  39.6 us (36%)
  starting transfers between devices  24.6 us (22%)
  local copies, waits for them, and re-layouts  2.05 us (2%)
    all_to_all x3, waiting for transfers between devices, exchange(): lax.all_to_all(value, 'group', split_axis=0, concat_axis=0, tiled=True)  18.5 us
    ppermute x6, waiting for transfers between devices, swap_chip(): return lax.ppermute(value, 'head', [(i, i ^ 2) for i in range(4)])  16.7 us
    all_to_all x3, starting transfers between devices, exchange(): lax.all_to_all(value, 'group', split_axis=0, concat_axis=0, tiled=True)  16.2 us
    pallas_call x1, Pallas kernels, fresh(): pl.pallas_call(fresh_kernel, in_specs=[vmem, vmem] + [hbm] * len(big), ou...  8.96 us
    pallas_call x2, Pallas kernels, block(): pl.pallas_call(functools.partial(block_kernel, first), in_specs=[vmem] *...  8.71 us
    pallas_call x2, Pallas kernels, merge(): pl.pallas_call(functools.partial(merge_kernel, capacity, steps, part, inn...  7.8 us
    ppermute x6, starting transfers between devices, swap_chip(): return lax.ppermute(value, 'head', [(i, i ^ 2) for i in range(4)])  7.1 us
    pallas_call x1, Pallas kernels, own_pages(): pl.pallas_call(own_kernel, grid=(OWNED_SLOTS // PAGE_BLOCK,), in_specs=[S...  6.89 us
  transfers between devices with their start and end apart: 19, of which 14 were waited for; matrix products, arithmetic and copies ran while one was open for 0% of the time, Pallas kernels for 34%

profile of v8, /device:TPU:0, one launch (start us, length us, event | category | flops | bytes accessed | tf_op | source)
XLA Modules:
  0.0 110.7 jit_solution(18005013723763653432)
XLA Ops:
  0.0 1.3 %broadcast_in_dim.3 = s32[8,1,48]{2,1,0:T(1,128)} broadcast(s32[48]{0:T(128)} %request_ref.5), dimensions={2} | broadcast | bytes 1728 | tf_op jit(solution)/shard_map/broadcast_in_dim | solution.py:725
  1.3 7.3 %all-to-all-start = ((s32[8,1,48]{2,1,0:T(1,128)}), s32[8,1,48]{2,1,0:T(1,128)S(1)}, u32[]{:S(2)}, u32[]{:S(2)}) async-start(s32[8,1,48]{2,1,0:T(1,128)} %broadcast_in_dim.3), calls=%async_computation | async-start | bytes 8192 | tf_op jit(solution)/shard_map/all_to_all | solution.py:723
  8.6 0.7 copy-done.3
  9.3 3.8 %queries.1 = (bf16[512,384]{1,0:T(8,128)(2,1)S(1)}, bf16[512,384]{1,0:T(8,128)(2,1)}, bf16[512,1536]{1,0:T(8,128)(2,1)}) custom-call(bf16[4,128,1536]{2,1,0:T(8,128)(2,1)} %tokens_hbm.1, f32[1536]{0:T(1024)S(1)} %copy-done.3, bf16[384,1536]{1,0:T(8,128)(2,1)} %wq_hbm.1), custom_call_target="tpu_custom_call" | custom-call | flops 603979776 | bytes 6291456 | tf_op jit(solution)/shard_map/queries/pallas_call | solution.py:124
  13.1 2.0 %all-to-all-done.ids_ref = s32[8,1,48]{2,1,0:T(1,128)S(1)} async-done(((s32[8,1,48]{2,1,0:T(1,128)}), s32[8,1,48]{2,1,0:T(1,128)S(1)}, u32[]{:S(2)}, u32[]{:S(2)}) %all-to-all-start) | async-done | bytes 1568 | tf_op jit(solution)/shard_map/all_to_all | solution.py:723
  15.1 2.0 %ask.1 = (s32[24]{0:T(128)S(1)}, bf16[24,32,384]{2,1,0:T(8,128)(2,1)}) custom-call(s32[48]{0:T(128)S(1)} %copy-done.4, s32[8,1,48]{2,1,0:T(1,128)S(1)} %all-to-all-done.ids_ref, bf16[512,384]{1,0:T(8,128)(2,1)S(1)} %get-tuple-element.55.q_ref), custom_call_target="tpu_custom_call" | custom-call | tf_op jit(solution)/shard_map/ask/pallas_call | solution.py:161
  17.1 1.6 %collective-permute-start = (bf16[384,1536]{1,0:T(8,128)(2,1)S(1)}, bf16[384,1536]{1,0:T(8,128)(2,1)S(1)}, u32[]{:S(2)}, u32[]{:S(2)}) collective-permute-start(bf16[384,1536]{1,0:T(8,128)(2,1)S(1)} %copy-done), channel_id=1, source_target_pairs={{0,2},{1,3},{2,0},{3,1},{4,6},{5,7},{6,4},{7,5},{8,10},{9,11},{10,... | collective-permute-start | bytes 3538952 | tf_op jit(solution)/shard_map/ppermute | solution.py:706
  18.6 4.0 %all-to-all-start.1 = ((bf16[8,96,384]{2,1,0:T(8,128)(2,1)}), bf16[8,96,384]{2,1,0:T(8,128)(2,1)S(1)}, u32[]{:S(2)}, u32[]{:S(2)}) async-start(bf16[8,96,384]{2,1,0:T(8,128)(2,1)} %bitcast), calls=%async_computation.1 | async-start | bytes 1179648 | tf_op jit(solution)/shard_map/all_to_all | solution.py:723
  22.7 6.9 %own_pages.1 = (f32[512,384]{1,0:T(8,128)}, f32[512,384]{1,0:T(8,128)}, f32[512,384]{1,0:T(8,128)}) custom-call(s32[48]{0:T(128)S(1)} %copy-done.4, s32[48]{0:T(128)S(1)} %copy-done.6, bf16[512,384]{1,0:T(8,128)(2,1)} %get-tuple-element.58.q_ref.q_hbm, bf16[48,384,128]{2,1,0:T(8,128)(2,1)} %keys_ref.3, bf16[48,384,128]{2,1,0:T(8,128)(2,1)} %values_ref.3, ...), custom_call_target="tpu_custom_call" | custom-call | flops 805306368 | bytes 6291456 | tf_op jit(solution)/shard_map/own_pages/pallas_call | solution.py:441
  29.6 8.2 %all-to-all-done.1 = bf16[8,96,384]{2,1,0:T(8,128)(2,1)S(1)} async-done(((bf16[8,96,384]{2,1,0:T(8,128)(2,1)}), bf16[8,96,384]{2,1,0:T(8,128)(2,1)S(1)}, u32[]{:S(2)}, u32[]{:S(2)}) %all-to-all-start.1) | async-done | bytes 589856 | tf_op jit(solution)/shard_map/all_to_all | solution.py:723
  37.7 4.5 %hosted_pages.1 = bf16[8,304,128]{2,1,0:T(8,128)(2,1)} custom-call(s32[48]{0:T(128)S(1)} %copy-done.4, s32[48]{0:T(128)S(1)} %copy-done.6, bf16[24,32,384]{2,1,0:T(8,128)(2,1)S(1)} %bitcast.9, bf16[48,384,128]{2,1,0:T(8,128)(2,1)} %keys_ref.3, bf16[48,384,128]{2,1,0:T(8,128)(2,1)} %values_ref.3, bf16[6,48,128]{2,1,0:T(8,128)(2,1)S(1)} %bitcast.11), custom_call_target="tpu_custom_call" | custom-call | flops 402653184 | bytes 3145728 | tf_op jit(solution)/shard_map/hosted_pages/pallas_call | solution.py:507
  42.3 1.1 %collective-permute-done.refs_2_ = bf16[384,1536]{1,0:T(8,128)(2,1)S(1)} collective-permute-done((bf16[384,1536]{1,0:T(8,128)(2,1)S(1)}, bf16[384,1536]{1,0:T(8,128)(2,1)S(1)}, u32[]{:S(2)}, u32[]{:S(2)}) %collective-permute-start) | collective-permute-done | bytes 1179680 | tf_op jit(solution)/shard_map/ppermute | solution.py:706
  43.4 4.9 %all-to-all-start.2 = ((bf16[8,304,128]{2,1,0:T(8,128)(2,1)}), bf16[8,304,128]{2,1,0:T(8,128)(2,1)S(1)}, u32[]{:S(2)}, u32[]{:S(2)}) async-start(bf16[8,304,128]{2,1,0:T(8,128)(2,1)} %hosted_pages.1), calls=%async_computation.2 | async-start | bytes 1245184 | tf_op jit(solution)/shard_map/all_to_all | solution.py:723
  48.3 9.0 %fresh.1 = (f32[2,16,16,384]{3,2,1,0:T(8,128)}, f32[2,16,16,384]{3,2,1,0:T(8,128)}) custom-call(s32[3,128]{1,0:T(4,128)S(1)} %copy-done.5, f32[1,6]{1,0:T(1,128)S(1)} %bitcast.12, bf16[512,1536]{1,0:T(8,128)(2,1)} %get-tuple-element.67.normed_hbm, bf16[384,1536]{1,0:T(8,128)(2,1)} %wk_hbm.1, bf16[384,1536]{1,0:T(8,128)(2,1)} %wv_hbm.1, ...), custom_call_target="tpu_custom_call" | custom-call | flops 1207959552 | bytes 12582912 | tf_op jit(solution)/shard_map/fresh/pallas_call | solution.py:326
  57.3 8.3 %all-to-all-done.2.back_ref = bf16[8,304,128]{2,1,0:T(8,128)(2,1)S(1)} async-done(((bf16[8,304,128]{2,1,0:T(8,128)(2,1)}), bf16[8,304,128]{2,1,0:T(8,128)(2,1)S(1)}, u32[]{:S(2)}, u32[]{:S(2)}) %all-to-all-start.2) | async-done | bytes 622624 | tf_op jit(solution)/shard_map/all_to_all | solution.py:723
  65.6 2.8 %merge.2 = (bf16[256,384]{1,0:T(8,128)(2,1)S(1)}, bf16[1536,1536]{1,0:T(8,128)(2,1)S(1)}) custom-call(s32[24]{0:T(128)S(1)} %get-tuple-element.66.table_ref, bf16[8,304,128]{2,1,0:T(8,128)(2,1)S(1)} %all-to-all-done.2.back_ref, f32[2,256,384]{2,1,0:T(8,128)} %bitcast.14, f32[2,256,384]{2,1,0:T(8,128)} %bitcast.16, bf16[384,1536]{1,0:T(8,128)(2,1)S(1)} %copy-done, ...), custom_call_target="tpu_custom_call" | custom-call | flops 3932160 | bytes 8388608 | tf_op jit(solution)/shard_map/merge/pallas_call | solution.py:594
  68.4 1.6 %collective-permute-start.4 = (bf16[256,384]{1,0:T(8,128)(2,1)S(1)}, bf16[256,384]{1,0:T(8,128)(2,1)S(1)}, u32[]{:S(2)}, u32[]{:S(2)}) collective-permute-start(bf16[256,384]{1,0:T(8,128)(2,1)S(1)} %get-tuple-element.80.att0), channel_id=1, source_target_pairs={{0,2},{1,3},{2,0},{3,1},{4,6},{5,7},{6,4},{7,5},{8,10},{9,11},{10,... | collective-permute-start | bytes 589832 | tf_op jit(solution)/shard_map/ppermute | solution.py:706
  70.0 5.0 %merge.3 = (bf16[256,384]{1,0:T(8,128)(2,1)S(1)}, bf16[1536,1024]{1,0:T(8,128)(2,1)S(1)}, bf16[1536,1024]{1,0:T(8,128)(2,1)S(1)}, bf16[1024,1536]{1,0:T(8,128)(2,1)S(1)}, bf16[512,1536]{1,0:T(8,128)(2,1)S(1)}) custom-call(s32[24]{0:T(128)S(1)} %get-tuple-element.66.table_ref, bf16[8,304,128]{2,1,0:T(8,128)(2,1)S(1)} %all-to-all-done.2.back_ref, ...), custom_call_target="tpu_custom_call" | custom-call | flops 3932160 | bytes 8388608 | tf_op jit(solution)/shard_map/merge/pallas_call | solution.py:594
  75.0 0.6 collective-permute-start.5
  75.6 0.6 collective-permute-start.7
  76.6 4.4 %block.2 = (f32[128,1536]{1,0:T(8,128)S(1)}, f32[128,1536]{1,0:T(8,128)S(1)}, bf16[128,1536]{1,0:T(8,128)(2,1)S(1)}) custom-call(bf16[256,384]{1,0:T(8,128)(2,1)S(1)} %get-tuple-element.80.att0, bf16[256,384]{1,0:T(8,128)(2,1)S(1)} %collective-permute-done.3.att1, bf16[256,384]{1,0:T(8,128)(2,1)S(1)} %collective-permute-done.4.att2, ...), custom_call_target="tpu_custom_call" | custom-call | flops 3623878656 | bytes 16777216 | tf_op jit(solution)/shard_map/block/pallas_call | solution.py:655
  81.0 1.4 %collective-permute-done.7.att2 = bf16[256,384]{1,0:T(8,128)(2,1)S(1)} collective-permute-done((bf16[256,384]{1,0:T(8,128)(2,1)S(1)}, bf16[256,384]{1,0:T(8,128)(2,1)S(1)}, u32[]{:S(2)}, u32[]{:S(2)}) %collective-permute-start.7) | collective-permute-done | bytes 196640 | tf_op jit(solution)/shard_map/ppermute | solution.py:706
  83.0 1.2 %collective-permute-done.9 = bf16[128,1536]{1,0:T(8,128)(2,1)S(1)} collective-permute-done((bf16[128,1536]{1,0:T(8,128)(2,1)S(1)}, bf16[128,1536]{1,0:T(8,128)(2,1)S(1)}, u32[]{:S(2)}, u32[]{:S(2)}) %collective-permute-start.9) | collective-permute-done | bytes 393248 | tf_op jit(solution)/shard_map/ppermute | solution.py:702
  84.7 1.1 collective-permute-start.10
  85.8 4.4 %block.3 = (f32[128,1536]{1,0:T(8,128)S(1)}, f32[128,1536]{1,0:T(8,128)S(1)}, bf16[128,1536]{1,0:T(8,128)(2,1)S(1)}) custom-call(bf16[256,384]{1,0:T(8,128)(2,1)S(1)} %get-tuple-element.96.att0, bf16[256,384]{1,0:T(8,128)(2,1)S(1)} %collective-permute-done.6.att1, bf16[256,384]{1,0:T(8,128)(2,1)S(1)} %collective-permute-done.7.att2, ...), custom_call_target="tpu_custom_call" | custom-call | flops 3623878656 | bytes 16777216 | tf_op jit(solution)/shard_map/block/pallas_call | solution.py:655
  90.2 2.6 %collective-permute-done.10 = bf16[80,1536]{1,0:T(8,128)(2,1)S(1)} collective-permute-done((bf16[80,1536]{1,0:T(8,128)(2,1)S(1)}, bf16[80,1536]{1,0:T(8,128)(2,1)S(1)}, u32[]{:S(2)}, u32[]{:S(2)}) %collective-permute-start.10) | collective-permute-done | bytes 245792 | tf_op jit(solution)/shard_map/ppermute | solution.py:706
  92.8 1.1 %collective-permute-start.11 = (bf16[48,1536]{1,0:T(8,128)(2,1)S(1)}, bf16[48,1536]{1,0:T(8,128)(2,1)S(1)}, u32[]{:S(2)}, u32[]{:S(2)}) collective-permute-start(bf16[48,1536]{1,0:T(8,128)(2,1)S(1)} %slice.9), channel_id=1, source_target_pairs={{0,2},{1,3},{2,0},{3,1},{4,6},{5,7},{6,4},{7,5},{8,10},{9,11},{10,... | collective-permute-start | bytes 442376 | tf_op jit(solution)/shard_map/ppermute | solution.py:706
  94.5 1.1 %collective-permute-start.14 = (bf16[128,1536]{1,0:T(8,128)(2,1)S(1)}, bf16[128,1536]{1,0:T(8,128)(2,1)S(1)}, u32[]{:S(2)}, u32[]{:S(2)}) collective-permute-start(bf16[128,1536]{1,0:T(8,128)(2,1)S(1)} %add_convert_fusion.1), channel_id=1, source_target_pairs={{0,2},{1,3},{2,0},{3,1},{4,6},{5,7},{6,4},{7,5},{8,10},{9,11},{10,... | collective-permute-start | bytes 1179656 | tf_op jit(solution)/shard_map/ppermute | solution.py:706
  95.7 3.8 %collective-permute-done.11 = bf16[48,1536]{1,0:T(8,128)(2,1)S(1)} collective-permute-done((bf16[48,1536]{1,0:T(8,128)(2,1)S(1)}, bf16[48,1536]{1,0:T(8,128)(2,1)S(1)}, u32[]{:S(2)}, u32[]{:S(2)}) %collective-permute-start.11) | collective-permute-done | bytes 147488 | tf_op jit(solution)/shard_map/ppermute | solution.py:706
  99.7 7.8 %collective-permute-done.14 = bf16[128,1536]{1,0:T(8,128)(2,1)S(1)} collective-permute-done((bf16[128,1536]{1,0:T(8,128)(2,1)S(1)}, bf16[128,1536]{1,0:T(8,128)(2,1)S(1)}, u32[]{:S(2)}, u32[]{:S(2)}) %collective-permute-start.14) | collective-permute-done | bytes 393248 | tf_op jit(solution)/shard_map/ppermute | solution.py:706
  107.7 1.7 %collective-permute-done.15.refs_3_ = bf16[128,1536]{1,0:T(8,128)(2,1)S(1)} collective-permute-done((bf16[128,1536]{1,0:T(8,128)(2,1)S(1)}, bf16[128,1536]{1,0:T(8,128)(2,1)S(1)}, u32[]{:S(2)}, u32[]{:S(2)}) %collective-permute-start.15) | collective-permute-done | bytes 393248 | tf_op jit(solution)/shard_map/ppermute | solution.py:702
  109.4 1.3 %finish.1 = bf16[512,1536]{1,0:T(8,128)(2,1)} custom-call(bf16[128,1536]{1,0:T(8,128)(2,1)S(1)} %add_convert_fusion.2.refs_0_, bf16[128,1536]{1,0:T(8,128)(2,1)S(1)} %collective-permute-done.12.refs_1_, bf16[128,1536]{1,0:T(8,128)(2,1)S(1)} %add_convert_fusion.refs_2_, bf16[128,1536]{1,0:T(8,128)(2,1)S(1)} %collective-permute-done.15.refs_3_), custom_call_target="tpu_custom_call" | custom-call | tf_op jit(solution)/shard_map/finish/pallas_call | solution.py:691
  (39 shorter events, 2.6 us)
Async XLA Ops:
  0.0 15.1 %copy-start.4 = (s32[48]{0:T(128)S(1)}, s32[48]{0:T(128)}, u32[]{:S(2)}) copy-start(s32[48]{0:T(128)} %request_ref.5) | copy-start | bytes 580
  1.3 13.7 %all-to-all-start = ((s32[8,1,48]{2,1,0:T(1,128)}), s32[8,1,48]{2,1,0:T(1,128)S(1)}, u32[]{:S(2)}, u32[]{:S(2)}) async-start(s32[8,1,48]{2,1,0:T(1,128)} %broadcast_in_dim.3), calls=%async_computation | async-start | bytes 8192 | tf_op jit(solution)/shard_map/all_to_all | solution.py:723
  8.6 0.7 copy-start.3
  9.3 7.8 %copy-start = (bf16[384,1536]{1,0:T(8,128)(2,1)S(1)}, bf16[384,1536]{1,0:T(8,128)(2,1)}, u32[]{:S(2)}) copy-start(bf16[384,1536]{1,0:T(8,128)(2,1)} %refs_0_.1) | copy-start | bytes 3538948
  9.3 13.4 %copy-start.1 = (bf16[48,6,128]{2,0,1:T(8,128)(2,1)S(1)}, bf16[48,6,128]{2,0,1:T(8,128)(2,1)}, u32[]{:S(2)}) copy-start(bf16[48,6,128]{2,0,1:T(8,128)(2,1)} %param.24) | copy-start | bytes 221188
  9.3 13.4 %copy-start.6 = (s32[48]{0:T(128)S(1)}, s32[48]{0:T(128)}, u32[]{:S(2)}) copy-start(s32[48]{0:T(128)} %fill_ref.3) | copy-start | bytes 580
  17.1 26.3 %collective-permute-start = (bf16[384,1536]{1,0:T(8,128)(2,1)S(1)}, bf16[384,1536]{1,0:T(8,128)(2,1)S(1)}, u32[]{:S(2)}, u32[]{:S(2)}) collective-permute-start(bf16[384,1536]{1,0:T(8,128)(2,1)S(1)} %copy-done), channel_id=1, source_target_pairs={{0,2},{1,3},{2,0},{3,1},{4,6},{5,7},{6,4},{7,5},{8,10},{9,11},{10,... | collective-permute-start | bytes 3538952 | tf_op jit(solution)/shard_map/ppermute | solution.py:706
  18.6 19.1 %all-to-all-start.1 = ((bf16[8,96,384]{2,1,0:T(8,128)(2,1)}), bf16[8,96,384]{2,1,0:T(8,128)(2,1)S(1)}, u32[]{:S(2)}, u32[]{:S(2)}) async-start(bf16[8,96,384]{2,1,0:T(8,128)(2,1)} %bitcast), calls=%async_computation.1 | async-start | bytes 1179648 | tf_op jit(solution)/shard_map/all_to_all | solution.py:723
  29.5 27.7 %collective-permute-start.1 = (bf16[384,1536]{1,0:T(8,128)(2,1)S(1)}, bf16[384,1536]{1,0:T(8,128)(2,1)}, u32[]{:S(2)}, u32[]{:S(2)}) collective-permute-start(bf16[384,1536]{1,0:T(8,128)(2,1)S(1)} %copy-done), channel_id=1, source_target_pairs={{0,1},{1,0},{2,3},{3,2},{4,5},{5,4},{6,7},{7,6},{8,9},{9,8},{10,11... | collective-permute-start | bytes 3538952 | tf_op jit(solution)/shard_map/ppermute | solution.py:702
  37.7 10.6 %copy-start.5 = (s32[3,128]{1,0:T(4,128)S(1)}, s32[3,128]{1,0:T(4,128)}, u32[]{:S(2)}) copy-start(s32[3,128]{1,0:T(4,128)} %parents_ref.1) | copy-start | bytes 4612
  37.7 10.6 %copy-start.7 = (f32[6]{0:T(128)S(1)}, f32[6]{0:T(128)}, u32[]{:S(2)}) copy-start(f32[6]{0:T(128)} %param.30) | copy-start | bytes 76
  43.4 13.9 %collective-permute-start.2 = (bf16[384,1536]{1,0:T(8,128)(2,1)S(1)}, bf16[384,1536]{1,0:T(8,128)(2,1)}, u32[]{:S(2)}, u32[]{:S(2)}) collective-permute-start(bf16[384,1536]{1,0:T(8,128)(2,1)S(1)} %collective-permute-done.refs_2_), channel_id=1, source_target_pairs={{0,1},{1,0},{2,3},{3,2},{4,5},{5,4},{6,7},{7,6},{8,9},{9,8},{10,11... | collective-permute-start | bytes 3538952 | tf_op jit(solution)/shard_map/ppermute | solution.py:702
  43.4 22.2 %all-to-all-start.2 = ((bf16[8,304,128]{2,1,0:T(8,128)(2,1)}), bf16[8,304,128]{2,1,0:T(8,128)(2,1)S(1)}, u32[]{:S(2)}, u32[]{:S(2)}) async-start(bf16[8,304,128]{2,1,0:T(8,128)(2,1)} %hosted_pages.1), calls=%async_computation.2 | async-start | bytes 1245184 | tf_op jit(solution)/shard_map/all_to_all | solution.py:723
  68.4 6.6 %collective-permute-start.4 = (bf16[256,384]{1,0:T(8,128)(2,1)S(1)}, bf16[256,384]{1,0:T(8,128)(2,1)S(1)}, u32[]{:S(2)}, u32[]{:S(2)}) collective-permute-start(bf16[256,384]{1,0:T(8,128)(2,1)S(1)} %get-tuple-element.80.att0), channel_id=1, source_target_pairs={{0,2},{1,3},{2,0},{3,1},{4,6},{5,7},{6,4},{7,5},{8,10},{9,11},{10,... | collective-permute-start | bytes 589832 | tf_op jit(solution)/shard_map/ppermute | solution.py:706
  70.0 6.2 %collective-permute-start.3 = (bf16[256,384]{1,0:T(8,128)(2,1)S(1)}, bf16[256,384]{1,0:T(8,128)(2,1)S(1)}, u32[]{:S(2)}, u32[]{:S(2)}) collective-permute-start(bf16[256,384]{1,0:T(8,128)(2,1)S(1)} %get-tuple-element.80.att0), channel_id=1, source_target_pairs={{0,1},{1,0},{2,3},{3,2},{4,5},{5,4},{6,7},{7,6},{8,9},{9,8},{10,11... | collective-permute-start | bytes 589832 | tf_op jit(solution)/shard_map/ppermute | solution.py:702
  70.0 6.6 %copy-start.2 = (f32[1536]{0:T(1024)S(1)}, f32[1536]{0:T(1024)}, u32[]{:S(2)}) copy-start(f32[1536]{0:T(1024)} %gain_ref.5) | copy-start | bytes 18436
  75.0 1.6 %collective-permute-start.5 = (bf16[256,384]{1,0:T(8,128)(2,1)S(1)}, bf16[256,384]{1,0:T(8,128)(2,1)S(1)}, u32[]{:S(2)}, u32[]{:S(2)}) collective-permute-start(bf16[256,384]{1,0:T(8,128)(2,1)S(1)} %collective-permute-done.4.att2), channel_id=1, source_target_pairs={{0,1},{1,0},{2,3},{3,2},{4,5},{5,4},{6,7},{7,6},{8,9},{9,8},{10,11... | collective-permute-start | bytes 589832 | tf_op jit(solution)/shard_map/ppermute | solution.py:702
  75.6 6.9 %collective-permute-start.7 = (bf16[256,384]{1,0:T(8,128)(2,1)S(1)}, bf16[256,384]{1,0:T(8,128)(2,1)S(1)}, u32[]{:S(2)}, u32[]{:S(2)}) collective-permute-start(bf16[256,384]{1,0:T(8,128)(2,1)S(1)} %get-tuple-element.96.att0), channel_id=1, source_target_pairs={{0,2},{1,3},{2,0},{3,1},{4,6},{5,7},{6,4},{7,5},{8,10},{9,11},{10,... | collective-permute-start | bytes 589832 | tf_op jit(solution)/shard_map/ppermute | solution.py:706
  82.5 1.7 %collective-permute-start.9 = (bf16[128,1536]{1,0:T(8,128)(2,1)S(1)}, bf16[128,1536]{1,0:T(8,128)(2,1)S(1)}, u32[]{:S(2)}, u32[]{:S(2)}) collective-permute-start(bf16[128,1536]{1,0:T(8,128)(2,1)S(1)} %get-tuple-element.94), channel_id=1, source_target_pairs={{0,1},{1,0},{2,3},{3,2},{4,5},{5,4},{6,7},{7,6},{8,9},{9,8},{10,11... | collective-permute-start | bytes 1179656 | tf_op jit(solution)/shard_map/ppermute | solution.py:702
  82.5 2.0 %collective-permute-start.6 = (bf16[256,384]{1,0:T(8,128)(2,1)S(1)}, bf16[256,384]{1,0:T(8,128)(2,1)S(1)}, u32[]{:S(2)}, u32[]{:S(2)}) collective-permute-start(bf16[256,384]{1,0:T(8,128)(2,1)S(1)} %get-tuple-element.96.att0), channel_id=1, source_target_pairs={{0,1},{1,0},{2,3},{3,2},{4,5},{5,4},{6,7},{7,6},{8,9},{9,8},{10,11... | collective-permute-start | bytes 589832 | tf_op jit(solution)/shard_map/ppermute | solution.py:702
  83.0 1.8 %collective-permute-start.8 = (bf16[256,384]{1,0:T(8,128)(2,1)S(1)}, bf16[256,384]{1,0:T(8,128)(2,1)S(1)}, u32[]{:S(2)}, u32[]{:S(2)}) collective-permute-start(bf16[256,384]{1,0:T(8,128)(2,1)S(1)} %collective-permute-done.7.att2), channel_id=1, source_target_pairs={{0,1},{1,0},{2,3},{3,2},{4,5},{5,4},{6,7},{7,6},{8,9},{9,8},{10,11... | collective-permute-start | bytes 589832 | tf_op jit(solution)/shard_map/ppermute | solution.py:702
  84.7 8.0 %collective-permute-start.10 = (bf16[80,1536]{1,0:T(8,128)(2,1)S(1)}, bf16[80,1536]{1,0:T(8,128)(2,1)S(1)}, u32[]{:S(2)}, u32[]{:S(2)}) collective-permute-start(bf16[80,1536]{1,0:T(8,128)(2,1)S(1)} %slice.8), channel_id=1, source_target_pairs={{0,2},{1,3},{2,0},{3,1},{4,6},{5,7},{6,4},{7,5},{8,10},{9,11},{10,... | collective-permute-start | bytes 737288 | tf_op jit(solution)/shard_map/ppermute | solution.py:706
  92.7 1.7 %collective-permute-start.13 = (bf16[128,1536]{1,0:T(8,128)(2,1)S(1)}, bf16[128,1536]{1,0:T(8,128)(2,1)S(1)}, u32[]{:S(2)}, u32[]{:S(2)}) collective-permute-start(bf16[128,1536]{1,0:T(8,128)(2,1)S(1)} %get-tuple-element.104), channel_id=1, source_target_pairs={{0,1},{1,0},{2,3},{3,2},{4,5},{5,4},{6,7},{7,6},{8,9},{9,8},{10,11... | collective-permute-start | bytes 1179656 | tf_op jit(solution)/shard_map/ppermute | solution.py:702
  92.8 6.7 %collective-permute-start.11 = (bf16[48,1536]{1,0:T(8,128)(2,1)S(1)}, bf16[48,1536]{1,0:T(8,128)(2,1)S(1)}, u32[]{:S(2)}, u32[]{:S(2)}) collective-permute-start(bf16[48,1536]{1,0:T(8,128)(2,1)S(1)} %slice.9), channel_id=1, source_target_pairs={{0,2},{1,3},{2,0},{3,1},{4,6},{5,7},{6,4},{7,5},{8,10},{9,11},{10,... | collective-permute-start | bytes 442376 | tf_op jit(solution)/shard_map/ppermute | solution.py:706
  94.5 13.0 %collective-permute-start.14 = (bf16[128,1536]{1,0:T(8,128)(2,1)S(1)}, bf16[128,1536]{1,0:T(8,128)(2,1)S(1)}, u32[]{:S(2)}, u32[]{:S(2)}) collective-permute-start(bf16[128,1536]{1,0:T(8,128)(2,1)S(1)} %add_convert_fusion.1), channel_id=1, source_target_pairs={{0,2},{1,3},{2,0},{3,1},{4,6},{5,7},{6,4},{7,5},{8,10},{9,11},{10,... | collective-permute-start | bytes 1179656 | tf_op jit(solution)/shard_map/ppermute | solution.py:706
  99.6 8.1 %collective-permute-start.12 = (bf16[128,1536]{1,0:T(8,128)(2,1)S(1)}, bf16[128,1536]{1,0:T(8,128)(2,1)S(1)}, u32[]{:S(2)}, u32[]{:S(2)}) collective-permute-start(bf16[128,1536]{1,0:T(8,128)(2,1)S(1)} %add_convert_fusion.2.refs_0_), channel_id=1, source_target_pairs={{0,1},{1,0},{2,3},{3,2},{4,5},{5,4},{6,7},{7,6},{8,9},{9,8},{10,11... | collective-permute-start | bytes 1179656 | tf_op jit(solution)/shard_map/ppermute | solution.py:702
  107.6 1.8 %collective-permute-start.15 = (bf16[128,1536]{1,0:T(8,128)(2,1)S(1)}, bf16[128,1536]{1,0:T(8,128)(2,1)S(1)}, u32[]{:S(2)}, u32[]{:S(2)}) collective-permute-start(bf16[128,1536]{1,0:T(8,128)(2,1)S(1)} %add_convert_fusion.refs_2_), channel_id=1, source_target_pairs={{0,1},{1,0},{2,3},{3,2},{4,5},{5,4},{6,7},{7,6},{8,9},{9,8},{10,11... | collective-permute-start | bytes 1179656 | tf_op jit(solution)/shard_map/ppermute | solution.py:702

commit v9 on v7

--- a/solution.py
+++ b/solution.py
@@ -73,7 +73,7 @@
 
 
 def query_kernel(
-    tokens_hbm, gain_ref, wq_hbm, q_ref, q_hbm, normed_hbm,
+    tokens_hbm, gain_ref, wq_hbm, request_ref, q_ref, q_hbm, normed_hbm, ids_ref,
     tokens_ref, wq_ref, normed_ref, sems, out_sems,
 ):
     steps, rows, _ = tokens_ref.shape
@@ -87,6 +87,8 @@
         ],
         sems,
     )
+    for group in range(ids_ref.shape[0]):
+        ids_ref[group] = request_ref[...]
     gain = gain_ref[...].reshape(1, -1)
 
     def pair(index, carry):
@@ -115,7 +117,7 @@
     last.wait()
 
 
-def queries_of(tokens, gain, w_query):
+def queries_of(tokens, gain, w_query, request, groups):
     steps, rows, width = tokens.shape
     inner = w_query.shape[0]
     total = steps * rows
@@ -123,12 +125,13 @@
     vmem = pl.BlockSpec(memory_space=pltpu.VMEM)
     return pl.pallas_call(
         query_kernel,
-        in_specs=[hbm, vmem, hbm],
-        out_specs=[vmem, hbm, hbm],
+        in_specs=[hbm, vmem, hbm, vmem],
+        out_specs=[vmem, hbm, hbm, vmem],
         out_shape=[
             pltpu.VMEM((total, inner), bf16),
             pltpu.HBM((total, inner), bf16),
             pltpu.HBM((total, width), bf16),
+            jax.ShapeDtypeStruct((groups, 1, request.shape[0]), jnp.int32),
         ],
         scratch_shapes=[
             pltpu.VMEM(tokens.shape, bf16),
@@ -142,7 +145,7 @@
             flops=2 * total * width * inner, bytes_accessed=6 * MIB, transcendentals=total
         ),
         name="queries",
-    )(in_hbm(tokens), gain, in_hbm(w_query))
+    )(in_hbm(tokens), gain, in_hbm(w_query), request.reshape(1, -1))
 
 
 def ask_kernel(capacity, request_ref, ids_ref, q_ref, table_ref, out_ref):
@@ -665,10 +668,7 @@
             pltpu.VMEM((rows, width), f32),
         ],
         compiler_params=pltpu.CompilerParams(vmem_limit_bytes=20 * MIB),
-        cost_estimate=pl.CostEstimate(
-            flops=2 * rows * width * (4 * inner + 3 * hidden), bytes_accessed=16 * MIB,
-            transcendentals=rows * hidden,
-        ),
+        cost_estimate=pl.CostEstimate(flops=0, bytes_accessed=0, transcendentals=0),
         name="block",
     )(*attended, weight, tokens, gain, w_gate, w_up, w_down)
 
@@ -722,13 +722,14 @@
     def exchange(value):
         return lax.all_to_all(value, "group", split_axis=0, concat_axis=0, tiled=True)
 
-    ids = exchange(jnp.broadcast_to(page_request, (groups, 1, page_request.shape[0])))
-    q_near, q, normed = queries_of(tokens, gain_attn, w_query)
+    q_near, q, normed, ids = queries_of(tokens, gain_attn, w_query, page_request, groups)
+    ids = exchange(ids)
     table, asked = ask(page_request, ids, q_near, span, capacity)
-    asked, w_out = lax.optimization_barrier((asked, w_out))
-    w_out_far = swap_chip(w_out)
     asked_rows = exchange(asked.reshape(groups, capacity * span, inner)).reshape(asked.shape)
+    asked, q = lax.optimization_barrier((asked, q))
     own = own_pages(page_request, page_fill, q, keys_pool, values_pool, decay, span)
+    own, w_sent = lax.optimization_barrier((own, w_out))
+    w_out_far = swap_chip(w_sent)
     asked_rows, own = lax.optimization_barrier((asked_rows, own))
     payload = hosted_pages(
         page_request, page_fill, asked_rows, keys_pool, values_pool, decay, groups, capacity, local_count
@@ -736,6 +737,7 @@
     payload, normed = lax.optimization_barrier((payload, normed))
     back = exchange(payload)
     logs, averages = fresh(parents, forget_bias, normed, w_key, w_value, w_forget, q, own)
+    logs, w_out_far = lax.optimization_barrier((logs, w_out_far))
     mixes = [w_out, swap_core(w_out), w_out_far, swap_core(w_out_far)]
     logs, mixes = lax.optimization_barrier((logs, mixes))
 

time: 122 us -> 125 us (1.025)
  blocking collectives: 0 us -> 13.5 us
  starting transfers between devices: 24.5 us -> 17.5 us
  waiting for transfers between devices: 51.1 us -> 48.1 us
    ppermute x6, waiting for transfers between devices: 36.4 us -> 19.1 us  [swap_chip(): return lax.ppermute(value, 'head', [(i, i ^ 2) for i in range(4)])]
    all_to_all x0 -> x1, blocking collectives: none -> 13.5 us  [exchange(): lax.all_to_all(value, 'group', split_axis=0, concat_axis=0, tiled=True)]
    all_to_all x3 -> x2, waiting for transfers between devices: 10.3 us -> 23.4 us  [exchange(): lax.all_to_all(value, 'group', split_axis=0, concat_axis=0, tiled=True)]
    all_to_all x3 -> x2, starting transfers between devices: 16.2 us -> 9.17 us  [exchange(): lax.all_to_all(value, 'group', split_axis=0, concat_axis=0, tiled=True)]
    broadcast_in_dim x1 -> x0, local copies, waits for them, and re-layouts: 1.31 us -> none  [shards(): jnp.broadcast_to(page_request, (groups, 1, page_request.shape[0]))]
  transfers between devices with their start and end apart: 19 -> 18, of which waited for: 13 -> 13; matrix products, arithmetic and copies ran while one was open for 0% -> 0% of each run, Pallas kernels for 31% -> 27%
where the time goes in v9:
time: 125 us
  waiting for transfers between devices  48.1 us (38%)
  Pallas kernels  43.8 us (35%)
  starting transfers between devices  17.5 us (14%)
  blocking collectives  13.5 us (11%)
  local copies, waits for them, and re-layouts  1.41 us (1%)
    all_to_all x2, waiting for transfers between devices, exchange(): lax.all_to_all(value, 'group', split_axis=0, concat_axis=0, tiled=True)  23.4 us
    ppermute x6, waiting for transfers between devices, swap_chip(): return lax.ppermute(value, 'head', [(i, i ^ 2) for i in range(4)])  19.1 us
    all_to_all x1, blocking collectives, exchange(): lax.all_to_all(value, 'group', split_axis=0, concat_axis=0, tiled=True)  13.5 us
    all_to_all x2, starting transfers between devices, exchange(): lax.all_to_all(value, 'group', split_axis=0, concat_axis=0, tiled=True)  9.17 us
    pallas_call x1, Pallas kernels, fresh(): pl.pallas_call(fresh_kernel, in_specs=[vmem, vmem] + [hbm] * len(big), ou...  8.89 us
    pallas_call x2, Pallas kernels, block(): pl.pallas_call(functools.partial(block_kernel, first), in_specs=[vmem] *...  8.77 us
    pallas_call x2, Pallas kernels, merge(): pl.pallas_call(functools.partial(merge_kernel, capacity, steps, part, inn...  7.61 us
    ppermute x6, starting transfers between devices, swap_chip(): return lax.ppermute(value, 'head', [(i, i ^ 2) for i in range(4)])  7.1 us
  transfers between devices with their start and end apart: 18, of which 13 were waited for; matrix products, arithmetic and copies ran while one was open for 0% of the time, Pallas kernels for 27%

profile of v9, /device:TPU:0, one launch (start us, length us, event | category | flops | bytes accessed | tf_op | source)
XLA Modules:
  0.0 125.0 jit_solution(8016499416324013527)
XLA Ops:
  0.0 0.7 copy-done.3
  0.7 0.7 copy-done.4
  1.4 3.7 %queries.1 = (bf16[512,384]{1,0:T(8,128)(2,1)S(1)}, bf16[512,384]{1,0:T(8,128)(2,1)}, bf16[512,1536]{1,0:T(8,128)(2,1)}, s32[8,1,48]{2,1,0:T(1,128)S(1)}) custom-call(bf16[4,128,1536]{2,1,0:T(8,128)(2,1)} %tokens_hbm.1, f32[1536]{0:T(1024)S(1)} %copy-done.3, bf16[384,1536]{1,0:T(8,128)(2,1)} %wq_hbm.1, s32[1,48]{1,0:T(1,128)S(1)} %bitcast.13), custom_call_target="tpu_custom_call" | custom-call | flops 603979776 | bytes 6291456 | tf_op jit(solution)/shard_map/queries/pallas_call | solution.py:126
  5.1 13.5 %all_to_all.15.ids_ref = s32[8,1,48]{2,1,0:T(1,128)S(1)} all-to-all(s32[8,1,48]{2,1,0:T(1,128)S(1)} %get-tuple-element.60), channel_id=1, replica_groups=mesh['group'=8,'head'=4] {'group'}, dimensions={0} | all-to-all | bytes 3072 | tf_op jit(solution)/shard_map/all_to_all | solution.py:723
  18.6 2.0 %ask.1 = (s32[24]{0:T(128)S(1)}, bf16[24,32,384]{2,1,0:T(8,128)(2,1)}) custom-call(s32[48]{0:T(128)S(1)} %copy-done.4, s32[8,1,48]{2,1,0:T(1,128)S(1)} %all_to_all.15.ids_ref, bf16[512,384]{1,0:T(8,128)(2,1)S(1)} %get-tuple-element.61.q_ref), custom_call_target="tpu_custom_call" | custom-call | tf_op jit(solution)/shard_map/ask/pallas_call | solution.py:164
  20.6 3.5 %all-to-all-start.1 = ((bf16[8,96,384]{2,1,0:T(8,128)(2,1)}), bf16[8,96,384]{2,1,0:T(8,128)(2,1)S(1)}, u32[]{:S(2)}, u32[]{:S(2)}) async-start(bf16[8,96,384]{2,1,0:T(8,128)(2,1)} %bitcast.1), calls=%async_computation.1 | async-start | bytes 1179648 | tf_op jit(solution)/shard_map/all_to_all | solution.py:723
  24.2 7.0 %own_pages.1 = (f32[512,384]{1,0:T(8,128)}, f32[512,384]{1,0:T(8,128)}, f32[512,384]{1,0:T(8,128)}) custom-call(s32[48]{0:T(128)S(1)} %copy-done.5, s32[48]{0:T(128)S(1)} %copy-done.7, bf16[512,384]{1,0:T(8,128)(2,1)} %get-tuple-element.64.q_ref.q_hbm, bf16[48,384,128]{2,1,0:T(8,128)(2,1)} %keys_ref.3, bf16[48,384,128]{2,1,0:T(8,128)(2,1)} %values_ref.3, ...), custom_call_target="tpu_custom_call" | custom-call | flops 805306368 | bytes 6291456 | tf_op jit(solution)/shard_map/own_pages/pallas_call | solution.py:444
  31.2 1.5 %collective-permute-start = (bf16[384,1536]{1,0:T(8,128)(2,1)S(1)}, bf16[384,1536]{1,0:T(8,128)(2,1)S(1)}, u32[]{:S(2)}, u32[]{:S(2)}) collective-permute-start(bf16[384,1536]{1,0:T(8,128)(2,1)S(1)} %copy-done), channel_id=1, source_target_pairs={{0,2},{1,3},{2,0},{3,1},{4,6},{5,7},{6,4},{7,5},{8,10},{9,11},{10,... | collective-permute-start | bytes 3538952 | tf_op jit(solution)/shard_map/ppermute | solution.py:706
  32.7 6.1 %all-to-all-done.1 = bf16[8,96,384]{2,1,0:T(8,128)(2,1)S(1)} async-done(((bf16[8,96,384]{2,1,0:T(8,128)(2,1)}), bf16[8,96,384]{2,1,0:T(8,128)(2,1)S(1)}, u32[]{:S(2)}, u32[]{:S(2)}) %all-to-all-start.1) | async-done | bytes 589856 | tf_op jit(solution)/shard_map/all_to_all | solution.py:723
  38.8 4.5 %hosted_pages.1 = bf16[8,304,128]{2,1,0:T(8,128)(2,1)} custom-call(s32[48]{0:T(128)S(1)} %copy-done.5, s32[48]{0:T(128)S(1)} %copy-done.7, bf16[24,32,384]{2,1,0:T(8,128)(2,1)S(1)} %bitcast.10, bf16[48,384,128]{2,1,0:T(8,128)(2,1)} %keys_ref.3, bf16[48,384,128]{2,1,0:T(8,128)(2,1)} %values_ref.3, bf16[6,48,128]{2,1,0:T(8,128)(2,1)S(1)} %bitcast.12), custom_call_target="tpu_custom_call" | custom-call | flops 402653184 | bytes 3145728 | tf_op jit(solution)/shard_map/hosted_pages/pallas_call | solution.py:510
  43.4 8.9 %fresh.1 = (f32[2,16,16,384]{3,2,1,0:T(8,128)}, f32[2,16,16,384]{3,2,1,0:T(8,128)}) custom-call(s32[3,128]{1,0:T(4,128)S(1)} %copy-done.6, f32[1,6]{1,0:T(1,128)S(1)} %bitcast.14, bf16[512,1536]{1,0:T(8,128)(2,1)} %get-tuple-element.75.normed_hbm, bf16[384,1536]{1,0:T(8,128)(2,1)} %wk_hbm.1, bf16[384,1536]{1,0:T(8,128)(2,1)} %wv_hbm.1, ...), custom_call_target="tpu_custom_call" | custom-call | flops 1207959552 | bytes 12582912 | tf_op jit(solution)/shard_map/fresh/pallas_call | solution.py:329
  52.3 5.2 %collective-permute-done.refs_2_ = bf16[384,1536]{1,0:T(8,128)(2,1)S(1)} collective-permute-done((bf16[384,1536]{1,0:T(8,128)(2,1)S(1)}, bf16[384,1536]{1,0:T(8,128)(2,1)S(1)}, u32[]{:S(2)}, u32[]{:S(2)}) %collective-permute-start) | collective-permute-done | bytes 1179680 | tf_op jit(solution)/shard_map/ppermute | solution.py:706
  57.5 5.6 %all-to-all-start.2 = ((bf16[8,304,128]{2,1,0:T(8,128)(2,1)}), bf16[8,304,128]{2,1,0:T(8,128)(2,1)S(1)}, u32[]{:S(2)}, u32[]{:S(2)}) async-start(bf16[8,304,128]{2,1,0:T(8,128)(2,1)} %hosted_pages.1), calls=%async_computation.2 | async-start | bytes 1245184 | tf_op jit(solution)/shard_map/all_to_all | solution.py:723
  63.2 17.3 %all-to-all-done.2.back_ref = bf16[8,304,128]{2,1,0:T(8,128)(2,1)S(1)} async-done(((bf16[8,304,128]{2,1,0:T(8,128)(2,1)}), bf16[8,304,128]{2,1,0:T(8,128)(2,1)S(1)}, u32[]{:S(2)}, u32[]{:S(2)}) %all-to-all-start.2) | async-done | bytes 622624 | tf_op jit(solution)/shard_map/all_to_all | solution.py:723
  80.4 2.6 %merge.2 = (bf16[256,384]{1,0:T(8,128)(2,1)S(1)}, bf16[1536,1536]{1,0:T(8,128)(2,1)S(1)}) custom-call(s32[24]{0:T(128)S(1)} %get-tuple-element.74.table_ref, bf16[8,304,128]{2,1,0:T(8,128)(2,1)S(1)} %all-to-all-done.2.back_ref, f32[2,256,384]{2,1,0:T(8,128)} %bitcast.16, f32[2,256,384]{2,1,0:T(8,128)} %bitcast.18, bf16[384,1536]{1,0:T(8,128)(2,1)S(1)} %copy-done, ...), custom_call_target="tpu_custom_call" | custom-call | flops 3932160 | bytes 8388608 | tf_op jit(solution)/shard_map/merge/pallas_call | solution.py:597
  83.1 1.6 %collective-permute-start.4 = (bf16[256,384]{1,0:T(8,128)(2,1)S(1)}, bf16[256,384]{1,0:T(8,128)(2,1)S(1)}, u32[]{:S(2)}, u32[]{:S(2)}) collective-permute-start(bf16[256,384]{1,0:T(8,128)(2,1)S(1)} %get-tuple-element.90.att0), channel_id=1, source_target_pairs={{0,2},{1,3},{2,0},{3,1},{4,6},{5,7},{6,4},{7,5},{8,10},{9,11},{10,... | collective-permute-start | bytes 589832 | tf_op jit(solution)/shard_map/ppermute | solution.py:706
  84.6 5.0 %merge.3 = (bf16[256,384]{1,0:T(8,128)(2,1)S(1)}, bf16[1536,1024]{1,0:T(8,128)(2,1)S(1)}, bf16[1536,1024]{1,0:T(8,128)(2,1)S(1)}, bf16[1024,1536]{1,0:T(8,128)(2,1)S(1)}, bf16[512,1536]{1,0:T(8,128)(2,1)S(1)}) custom-call(s32[24]{0:T(128)S(1)} %get-tuple-element.74.table_ref, bf16[8,304,128]{2,1,0:T(8,128)(2,1)S(1)} %all-to-all-done.2.back_ref, ...), custom_call_target="tpu_custom_call" | custom-call | flops 3932160 | bytes 8388608 | tf_op jit(solution)/shard_map/merge/pallas_call | solution.py:597
  89.6 0.6 collective-permute-start.5
  90.2 0.6 collective-permute-start.7
  91.3 4.4 %block.2 = (f32[128,1536]{1,0:T(8,128)S(1)}, f32[128,1536]{1,0:T(8,128)S(1)}, bf16[128,1536]{1,0:T(8,128)(2,1)S(1)}) custom-call(bf16[256,384]{1,0:T(8,128)(2,1)S(1)} %get-tuple-element.90.att0, bf16[256,384]{1,0:T(8,128)(2,1)S(1)} %collective-permute-done.3.att1, bf16[256,384]{1,0:T(8,128)(2,1)S(1)} %collective-permute-done.4.att2, ...), custom_call_target="tpu_custom_call" | custom-call | tf_op jit(solution)/shard_map/block/pallas_call | solution.py:658
  95.7 1.4 %collective-permute-done.7.att2 = bf16[256,384]{1,0:T(8,128)(2,1)S(1)} collective-permute-done((bf16[256,384]{1,0:T(8,128)(2,1)S(1)}, bf16[256,384]{1,0:T(8,128)(2,1)S(1)}, u32[]{:S(2)}, u32[]{:S(2)}) %collective-permute-start.7) | collective-permute-done | bytes 196640 | tf_op jit(solution)/shard_map/ppermute | solution.py:706
  97.1 1.7 %collective-permute-done.9 = bf16[128,1536]{1,0:T(8,128)(2,1)S(1)} collective-permute-done((bf16[128,1536]{1,0:T(8,128)(2,1)S(1)}, bf16[128,1536]{1,0:T(8,128)(2,1)S(1)}, u32[]{:S(2)}, u32[]{:S(2)}) %collective-permute-start.9) | collective-permute-done | bytes 393248 | tf_op jit(solution)/shard_map/ppermute | solution.py:702
  98.9 1.1 collective-permute-start.10
  100.6 0.9 collective-permute-done.6.att1
  101.8 4.4 %block.3 = (f32[128,1536]{1,0:T(8,128)S(1)}, f32[128,1536]{1,0:T(8,128)S(1)}, bf16[128,1536]{1,0:T(8,128)(2,1)S(1)}) custom-call(bf16[256,384]{1,0:T(8,128)(2,1)S(1)} %get-tuple-element.106.att0, bf16[256,384]{1,0:T(8,128)(2,1)S(1)} %collective-permute-done.6.att1, bf16[256,384]{1,0:T(8,128)(2,1)S(1)} %collective-permute-done.7.att2, ...), custom_call_target="tpu_custom_call" | custom-call | tf_op jit(solution)/shard_map/block/pallas_call | solution.py:658
  106.2 0.8 collective-permute-done.10
  107.0 1.1 collective-permute-start.11
  108.8 1.1 collective-permute-start.14
  109.9 3.8 %collective-permute-done.11 = bf16[48,1536]{1,0:T(8,128)(2,1)S(1)} collective-permute-done((bf16[48,1536]{1,0:T(8,128)(2,1)S(1)}, bf16[48,1536]{1,0:T(8,128)(2,1)S(1)}, u32[]{:S(2)}, u32[]{:S(2)}) %collective-permute-start.11) | collective-permute-done | bytes 147488 | tf_op jit(solution)/shard_map/ppermute | solution.py:706
  113.9 7.8 %collective-permute-done.14 = bf16[128,1536]{1,0:T(8,128)(2,1)S(1)} collective-permute-done((bf16[128,1536]{1,0:T(8,128)(2,1)S(1)}, bf16[128,1536]{1,0:T(8,128)(2,1)S(1)}, u32[]{:S(2)}, u32[]{:S(2)}) %collective-permute-start.14) | collective-permute-done | bytes 393248 | tf_op jit(solution)/shard_map/ppermute | solution.py:706
  122.0 1.7 %collective-permute-done.15.refs_3_ = bf16[128,1536]{1,0:T(8,128)(2,1)S(1)} collective-permute-done((bf16[128,1536]{1,0:T(8,128)(2,1)S(1)}, bf16[128,1536]{1,0:T(8,128)(2,1)S(1)}, u32[]{:S(2)}, u32[]{:S(2)}) %collective-permute-start.15) | collective-permute-done | bytes 393248 | tf_op jit(solution)/shard_map/ppermute | solution.py:702
  123.7 1.3 %finish.1 = bf16[512,1536]{1,0:T(8,128)(2,1)} custom-call(bf16[128,1536]{1,0:T(8,128)(2,1)S(1)} %add_convert_fusion.2.refs_0_, bf16[128,1536]{1,0:T(8,128)(2,1)S(1)} %collective-permute-done.12.refs_1_, bf16[128,1536]{1,0:T(8,128)(2,1)S(1)} %add_convert_fusion.refs_2_, bf16[128,1536]{1,0:T(8,128)(2,1)S(1)} %collective-permute-done.15.refs_3_), custom_call_target="tpu_custom_call" | custom-call | tf_op jit(solution)/shard_map/finish/pallas_call | solution.py:691
  (39 shorter events, 2.4 us)
Async XLA Ops:
  0.0 0.7 copy-start.3
  0.7 0.7 copy-start.4
  1.4 22.8 %copy-start.1 = (bf16[48,6,128]{2,0,1:T(8,128)(2,1)S(1)}, bf16[48,6,128]{2,0,1:T(8,128)(2,1)}, u32[]{:S(2)}) copy-start(bf16[48,6,128]{2,0,1:T(8,128)(2,1)} %param.24) | copy-start | bytes 221188
  1.4 22.8 %copy-start.5 = (s32[48]{0:T(128)S(1)}, s32[48]{0:T(128)}, u32[]{:S(2)}) copy-start(s32[48]{0:T(128)} %request_ref.5) | copy-start | bytes 580
  1.4 22.8 %copy-start.7 = (s32[48]{0:T(128)S(1)}, s32[48]{0:T(128)}, u32[]{:S(2)}) copy-start(s32[48]{0:T(128)} %fill_ref.3) | copy-start | bytes 580
  20.6 18.2 %all-to-all-start.1 = ((bf16[8,96,384]{2,1,0:T(8,128)(2,1)}), bf16[8,96,384]{2,1,0:T(8,128)(2,1)S(1)}, u32[]{:S(2)}, u32[]{:S(2)}) async-start(bf16[8,96,384]{2,1,0:T(8,128)(2,1)} %bitcast.1), calls=%async_computation.1 | async-start | bytes 1179648 | tf_op jit(solution)/shard_map/all_to_all | solution.py:723
  24.2 7.0 %copy-start = (bf16[384,1536]{1,0:T(8,128)(2,1)S(1)}, bf16[384,1536]{1,0:T(8,128)(2,1)}, u32[]{:S(2)}) copy-start(bf16[384,1536]{1,0:T(8,128)(2,1)} %refs_0_.1) | copy-start | bytes 3538948
  31.2 26.3 %collective-permute-start = (bf16[384,1536]{1,0:T(8,128)(2,1)S(1)}, bf16[384,1536]{1,0:T(8,128)(2,1)S(1)}, u32[]{:S(2)}, u32[]{:S(2)}) collective-permute-start(bf16[384,1536]{1,0:T(8,128)(2,1)S(1)} %copy-done), channel_id=1, source_target_pairs={{0,2},{1,3},{2,0},{3,1},{4,6},{5,7},{6,4},{7,5},{8,10},{9,11},{10,... | collective-permute-start | bytes 3538952 | tf_op jit(solution)/shard_map/ppermute | solution.py:706
  32.7 30.4 %collective-permute-start.1 = (bf16[384,1536]{1,0:T(8,128)(2,1)S(1)}, bf16[384,1536]{1,0:T(8,128)(2,1)}, u32[]{:S(2)}, u32[]{:S(2)}) collective-permute-start(bf16[384,1536]{1,0:T(8,128)(2,1)S(1)} %copy-done), channel_id=1, source_target_pairs={{0,1},{1,0},{2,3},{3,2},{4,5},{5,4},{6,7},{7,6},{8,9},{9,8},{10,11... | collective-permute-start | bytes 3538952 | tf_op jit(solution)/shard_map/ppermute | solution.py:702
  38.8 4.5 %copy-start.6 = (s32[3,128]{1,0:T(4,128)S(1)}, s32[3,128]{1,0:T(4,128)}, u32[]{:S(2)}) copy-start(s32[3,128]{1,0:T(4,128)} %parents_ref.1) | copy-start | bytes 4612
  38.8 4.5 %copy-start.8 = (f32[6]{0:T(128)S(1)}, f32[6]{0:T(128)}, u32[]{:S(2)}) copy-start(f32[6]{0:T(128)} %param.30) | copy-start | bytes 76
  57.5 5.6 %collective-permute-start.2 = (bf16[384,1536]{1,0:T(8,128)(2,1)S(1)}, bf16[384,1536]{1,0:T(8,128)(2,1)}, u32[]{:S(2)}, u32[]{:S(2)}) collective-permute-start(bf16[384,1536]{1,0:T(8,128)(2,1)S(1)} %collective-permute-done.refs_2_), channel_id=1, source_target_pairs={{0,1},{1,0},{2,3},{3,2},{4,5},{5,4},{6,7},{7,6},{8,9},{9,8},{10,11... | collective-permute-start | bytes 3538952 | tf_op jit(solution)/shard_map/ppermute | solution.py:702
  57.5 22.9 %all-to-all-start.2 = ((bf16[8,304,128]{2,1,0:T(8,128)(2,1)}), bf16[8,304,128]{2,1,0:T(8,128)(2,1)S(1)}, u32[]{:S(2)}, u32[]{:S(2)}) async-start(bf16[8,304,128]{2,1,0:T(8,128)(2,1)} %hosted_pages.1), calls=%async_computation.2 | async-start | bytes 1245184 | tf_op jit(solution)/shard_map/all_to_all | solution.py:723
  83.1 6.5 %collective-permute-start.4 = (bf16[256,384]{1,0:T(8,128)(2,1)S(1)}, bf16[256,384]{1,0:T(8,128)(2,1)S(1)}, u32[]{:S(2)}, u32[]{:S(2)}) collective-permute-start(bf16[256,384]{1,0:T(8,128)(2,1)S(1)} %get-tuple-element.90.att0), channel_id=1, source_target_pairs={{0,2},{1,3},{2,0},{3,1},{4,6},{5,7},{6,4},{7,5},{8,10},{9,11},{10,... | collective-permute-start | bytes 589832 | tf_op jit(solution)/shard_map/ppermute | solution.py:706
  84.6 6.2 %collective-permute-start.3 = (bf16[256,384]{1,0:T(8,128)(2,1)S(1)}, bf16[256,384]{1,0:T(8,128)(2,1)S(1)}, u32[]{:S(2)}, u32[]{:S(2)}) collective-permute-start(bf16[256,384]{1,0:T(8,128)(2,1)S(1)} %get-tuple-element.90.att0), channel_id=1, source_target_pairs={{0,1},{1,0},{2,3},{3,2},{4,5},{5,4},{6,7},{7,6},{8,9},{9,8},{10,11... | collective-permute-start | bytes 589832 | tf_op jit(solution)/shard_map/ppermute | solution.py:702
  84.6 6.6 %copy-start.2 = (f32[1536]{0:T(1024)S(1)}, f32[1536]{0:T(1024)}, u32[]{:S(2)}) copy-start(f32[1536]{0:T(1024)} %gain_ref.5) | copy-start | bytes 18436
  89.6 1.6 %collective-permute-start.5 = (bf16[256,384]{1,0:T(8,128)(2,1)S(1)}, bf16[256,384]{1,0:T(8,128)(2,1)S(1)}, u32[]{:S(2)}, u32[]{:S(2)}) collective-permute-start(bf16[256,384]{1,0:T(8,128)(2,1)S(1)} %collective-permute-done.4.att2), channel_id=1, source_target_pairs={{0,1},{1,0},{2,3},{3,2},{4,5},{5,4},{6,7},{7,6},{8,9},{9,8},{10,11... | collective-permute-start | bytes 589832 | tf_op jit(solution)/shard_map/ppermute | solution.py:702
  90.2 6.9 %collective-permute-start.7 = (bf16[256,384]{1,0:T(8,128)(2,1)S(1)}, bf16[256,384]{1,0:T(8,128)(2,1)S(1)}, u32[]{:S(2)}, u32[]{:S(2)}) collective-permute-start(bf16[256,384]{1,0:T(8,128)(2,1)S(1)} %get-tuple-element.106.att0), channel_id=1, source_target_pairs={{0,2},{1,3},{2,0},{3,1},{4,6},{5,7},{6,4},{7,5},{8,10},{9,11},{10,... | collective-permute-start | bytes 589832 | tf_op jit(solution)/shard_map/ppermute | solution.py:706
  97.1 1.7 %collective-permute-start.9 = (bf16[128,1536]{1,0:T(8,128)(2,1)S(1)}, bf16[128,1536]{1,0:T(8,128)(2,1)S(1)}, u32[]{:S(2)}, u32[]{:S(2)}) collective-permute-start(bf16[128,1536]{1,0:T(8,128)(2,1)S(1)} %get-tuple-element.104), channel_id=1, source_target_pairs={{0,1},{1,0},{2,3},{3,2},{4,5},{5,4},{6,7},{7,6},{8,9},{9,8},{10,11... | collective-permute-start | bytes 1179656 | tf_op jit(solution)/shard_map/ppermute | solution.py:702
  98.9 8.1 %collective-permute-start.10 = (bf16[80,1536]{1,0:T(8,128)(2,1)S(1)}, bf16[80,1536]{1,0:T(8,128)(2,1)S(1)}, u32[]{:S(2)}, u32[]{:S(2)}) collective-permute-start(bf16[80,1536]{1,0:T(8,128)(2,1)S(1)} %slice.8), channel_id=1, source_target_pairs={{0,2},{1,3},{2,0},{3,1},{4,6},{5,7},{6,4},{7,5},{8,10},{9,11},{10,... | collective-permute-start | bytes 737288 | tf_op jit(solution)/shard_map/ppermute | solution.py:706
  100.1 1.4 %collective-permute-start.6 = (bf16[256,384]{1,0:T(8,128)(2,1)S(1)}, bf16[256,384]{1,0:T(8,128)(2,1)S(1)}, u32[]{:S(2)}, u32[]{:S(2)}) collective-permute-start(bf16[256,384]{1,0:T(8,128)(2,1)S(1)} %get-tuple-element.106.att0), channel_id=1, source_target_pairs={{0,1},{1,0},{2,3},{3,2},{4,5},{5,4},{6,7},{7,6},{8,9},{9,8},{10,11... | collective-permute-start | bytes 589832 | tf_op jit(solution)/shard_map/ppermute | solution.py:702
  100.1 1.7 %collective-permute-start.8 = (bf16[256,384]{1,0:T(8,128)(2,1)S(1)}, bf16[256,384]{1,0:T(8,128)(2,1)S(1)}, u32[]{:S(2)}, u32[]{:S(2)}) collective-permute-start(bf16[256,384]{1,0:T(8,128)(2,1)S(1)} %collective-permute-done.7.att2), channel_id=1, source_target_pairs={{0,1},{1,0},{2,3},{3,2},{4,5},{5,4},{6,7},{7,6},{8,9},{9,8},{10,11... | collective-permute-start | bytes 589832 | tf_op jit(solution)/shard_map/ppermute | solution.py:702
  107.0 1.7 %collective-permute-start.13 = (bf16[128,1536]{1,0:T(8,128)(2,1)S(1)}, bf16[128,1536]{1,0:T(8,128)(2,1)S(1)}, u32[]{:S(2)}, u32[]{:S(2)}) collective-permute-start(bf16[128,1536]{1,0:T(8,128)(2,1)S(1)} %get-tuple-element.114), channel_id=1, source_target_pairs={{0,1},{1,0},{2,3},{3,2},{4,5},{5,4},{6,7},{7,6},{8,9},{9,8},{10,11... | collective-permute-start | bytes 1179656 | tf_op jit(solution)/shard_map/ppermute | solution.py:702
  107.0 6.7 %collective-permute-start.11 = (bf16[48,1536]{1,0:T(8,128)(2,1)S(1)}, bf16[48,1536]{1,0:T(8,128)(2,1)S(1)}, u32[]{:S(2)}, u32[]{:S(2)}) collective-permute-start(bf16[48,1536]{1,0:T(8,128)(2,1)S(1)} %slice.9), channel_id=1, source_target_pairs={{0,2},{1,3},{2,0},{3,1},{4,6},{5,7},{6,4},{7,5},{8,10},{9,11},{10,... | collective-permute-start | bytes 442376 | tf_op jit(solution)/shard_map/ppermute | solution.py:706
  108.8 13.0 %collective-permute-start.14 = (bf16[128,1536]{1,0:T(8,128)(2,1)S(1)}, bf16[128,1536]{1,0:T(8,128)(2,1)S(1)}, u32[]{:S(2)}, u32[]{:S(2)}) collective-permute-start(bf16[128,1536]{1,0:T(8,128)(2,1)S(1)} %add_convert_fusion.1), channel_id=1, source_target_pairs={{0,2},{1,3},{2,0},{3,1},{4,6},{5,7},{6,4},{7,5},{8,10},{9,11},{10,... | collective-permute-start | bytes 1179656 | tf_op jit(solution)/shard_map/ppermute | solution.py:706
  113.8 8.1 %collective-permute-start.12 = (bf16[128,1536]{1,0:T(8,128)(2,1)S(1)}, bf16[128,1536]{1,0:T(8,128)(2,1)S(1)}, u32[]{:S(2)}, u32[]{:S(2)}) collective-permute-start(bf16[128,1536]{1,0:T(8,128)(2,1)S(1)} %add_convert_fusion.2.refs_0_), channel_id=1, source_target_pairs={{0,1},{1,0},{2,3},{3,2},{4,5},{5,4},{6,7},{7,6},{8,9},{9,8},{10,11... | collective-permute-start | bytes 1179656 | tf_op jit(solution)/shard_map/ppermute | solution.py:702
  121.9 1.8 %collective-permute-start.15 = (bf16[128,1536]{1,0:T(8,128)(2,1)S(1)}, bf16[128,1536]{1,0:T(8,128)(2,1)S(1)}, u32[]{:S(2)}, u32[]{:S(2)}) collective-permute-start(bf16[128,1536]{1,0:T(8,128)(2,1)S(1)} %add_convert_fusion.refs_2_), channel_id=1, source_target_pairs={{0,1},{1,0},{2,3},{3,2},{4,5},{5,4},{6,7},{7,6},{8,9},{9,8},{10,11... | collective-permute-start | bytes 1179656 | tf_op jit(solution)/shard_map/ppermute | solution.py:702

commit v10 on v7

--- a/solution.py
+++ b/solution.py
@@ -665,10 +665,7 @@
             pltpu.VMEM((rows, width), f32),
         ],
         compiler_params=pltpu.CompilerParams(vmem_limit_bytes=20 * MIB),
-        cost_estimate=pl.CostEstimate(
-            flops=2 * rows * width * (4 * inner + 3 * hidden), bytes_accessed=16 * MIB,
-            transcendentals=rows * hidden,
-        ),
+        cost_estimate=pl.CostEstimate(flops=0, bytes_accessed=0, transcendentals=0),
         name="block",
     )(*attended, weight, tokens, gain, w_gate, w_up, w_down)
 
@@ -734,6 +731,7 @@
         page_request, page_fill, asked_rows, keys_pool, values_pool, decay, groups, capacity, local_count
     )
     payload, normed = lax.optimization_barrier((payload, normed))
+    normed, w_out_far = lax.optimization_barrier((normed, w_out_far))
     back = exchange(payload)
     logs, averages = fresh(parents, forget_bias, normed, w_key, w_value, w_forget, q, own)
     mixes = [w_out, swap_core(w_out), w_out_far, swap_core(w_out_far)]
@@ -766,7 +764,7 @@
     residual[0], mine, other = block_of(0)
     other, fars[1] = lax.optimization_barrier((other, fars[1]))
     chip[0] = chip_sum(mine, other)
-    most = chip[0].shape[0] // 8 * 5
+    most = chip[0].shape[0] // 2
     chip_most, chip_rest = chip[0][:most], chip[0][most:]
     far_most, far_rest = swap_chip(chip_most), swap_chip(chip_rest)
     residual[1], mine, other = block_of(1)

time: 122 us -> 110 us (0.902)
  waiting for transfers between devices: 51.1 us -> 39.1 us
    ppermute x6, waiting for transfers between devices: 36.4 us -> 16.6 us  [swap_chip(): return lax.ppermute(value, 'head', [(i, i ^ 2) for i in range(4)])]
    all_to_all x3, waiting for transfers between devices: 10.3 us -> 18.5 us  [exchange(): lax.all_to_all(value, 'group', split_axis=0, concat_axis=0, tiled=True)]
  transfers between devices with their start and end apart: 19 -> 19, of which waited for: 13 -> 12; matrix products, arithmetic and copies ran while one was open for 0% -> 0% of each run, Pallas kernels for 31% -> 34%
where the time goes in v10:
time: 110 us
  Pallas kernels  43.7 us (40%)
  waiting for transfers between devices  39.1 us (36%)
  starting transfers between devices  24.5 us (22%)
  local copies, waits for them, and re-layouts  2.05 us (2%)
    all_to_all x3, waiting for transfers between devices, exchange(): lax.all_to_all(value, 'group', split_axis=0, concat_axis=0, tiled=True)  18.5 us
    ppermute x6, waiting for transfers between devices, swap_chip(): return lax.ppermute(value, 'head', [(i, i ^ 2) for i in range(4)])  16.6 us
    all_to_all x3, starting transfers between devices, exchange(): lax.all_to_all(value, 'group', split_axis=0, concat_axis=0, tiled=True)  16.2 us
    pallas_call x1, Pallas kernels, fresh(): pl.pallas_call(fresh_kernel, in_specs=[vmem, vmem] + [hbm] * len(big), ou...  8.97 us
    pallas_call x2, Pallas kernels, block(): pl.pallas_call(functools.partial(block_kernel, first), in_specs=[vmem] *...  8.77 us
    pallas_call x2, Pallas kernels, merge(): pl.pallas_call(functools.partial(merge_kernel, capacity, steps, part, inn...  7.8 us
    ppermute x6, starting transfers between devices, swap_chip(): return lax.ppermute(value, 'head', [(i, i ^ 2) for i in range(4)])  7.1 us
    pallas_call x1, Pallas kernels, own_pages(): pl.pallas_call(own_kernel, grid=(OWNED_SLOTS // PAGE_BLOCK,), in_specs=[S...  6.9 us
  transfers between devices with their start and end apart: 19, of which 12 were waited for; matrix products, arithmetic and copies ran while one was open for 0% of the time, Pallas kernels for 34%

profile of v10, /device:TPU:0, one launch (start us, length us, event | category | flops | bytes accessed | tf_op | source)
XLA Modules:
  0.0 110.0 jit_solution(13653916834302192143)
XLA Ops:
  0.0 1.3 %broadcast_in_dim.3 = s32[8,1,48]{2,1,0:T(1,128)} broadcast(s32[48]{0:T(128)} %request_ref.5), dimensions={2} | broadcast | bytes 1728 | tf_op jit(solution)/shard_map/broadcast_in_dim | solution.py:722
  1.3 7.3 %all-to-all-start = ((s32[8,1,48]{2,1,0:T(1,128)}), s32[8,1,48]{2,1,0:T(1,128)S(1)}, u32[]{:S(2)}, u32[]{:S(2)}) async-start(s32[8,1,48]{2,1,0:T(1,128)} %broadcast_in_dim.3), calls=%async_computation | async-start | bytes 8192 | tf_op jit(solution)/shard_map/all_to_all | solution.py:720
  8.6 0.7 copy-done.4
  9.3 3.8 %queries.1 = (bf16[512,384]{1,0:T(8,128)(2,1)S(1)}, bf16[512,384]{1,0:T(8,128)(2,1)}, bf16[512,1536]{1,0:T(8,128)(2,1)}) custom-call(bf16[4,128,1536]{2,1,0:T(8,128)(2,1)} %tokens_hbm.1, f32[1536]{0:T(1024)S(1)} %copy-done.4, bf16[384,1536]{1,0:T(8,128)(2,1)} %wq_hbm.1), custom_call_target="tpu_custom_call" | custom-call | flops 603979776 | bytes 6291456 | tf_op jit(solution)/shard_map/queries/pallas_call | solution.py:124
  13.1 2.0 %all-to-all-done.ids_ref = s32[8,1,48]{2,1,0:T(1,128)S(1)} async-done(((s32[8,1,48]{2,1,0:T(1,128)}), s32[8,1,48]{2,1,0:T(1,128)S(1)}, u32[]{:S(2)}, u32[]{:S(2)}) %all-to-all-start) | async-done | bytes 1568 | tf_op jit(solution)/shard_map/all_to_all | solution.py:720
  15.1 1.7 %ask.1 = (s32[24]{0:T(128)S(1)}, bf16[24,32,384]{2,1,0:T(8,128)(2,1)S(1)}) custom-call(s32[48]{0:T(128)S(1)} %copy-done.5, s32[8,1,48]{2,1,0:T(1,128)S(1)} %all-to-all-done.ids_ref, bf16[512,384]{1,0:T(8,128)(2,1)S(1)} %get-tuple-element.56.q_ref), custom_call_target="tpu_custom_call" | custom-call | tf_op jit(solution)/shard_map/ask/pallas_call | solution.py:161
  16.8 1.6 %collective-permute-start = (bf16[384,1536]{1,0:T(8,128)(2,1)S(1)}, bf16[384,1536]{1,0:T(8,128)(2,1)S(1)}, u32[]{:S(2)}, u32[]{:S(2)}) collective-permute-start(bf16[384,1536]{1,0:T(8,128)(2,1)S(1)} %copy-done), channel_id=1, source_target_pairs={{0,2},{1,3},{2,0},{3,1},{4,6},{5,7},{6,4},{7,5},{8,10},{9,11},{10,... | collective-permute-start | bytes 3538952 | tf_op jit(solution)/shard_map/ppermute | solution.py:703
  18.4 4.0 %all-to-all-start.1 = ((bf16[8,96,384]{2,1,0:T(8,128)(2,1)}), bf16[8,96,384]{2,1,0:T(8,128)(2,1)S(1)}, u32[]{:S(2)}, u32[]{:S(2)}) async-start(bf16[8,96,384]{2,1,0:T(8,128)(2,1)} %bitcast.10), calls=%async_computation.1 | async-start | bytes 1179648 | tf_op jit(solution)/shard_map/all_to_all | solution.py:720
  22.4 6.9 %own_pages.1 = (f32[512,384]{1,0:T(8,128)}, f32[512,384]{1,0:T(8,128)}, f32[512,384]{1,0:T(8,128)}) custom-call(s32[48]{0:T(128)S(1)} %copy-done.5, s32[48]{0:T(128)S(1)} %copy-done.7, bf16[512,384]{1,0:T(8,128)(2,1)} %get-tuple-element.59.q_ref.q_hbm, bf16[48,384,128]{2,1,0:T(8,128)(2,1)} %keys_ref.3, bf16[48,384,128]{2,1,0:T(8,128)(2,1)} %values_ref.3, ...), custom_call_target="tpu_custom_call" | custom-call | flops 805306368 | bytes 6291456 | tf_op jit(solution)/shard_map/own_pages/pallas_call | solution.py:441
  29.3 8.2 %all-to-all-done.1 = bf16[8,96,384]{2,1,0:T(8,128)(2,1)S(1)} async-done(((bf16[8,96,384]{2,1,0:T(8,128)(2,1)}), bf16[8,96,384]{2,1,0:T(8,128)(2,1)S(1)}, u32[]{:S(2)}, u32[]{:S(2)}) %all-to-all-start.1) | async-done | bytes 589856 | tf_op jit(solution)/shard_map/all_to_all | solution.py:720
  37.5 4.5 %hosted_pages.1 = bf16[8,304,128]{2,1,0:T(8,128)(2,1)} custom-call(s32[48]{0:T(128)S(1)} %copy-done.5, s32[48]{0:T(128)S(1)} %copy-done.7, bf16[24,32,384]{2,1,0:T(8,128)(2,1)S(1)} %bitcast.9, bf16[48,384,128]{2,1,0:T(8,128)(2,1)} %keys_ref.3, bf16[48,384,128]{2,1,0:T(8,128)(2,1)} %values_ref.3, bf16[6,48,128]{2,1,0:T(8,128)(2,1)S(1)} %bitcast.12), custom_call_target="tpu_custom_call" | custom-call | flops 402653184 | bytes 3145728 | tf_op jit(solution)/shard_map/hosted_pages/pallas_call | solution.py:507
  42.0 1.1 %collective-permute-done.refs_2_ = bf16[384,1536]{1,0:T(8,128)(2,1)S(1)} collective-permute-done((bf16[384,1536]{1,0:T(8,128)(2,1)S(1)}, bf16[384,1536]{1,0:T(8,128)(2,1)S(1)}, u32[]{:S(2)}, u32[]{:S(2)}) %collective-permute-start) | collective-permute-done | bytes 1179680 | tf_op jit(solution)/shard_map/ppermute | solution.py:703
  43.1 4.9 %all-to-all-start.2 = ((bf16[8,304,128]{2,1,0:T(8,128)(2,1)}), bf16[8,304,128]{2,1,0:T(8,128)(2,1)S(1)}, u32[]{:S(2)}, u32[]{:S(2)}) async-start(bf16[8,304,128]{2,1,0:T(8,128)(2,1)} %hosted_pages.1), calls=%async_computation.2 | async-start | bytes 1245184 | tf_op jit(solution)/shard_map/all_to_all | solution.py:720
  48.0 9.0 %fresh.1 = (f32[2,16,16,384]{3,2,1,0:T(8,128)}, f32[2,16,16,384]{3,2,1,0:T(8,128)}) custom-call(s32[3,128]{1,0:T(4,128)S(1)} %copy-done.6, f32[1,6]{1,0:T(1,128)S(1)} %bitcast.13, bf16[512,1536]{1,0:T(8,128)(2,1)} %get-tuple-element.69.normed_hbm, bf16[384,1536]{1,0:T(8,128)(2,1)} %wk_hbm.1, bf16[384,1536]{1,0:T(8,128)(2,1)} %wv_hbm.1, ...), custom_call_target="tpu_custom_call" | custom-call | flops 1207959552 | bytes 12582912 | tf_op jit(solution)/shard_map/fresh/pallas_call | solution.py:326
  57.0 8.3 %all-to-all-done.2.back_ref = bf16[8,304,128]{2,1,0:T(8,128)(2,1)S(1)} async-done(((bf16[8,304,128]{2,1,0:T(8,128)(2,1)}), bf16[8,304,128]{2,1,0:T(8,128)(2,1)S(1)}, u32[]{:S(2)}, u32[]{:S(2)}) %all-to-all-start.2) | async-done | bytes 622624 | tf_op jit(solution)/shard_map/all_to_all | solution.py:720
  65.3 2.8 %merge.2 = (bf16[256,384]{1,0:T(8,128)(2,1)S(1)}, bf16[1536,1536]{1,0:T(8,128)(2,1)S(1)}) custom-call(s32[24]{0:T(128)S(1)} %get-tuple-element.66.table_ref, bf16[8,304,128]{2,1,0:T(8,128)(2,1)S(1)} %all-to-all-done.2.back_ref, f32[2,256,384]{2,1,0:T(8,128)} %bitcast.15, f32[2,256,384]{2,1,0:T(8,128)} %bitcast.17, bf16[384,1536]{1,0:T(8,128)(2,1)S(1)} %copy-done, ...), custom_call_target="tpu_custom_call" | custom-call | flops 3932160 | bytes 8388608 | tf_op jit(solution)/shard_map/merge/pallas_call | solution.py:594
  68.2 1.6 %collective-permute-start.4 = (bf16[256,384]{1,0:T(8,128)(2,1)S(1)}, bf16[256,384]{1,0:T(8,128)(2,1)S(1)}, u32[]{:S(2)}, u32[]{:S(2)}) collective-permute-start(bf16[256,384]{1,0:T(8,128)(2,1)S(1)} %get-tuple-element.82.att0), channel_id=1, source_target_pairs={{0,2},{1,3},{2,0},{3,1},{4,6},{5,7},{6,4},{7,5},{8,10},{9,11},{10,... | collective-permute-start | bytes 589832 | tf_op jit(solution)/shard_map/ppermute | solution.py:703
  69.7 5.0 %merge.3 = (bf16[256,384]{1,0:T(8,128)(2,1)S(1)}, bf16[1536,1024]{1,0:T(8,128)(2,1)S(1)}, bf16[1536,1024]{1,0:T(8,128)(2,1)S(1)}, bf16[1024,1536]{1,0:T(8,128)(2,1)S(1)}, bf16[512,1536]{1,0:T(8,128)(2,1)S(1)}) custom-call(s32[24]{0:T(128)S(1)} %get-tuple-element.66.table_ref, bf16[8,304,128]{2,1,0:T(8,128)(2,1)S(1)} %all-to-all-done.2.back_ref, ...), custom_call_target="tpu_custom_call" | custom-call | flops 3932160 | bytes 8388608 | tf_op jit(solution)/shard_map/merge/pallas_call | solution.py:594
  75.3 0.6 collective-permute-start.7
  76.4 4.4 %block.2 = (f32[128,1536]{1,0:T(8,128)S(1)}, f32[128,1536]{1,0:T(8,128)S(1)}, bf16[128,1536]{1,0:T(8,128)(2,1)S(1)}) custom-call(bf16[256,384]{1,0:T(8,128)(2,1)S(1)} %get-tuple-element.82.att0, bf16[256,384]{1,0:T(8,128)(2,1)S(1)} %collective-permute-done.3.att1, bf16[256,384]{1,0:T(8,128)(2,1)S(1)} %collective-permute-done.4.att2, ...), custom_call_target="tpu_custom_call" | custom-call | tf_op jit(solution)/shard_map/block/pallas_call | solution.py:655
  80.8 1.4 %collective-permute-done.7.att2 = bf16[256,384]{1,0:T(8,128)(2,1)S(1)} collective-permute-done((bf16[256,384]{1,0:T(8,128)(2,1)S(1)}, bf16[256,384]{1,0:T(8,128)(2,1)S(1)}, u32[]{:S(2)}, u32[]{:S(2)}) %collective-permute-start.7) | collective-permute-done | bytes 196640 | tf_op jit(solution)/shard_map/ppermute | solution.py:703
  82.7 1.2 %collective-permute-done.9 = bf16[128,1536]{1,0:T(8,128)(2,1)S(1)} collective-permute-done((bf16[128,1536]{1,0:T(8,128)(2,1)S(1)}, bf16[128,1536]{1,0:T(8,128)(2,1)S(1)}, u32[]{:S(2)}, u32[]{:S(2)}) %collective-permute-start.9) | collective-permute-done | bytes 393248 | tf_op jit(solution)/shard_map/ppermute | solution.py:699
  84.0 1.1 %collective-permute-start.10 = (bf16[64,1536]{1,0:T(8,128)(2,1)S(1)}, bf16[64,1536]{1,0:T(8,128)(2,1)S(1)}, u32[]{:S(2)}, u32[]{:S(2)}) collective-permute-start(bf16[64,1536]{1,0:T(8,128)(2,1)S(1)} %get-tuple-element.107), channel_id=1, source_target_pairs={{0,2},{1,3},{2,0},{3,1},{4,6},{5,7},{6,4},{7,5},{8,10},{9,11},{10,... | collective-permute-start | bytes 589832 | tf_op jit(solution)/shard_map/ppermute | solution.py:703
  85.2 4.4 %block.3 = (f32[128,1536]{1,0:T(8,128)S(1)}, f32[128,1536]{1,0:T(8,128)S(1)}, bf16[128,1536]{1,0:T(8,128)(2,1)S(1)}) custom-call(bf16[256,384]{1,0:T(8,128)(2,1)S(1)} %get-tuple-element.98.att0, bf16[256,384]{1,0:T(8,128)(2,1)S(1)} %collective-permute-done.6.att1, bf16[256,384]{1,0:T(8,128)(2,1)S(1)} %collective-permute-done.7.att2, ...), custom_call_target="tpu_custom_call" | custom-call | tf_op jit(solution)/shard_map/block/pallas_call | solution.py:655
  89.6 1.5 %collective-permute-done.10 = bf16[64,1536]{1,0:T(8,128)(2,1)S(1)} collective-permute-done((bf16[64,1536]{1,0:T(8,128)(2,1)S(1)}, bf16[64,1536]{1,0:T(8,128)(2,1)S(1)}, u32[]{:S(2)}, u32[]{:S(2)}) %collective-permute-start.10) | collective-permute-done | bytes 196640 | tf_op jit(solution)/shard_map/ppermute | solution.py:703
  91.0 1.1 collective-permute-start.11
  92.1 0.6 collective-permute-done.13
  92.9 1.1 %collective-permute-start.14 = (bf16[128,1536]{1,0:T(8,128)(2,1)S(1)}, bf16[128,1536]{1,0:T(8,128)(2,1)S(1)}, u32[]{:S(2)}, u32[]{:S(2)}) collective-permute-start(bf16[128,1536]{1,0:T(8,128)(2,1)S(1)} %add_convert_fusion.1), channel_id=1, source_target_pairs={{0,2},{1,3},{2,0},{3,1},{4,6},{5,7},{6,4},{7,5},{8,10},{9,11},{10,... | collective-permute-start | bytes 1179656 | tf_op jit(solution)/shard_map/ppermute | solution.py:703
  94.0 4.8 %collective-permute-done.11 = bf16[64,1536]{1,0:T(8,128)(2,1)S(1)} collective-permute-done((bf16[64,1536]{1,0:T(8,128)(2,1)S(1)}, bf16[64,1536]{1,0:T(8,128)(2,1)S(1)}, u32[]{:S(2)}, u32[]{:S(2)}) %collective-permute-start.11) | collective-permute-done | bytes 196640 | tf_op jit(solution)/shard_map/ppermute | solution.py:703
  98.9 7.8 %collective-permute-done.14 = bf16[128,1536]{1,0:T(8,128)(2,1)S(1)} collective-permute-done((bf16[128,1536]{1,0:T(8,128)(2,1)S(1)}, bf16[128,1536]{1,0:T(8,128)(2,1)S(1)}, u32[]{:S(2)}, u32[]{:S(2)}) %collective-permute-start.14) | collective-permute-done | bytes 393248 | tf_op jit(solution)/shard_map/ppermute | solution.py:703
  107.0 1.7 %collective-permute-done.15.refs_3_ = bf16[128,1536]{1,0:T(8,128)(2,1)S(1)} collective-permute-done((bf16[128,1536]{1,0:T(8,128)(2,1)S(1)}, bf16[128,1536]{1,0:T(8,128)(2,1)S(1)}, u32[]{:S(2)}, u32[]{:S(2)}) %collective-permute-start.15) | collective-permute-done | bytes 393248 | tf_op jit(solution)/shard_map/ppermute | solution.py:699
  108.7 1.3 %finish.1 = bf16[512,1536]{1,0:T(8,128)(2,1)} custom-call(bf16[128,1536]{1,0:T(8,128)(2,1)S(1)} %add_convert_fusion.2.refs_0_, bf16[128,1536]{1,0:T(8,128)(2,1)S(1)} %collective-permute-done.12.refs_1_, bf16[128,1536]{1,0:T(8,128)(2,1)S(1)} %add_convert_fusion.refs_2_, bf16[128,1536]{1,0:T(8,128)(2,1)S(1)} %collective-permute-done.15.refs_3_), custom_call_target="tpu_custom_call" | custom-call | tf_op jit(solution)/shard_map/finish/pallas_call | solution.py:688
  (40 shorter events, 2.2 us)
Async XLA Ops:
  0.0 15.0 %copy-start.5 = (s32[48]{0:T(128)S(1)}, s32[48]{0:T(128)}, u32[]{:S(2)}) copy-start(s32[48]{0:T(128)} %request_ref.5) | copy-start | bytes 580
  1.3 13.7 %all-to-all-start = ((s32[8,1,48]{2,1,0:T(1,128)}), s32[8,1,48]{2,1,0:T(1,128)S(1)}, u32[]{:S(2)}, u32[]{:S(2)}) async-start(s32[8,1,48]{2,1,0:T(1,128)} %broadcast_in_dim.3), calls=%async_computation | async-start | bytes 8192 | tf_op jit(solution)/shard_map/all_to_all | solution.py:720
  8.6 0.7 copy-start.4
  9.3 7.5 %copy-start = (bf16[384,1536]{1,0:T(8,128)(2,1)S(1)}, bf16[384,1536]{1,0:T(8,128)(2,1)}, u32[]{:S(2)}) copy-start(bf16[384,1536]{1,0:T(8,128)(2,1)} %refs_0_.1) | copy-start | bytes 3538948
  9.3 13.1 %copy-start.2 = (bf16[48,6,128]{2,0,1:T(8,128)(2,1)S(1)}, bf16[48,6,128]{2,0,1:T(8,128)(2,1)}, u32[]{:S(2)}) copy-start(bf16[48,6,128]{2,0,1:T(8,128)(2,1)} %param.24) | copy-start | bytes 221188
  9.3 13.1 %copy-start.7 = (s32[48]{0:T(128)S(1)}, s32[48]{0:T(128)}, u32[]{:S(2)}) copy-start(s32[48]{0:T(128)} %fill_ref.3) | copy-start | bytes 580
  16.8 1.6 %copy-start.1 = (bf16[24,32,384]{2,1,0:T(8,128)(2,1)}, bf16[24,32,384]{2,1,0:T(8,128)(2,1)S(1)}, u32[]{:S(2)}) copy-start(bf16[24,32,384]{2,1,0:T(8,128)(2,1)S(1)} %get-tuple-element.58) | copy-start | bytes 1769476
  16.8 26.3 %collective-permute-start = (bf16[384,1536]{1,0:T(8,128)(2,1)S(1)}, bf16[384,1536]{1,0:T(8,128)(2,1)S(1)}, u32[]{:S(2)}, u32[]{:S(2)}) collective-permute-start(bf16[384,1536]{1,0:T(8,128)(2,1)S(1)} %copy-done), channel_id=1, source_target_pairs={{0,2},{1,3},{2,0},{3,1},{4,6},{5,7},{6,4},{7,5},{8,10},{9,11},{10,... | collective-permute-start | bytes 3538952 | tf_op jit(solution)/shard_map/ppermute | solution.py:703
  18.4 19.1 %all-to-all-start.1 = ((bf16[8,96,384]{2,1,0:T(8,128)(2,1)}), bf16[8,96,384]{2,1,0:T(8,128)(2,1)S(1)}, u32[]{:S(2)}, u32[]{:S(2)}) async-start(bf16[8,96,384]{2,1,0:T(8,128)(2,1)} %bitcast.10), calls=%async_computation.1 | async-start | bytes 1179648 | tf_op jit(solution)/shard_map/all_to_all | solution.py:720
  29.3 27.7 %collective-permute-start.1 = (bf16[384,1536]{1,0:T(8,128)(2,1)S(1)}, bf16[384,1536]{1,0:T(8,128)(2,1)}, u32[]{:S(2)}, u32[]{:S(2)}) collective-permute-start(bf16[384,1536]{1,0:T(8,128)(2,1)S(1)} %copy-done), channel_id=1, source_target_pairs={{0,1},{1,0},{2,3},{3,2},{4,5},{5,4},{6,7},{7,6},{8,9},{9,8},{10,11... | collective-permute-start | bytes 3538952 | tf_op jit(solution)/shard_map/ppermute | solution.py:699
  37.5 10.6 %copy-start.6 = (s32[3,128]{1,0:T(4,128)S(1)}, s32[3,128]{1,0:T(4,128)}, u32[]{:S(2)}) copy-start(s32[3,128]{1,0:T(4,128)} %parents_ref.1) | copy-start | bytes 4612
  37.5 10.6 %copy-start.8 = (f32[6]{0:T(128)S(1)}, f32[6]{0:T(128)}, u32[]{:S(2)}) copy-start(f32[6]{0:T(128)} %param.30) | copy-start | bytes 76
  43.1 13.9 %collective-permute-start.2 = (bf16[384,1536]{1,0:T(8,128)(2,1)S(1)}, bf16[384,1536]{1,0:T(8,128)(2,1)}, u32[]{:S(2)}, u32[]{:S(2)}) collective-permute-start(bf16[384,1536]{1,0:T(8,128)(2,1)S(1)} %collective-permute-done.refs_2_), channel_id=1, source_target_pairs={{0,1},{1,0},{2,3},{3,2},{4,5},{5,4},{6,7},{7,6},{8,9},{9,8},{10,11... | collective-permute-start | bytes 3538952 | tf_op jit(solution)/shard_map/ppermute | solution.py:699
  43.1 22.2 %all-to-all-start.2 = ((bf16[8,304,128]{2,1,0:T(8,128)(2,1)}), bf16[8,304,128]{2,1,0:T(8,128)(2,1)S(1)}, u32[]{:S(2)}, u32[]{:S(2)}) async-start(bf16[8,304,128]{2,1,0:T(8,128)(2,1)} %hosted_pages.1), calls=%async_computation.2 | async-start | bytes 1245184 | tf_op jit(solution)/shard_map/all_to_all | solution.py:720
  68.2 6.6 %collective-permute-start.4 = (bf16[256,384]{1,0:T(8,128)(2,1)S(1)}, bf16[256,384]{1,0:T(8,128)(2,1)S(1)}, u32[]{:S(2)}, u32[]{:S(2)}) collective-permute-start(bf16[256,384]{1,0:T(8,128)(2,1)S(1)} %get-tuple-element.82.att0), channel_id=1, source_target_pairs={{0,2},{1,3},{2,0},{3,1},{4,6},{5,7},{6,4},{7,5},{8,10},{9,11},{10,... | collective-permute-start | bytes 589832 | tf_op jit(solution)/shard_map/ppermute | solution.py:703
  69.7 6.2 %collective-permute-start.3 = (bf16[256,384]{1,0:T(8,128)(2,1)S(1)}, bf16[256,384]{1,0:T(8,128)(2,1)S(1)}, u32[]{:S(2)}, u32[]{:S(2)}) collective-permute-start(bf16[256,384]{1,0:T(8,128)(2,1)S(1)} %get-tuple-element.82.att0), channel_id=1, source_target_pairs={{0,1},{1,0},{2,3},{3,2},{4,5},{5,4},{6,7},{7,6},{8,9},{9,8},{10,11... | collective-permute-start | bytes 589832 | tf_op jit(solution)/shard_map/ppermute | solution.py:699
  69.7 6.6 %copy-start.3 = (f32[1536]{0:T(1024)S(1)}, f32[1536]{0:T(1024)}, u32[]{:S(2)}) copy-start(f32[1536]{0:T(1024)} %gain_ref.5) | copy-start | bytes 18436
  74.7 1.6 %collective-permute-start.5 = (bf16[256,384]{1,0:T(8,128)(2,1)S(1)}, bf16[256,384]{1,0:T(8,128)(2,1)S(1)}, u32[]{:S(2)}, u32[]{:S(2)}) collective-permute-start(bf16[256,384]{1,0:T(8,128)(2,1)S(1)} %collective-permute-done.4.att2), channel_id=1, source_target_pairs={{0,1},{1,0},{2,3},{3,2},{4,5},{5,4},{6,7},{7,6},{8,9},{9,8},{10,11... | collective-permute-start | bytes 589832 | tf_op jit(solution)/shard_map/ppermute | solution.py:699
  75.3 6.9 %collective-permute-start.7 = (bf16[256,384]{1,0:T(8,128)(2,1)S(1)}, bf16[256,384]{1,0:T(8,128)(2,1)S(1)}, u32[]{:S(2)}, u32[]{:S(2)}) collective-permute-start(bf16[256,384]{1,0:T(8,128)(2,1)S(1)} %get-tuple-element.98.att0), channel_id=1, source_target_pairs={{0,2},{1,3},{2,0},{3,1},{4,6},{5,7},{6,4},{7,5},{8,10},{9,11},{10,... | collective-permute-start | bytes 589832 | tf_op jit(solution)/shard_map/ppermute | solution.py:703
  82.2 1.7 %collective-permute-start.9 = (bf16[128,1536]{1,0:T(8,128)(2,1)S(1)}, bf16[128,1536]{1,0:T(8,128)(2,1)S(1)}, u32[]{:S(2)}, u32[]{:S(2)}) collective-permute-start(bf16[128,1536]{1,0:T(8,128)(2,1)S(1)} %get-tuple-element.96), channel_id=1, source_target_pairs={{0,1},{1,0},{2,3},{3,2},{4,5},{5,4},{6,7},{7,6},{8,9},{9,8},{10,11... | collective-permute-start | bytes 1179656 | tf_op jit(solution)/shard_map/ppermute | solution.py:699
  82.2 3.0 %collective-permute-start.6 = (bf16[256,384]{1,0:T(8,128)(2,1)S(1)}, bf16[256,384]{1,0:T(8,128)(2,1)S(1)}, u32[]{:S(2)}, u32[]{:S(2)}) collective-permute-start(bf16[256,384]{1,0:T(8,128)(2,1)S(1)} %get-tuple-element.98.att0), channel_id=1, source_target_pairs={{0,1},{1,0},{2,3},{3,2},{4,5},{5,4},{6,7},{7,6},{8,9},{9,8},{10,11... | collective-permute-start | bytes 589832 | tf_op jit(solution)/shard_map/ppermute | solution.py:699
  82.7 2.5 %collective-permute-start.8 = (bf16[256,384]{1,0:T(8,128)(2,1)S(1)}, bf16[256,384]{1,0:T(8,128)(2,1)S(1)}, u32[]{:S(2)}, u32[]{:S(2)}) collective-permute-start(bf16[256,384]{1,0:T(8,128)(2,1)S(1)} %collective-permute-done.7.att2), channel_id=1, source_target_pairs={{0,1},{1,0},{2,3},{3,2},{4,5},{5,4},{6,7},{7,6},{8,9},{9,8},{10,11... | collective-permute-start | bytes 589832 | tf_op jit(solution)/shard_map/ppermute | solution.py:699
  84.0 7.0 %collective-permute-start.10 = (bf16[64,1536]{1,0:T(8,128)(2,1)S(1)}, bf16[64,1536]{1,0:T(8,128)(2,1)S(1)}, u32[]{:S(2)}, u32[]{:S(2)}) collective-permute-start(bf16[64,1536]{1,0:T(8,128)(2,1)S(1)} %get-tuple-element.107), channel_id=1, source_target_pairs={{0,2},{1,3},{2,0},{3,1},{4,6},{5,7},{6,4},{7,5},{8,10},{9,11},{10,... | collective-permute-start | bytes 589832 | tf_op jit(solution)/shard_map/ppermute | solution.py:703
  91.0 1.7 %collective-permute-start.13 = (bf16[128,1536]{1,0:T(8,128)(2,1)S(1)}, bf16[128,1536]{1,0:T(8,128)(2,1)S(1)}, u32[]{:S(2)}, u32[]{:S(2)}) collective-permute-start(bf16[128,1536]{1,0:T(8,128)(2,1)S(1)} %get-tuple-element.106), channel_id=1, source_target_pairs={{0,1},{1,0},{2,3},{3,2},{4,5},{5,4},{6,7},{7,6},{8,9},{9,8},{10,11... | collective-permute-start | bytes 1179656 | tf_op jit(solution)/shard_map/ppermute | solution.py:699
  91.0 7.7 %collective-permute-start.11 = (bf16[64,1536]{1,0:T(8,128)(2,1)S(1)}, bf16[64,1536]{1,0:T(8,128)(2,1)S(1)}, u32[]{:S(2)}, u32[]{:S(2)}) collective-permute-start(bf16[64,1536]{1,0:T(8,128)(2,1)S(1)} %get-tuple-element.108), channel_id=1, source_target_pairs={{0,2},{1,3},{2,0},{3,1},{4,6},{5,7},{6,4},{7,5},{8,10},{9,11},{10,... | collective-permute-start | bytes 589832 | tf_op jit(solution)/shard_map/ppermute | solution.py:703
  92.9 13.9 %collective-permute-start.14 = (bf16[128,1536]{1,0:T(8,128)(2,1)S(1)}, bf16[128,1536]{1,0:T(8,128)(2,1)S(1)}, u32[]{:S(2)}, u32[]{:S(2)}) collective-permute-start(bf16[128,1536]{1,0:T(8,128)(2,1)S(1)} %add_convert_fusion.1), channel_id=1, source_target_pairs={{0,2},{1,3},{2,0},{3,1},{4,6},{5,7},{6,4},{7,5},{8,10},{9,11},{10,... | collective-permute-start | bytes 1179656 | tf_op jit(solution)/shard_map/ppermute | solution.py:703
  98.9 8.1 %collective-permute-start.12 = (bf16[128,1536]{1,0:T(8,128)(2,1)S(1)}, bf16[128,1536]{1,0:T(8,128)(2,1)S(1)}, u32[]{:S(2)}, u32[]{:S(2)}) collective-permute-start(bf16[128,1536]{1,0:T(8,128)(2,1)S(1)} %add_convert_fusion.2.refs_0_), channel_id=1, source_target_pairs={{0,1},{1,0},{2,3},{3,2},{4,5},{5,4},{6,7},{7,6},{8,9},{9,8},{10,11... | collective-permute-start | bytes 1179656 | tf_op jit(solution)/shard_map/ppermute | solution.py:699
  106.9 1.8 %collective-permute-start.15 = (bf16[128,1536]{1,0:T(8,128)(2,1)S(1)}, bf16[128,1536]{1,0:T(8,128)(2,1)S(1)}, u32[]{:S(2)}, u32[]{:S(2)}) collective-permute-start(bf16[128,1536]{1,0:T(8,128)(2,1)S(1)} %add_convert_fusion.refs_2_), channel_id=1, source_target_pairs={{0,1},{1,0},{2,3},{3,2},{4,5},{5,4},{6,7},{7,6},{8,9},{9,8},{10,11... | collective-permute-start | bytes 1179656 | tf_op jit(solution)/shard_map/ppermute | solution.py:699

commit v11 on v10

--- a/solution.py
+++ b/solution.py
@@ -521,9 +521,13 @@
 
 
 def merge_kernel(capacity, steps, part, heads, table_ref, back_ref, log_hbm, average_hbm, *refs):
-    top_ref, total_ref, numer_ref, tops_ref, sems, load_sems = refs[-6:]
-    count = load_sems.shape[0]
-    sources, (out_ref, *targets) = refs[:count], refs[count:-6]
+    sources, targets, load_sems = [], [], None
+    if len(refs) > 6:
+        *refs, load_sems = refs
+        count = load_sems.shape[0]
+        sources, refs = refs[:count], refs[count:]
+        targets, refs = refs[1:-5], (refs[0], *refs[-5:])
+    out_ref, top_ref, total_ref, numer_ref, tops_ref, sems = refs
     groups = back_ref.shape[0]
     inner = heads * 64
     rows = steps * BEAMS
@@ -531,7 +535,7 @@
     state = (top_ref, total_ref, numer_ref)
     copies = start_all([(log_hbm.at[part], top_ref), (average_hbm.at[part], numer_ref)], sems)
     pairs = []
-    if part == 0:
+    if sources:
         weight_ref, *targets = targets
         height = sources[0].shape[0]
         head = lax.axis_index("head")
@@ -586,7 +590,7 @@
     vmem = pl.BlockSpec(memory_space=pltpu.VMEM)
     hbm = pl.BlockSpec(memory_space=pltpu.HBM)
     anywhere = pl.BlockSpec(memory_space=pl.ANY)
-    mixes = sources[:4] if part == 0 else []
+    mixes = sources[:4]
     others = sources[len(mixes) :]
     kept = [jax.ShapeDtypeStruct(x.shape, x.dtype) for x in others]
     if mixes:
@@ -599,8 +603,8 @@
         + [
             pltpu.VMEM((back.shape[0] * span, capacity * inner), f32),
             pltpu.SemaphoreType.DMA((2,)),
-            pltpu.SemaphoreType.DMA((len(sources),)),
-        ],
+        ]
+        + [pltpu.SemaphoreType.DMA((len(sources),))] * bool(sources),
         compiler_params=pltpu.CompilerParams(vmem_limit_bytes=10 * MIB),
         cost_estimate=pl.CostEstimate(
             flops=40 * rows * inner, bytes_accessed=8 * MIB, transcendentals=4 * rows * inner
@@ -670,29 +674,37 @@
     )(*attended, weight, tokens, gain, w_gate, w_up, w_down)
 
 
-def finish_kernel(*refs):
-    parts, out_ref = refs[:-1], refs[-1]
+def finish_kernel(first, half, places, *refs):
+    count = 2 * len(places)
+    parts, out_ref, sems = refs[-2 - count : -2], refs[-2], refs[-1]
     core = lax.axis_index("head") % 2
-    first = 0
-    for index in range(0, len(parts), 2):
-        half = parts[index].shape[0]
-        for part, place in ((parts[index], core), (parts[index + 1], 1 - core)):
-            rows = pl.ds(pl.multiple_of(first + place * half, half), half)
-            out_ref[rows, :] = part[...]
-        first += 2 * half
-
-
-def finish(parts):
+    pairs = []
+    for index, place in enumerate(places):
+        for part, owner in ((parts[2 * index], core), (parts[2 * index + 1], 1 - core)):
+            start = pl.multiple_of(first + owner * half + place, 16)
+            pairs.append((part, out_ref.at[pl.ds(start, part.shape[0])]))
+    for copy in start_all(pairs, sems):
+        copy.wait()
+
+
+def finish(first, half, pieces, rows, before=()):
     vmem = pl.BlockSpec(memory_space=pltpu.VMEM)
-    rows, width = sum(part.shape[0] for part in parts), parts[0].shape[1]
+    hbm = pl.BlockSpec(memory_space=pltpu.HBM)
+    places, parts = [], []
+    for place, done in pieces:
+        places.append(place)
+        parts.extend([done, swap_core(done)])
+    width = parts[0].shape[1]
     return pl.pallas_call(
-        finish_kernel,
-        in_specs=[vmem] * len(parts),
-        out_specs=vmem,
-        out_shape=jax.ShapeDtypeStruct((rows, width), parts[0].dtype),
-        compiler_params=pltpu.CompilerParams(vmem_limit_bytes=12 * MIB),
+        functools.partial(finish_kernel, first, half, places),
+        in_specs=[hbm] * len(before) + [vmem] * len(parts),
+        out_specs=hbm,
+        out_shape=pltpu.HBM((rows, width), parts[0].dtype),
+        input_output_aliases={0: 0} if before else {},
+        scratch_shapes=[pltpu.SemaphoreType.DMA((len(parts),))],
+        compiler_params=pltpu.CompilerParams(vmem_limit_bytes=8 * MIB),
         name="finish",
-    )(*parts)
+    )(*[in_hbm(x) for x in before], *parts)
 
 
 def swap_core(value):
@@ -722,29 +734,28 @@
     ids = exchange(jnp.broadcast_to(page_request, (groups, 1, page_request.shape[0])))
     q_near, q, normed = queries_of(tokens, gain_attn, w_query)
     table, asked = ask(page_request, ids, q_near, span, capacity)
-    asked, w_out = lax.optimization_barrier((asked, w_out))
-    w_out_far = swap_chip(w_out)
     asked_rows = exchange(asked.reshape(groups, capacity * span, inner)).reshape(asked.shape)
+    asked, q = lax.optimization_barrier((asked, q))
     own = own_pages(page_request, page_fill, q, keys_pool, values_pool, decay, span)
+    own, w_sent = lax.optimization_barrier((own, w_out))
+    w_out_far = swap_chip(w_sent)
     asked_rows, own = lax.optimization_barrier((asked_rows, own))
     payload = hosted_pages(
         page_request, page_fill, asked_rows, keys_pool, values_pool, decay, groups, capacity, local_count
     )
     payload, normed = lax.optimization_barrier((payload, normed))
-    normed, w_out_far = lax.optimization_barrier((normed, w_out_far))
     back = exchange(payload)
     logs, averages = fresh(parents, forget_bias, normed, w_key, w_value, w_forget, q, own)
+    back, w_out_far = lax.optimization_barrier((back, w_out_far))
     mixes = [w_out, swap_core(w_out), w_out_far, swap_core(w_out_far)]
-    logs, mixes = lax.optimization_barrier((logs, mixes))
 
     flat = tokens.reshape(steps * rows, width)
     each = steps // PARTS
     sums = (table, back, logs, averages, each, capacity)
-    here, weight = merge(0, *sums, mixes)
-    heres = [here]
+    heres = list(merge(0, *sums, []))
     back, heres[0] = lax.optimization_barrier((back, heres[0]))
     sums = (table, back, logs, averages, each, capacity)
-    here, w_gate, w_up, w_down, flat = merge(1, *sums, [w_gate, w_up, w_down, flat])
+    here, weight, w_gate, w_up, w_down, flat = merge(1, *sums, mixes + [w_gate, w_up, w_down, flat])
     heres.append(here)
     fars = [swap_chip(here) for here in heres]
     fars[0], heres[1] = lax.optimization_barrier((fars[0], heres[1]))
@@ -770,13 +781,24 @@
     residual[1], mine, other = block_of(1)
     other, far_most = lax.optimization_barrier((other, far_most))
     chip[1] = chip_sum(mine, other)
-    far_chip = [jnp.concatenate([far_most, far_rest], axis=0), swap_chip(chip[1])]
-    parts = []
-    for index in range(PARTS):
-        both = chip[index].astype(f32) + far_chip[index].astype(f32)
-        done = (residual[index] + both).astype(bf16)
-        parts.extend([done, swap_core(done)])
-    return finish(parts).reshape(steps, rows, width)
+    half = chip[1].shape[0]
+    cut = half // 4 * 3
+    far_first, far_last = swap_chip(chip[1][:cut]), swap_chip(chip[1][cut:])
+
+    def done(residual, chip, far):
+        return (residual + (chip.astype(f32) + far.astype(f32))).astype(bf16)
+
+    pieces = [
+        (0, done(residual[0][:most], chip_most, far_most)),
+        (most, done(residual[0][most:], chip_rest, far_rest)),
+    ]
+    result = finish(0, half, pieces, steps * rows)
+    pieces = [
+        (0, done(residual[1][:cut], chip[1][:cut], far_first)),
+        (cut, done(residual[1][cut:], chip[1][cut:], far_last)),
+    ]
+    result = finish(2 * half, half, pieces, steps * rows, [result])
+    return result.reshape(steps, rows, width)
 
 
 def solution(mesh):

time: 110 us -> 115 us (1.045)
  waiting for transfers between devices: 39.1 us -> 41.2 us
    ppermute x6 -> x7, waiting for transfers between devices: 16.6 us -> 23.8 us  [swap_chip(): return lax.ppermute(value, 'head', [(i, i ^ 2) for i in range(4)])]
    all_to_all x3, waiting for transfers between devices: 18.5 us -> 15 us  [exchange(): lax.all_to_all(value, 'group', split_axis=0, concat_axis=0, tiled=True)]
    ppermute x10 -> x12, waiting for transfers between devices: 4 us -> 2.45 us  [swap_core(): return lax.ppermute(value, 'head', [(i, i ^ 1) for i in range(4)])]
    ppermute x6 -> x7, starting transfers between devices: 7.1 us -> 8.63 us  [swap_chip(): return lax.ppermute(value, 'head', [(i, i ^ 2) for i in range(4)])]
    all_to_all x3, starting transfers between devices: 16.2 us -> 14.9 us  [exchange(): lax.all_to_all(value, 'group', split_axis=0, concat_axis=0, tiled=True)]
  transfers between devices with their start and end apart: 19 -> 22, of which waited for: 12 -> 13; matrix products, arithmetic and copies ran while one was open for 0% -> 0% of each run, Pallas kernels for 34% -> 37%
where the time goes in v11:
time: 115 us; the launch traced here: 114 us
  Pallas kernels  44.7 us (39%)
  waiting for transfers between devices  41.2 us (36%)
  starting transfers between devices  25.3 us (22%)
  local copies, waits for them, and re-layouts  2.09 us (2%)
    ppermute x7, waiting for transfers between devices, swap_chip(): return lax.ppermute(value, 'head', [(i, i ^ 2) for i in range(4)])  23.8 us
    all_to_all x3, waiting for transfers between devices, exchange(): lax.all_to_all(value, 'group', split_axis=0, concat_axis=0, tiled=True)  15 us
    all_to_all x3, starting transfers between devices, exchange(): lax.all_to_all(value, 'group', split_axis=0, concat_axis=0, tiled=True)  14.9 us
    pallas_call x1, Pallas kernels, fresh(): pl.pallas_call(fresh_kernel, in_specs=[vmem, vmem] + [hbm] * len(big), ou...  8.93 us
    pallas_call x2, Pallas kernels, block(): pl.pallas_call(functools.partial(block_kernel, first), in_specs=[vmem] *...  8.79 us
    ppermute x7, starting transfers between devices, swap_chip(): return lax.ppermute(value, 'head', [(i, i ^ 2) for i in range(4)])  8.63 us
    pallas_call x2, Pallas kernels, merge(): pl.pallas_call(functools.partial(merge_kernel, capacity, steps, part, inn...  7.91 us
    pallas_call x1, Pallas kernels, own_pages(): pl.pallas_call(own_kernel, grid=(OWNED_SLOTS // PAGE_BLOCK,), in_specs=[S...  7.02 us
  transfers between devices with their start and end apart: 22, of which 13 were waited for; matrix products, arithmetic and copies ran while one was open for 0% of the time, Pallas kernels for 37%

profile of v11, /device:TPU:0, one launch (start us, length us, event | category | flops | bytes accessed | tf_op | source)
XLA Modules:
  0.0 114.1 jit_solution(15335407378928041374)
XLA Ops:
  0.0 1.3 %broadcast_in_dim.3 = s32[8,1,48]{2,1,0:T(1,128)} broadcast(s32[48]{0:T(128)} %request_ref.5), dimensions={2} | broadcast | bytes 1728 | tf_op jit(solution)/shard_map/broadcast_in_dim | solution.py:734
  1.3 7.3 %all-to-all-start = ((s32[8,1,48]{2,1,0:T(1,128)}), s32[8,1,48]{2,1,0:T(1,128)S(1)}, u32[]{:S(2)}, u32[]{:S(2)}) async-start(s32[8,1,48]{2,1,0:T(1,128)} %broadcast_in_dim.3), calls=%async_computation | async-start | bytes 8192 | tf_op jit(solution)/shard_map/all_to_all | solution.py:732
  9.3 3.7 %queries.1 = (bf16[512,384]{1,0:T(8,128)(2,1)S(1)}, bf16[512,384]{1,0:T(8,128)(2,1)}, bf16[512,1536]{1,0:T(8,128)(2,1)}) custom-call(bf16[4,128,1536]{2,1,0:T(8,128)(2,1)} %tokens_hbm.1, f32[1536]{0:T(1024)S(1)} %copy-done.3, bf16[384,1536]{1,0:T(8,128)(2,1)} %wq_hbm.1), custom_call_target="tpu_custom_call" | custom-call | flops 603979776 | bytes 6291456 | tf_op jit(solution)/shard_map/queries/pallas_call | solution.py:124
  13.0 2.1 %all-to-all-done.ids_ref = s32[8,1,48]{2,1,0:T(1,128)S(1)} async-done(((s32[8,1,48]{2,1,0:T(1,128)}), s32[8,1,48]{2,1,0:T(1,128)S(1)}, u32[]{:S(2)}, u32[]{:S(2)}) %all-to-all-start) | async-done | bytes 1568 | tf_op jit(solution)/shard_map/all_to_all | solution.py:732
  15.1 2.0 %ask.1 = (s32[24]{0:T(128)S(1)}, bf16[24,32,384]{2,1,0:T(8,128)(2,1)}) custom-call(s32[48]{0:T(128)S(1)} %copy-done.4, s32[8,1,48]{2,1,0:T(1,128)S(1)} %all-to-all-done.ids_ref, bf16[512,384]{1,0:T(8,128)(2,1)S(1)} %get-tuple-element.52.q_ref), custom_call_target="tpu_custom_call" | custom-call | tf_op jit(solution)/shard_map/ask/pallas_call | solution.py:161
  17.0 4.0 %all-to-all-start.1 = ((bf16[8,96,384]{2,1,0:T(8,128)(2,1)}), bf16[8,96,384]{2,1,0:T(8,128)(2,1)S(1)}, u32[]{:S(2)}, u32[]{:S(2)}) async-start(bf16[8,96,384]{2,1,0:T(8,128)(2,1)} %bitcast), calls=%async_computation.1 | async-start | bytes 1179648 | tf_op jit(solution)/shard_map/all_to_all | solution.py:732
  21.0 7.0 %own_pages.1 = (f32[512,384]{1,0:T(8,128)}, f32[512,384]{1,0:T(8,128)}, f32[512,384]{1,0:T(8,128)}) custom-call(s32[48]{0:T(128)S(1)} %copy-done.4, s32[48]{0:T(128)S(1)} %copy-done.6, bf16[512,384]{1,0:T(8,128)(2,1)} %get-tuple-element.55.q_ref.q_hbm, bf16[48,384,128]{2,1,0:T(8,128)(2,1)} %keys_ref.3, bf16[48,384,128]{2,1,0:T(8,128)(2,1)} %values_ref.3, ...), custom_call_target="tpu_custom_call" | custom-call | flops 805306368 | bytes 6291456 | tf_op jit(solution)/shard_map/own_pages/pallas_call | solution.py:441
  28.0 1.5 %collective-permute-start = (bf16[384,1536]{1,0:T(8,128)(2,1)S(1)}, bf16[384,1536]{1,0:T(8,128)(2,1)S(1)}, u32[]{:S(2)}, u32[]{:S(2)}) collective-permute-start(bf16[384,1536]{1,0:T(8,128)(2,1)S(1)} %copy-done), channel_id=1, source_target_pairs={{0,2},{1,3},{2,0},{3,1},{4,6},{5,7},{6,4},{7,5},{8,10},{9,11},{10,... | collective-permute-start | bytes 3538952 | tf_op jit(solution)/shard_map/ppermute | solution.py:715
  29.5 6.8 %all-to-all-done.1 = bf16[8,96,384]{2,1,0:T(8,128)(2,1)S(1)} async-done(((bf16[8,96,384]{2,1,0:T(8,128)(2,1)}), bf16[8,96,384]{2,1,0:T(8,128)(2,1)S(1)}, u32[]{:S(2)}, u32[]{:S(2)}) %all-to-all-start.1) | async-done | bytes 589856 | tf_op jit(solution)/shard_map/all_to_all | solution.py:732
  36.4 4.5 %hosted_pages.1 = bf16[8,304,128]{2,1,0:T(8,128)(2,1)} custom-call(s32[48]{0:T(128)S(1)} %copy-done.4, s32[48]{0:T(128)S(1)} %copy-done.6, bf16[24,32,384]{2,1,0:T(8,128)(2,1)S(1)} %bitcast.9, bf16[48,384,128]{2,1,0:T(8,128)(2,1)} %keys_ref.3, bf16[48,384,128]{2,1,0:T(8,128)(2,1)} %values_ref.3, bf16[6,48,128]{2,1,0:T(8,128)(2,1)S(1)} %bitcast.11), custom_call_target="tpu_custom_call" | custom-call | flops 402653184 | bytes 3145728 | tf_op jit(solution)/shard_map/hosted_pages/pallas_call | solution.py:507
  40.9 3.6 %all-to-all-start.2 = ((bf16[8,304,128]{2,1,0:T(8,128)(2,1)}), bf16[8,304,128]{2,1,0:T(8,128)(2,1)S(1)}, u32[]{:S(2)}, u32[]{:S(2)}) async-start(bf16[8,304,128]{2,1,0:T(8,128)(2,1)} %hosted_pages.1), calls=%async_computation.2 | async-start | bytes 1245184 | tf_op jit(solution)/shard_map/all_to_all | solution.py:732
  44.6 10.3 %collective-permute-done.refs_2_ = bf16[384,1536]{1,0:T(8,128)(2,1)S(1)} collective-permute-done((bf16[384,1536]{1,0:T(8,128)(2,1)S(1)}, bf16[384,1536]{1,0:T(8,128)(2,1)S(1)}, u32[]{:S(2)}, u32[]{:S(2)}) %collective-permute-start) | collective-permute-done | bytes 1179680 | tf_op jit(solution)/shard_map/ppermute | solution.py:715
  54.9 6.1 %all-to-all-done.2.back_ref = bf16[8,304,128]{2,1,0:T(8,128)(2,1)S(1)} async-done(((bf16[8,304,128]{2,1,0:T(8,128)(2,1)}), bf16[8,304,128]{2,1,0:T(8,128)(2,1)S(1)}, u32[]{:S(2)}, u32[]{:S(2)}) %all-to-all-start.2) | async-done | bytes 622624 | tf_op jit(solution)/shard_map/all_to_all | solution.py:732
  61.0 8.9 %fresh.1 = (f32[2,16,16,384]{3,2,1,0:T(8,128)}, f32[2,16,16,384]{3,2,1,0:T(8,128)}) custom-call(s32[3,128]{1,0:T(4,128)S(1)} %copy-done.5, f32[1,6]{1,0:T(1,128)S(1)} %bitcast.12, bf16[512,1536]{1,0:T(8,128)(2,1)} %get-tuple-element.68.normed_hbm, bf16[384,1536]{1,0:T(8,128)(2,1)} %wk_hbm.1, bf16[384,1536]{1,0:T(8,128)(2,1)} %wv_hbm.1, ...), custom_call_target="tpu_custom_call" | custom-call | flops 1207959552 | bytes 12582912 | tf_op jit(solution)/shard_map/fresh/pallas_call | solution.py:326
  70.0 2.0 %merge.2.att0 = bf16[256,384]{1,0:T(8,128)(2,1)S(1)} custom-call(s32[24]{0:T(128)S(1)} %get-tuple-element.67.table_ref, bf16[8,304,128]{2,1,0:T(8,128)(2,1)S(1)} %all-to-all-done.2.back_ref, f32[2,256,384]{2,1,0:T(8,128)} %bitcast.14, f32[2,256,384]{2,1,0:T(8,128)} %bitcast.16), custom_call_target="tpu_custom_call" | custom-call | flops 3932160 | bytes 8388608 | tf_op jit(solution)/shard_map/merge/pallas_call | solution.py:598
  72.0 1.6 %collective-permute-start.2 = (bf16[256,384]{1,0:T(8,128)(2,1)S(1)}, bf16[256,384]{1,0:T(8,128)(2,1)S(1)}, u32[]{:S(2)}, u32[]{:S(2)}) collective-permute-start(bf16[256,384]{1,0:T(8,128)(2,1)S(1)} %merge.2.att0), channel_id=1, source_target_pairs={{0,2},{1,3},{2,0},{3,1},{4,6},{5,7},{6,4},{7,5},{8,10},{9,11},{10,... | collective-permute-start | bytes 589832 | tf_op jit(solution)/shard_map/ppermute | solution.py:715
  73.8 5.9 %merge.3 = (bf16[256,384]{1,0:T(8,128)(2,1)S(1)}, bf16[1536,1536]{1,0:T(8,128)(2,1)S(1)}, bf16[1536,1024]{1,0:T(8,128)(2,1)S(1)}, bf16[1536,1024]{1,0:T(8,128)(2...) custom-call(s32[24]{0:T(128)S(1)} %get-tuple-element.67.table_ref, ...), custom_call_target="tpu_custom_call" | custom-call | flops 3932160 | bytes 8388608 | tf_op jit(solution)/shard_map/merge/pallas_call | solution.py:598
  80.0 0.8 collective-permute-start.6
  81.2 4.4 %block.2 = (f32[128,1536]{1,0:T(8,128)S(1)}, f32[128,1536]{1,0:T(8,128)S(1)}, bf16[128,1536]{1,0:T(8,128)(2,1)S(1)}) custom-call(bf16[256,384]{1,0:T(8,128)(2,1)S(1)} %merge.2.att0, bf16[256,384]{1,0:T(8,128)(2,1)S(1)} %collective-permute-done.1.att1, bf16[256,384]{1,0:T(8,128)(2,1)S(1)} %collective-permute-done.2.att2, ...), custom_call_target="tpu_custom_call" | custom-call | tf_op jit(solution)/shard_map/block/pallas_call | solution.py:659
  85.6 1.5 %collective-permute-done.6.att2 = bf16[256,384]{1,0:T(8,128)(2,1)S(1)} collective-permute-done((bf16[256,384]{1,0:T(8,128)(2,1)S(1)}, bf16[256,384]{1,0:T(8,128)(2,1)S(1)}, u32[]{:S(2)}, u32[]{:S(2)}) %collective-permute-start.6) | collective-permute-done | bytes 196640 | tf_op jit(solution)/shard_map/ppermute | solution.py:715
  87.6 1.2 %collective-permute-done.7 = bf16[128,1536]{1,0:T(8,128)(2,1)S(1)} collective-permute-done((bf16[128,1536]{1,0:T(8,128)(2,1)S(1)}, bf16[128,1536]{1,0:T(8,128)(2,1)S(1)}, u32[]{:S(2)}, u32[]{:S(2)}) %collective-permute-start.7) | collective-permute-done | bytes 393248 | tf_op jit(solution)/shard_map/ppermute | solution.py:711
  88.9 1.2 %collective-permute-start.10 = (bf16[64,1536]{1,0:T(8,128)(2,1)S(1)}, bf16[64,1536]{1,0:T(8,128)(2,1)S(1)}, u32[]{:S(2)}, u32[]{:S(2)}) collective-permute-start(bf16[64,1536]{1,0:T(8,128)(2,1)S(1)} %get-tuple-element.102), channel_id=1, source_target_pairs={{0,2},{1,3},{2,0},{3,1},{4,6},{5,7},{6,4},{7,5},{8,10},{9,11},{10,... | collective-permute-start | bytes 589832 | tf_op jit(solution)/shard_map/ppermute | solution.py:715
  90.1 4.4 %block.3 = (f32[128,1536]{1,0:T(8,128)S(1)}, f32[128,1536]{1,0:T(8,128)S(1)}, bf16[128,1536]{1,0:T(8,128)(2,1)S(1)}) custom-call(bf16[256,384]{1,0:T(8,128)(2,1)S(1)} %get-tuple-element.90.att0, bf16[256,384]{1,0:T(8,128)(2,1)S(1)} %collective-permute-done.8.att1, bf16[256,384]{1,0:T(8,128)(2,1)S(1)} %collective-permute-done.6.att2, ...), custom_call_target="tpu_custom_call" | custom-call | tf_op jit(solution)/shard_map/block/pallas_call | solution.py:659
  94.5 1.4 %collective-permute-done.10 = bf16[64,1536]{1,0:T(8,128)(2,1)S(1)} collective-permute-done((bf16[64,1536]{1,0:T(8,128)(2,1)S(1)}, bf16[64,1536]{1,0:T(8,128)(2,1)S(1)}, u32[]{:S(2)}, u32[]{:S(2)}) %collective-permute-start.10) | collective-permute-done | bytes 196640 | tf_op jit(solution)/shard_map/ppermute | solution.py:715
  95.9 1.1 collective-permute-start.12
  97.8 1.2 %collective-permute-start.15 = (bf16[96,1536]{1,0:T(8,128)(2,1)S(1)}, bf16[96,1536]{1,0:T(8,128)(2,1)S(1)}, u32[]{:S(2)}, u32[]{:S(2)}) collective-permute-start(bf16[96,1536]{1,0:T(8,128)(2,1)S(1)} %slice.36), channel_id=1, source_target_pairs={{0,2},{1,3},{2,0},{3,1},{4,6},{5,7},{6,4},{7,5},{8,10},{9,11},{10,... | collective-permute-start | bytes 884744 | tf_op jit(solution)/shard_map/ppermute | solution.py:715
  99.0 4.7 %collective-permute-done.12 = bf16[64,1536]{1,0:T(8,128)(2,1)S(1)} collective-permute-done((bf16[64,1536]{1,0:T(8,128)(2,1)S(1)}, bf16[64,1536]{1,0:T(8,128)(2,1)S(1)}, u32[]{:S(2)}, u32[]{:S(2)}) %collective-permute-start.12) | collective-permute-done | bytes 196640 | tf_op jit(solution)/shard_map/ppermute | solution.py:715
  104.3 1.2 %collective-permute-start.17 = (bf16[32,1536]{1,0:T(8,128)(2,1)S(1)}, bf16[32,1536]{1,0:T(8,128)(2,1)S(1)}, u32[]{:S(2)}, u32[]{:S(2)}) collective-permute-start(bf16[32,1536]{1,0:T(8,128)(2,1)S(1)} %slice.37), channel_id=1, source_target_pairs={{0,2},{1,3},{2,0},{3,1},{4,6},{5,7},{6,4},{7,5},{8,10},{9,11},{10,... | collective-permute-start | bytes 294920 | tf_op jit(solution)/shard_map/ppermute | solution.py:715
  105.5 4.4 %collective-permute-done.15 = bf16[96,1536]{1,0:T(8,128)(2,1)S(1)} collective-permute-done((bf16[96,1536]{1,0:T(8,128)(2,1)S(1)}, bf16[96,1536]{1,0:T(8,128)(2,1)S(1)}, u32[]{:S(2)}, u32[]{:S(2)}) %collective-permute-start.15) | collective-permute-done | bytes 294944 | tf_op jit(solution)/shard_map/ppermute | solution.py:715
  110.1 1.5 %collective-permute-done.17 = bf16[32,1536]{1,0:T(8,128)(2,1)S(1)} collective-permute-done((bf16[32,1536]{1,0:T(8,128)(2,1)S(1)}, bf16[32,1536]{1,0:T(8,128)(2,1)S(1)}, u32[]{:S(2)}, u32[]{:S(2)}) %collective-permute-start.17) | collective-permute-done | bytes 98336 | tf_op jit(solution)/shard_map/ppermute | solution.py:715
  111.8 0.9 finish.2.refs_0_
  113.1 0.9 finish.3
  (48 shorter events, 4.3 us)
Async XLA Ops:
  0.0 15.1 %copy-start.4 = (s32[48]{0:T(128)S(1)}, s32[48]{0:T(128)}, u32[]{:S(2)}) copy-start(s32[48]{0:T(128)} %request_ref.5) | copy-start | bytes 580
  1.3 13.7 %all-to-all-start = ((s32[8,1,48]{2,1,0:T(1,128)}), s32[8,1,48]{2,1,0:T(1,128)S(1)}, u32[]{:S(2)}, u32[]{:S(2)}) async-start(s32[8,1,48]{2,1,0:T(1,128)} %broadcast_in_dim.3), calls=%async_computation | async-start | bytes 8192 | tf_op jit(solution)/shard_map/all_to_all | solution.py:732
  8.6 0.7 copy-start.3
  9.3 11.7 %copy-start.1 = (bf16[48,6,128]{2,0,1:T(8,128)(2,1)S(1)}, bf16[48,6,128]{2,0,1:T(8,128)(2,1)}, u32[]{:S(2)}) copy-start(bf16[48,6,128]{2,0,1:T(8,128)(2,1)} %param.24) | copy-start | bytes 221188
  9.3 11.7 %copy-start.6 = (s32[48]{0:T(128)S(1)}, s32[48]{0:T(128)}, u32[]{:S(2)}) copy-start(s32[48]{0:T(128)} %fill_ref.3) | copy-start | bytes 580
  17.0 19.4 %all-to-all-start.1 = ((bf16[8,96,384]{2,1,0:T(8,128)(2,1)}), bf16[8,96,384]{2,1,0:T(8,128)(2,1)S(1)}, u32[]{:S(2)}, u32[]{:S(2)}) async-start(bf16[8,96,384]{2,1,0:T(8,128)(2,1)} %bitcast), calls=%async_computation.1 | async-start | bytes 1179648 | tf_op jit(solution)/shard_map/all_to_all | solution.py:732
  21.0 7.0 %copy-start = (bf16[384,1536]{1,0:T(8,128)(2,1)S(1)}, bf16[384,1536]{1,0:T(8,128)(2,1)}, u32[]{:S(2)}) copy-start(bf16[384,1536]{1,0:T(8,128)(2,1)} %refs_0_.1) | copy-start | bytes 3538948
  28.0 26.9 %collective-permute-start = (bf16[384,1536]{1,0:T(8,128)(2,1)S(1)}, bf16[384,1536]{1,0:T(8,128)(2,1)S(1)}, u32[]{:S(2)}, u32[]{:S(2)}) collective-permute-start(bf16[384,1536]{1,0:T(8,128)(2,1)S(1)} %copy-done), channel_id=1, source_target_pairs={{0,2},{1,3},{2,0},{3,1},{4,6},{5,7},{6,4},{7,5},{8,10},{9,11},{10,... | collective-permute-start | bytes 3538952 | tf_op jit(solution)/shard_map/ppermute | solution.py:715
  36.4 24.6 %copy-start.5 = (s32[3,128]{1,0:T(4,128)S(1)}, s32[3,128]{1,0:T(4,128)}, u32[]{:S(2)}) copy-start(s32[3,128]{1,0:T(4,128)} %parents_ref.1) | copy-start | bytes 4612
  36.4 24.6 %copy-start.7 = (f32[6]{0:T(128)S(1)}, f32[6]{0:T(128)}, u32[]{:S(2)}) copy-start(f32[6]{0:T(128)} %param.30) | copy-start | bytes 76
  40.9 20.1 %all-to-all-start.2 = ((bf16[8,304,128]{2,1,0:T(8,128)(2,1)}), bf16[8,304,128]{2,1,0:T(8,128)(2,1)S(1)}, u32[]{:S(2)}, u32[]{:S(2)}) async-start(bf16[8,304,128]{2,1,0:T(8,128)(2,1)} %hosted_pages.1), calls=%async_computation.2 | async-start | bytes 1245184 | tf_op jit(solution)/shard_map/all_to_all | solution.py:732
  44.5 29.2 %collective-permute-start.3 = (bf16[384,1536]{1,0:T(8,128)(2,1)S(1)}, bf16[384,1536]{1,0:T(8,128)(2,1)}, u32[]{:S(2)}, u32[]{:S(2)}) collective-permute-start(bf16[384,1536]{1,0:T(8,128)(2,1)S(1)} %copy-done), channel_id=1, source_target_pairs={{0,1},{1,0},{2,3},{3,2},{4,5},{5,4},{6,7},{7,6},{8,9},{9,8},{10,11... | collective-permute-start | bytes 3538952 | tf_op jit(solution)/shard_map/ppermute | solution.py:711
  61.0 12.8 %collective-permute-start.4 = (bf16[384,1536]{1,0:T(8,128)(2,1)S(1)}, bf16[384,1536]{1,0:T(8,128)(2,1)S(1)}, u32[]{:S(2)}, u32[]{:S(2)}) collective-permute-start(bf16[384,1536]{1,0:T(8,128)(2,1)S(1)} %collective-permute-done.refs_2_), channel_id=1, source_target_pairs={{0,1},{1,0},{2,3},{3,2},{4,5},{5,4},{6,7},{7,6},{8,9},{9,8},{10,11... | collective-permute-start | bytes 3538952 | tf_op jit(solution)/shard_map/ppermute | solution.py:711
  72.0 7.7 %collective-permute-start.2 = (bf16[256,384]{1,0:T(8,128)(2,1)S(1)}, bf16[256,384]{1,0:T(8,128)(2,1)S(1)}, u32[]{:S(2)}, u32[]{:S(2)}) collective-permute-start(bf16[256,384]{1,0:T(8,128)(2,1)S(1)} %merge.2.att0), channel_id=1, source_target_pairs={{0,2},{1,3},{2,0},{3,1},{4,6},{5,7},{6,4},{7,5},{8,10},{9,11},{10,... | collective-permute-start | bytes 589832 | tf_op jit(solution)/shard_map/ppermute | solution.py:715
  73.6 7.3 %collective-permute-start.1 = (bf16[256,384]{1,0:T(8,128)(2,1)S(1)}, bf16[256,384]{1,0:T(8,128)(2,1)S(1)}, u32[]{:S(2)}, u32[]{:S(2)}) collective-permute-start(bf16[256,384]{1,0:T(8,128)(2,1)S(1)} %merge.2.att0), channel_id=1, source_target_pairs={{0,1},{1,0},{2,3},{3,2},{4,5},{5,4},{6,7},{7,6},{8,9},{9,8},{10,11... | collective-permute-start | bytes 589832 | tf_op jit(solution)/shard_map/ppermute | solution.py:711
  73.8 7.4 %copy-start.2 = (f32[1536]{0:T(1024)S(1)}, f32[1536]{0:T(1024)}, u32[]{:S(2)}) copy-start(f32[1536]{0:T(1024)} %gain_ref.5) | copy-start | bytes 18436
  79.7 1.5 %collective-permute-start.5 = (bf16[256,384]{1,0:T(8,128)(2,1)S(1)}, bf16[256,384]{1,0:T(8,128)(2,1)S(1)}, u32[]{:S(2)}, u32[]{:S(2)}) collective-permute-start(bf16[256,384]{1,0:T(8,128)(2,1)S(1)} %collective-permute-done.2.att2), channel_id=1, source_target_pairs={{0,1},{1,0},{2,3},{3,2},{4,5},{5,4},{6,7},{7,6},{8,9},{9,8},{10,11... | collective-permute-start | bytes 589832 | tf_op jit(solution)/shard_map/ppermute | solution.py:711
  80.0 7.0 %collective-permute-start.6 = (bf16[256,384]{1,0:T(8,128)(2,1)S(1)}, bf16[256,384]{1,0:T(8,128)(2,1)S(1)}, u32[]{:S(2)}, u32[]{:S(2)}) collective-permute-start(bf16[256,384]{1,0:T(8,128)(2,1)S(1)} %get-tuple-element.90.att0), channel_id=1, source_target_pairs={{0,2},{1,3},{2,0},{3,1},{4,6},{5,7},{6,4},{7,5},{8,10},{9,11},{10,... | collective-permute-start | bytes 589832 | tf_op jit(solution)/shard_map/ppermute | solution.py:715
  87.1 1.7 %collective-permute-start.7 = (bf16[128,1536]{1,0:T(8,128)(2,1)S(1)}, bf16[128,1536]{1,0:T(8,128)(2,1)S(1)}, u32[]{:S(2)}, u32[]{:S(2)}) collective-permute-start(bf16[128,1536]{1,0:T(8,128)(2,1)S(1)} %get-tuple-element.87), channel_id=1, source_target_pairs={{0,1},{1,0},{2,3},{3,2},{4,5},{5,4},{6,7},{7,6},{8,9},{9,8},{10,11... | collective-permute-start | bytes 1179656 | tf_op jit(solution)/shard_map/ppermute | solution.py:711
  87.1 3.0 %collective-permute-start.8 = (bf16[256,384]{1,0:T(8,128)(2,1)S(1)}, bf16[256,384]{1,0:T(8,128)(2,1)S(1)}, u32[]{:S(2)}, u32[]{:S(2)}) collective-permute-start(bf16[256,384]{1,0:T(8,128)(2,1)S(1)} %get-tuple-element.90.att0), channel_id=1, source_target_pairs={{0,1},{1,0},{2,3},{3,2},{4,5},{5,4},{6,7},{7,6},{8,9},{9,8},{10,11... | collective-permute-start | bytes 589832 | tf_op jit(solution)/shard_map/ppermute | solution.py:711
  87.6 2.5 %collective-permute-start.9 = (bf16[256,384]{1,0:T(8,128)(2,1)S(1)}, bf16[256,384]{1,0:T(8,128)(2,1)S(1)}, u32[]{:S(2)}, u32[]{:S(2)}) collective-permute-start(bf16[256,384]{1,0:T(8,128)(2,1)S(1)} %collective-permute-done.6.att2), channel_id=1, source_target_pairs={{0,1},{1,0},{2,3},{3,2},{4,5},{5,4},{6,7},{7,6},{8,9},{9,8},{10,11... | collective-permute-start | bytes 589832 | tf_op jit(solution)/shard_map/ppermute | solution.py:711
  88.9 7.0 %collective-permute-start.10 = (bf16[64,1536]{1,0:T(8,128)(2,1)S(1)}, bf16[64,1536]{1,0:T(8,128)(2,1)S(1)}, u32[]{:S(2)}, u32[]{:S(2)}) collective-permute-start(bf16[64,1536]{1,0:T(8,128)(2,1)S(1)} %get-tuple-element.102), channel_id=1, source_target_pairs={{0,2},{1,3},{2,0},{3,1},{4,6},{5,7},{6,4},{7,5},{8,10},{9,11},{10,... | collective-permute-start | bytes 589832 | tf_op jit(solution)/shard_map/ppermute | solution.py:715
  95.9 1.7 %collective-permute-start.14 = (bf16[128,1536]{1,0:T(8,128)(2,1)S(1)}, bf16[128,1536]{1,0:T(8,128)(2,1)S(1)}, u32[]{:S(2)}, u32[]{:S(2)}) collective-permute-start(bf16[128,1536]{1,0:T(8,128)(2,1)S(1)} %get-tuple-element.98), channel_id=1, source_target_pairs={{0,1},{1,0},{2,3},{3,2},{4,5},{5,4},{6,7},{7,6},{8,9},{9,8},{10,11... | collective-permute-start | bytes 1179656 | tf_op jit(solution)/shard_map/ppermute | solution.py:711
  95.9 7.7 %collective-permute-start.12 = (bf16[64,1536]{1,0:T(8,128)(2,1)S(1)}, bf16[64,1536]{1,0:T(8,128)(2,1)S(1)}, u32[]{:S(2)}, u32[]{:S(2)}) collective-permute-start(bf16[64,1536]{1,0:T(8,128)(2,1)S(1)} %get-tuple-element.101), channel_id=1, source_target_pairs={{0,2},{1,3},{2,0},{3,1},{4,6},{5,7},{6,4},{7,5},{8,10},{9,11},{10,... | collective-permute-start | bytes 589832 | tf_op jit(solution)/shard_map/ppermute | solution.py:715
  97.8 12.2 %collective-permute-start.15 = (bf16[96,1536]{1,0:T(8,128)(2,1)S(1)}, bf16[96,1536]{1,0:T(8,128)(2,1)S(1)}, u32[]{:S(2)}, u32[]{:S(2)}) collective-permute-start(bf16[96,1536]{1,0:T(8,128)(2,1)S(1)} %slice.36), channel_id=1, source_target_pairs={{0,2},{1,3},{2,0},{3,1},{4,6},{5,7},{6,4},{7,5},{8,10},{9,11},{10,... | collective-permute-start | bytes 884744 | tf_op jit(solution)/shard_map/ppermute | solution.py:715
  103.7 8.0 %collective-permute-start.11 = (bf16[64,1536]{1,0:T(8,128)(2,1)S(1)}, bf16[64,1536]{1,0:T(8,128)(2,1)S(1)}, u32[]{:S(2)}, u32[]{:S(2)}) collective-permute-start(bf16[64,1536]{1,0:T(8,128)(2,1)S(1)} %get-tuple-element.100.refs_0_), channel_id=1, source_target_pairs={{0,1},{1,0},{2,3},{3,2},{4,5},{5,4},{6,7},{7,6},{8,9},{9,8},{10,11... | collective-permute-start | bytes 589832 | tf_op jit(solution)/shard_map/ppermute | solution.py:711
  103.8 8.0 %collective-permute-start.13 = (bf16[64,1536]{1,0:T(8,128)(2,1)S(1)}, bf16[64,1536]{1,0:T(8,128)(2,1)S(1)}, u32[]{:S(2)}, u32[]{:S(2)}) collective-permute-start(bf16[64,1536]{1,0:T(8,128)(2,1)S(1)} %get-tuple-element.99.refs_2_), channel_id=1, source_target_pairs={{0,1},{1,0},{2,3},{3,2},{4,5},{5,4},{6,7},{7,6},{8,9},{9,8},{10,11... | collective-permute-start | bytes 589832 | tf_op jit(solution)/shard_map/ppermute | solution.py:711
  104.3 7.3 %collective-permute-start.17 = (bf16[32,1536]{1,0:T(8,128)(2,1)S(1)}, bf16[32,1536]{1,0:T(8,128)(2,1)S(1)}, u32[]{:S(2)}, u32[]{:S(2)}) collective-permute-start(bf16[32,1536]{1,0:T(8,128)(2,1)S(1)} %slice.37), channel_id=1, source_target_pairs={{0,2},{1,3},{2,0},{3,1},{4,6},{5,7},{6,4},{7,5},{8,10},{9,11},{10,... | collective-permute-start | bytes 294920 | tf_op jit(solution)/shard_map/ppermute | solution.py:715
  110.0 3.0 %collective-permute-start.16 = (bf16[96,1536]{1,0:T(8,128)(2,1)S(1)}, bf16[96,1536]{1,0:T(8,128)(2,1)S(1)}, u32[]{:S(2)}, u32[]{:S(2)}) collective-permute-start(bf16[96,1536]{1,0:T(8,128)(2,1)S(1)} %add_convert_fusion.2.refs_1_), channel_id=1, source_target_pairs={{0,1},{1,0},{2,3},{3,2},{4,5},{5,4},{6,7},{7,6},{8,9},{9,8},{10,11... | collective-permute-start | bytes 884744 | tf_op jit(solution)/shard_map/ppermute | solution.py:711
  111.7 1.4 %collective-permute-start.18 = (bf16[32,1536]{1,0:T(8,128)(2,1)S(1)}, bf16[32,1536]{1,0:T(8,128)(2,1)S(1)}, u32[]{:S(2)}, u32[]{:S(2)}) collective-permute-start(bf16[32,1536]{1,0:T(8,128)(2,1)S(1)} %add_convert_fusion.5.refs_3_), channel_id=1, source_target_pairs={{0,1},{1,0},{2,3},{3,2},{4,5},{5,4},{6,7},{7,6},{8,9},{9,8},{10,11... | collective-permute-start | bytes 294920 | tf_op jit(solution)/shard_map/ppermute | solution.py:711

commit v12 on v11

--- a/solution.py
+++ b/solution.py
@@ -746,7 +746,7 @@
     payload, normed = lax.optimization_barrier((payload, normed))
     back = exchange(payload)
     logs, averages = fresh(parents, forget_bias, normed, w_key, w_value, w_forget, q, own)
-    back, w_out_far = lax.optimization_barrier((back, w_out_far))
+    logs, w_out_far = lax.optimization_barrier((logs, w_out_far))
     mixes = [w_out, swap_core(w_out), w_out_far, swap_core(w_out_far)]
 
     flat = tokens.reshape(steps * rows, width)

time: 115 us -> 106 us (0.922)
  waiting for transfers between devices: 41.2 us -> 35 us
  starting transfers between devices: 25.3 us -> 22.6 us
    ppermute x7, waiting for transfers between devices: 23.8 us -> 16.7 us  [swap_chip(): return lax.ppermute(value, 'head', [(i, i ^ 2) for i in range(4)])]
    ppermute x7, starting transfers between devices: 8.63 us -> 5.89 us  [swap_chip(): return lax.ppermute(value, 'head', [(i, i ^ 2) for i in range(4)])]
  transfers between devices with their start and end apart: 22 -> 22, of which waited for: 13 -> 13; matrix products, arithmetic and copies ran while one was open for 0% -> 0% of each run, Pallas kernels for 37% -> 40%
where the time goes in v12:
time: 106 us; the launch traced here: 105 us
  Pallas kernels  44.7 us (42%)
  waiting for transfers between devices  35 us (33%)
  starting transfers between devices  22.6 us (21%)
  local copies, waits for them, and re-layouts  2.09 us (2%)
    ppermute x7, waiting for transfers between devices, swap_chip(): return lax.ppermute(value, 'head', [(i, i ^ 2) for i in range(4)])  16.7 us
    all_to_all x3, waiting for transfers between devices, exchange(): lax.all_to_all(value, 'group', split_axis=0, concat_axis=0, tiled=True)  15 us
    all_to_all x3, starting transfers between devices, exchange(): lax.all_to_all(value, 'group', split_axis=0, concat_axis=0, tiled=True)  14.9 us
    pallas_call x1, Pallas kernels, fresh(): pl.pallas_call(fresh_kernel, in_specs=[vmem, vmem] + [hbm] * len(big), ou...  8.93 us
    pallas_call x2, Pallas kernels, block(): pl.pallas_call(functools.partial(block_kernel, first), in_specs=[vmem] *...  8.75 us
    pallas_call x2, Pallas kernels, merge(): pl.pallas_call(functools.partial(merge_kernel, capacity, steps, part, inn...  8.01 us
    pallas_call x1, Pallas kernels, own_pages(): pl.pallas_call(own_kernel, grid=(OWNED_SLOTS // PAGE_BLOCK,), in_specs=[S...  7.02 us
    ppermute x7, starting transfers between devices, swap_chip(): return lax.ppermute(value, 'head', [(i, i ^ 2) for i in range(4)])  5.89 us
  transfers between devices with their start and end apart: 22, of which 13 were waited for; matrix products, arithmetic and copies ran while one was open for 0% of the time, Pallas kernels for 40%

profile of v12, /device:TPU:0, one launch (start us, length us, event | category | flops | bytes accessed | tf_op | source)
XLA Modules:
  0.0 105.2 jit_solution(14607190118811870007)
XLA Ops:
  0.0 1.3 %broadcast_in_dim.3 = s32[8,1,48]{2,1,0:T(1,128)} broadcast(s32[48]{0:T(128)} %request_ref.5), dimensions={2} | broadcast | bytes 1728 | tf_op jit(solution)/shard_map/broadcast_in_dim | solution.py:734
  1.3 7.3 %all-to-all-start = ((s32[8,1,48]{2,1,0:T(1,128)}), s32[8,1,48]{2,1,0:T(1,128)S(1)}, u32[]{:S(2)}, u32[]{:S(2)}) async-start(s32[8,1,48]{2,1,0:T(1,128)} %broadcast_in_dim.3), calls=%async_computation | async-start | bytes 8192 | tf_op jit(solution)/shard_map/all_to_all | solution.py:732
  8.6 0.7 copy-done.3
  9.3 3.7 %queries.1 = (bf16[512,384]{1,0:T(8,128)(2,1)S(1)}, bf16[512,384]{1,0:T(8,128)(2,1)}, bf16[512,1536]{1,0:T(8,128)(2,1)}) custom-call(bf16[4,128,1536]{2,1,0:T(8,128)(2,1)} %tokens_hbm.1, f32[1536]{0:T(1024)S(1)} %copy-done.3, bf16[384,1536]{1,0:T(8,128)(2,1)} %wq_hbm.1), custom_call_target="tpu_custom_call" | custom-call | flops 603979776 | bytes 6291456 | tf_op jit(solution)/shard_map/queries/pallas_call | solution.py:124
  13.0 2.1 %all-to-all-done.ids_ref = s32[8,1,48]{2,1,0:T(1,128)S(1)} async-done(((s32[8,1,48]{2,1,0:T(1,128)}), s32[8,1,48]{2,1,0:T(1,128)S(1)}, u32[]{:S(2)}, u32[]{:S(2)}) %all-to-all-start) | async-done | bytes 1568 | tf_op jit(solution)/shard_map/all_to_all | solution.py:732
  15.1 2.0 %ask.1 = (s32[24]{0:T(128)S(1)}, bf16[24,32,384]{2,1,0:T(8,128)(2,1)}) custom-call(s32[48]{0:T(128)S(1)} %copy-done.4, s32[8,1,48]{2,1,0:T(1,128)S(1)} %all-to-all-done.ids_ref, bf16[512,384]{1,0:T(8,128)(2,1)S(1)} %get-tuple-element.52.q_ref), custom_call_target="tpu_custom_call" | custom-call | tf_op jit(solution)/shard_map/ask/pallas_call | solution.py:161
  17.0 4.0 %all-to-all-start.1 = ((bf16[8,96,384]{2,1,0:T(8,128)(2,1)}), bf16[8,96,384]{2,1,0:T(8,128)(2,1)S(1)}, u32[]{:S(2)}, u32[]{:S(2)}) async-start(bf16[8,96,384]{2,1,0:T(8,128)(2,1)} %bitcast), calls=%async_computation.1 | async-start | bytes 1179648 | tf_op jit(solution)/shard_map/all_to_all | solution.py:732
  21.0 7.0 %own_pages.1 = (f32[512,384]{1,0:T(8,128)}, f32[512,384]{1,0:T(8,128)}, f32[512,384]{1,0:T(8,128)}) custom-call(s32[48]{0:T(128)S(1)} %copy-done.4, s32[48]{0:T(128)S(1)} %copy-done.6, bf16[512,384]{1,0:T(8,128)(2,1)} %get-tuple-element.55.q_ref.q_hbm, bf16[48,384,128]{2,1,0:T(8,128)(2,1)} %keys_ref.3, bf16[48,384,128]{2,1,0:T(8,128)(2,1)} %values_ref.3, ...), custom_call_target="tpu_custom_call" | custom-call | flops 805306368 | bytes 6291456 | tf_op jit(solution)/shard_map/own_pages/pallas_call | solution.py:441
  28.1 1.5 %collective-permute-start = (bf16[384,1536]{1,0:T(8,128)(2,1)S(1)}, bf16[384,1536]{1,0:T(8,128)(2,1)S(1)}, u32[]{:S(2)}, u32[]{:S(2)}) collective-permute-start(bf16[384,1536]{1,0:T(8,128)(2,1)S(1)} %copy-done), channel_id=1, source_target_pairs={{0,2},{1,3},{2,0},{3,1},{4,6},{5,7},{6,4},{7,5},{8,10},{9,11},{10,... | collective-permute-start | bytes 3538952 | tf_op jit(solution)/shard_map/ppermute | solution.py:715
  29.6 6.8 %all-to-all-done.1 = bf16[8,96,384]{2,1,0:T(8,128)(2,1)S(1)} async-done(((bf16[8,96,384]{2,1,0:T(8,128)(2,1)}), bf16[8,96,384]{2,1,0:T(8,128)(2,1)S(1)}, u32[]{:S(2)}, u32[]{:S(2)}) %all-to-all-start.1) | async-done | bytes 589856 | tf_op jit(solution)/shard_map/all_to_all | solution.py:732
  36.4 4.5 %hosted_pages.1 = bf16[8,304,128]{2,1,0:T(8,128)(2,1)} custom-call(s32[48]{0:T(128)S(1)} %copy-done.4, s32[48]{0:T(128)S(1)} %copy-done.6, bf16[24,32,384]{2,1,0:T(8,128)(2,1)S(1)} %bitcast.9, bf16[48,384,128]{2,1,0:T(8,128)(2,1)} %keys_ref.3, bf16[48,384,128]{2,1,0:T(8,128)(2,1)} %values_ref.3, bf16[6,48,128]{2,1,0:T(8,128)(2,1)S(1)} %bitcast.11), custom_call_target="tpu_custom_call" | custom-call | flops 402653184 | bytes 3145728 | tf_op jit(solution)/shard_map/hosted_pages/pallas_call | solution.py:507
  40.9 3.6 %all-to-all-start.2 = ((bf16[8,304,128]{2,1,0:T(8,128)(2,1)}), bf16[8,304,128]{2,1,0:T(8,128)(2,1)S(1)}, u32[]{:S(2)}, u32[]{:S(2)}) async-start(bf16[8,304,128]{2,1,0:T(8,128)(2,1)} %hosted_pages.1), calls=%async_computation.2 | async-start | bytes 1245184 | tf_op jit(solution)/shard_map/all_to_all | solution.py:732
  44.6 8.9 %fresh.1 = (f32[2,16,16,384]{3,2,1,0:T(8,128)}, f32[2,16,16,384]{3,2,1,0:T(8,128)}) custom-call(s32[3,128]{1,0:T(4,128)S(1)} %copy-done.5, f32[1,6]{1,0:T(1,128)S(1)} %bitcast.12, bf16[512,1536]{1,0:T(8,128)(2,1)} %get-tuple-element.66.normed_hbm, bf16[384,1536]{1,0:T(8,128)(2,1)} %wk_hbm.1, bf16[384,1536]{1,0:T(8,128)(2,1)} %wv_hbm.1, ...), custom_call_target="tpu_custom_call" | custom-call | flops 1207959552 | bytes 12582912 | tf_op jit(solution)/shard_map/fresh/pallas_call | solution.py:326
  53.5 1.4 %collective-permute-done.refs_2_ = bf16[384,1536]{1,0:T(8,128)(2,1)S(1)} collective-permute-done((bf16[384,1536]{1,0:T(8,128)(2,1)S(1)}, bf16[384,1536]{1,0:T(8,128)(2,1)S(1)}, u32[]{:S(2)}, u32[]{:S(2)}) %collective-permute-start) | collective-permute-done | bytes 1179680 | tf_op jit(solution)/shard_map/ppermute | solution.py:715
  54.9 6.1 %all-to-all-done.2.back_ref = bf16[8,304,128]{2,1,0:T(8,128)(2,1)S(1)} async-done(((bf16[8,304,128]{2,1,0:T(8,128)(2,1)}), bf16[8,304,128]{2,1,0:T(8,128)(2,1)S(1)}, u32[]{:S(2)}, u32[]{:S(2)}) %all-to-all-start.2) | async-done | bytes 622624 | tf_op jit(solution)/shard_map/all_to_all | solution.py:732
  61.0 2.0 %merge.2.att0 = bf16[256,384]{1,0:T(8,128)(2,1)S(1)} custom-call(s32[24]{0:T(128)S(1)} %get-tuple-element.65.table_ref, bf16[8,304,128]{2,1,0:T(8,128)(2,1)S(1)} %all-to-all-done.2.back_ref, f32[2,256,384]{2,1,0:T(8,128)} %bitcast.14, f32[2,256,384]{2,1,0:T(8,128)} %bitcast.16), custom_call_target="tpu_custom_call" | custom-call | flops 3932160 | bytes 8388608 | tf_op jit(solution)/shard_map/merge/pallas_call | solution.py:598
  63.1 1.6 %collective-permute-start.2 = (bf16[256,384]{1,0:T(8,128)(2,1)S(1)}, bf16[256,384]{1,0:T(8,128)(2,1)S(1)}, u32[]{:S(2)}, u32[]{:S(2)}) collective-permute-start(bf16[256,384]{1,0:T(8,128)(2,1)S(1)} %merge.2.att0), channel_id=1, source_target_pairs={{0,2},{1,3},{2,0},{3,1},{4,6},{5,7},{6,4},{7,5},{8,10},{9,11},{10,... | collective-permute-start | bytes 589832 | tf_op jit(solution)/shard_map/ppermute | solution.py:715
  64.7 6.0 %merge.3 = (bf16[256,384]{1,0:T(8,128)(2,1)S(1)}, bf16[1536,1536]{1,0:T(8,128)(2,1)S(1)}, bf16[1536,1024]{1,0:T(8,128)(2,1)S(1)}, bf16[1536,1024]{1,0:T(8,128)(2...) custom-call(s32[24]{0:T(128)S(1)} %get-tuple-element.65.table_ref, ...), custom_call_target="tpu_custom_call" | custom-call | flops 3932160 | bytes 8388608 | tf_op jit(solution)/shard_map/merge/pallas_call | solution.py:598
  72.3 4.4 %block.2 = (f32[128,1536]{1,0:T(8,128)S(1)}, f32[128,1536]{1,0:T(8,128)S(1)}, bf16[128,1536]{1,0:T(8,128)(2,1)S(1)}) custom-call(bf16[256,384]{1,0:T(8,128)(2,1)S(1)} %merge.2.att0, bf16[256,384]{1,0:T(8,128)(2,1)S(1)} %collective-permute-done.1.att1, bf16[256,384]{1,0:T(8,128)(2,1)S(1)} %collective-permute-done.2.att2, ...), custom_call_target="tpu_custom_call" | custom-call | tf_op jit(solution)/shard_map/block/pallas_call | solution.py:659
  76.7 1.4 %collective-permute-done.6.att2 = bf16[256,384]{1,0:T(8,128)(2,1)S(1)} collective-permute-done((bf16[256,384]{1,0:T(8,128)(2,1)S(1)}, bf16[256,384]{1,0:T(8,128)(2,1)S(1)}, u32[]{:S(2)}, u32[]{:S(2)}) %collective-permute-start.6) | collective-permute-done | bytes 196640 | tf_op jit(solution)/shard_map/ppermute | solution.py:715
  78.6 1.2 %collective-permute-done.7 = bf16[128,1536]{1,0:T(8,128)(2,1)S(1)} collective-permute-done((bf16[128,1536]{1,0:T(8,128)(2,1)S(1)}, bf16[128,1536]{1,0:T(8,128)(2,1)S(1)}, u32[]{:S(2)}, u32[]{:S(2)}) %collective-permute-start.7) | collective-permute-done | bytes 393248 | tf_op jit(solution)/shard_map/ppermute | solution.py:711
  79.9 0.6 collective-permute-start.10
  80.5 4.4 %block.3 = (f32[128,1536]{1,0:T(8,128)S(1)}, f32[128,1536]{1,0:T(8,128)S(1)}, bf16[128,1536]{1,0:T(8,128)(2,1)S(1)}) custom-call(bf16[256,384]{1,0:T(8,128)(2,1)S(1)} %get-tuple-element.90.att0, bf16[256,384]{1,0:T(8,128)(2,1)S(1)} %collective-permute-done.8.att1, bf16[256,384]{1,0:T(8,128)(2,1)S(1)} %collective-permute-done.6.att2, ...), custom_call_target="tpu_custom_call" | custom-call | tf_op jit(solution)/shard_map/block/pallas_call | solution.py:659
  84.9 2.0 %collective-permute-done.10 = bf16[64,1536]{1,0:T(8,128)(2,1)S(1)} collective-permute-done((bf16[64,1536]{1,0:T(8,128)(2,1)S(1)}, bf16[64,1536]{1,0:T(8,128)(2,1)S(1)}, u32[]{:S(2)}, u32[]{:S(2)}) %collective-permute-start.10) | collective-permute-done | bytes 196640 | tf_op jit(solution)/shard_map/ppermute | solution.py:715
  87.5 1.2 %collective-permute-done.14 = bf16[128,1536]{1,0:T(8,128)(2,1)S(1)} collective-permute-done((bf16[128,1536]{1,0:T(8,128)(2,1)S(1)}, bf16[128,1536]{1,0:T(8,128)(2,1)S(1)}, u32[]{:S(2)}, u32[]{:S(2)}) %collective-permute-start.14) | collective-permute-done | bytes 393248 | tf_op jit(solution)/shard_map/ppermute | solution.py:711
  88.8 0.6 collective-permute-start.15
  89.4 5.3 %collective-permute-done.12 = bf16[64,1536]{1,0:T(8,128)(2,1)S(1)} collective-permute-done((bf16[64,1536]{1,0:T(8,128)(2,1)S(1)}, bf16[64,1536]{1,0:T(8,128)(2,1)S(1)}, u32[]{:S(2)}, u32[]{:S(2)}) %collective-permute-start.12) | collective-permute-done | bytes 196640 | tf_op jit(solution)/shard_map/ppermute | solution.py:715
  95.3 0.6 collective-permute-start.17
  95.9 5.0 %collective-permute-done.15 = bf16[96,1536]{1,0:T(8,128)(2,1)S(1)} collective-permute-done((bf16[96,1536]{1,0:T(8,128)(2,1)S(1)}, bf16[96,1536]{1,0:T(8,128)(2,1)S(1)}, u32[]{:S(2)}, u32[]{:S(2)}) %collective-permute-start.15) | collective-permute-done | bytes 294944 | tf_op jit(solution)/shard_map/ppermute | solution.py:715
  101.1 1.5 %collective-permute-done.17 = bf16[32,1536]{1,0:T(8,128)(2,1)S(1)} collective-permute-done((bf16[32,1536]{1,0:T(8,128)(2,1)S(1)}, bf16[32,1536]{1,0:T(8,128)(2,1)S(1)}, u32[]{:S(2)}, u32[]{:S(2)}) %collective-permute-start.17) | collective-permute-done | bytes 98336 | tf_op jit(solution)/shard_map/ppermute | solution.py:715
  102.8 0.9 finish.2.refs_0_
  104.1 0.9 finish.3
  (48 shorter events, 4.3 us)
Async XLA Ops:
  0.0 15.1 %copy-start.4 = (s32[48]{0:T(128)S(1)}, s32[48]{0:T(128)}, u32[]{:S(2)}) copy-start(s32[48]{0:T(128)} %request_ref.5) | copy-start | bytes 580
  1.3 13.7 %all-to-all-start = ((s32[8,1,48]{2,1,0:T(1,128)}), s32[8,1,48]{2,1,0:T(1,128)S(1)}, u32[]{:S(2)}, u32[]{:S(2)}) async-start(s32[8,1,48]{2,1,0:T(1,128)} %broadcast_in_dim.3), calls=%async_computation | async-start | bytes 8192 | tf_op jit(solution)/shard_map/all_to_all | solution.py:732
  8.6 0.7 copy-start.3
  9.3 11.7 %copy-start.1 = (bf16[48,6,128]{2,0,1:T(8,128)(2,1)S(1)}, bf16[48,6,128]{2,0,1:T(8,128)(2,1)}, u32[]{:S(2)}) copy-start(bf16[48,6,128]{2,0,1:T(8,128)(2,1)} %param.24) | copy-start | bytes 221188
  9.3 11.7 %copy-start.6 = (s32[48]{0:T(128)S(1)}, s32[48]{0:T(128)}, u32[]{:S(2)}) copy-start(s32[48]{0:T(128)} %fill_ref.3) | copy-start | bytes 580
  17.0 19.4 %all-to-all-start.1 = ((bf16[8,96,384]{2,1,0:T(8,128)(2,1)}), bf16[8,96,384]{2,1,0:T(8,128)(2,1)S(1)}, u32[]{:S(2)}, u32[]{:S(2)}) async-start(bf16[8,96,384]{2,1,0:T(8,128)(2,1)} %bitcast), calls=%async_computation.1 | async-start | bytes 1179648 | tf_op jit(solution)/shard_map/all_to_all | solution.py:732
  21.0 7.0 %copy-start = (bf16[384,1536]{1,0:T(8,128)(2,1)S(1)}, bf16[384,1536]{1,0:T(8,128)(2,1)}, u32[]{:S(2)}) copy-start(bf16[384,1536]{1,0:T(8,128)(2,1)} %refs_0_.1) | copy-start | bytes 3538948
  28.1 26.9 %collective-permute-start = (bf16[384,1536]{1,0:T(8,128)(2,1)S(1)}, bf16[384,1536]{1,0:T(8,128)(2,1)S(1)}, u32[]{:S(2)}, u32[]{:S(2)}) collective-permute-start(bf16[384,1536]{1,0:T(8,128)(2,1)S(1)} %copy-done), channel_id=1, source_target_pairs={{0,2},{1,3},{2,0},{3,1},{4,6},{5,7},{6,4},{7,5},{8,10},{9,11},{10,... | collective-permute-start | bytes 3538952 | tf_op jit(solution)/shard_map/ppermute | solution.py:715
  29.6 35.1 %collective-permute-start.3 = (bf16[384,1536]{1,0:T(8,128)(2,1)S(1)}, bf16[384,1536]{1,0:T(8,128)(2,1)}, u32[]{:S(2)}, u32[]{:S(2)}) collective-permute-start(bf16[384,1536]{1,0:T(8,128)(2,1)S(1)} %copy-done), channel_id=1, source_target_pairs={{0,1},{1,0},{2,3},{3,2},{4,5},{5,4},{6,7},{7,6},{8,9},{9,8},{10,11... | collective-permute-start | bytes 3538952 | tf_op jit(solution)/shard_map/ppermute | solution.py:711
  36.4 8.2 %copy-start.5 = (s32[3,128]{1,0:T(4,128)S(1)}, s32[3,128]{1,0:T(4,128)}, u32[]{:S(2)}) copy-start(s32[3,128]{1,0:T(4,128)} %parents_ref.1) | copy-start | bytes 4612
  36.4 8.2 %copy-start.7 = (f32[6]{0:T(128)S(1)}, f32[6]{0:T(128)}, u32[]{:S(2)}) copy-start(f32[6]{0:T(128)} %param.30) | copy-start | bytes 76
  40.9 20.1 %all-to-all-start.2 = ((bf16[8,304,128]{2,1,0:T(8,128)(2,1)}), bf16[8,304,128]{2,1,0:T(8,128)(2,1)S(1)}, u32[]{:S(2)}, u32[]{:S(2)}) async-start(bf16[8,304,128]{2,1,0:T(8,128)(2,1)} %hosted_pages.1), calls=%async_computation.2 | async-start | bytes 1245184 | tf_op jit(solution)/shard_map/all_to_all | solution.py:732
  54.9 9.7 %collective-permute-start.4 = (bf16[384,1536]{1,0:T(8,128)(2,1)S(1)}, bf16[384,1536]{1,0:T(8,128)(2,1)}, u32[]{:S(2)}, u32[]{:S(2)}) collective-permute-start(bf16[384,1536]{1,0:T(8,128)(2,1)S(1)} %collective-permute-done.refs_2_), channel_id=1, source_target_pairs={{0,1},{1,0},{2,3},{3,2},{4,5},{5,4},{6,7},{7,6},{8,9},{9,8},{10,11... | collective-permute-start | bytes 3538952 | tf_op jit(solution)/shard_map/ppermute | solution.py:711
  63.1 7.6 %collective-permute-start.2 = (bf16[256,384]{1,0:T(8,128)(2,1)S(1)}, bf16[256,384]{1,0:T(8,128)(2,1)S(1)}, u32[]{:S(2)}, u32[]{:S(2)}) collective-permute-start(bf16[256,384]{1,0:T(8,128)(2,1)S(1)} %merge.2.att0), channel_id=1, source_target_pairs={{0,2},{1,3},{2,0},{3,1},{4,6},{5,7},{6,4},{7,5},{8,10},{9,11},{10,... | collective-permute-start | bytes 589832 | tf_op jit(solution)/shard_map/ppermute | solution.py:715
  64.6 7.1 %collective-permute-start.1 = (bf16[256,384]{1,0:T(8,128)(2,1)S(1)}, bf16[256,384]{1,0:T(8,128)(2,1)S(1)}, u32[]{:S(2)}, u32[]{:S(2)}) collective-permute-start(bf16[256,384]{1,0:T(8,128)(2,1)S(1)} %merge.2.att0), channel_id=1, source_target_pairs={{0,1},{1,0},{2,3},{3,2},{4,5},{5,4},{6,7},{7,6},{8,9},{9,8},{10,11... | collective-permute-start | bytes 589832 | tf_op jit(solution)/shard_map/ppermute | solution.py:711
  64.6 7.6 %copy-start.2 = (f32[1536]{0:T(1024)S(1)}, f32[1536]{0:T(1024)}, u32[]{:S(2)}) copy-start(f32[1536]{0:T(1024)} %gain_ref.5) | copy-start | bytes 18436
  70.6 1.6 %collective-permute-start.5 = (bf16[256,384]{1,0:T(8,128)(2,1)S(1)}, bf16[256,384]{1,0:T(8,128)(2,1)S(1)}, u32[]{:S(2)}, u32[]{:S(2)}) collective-permute-start(bf16[256,384]{1,0:T(8,128)(2,1)S(1)} %collective-permute-done.2.att2), channel_id=1, source_target_pairs={{0,1},{1,0},{2,3},{3,2},{4,5},{5,4},{6,7},{7,6},{8,9},{9,8},{10,11... | collective-permute-start | bytes 589832 | tf_op jit(solution)/shard_map/ppermute | solution.py:711
  71.2 6.9 %collective-permute-start.6 = (bf16[256,384]{1,0:T(8,128)(2,1)S(1)}, bf16[256,384]{1,0:T(8,128)(2,1)S(1)}, u32[]{:S(2)}, u32[]{:S(2)}) collective-permute-start(bf16[256,384]{1,0:T(8,128)(2,1)S(1)} %get-tuple-element.90.att0), channel_id=1, source_target_pairs={{0,2},{1,3},{2,0},{3,1},{4,6},{5,7},{6,4},{7,5},{8,10},{9,11},{10,... | collective-permute-start | bytes 589832 | tf_op jit(solution)/shard_map/ppermute | solution.py:715
  78.1 1.7 %collective-permute-start.7 = (bf16[128,1536]{1,0:T(8,128)(2,1)S(1)}, bf16[128,1536]{1,0:T(8,128)(2,1)S(1)}, u32[]{:S(2)}, u32[]{:S(2)}) collective-permute-start(bf16[128,1536]{1,0:T(8,128)(2,1)S(1)} %get-tuple-element.87), channel_id=1, source_target_pairs={{0,1},{1,0},{2,3},{3,2},{4,5},{5,4},{6,7},{7,6},{8,9},{9,8},{10,11... | collective-permute-start | bytes 1179656 | tf_op jit(solution)/shard_map/ppermute | solution.py:711
  78.1 2.4 %collective-permute-start.8 = (bf16[256,384]{1,0:T(8,128)(2,1)S(1)}, bf16[256,384]{1,0:T(8,128)(2,1)S(1)}, u32[]{:S(2)}, u32[]{:S(2)}) collective-permute-start(bf16[256,384]{1,0:T(8,128)(2,1)S(1)} %get-tuple-element.90.att0), channel_id=1, source_target_pairs={{0,1},{1,0},{2,3},{3,2},{4,5},{5,4},{6,7},{7,6},{8,9},{9,8},{10,11... | collective-permute-start | bytes 589832 | tf_op jit(solution)/shard_map/ppermute | solution.py:711
  78.6 1.9 %collective-permute-start.9 = (bf16[256,384]{1,0:T(8,128)(2,1)S(1)}, bf16[256,384]{1,0:T(8,128)(2,1)S(1)}, u32[]{:S(2)}, u32[]{:S(2)}) collective-permute-start(bf16[256,384]{1,0:T(8,128)(2,1)S(1)} %collective-permute-done.6.att2), channel_id=1, source_target_pairs={{0,1},{1,0},{2,3},{3,2},{4,5},{5,4},{6,7},{7,6},{8,9},{9,8},{10,11... | collective-permute-start | bytes 589832 | tf_op jit(solution)/shard_map/ppermute | solution.py:711
  79.9 7.0 %collective-permute-start.10 = (bf16[64,1536]{1,0:T(8,128)(2,1)S(1)}, bf16[64,1536]{1,0:T(8,128)(2,1)S(1)}, u32[]{:S(2)}, u32[]{:S(2)}) collective-permute-start(bf16[64,1536]{1,0:T(8,128)(2,1)S(1)} %get-tuple-element.102), channel_id=1, source_target_pairs={{0,2},{1,3},{2,0},{3,1},{4,6},{5,7},{6,4},{7,5},{8,10},{9,11},{10,... | collective-permute-start | bytes 589832 | tf_op jit(solution)/shard_map/ppermute | solution.py:715
  86.9 1.7 %collective-permute-start.14 = (bf16[128,1536]{1,0:T(8,128)(2,1)S(1)}, bf16[128,1536]{1,0:T(8,128)(2,1)S(1)}, u32[]{:S(2)}, u32[]{:S(2)}) collective-permute-start(bf16[128,1536]{1,0:T(8,128)(2,1)S(1)} %get-tuple-element.98), channel_id=1, source_target_pairs={{0,1},{1,0},{2,3},{3,2},{4,5},{5,4},{6,7},{7,6},{8,9},{9,8},{10,11... | collective-permute-start | bytes 1179656 | tf_op jit(solution)/shard_map/ppermute | solution.py:711
  86.9 7.7 %collective-permute-start.12 = (bf16[64,1536]{1,0:T(8,128)(2,1)S(1)}, bf16[64,1536]{1,0:T(8,128)(2,1)S(1)}, u32[]{:S(2)}, u32[]{:S(2)}) collective-permute-start(bf16[64,1536]{1,0:T(8,128)(2,1)S(1)} %get-tuple-element.101), channel_id=1, source_target_pairs={{0,2},{1,3},{2,0},{3,1},{4,6},{5,7},{6,4},{7,5},{8,10},{9,11},{10,... | collective-permute-start | bytes 589832 | tf_op jit(solution)/shard_map/ppermute | solution.py:715
  88.8 12.2 %collective-permute-start.15 = (bf16[96,1536]{1,0:T(8,128)(2,1)S(1)}, bf16[96,1536]{1,0:T(8,128)(2,1)S(1)}, u32[]{:S(2)}, u32[]{:S(2)}) collective-permute-start(bf16[96,1536]{1,0:T(8,128)(2,1)S(1)} %slice.36), channel_id=1, source_target_pairs={{0,2},{1,3},{2,0},{3,1},{4,6},{5,7},{6,4},{7,5},{8,10},{9,11},{10,... | collective-permute-start | bytes 884744 | tf_op jit(solution)/shard_map/ppermute | solution.py:715
  94.8 8.0 %collective-permute-start.11 = (bf16[64,1536]{1,0:T(8,128)(2,1)S(1)}, bf16[64,1536]{1,0:T(8,128)(2,1)S(1)}, u32[]{:S(2)}, u32[]{:S(2)}) collective-permute-start(bf16[64,1536]{1,0:T(8,128)(2,1)S(1)} %get-tuple-element.100.refs_0_), channel_id=1, source_target_pairs={{0,1},{1,0},{2,3},{3,2},{4,5},{5,4},{6,7},{7,6},{8,9},{9,8},{10,11... | collective-permute-start | bytes 589832 | tf_op jit(solution)/shard_map/ppermute | solution.py:711
  94.8 8.0 %collective-permute-start.13 = (bf16[64,1536]{1,0:T(8,128)(2,1)S(1)}, bf16[64,1536]{1,0:T(8,128)(2,1)S(1)}, u32[]{:S(2)}, u32[]{:S(2)}) collective-permute-start(bf16[64,1536]{1,0:T(8,128)(2,1)S(1)} %get-tuple-element.99.refs_2_), channel_id=1, source_target_pairs={{0,1},{1,0},{2,3},{3,2},{4,5},{5,4},{6,7},{7,6},{8,9},{9,8},{10,11... | collective-permute-start | bytes 589832 | tf_op jit(solution)/shard_map/ppermute | solution.py:711
  95.3 7.3 %collective-permute-start.17 = (bf16[32,1536]{1,0:T(8,128)(2,1)S(1)}, bf16[32,1536]{1,0:T(8,128)(2,1)S(1)}, u32[]{:S(2)}, u32[]{:S(2)}) collective-permute-start(bf16[32,1536]{1,0:T(8,128)(2,1)S(1)} %slice.37), channel_id=1, source_target_pairs={{0,2},{1,3},{2,0},{3,1},{4,6},{5,7},{6,4},{7,5},{8,10},{9,11},{10,... | collective-permute-start | bytes 294920 | tf_op jit(solution)/shard_map/ppermute | solution.py:715
  101.1 3.0 %collective-permute-start.16 = (bf16[96,1536]{1,0:T(8,128)(2,1)S(1)}, bf16[96,1536]{1,0:T(8,128)(2,1)S(1)}, u32[]{:S(2)}, u32[]{:S(2)}) collective-permute-start(bf16[96,1536]{1,0:T(8,128)(2,1)S(1)} %add_convert_fusion.2.refs_1_), channel_id=1, source_target_pairs={{0,1},{1,0},{2,3},{3,2},{4,5},{5,4},{6,7},{7,6},{8,9},{9,8},{10,11... | collective-permute-start | bytes 884744 | tf_op jit(solution)/shard_map/ppermute | solution.py:711
  102.7 1.4 %collective-permute-start.18 = (bf16[32,1536]{1,0:T(8,128)(2,1)S(1)}, bf16[32,1536]{1,0:T(8,128)(2,1)S(1)}, u32[]{:S(2)}, u32[]{:S(2)}) collective-permute-start(bf16[32,1536]{1,0:T(8,128)(2,1)S(1)} %add_convert_fusion.5.refs_3_), channel_id=1, source_target_pairs={{0,1},{1,0},{2,3},{3,2},{4,5},{5,4},{6,7},{7,6},{8,9},{9,8},{10,11... | collective-permute-start | bytes 294920 | tf_op jit(solution)/shard_map/ppermute | solution.py:711

commit v13 on v12

--- a/solution.py
+++ b/solution.py
@@ -535,7 +535,7 @@
     state = (top_ref, total_ref, numer_ref)
     copies = start_all([(log_hbm.at[part], top_ref), (average_hbm.at[part], numer_ref)], sems)
     pairs = []
-    if sources:
+    if len(sources) > 4:
         weight_ref, *targets = targets
         height = sources[0].shape[0]
         head = lax.axis_index("head")
@@ -590,7 +590,7 @@
     vmem = pl.BlockSpec(memory_space=pltpu.VMEM)
     hbm = pl.BlockSpec(memory_space=pltpu.HBM)
     anywhere = pl.BlockSpec(memory_space=pl.ANY)
-    mixes = sources[:4]
+    mixes = sources[:4] if len(sources) > 4 else []
     others = sources[len(mixes) :]
     kept = [jax.ShapeDtypeStruct(x.shape, x.dtype) for x in others]
     if mixes:
@@ -752,10 +752,11 @@
     flat = tokens.reshape(steps * rows, width)
     each = steps // PARTS
     sums = (table, back, logs, averages, each, capacity)
-    heres = list(merge(0, *sums, []))
+    here, flat = merge(0, *sums, [flat])
+    heres = [here]
     back, heres[0] = lax.optimization_barrier((back, heres[0]))
     sums = (table, back, logs, averages, each, capacity)
-    here, weight, w_gate, w_up, w_down, flat = merge(1, *sums, mixes + [w_gate, w_up, w_down, flat])
+    here, weight, w_gate, w_up, w_down = merge(1, *sums, mixes + [w_gate, w_up, w_down])
     heres.append(here)
     fars = [swap_chip(here) for here in heres]
     fars[0], heres[1] = lax.optimization_barrier((fars[0], heres[1]))
@@ -775,7 +776,7 @@
     residual[0], mine, other = block_of(0)
     other, fars[1] = lax.optimization_barrier((other, fars[1]))
     chip[0] = chip_sum(mine, other)
-    most = chip[0].shape[0] // 2
+    most = chip[0].shape[0] // 8 * 3
     chip_most, chip_rest = chip[0][:most], chip[0][most:]
     far_most, far_rest = swap_chip(chip_most), swap_chip(chip_rest)
     residual[1], mine, other = block_of(1)

time: 106 us -> 102 us (0.962)
  waiting for transfers between devices: 35 us -> 30.9 us
  starting transfers between devices: 22.6 us -> 23.7 us
    ppermute x7, waiting for transfers between devices: 16.7 us -> 12.7 us  [swap_chip(): return lax.ppermute(value, 'head', [(i, i ^ 2) for i in range(4)])]
  transfers between devices with their start and end apart: 22 -> 22, of which waited for: 13 -> 13; matrix products, arithmetic and copies ran while one was open for 0% -> 0% of each run, Pallas kernels for 40% -> 41%
where the time goes in v13:
time: 102 us
  Pallas kernels  44.5 us (44%)
  waiting for transfers between devices  30.9 us (30%)
  starting transfers between devices  23.7 us (23%)
  local copies, waits for them, and re-layouts  2.1 us (2%)
    all_to_all x3, waiting for transfers between devices, exchange(): lax.all_to_all(value, 'group', split_axis=0, concat_axis=0, tiled=True)  15 us
    all_to_all x3, starting transfers between devices, exchange(): lax.all_to_all(value, 'group', split_axis=0, concat_axis=0, tiled=True)  14.9 us
    ppermute x7, waiting for transfers between devices, swap_chip(): return lax.ppermute(value, 'head', [(i, i ^ 2) for i in range(4)])  12.7 us
    pallas_call x1, Pallas kernels, fresh(): pl.pallas_call(fresh_kernel, in_specs=[vmem, vmem] + [hbm] * len(big), ou...  8.92 us
    pallas_call x2, Pallas kernels, block(): pl.pallas_call(functools.partial(block_kernel, first), in_specs=[vmem] *...  8.76 us
    pallas_call x2, Pallas kernels, merge(): pl.pallas_call(functools.partial(merge_kernel, capacity, steps, part, inn...  7.75 us
    pallas_call x1, Pallas kernels, own_pages(): pl.pallas_call(own_kernel, grid=(OWNED_SLOTS // PAGE_BLOCK,), in_specs=[S...  7.01 us
    ppermute x7, starting transfers between devices, swap_chip(): return lax.ppermute(value, 'head', [(i, i ^ 2) for i in range(4)])  6.91 us
  transfers between devices with their start and end apart: 22, of which 13 were waited for; matrix products, arithmetic and copies ran while one was open for 0% of the time, Pallas kernels for 41%

profile of v13, /device:TPU:0, one launch (start us, length us, event | category | flops | bytes accessed | tf_op | source)
XLA Modules:
  0.0 102.0 jit_solution(532122510192222638)
XLA Ops:
  0.0 1.3 %broadcast_in_dim.3 = s32[8,1,48]{2,1,0:T(1,128)} broadcast(s32[48]{0:T(128)} %request_ref.5), dimensions={2} | broadcast | bytes 1728 | tf_op jit(solution)/shard_map/broadcast_in_dim | solution.py:734
  1.3 7.3 %all-to-all-start = ((s32[8,1,48]{2,1,0:T(1,128)}), s32[8,1,48]{2,1,0:T(1,128)S(1)}, u32[]{:S(2)}, u32[]{:S(2)}) async-start(s32[8,1,48]{2,1,0:T(1,128)} %broadcast_in_dim.3), calls=%async_computation | async-start | bytes 8192 | tf_op jit(solution)/shard_map/all_to_all | solution.py:732
  8.6 0.7 copy-done.3
  9.3 3.7 %queries.1 = (bf16[512,384]{1,0:T(8,128)(2,1)S(1)}, bf16[512,384]{1,0:T(8,128)(2,1)}, bf16[512,1536]{1,0:T(8,128)(2,1)}) custom-call(bf16[4,128,1536]{2,1,0:T(8,128)(2,1)} %tokens_hbm.1, f32[1536]{0:T(1024)S(1)} %copy-done.3, bf16[384,1536]{1,0:T(8,128)(2,1)} %wq_hbm.1), custom_call_target="tpu_custom_call" | custom-call | flops 603979776 | bytes 6291456 | tf_op jit(solution)/shard_map/queries/pallas_call | solution.py:124
  13.0 2.1 %all-to-all-done.ids_ref = s32[8,1,48]{2,1,0:T(1,128)S(1)} async-done(((s32[8,1,48]{2,1,0:T(1,128)}), s32[8,1,48]{2,1,0:T(1,128)S(1)}, u32[]{:S(2)}, u32[]{:S(2)}) %all-to-all-start) | async-done | bytes 1568 | tf_op jit(solution)/shard_map/all_to_all | solution.py:732
  15.1 2.0 %ask.1 = (s32[24]{0:T(128)S(1)}, bf16[24,32,384]{2,1,0:T(8,128)(2,1)}) custom-call(s32[48]{0:T(128)S(1)} %copy-done.4, s32[8,1,48]{2,1,0:T(1,128)S(1)} %all-to-all-done.ids_ref, bf16[512,384]{1,0:T(8,128)(2,1)S(1)} %get-tuple-element.53.q_ref), custom_call_target="tpu_custom_call" | custom-call | tf_op jit(solution)/shard_map/ask/pallas_call | solution.py:161
  17.1 4.0 %all-to-all-start.1 = ((bf16[8,96,384]{2,1,0:T(8,128)(2,1)}), bf16[8,96,384]{2,1,0:T(8,128)(2,1)S(1)}, u32[]{:S(2)}, u32[]{:S(2)}) async-start(bf16[8,96,384]{2,1,0:T(8,128)(2,1)} %bitcast), calls=%async_computation.1 | async-start | bytes 1179648 | tf_op jit(solution)/shard_map/all_to_all | solution.py:732
  21.1 7.0 %own_pages.1 = (f32[512,384]{1,0:T(8,128)}, f32[512,384]{1,0:T(8,128)}, f32[512,384]{1,0:T(8,128)}) custom-call(s32[48]{0:T(128)S(1)} %copy-done.4, s32[48]{0:T(128)S(1)} %copy-done.6, bf16[512,384]{1,0:T(8,128)(2,1)} %get-tuple-element.56.q_ref.q_hbm, bf16[48,384,128]{2,1,0:T(8,128)(2,1)} %keys_ref.3, bf16[48,384,128]{2,1,0:T(8,128)(2,1)} %values_ref.3, ...), custom_call_target="tpu_custom_call" | custom-call | flops 805306368 | bytes 6291456 | tf_op jit(solution)/shard_map/own_pages/pallas_call | solution.py:441
  28.1 1.5 %collective-permute-start = (bf16[384,1536]{1,0:T(8,128)(2,1)S(1)}, bf16[384,1536]{1,0:T(8,128)(2,1)S(1)}, u32[]{:S(2)}, u32[]{:S(2)}) collective-permute-start(bf16[384,1536]{1,0:T(8,128)(2,1)S(1)} %copy-done), channel_id=1, source_target_pairs={{0,2},{1,3},{2,0},{3,1},{4,6},{5,7},{6,4},{7,5},{8,10},{9,11},{10,... | collective-permute-start | bytes 3538952 | tf_op jit(solution)/shard_map/ppermute | solution.py:715
  29.6 6.8 %all-to-all-done.1 = bf16[8,96,384]{2,1,0:T(8,128)(2,1)S(1)} async-done(((bf16[8,96,384]{2,1,0:T(8,128)(2,1)}), bf16[8,96,384]{2,1,0:T(8,128)(2,1)S(1)}, u32[]{:S(2)}, u32[]{:S(2)}) %all-to-all-start.1) | async-done | bytes 589856 | tf_op jit(solution)/shard_map/all_to_all | solution.py:732
  36.4 4.5 %hosted_pages.1 = bf16[8,304,128]{2,1,0:T(8,128)(2,1)} custom-call(s32[48]{0:T(128)S(1)} %copy-done.4, s32[48]{0:T(128)S(1)} %copy-done.6, bf16[24,32,384]{2,1,0:T(8,128)(2,1)S(1)} %bitcast.9, bf16[48,384,128]{2,1,0:T(8,128)(2,1)} %keys_ref.3, bf16[48,384,128]{2,1,0:T(8,128)(2,1)} %values_ref.3, bf16[6,48,128]{2,1,0:T(8,128)(2,1)S(1)} %bitcast.11), custom_call_target="tpu_custom_call" | custom-call | flops 402653184 | bytes 3145728 | tf_op jit(solution)/shard_map/hosted_pages/pallas_call | solution.py:507
  41.0 3.6 %all-to-all-start.2 = ((bf16[8,304,128]{2,1,0:T(8,128)(2,1)}), bf16[8,304,128]{2,1,0:T(8,128)(2,1)S(1)}, u32[]{:S(2)}, u32[]{:S(2)}) async-start(bf16[8,304,128]{2,1,0:T(8,128)(2,1)} %hosted_pages.1), calls=%async_computation.2 | async-start | bytes 1245184 | tf_op jit(solution)/shard_map/all_to_all | solution.py:732
  44.6 8.9 %fresh.1 = (f32[2,16,16,384]{3,2,1,0:T(8,128)}, f32[2,16,16,384]{3,2,1,0:T(8,128)}) custom-call(s32[3,128]{1,0:T(4,128)S(1)} %copy-done.5, f32[1,6]{1,0:T(1,128)S(1)} %bitcast.12, bf16[512,1536]{1,0:T(8,128)(2,1)} %get-tuple-element.67.normed_hbm, bf16[384,1536]{1,0:T(8,128)(2,1)} %wk_hbm.1, bf16[384,1536]{1,0:T(8,128)(2,1)} %wv_hbm.1, ...), custom_call_target="tpu_custom_call" | custom-call | flops 1207959552 | bytes 12582912 | tf_op jit(solution)/shard_map/fresh/pallas_call | solution.py:326
  53.5 1.4 %collective-permute-done.refs_2_ = bf16[384,1536]{1,0:T(8,128)(2,1)S(1)} collective-permute-done((bf16[384,1536]{1,0:T(8,128)(2,1)S(1)}, bf16[384,1536]{1,0:T(8,128)(2,1)S(1)}, u32[]{:S(2)}, u32[]{:S(2)}) %collective-permute-start) | collective-permute-done | bytes 1179680 | tf_op jit(solution)/shard_map/ppermute | solution.py:715
  54.9 6.1 %all-to-all-done.2.back_ref = bf16[8,304,128]{2,1,0:T(8,128)(2,1)S(1)} async-done(((bf16[8,304,128]{2,1,0:T(8,128)(2,1)}), bf16[8,304,128]{2,1,0:T(8,128)(2,1)S(1)}, u32[]{:S(2)}, u32[]{:S(2)}) %all-to-all-start.2) | async-done | bytes 622624 | tf_op jit(solution)/shard_map/all_to_all | solution.py:732
  61.0 2.2 %merge.2 = (bf16[256,384]{1,0:T(8,128)(2,1)S(1)}, bf16[512,1536]{1,0:T(8,128)(2,1)S(1)}) custom-call(s32[24]{0:T(128)S(1)} %get-tuple-element.66.table_ref, bf16[8,304,128]{2,1,0:T(8,128)(2,1)S(1)} %all-to-all-done.2.back_ref, f32[2,256,384]{2,1,0:T(8,128)} %bitcast.14, f32[2,256,384]{2,1,0:T(8,128)} %bitcast.16, bf16[512,1536]{1,0:T(8,128)(2,1)} %bitcast.13), custom_call_target="tpu_custom_call" | custom-call | flops 3932160 | bytes 8388608 | tf_op jit(solution)/shard_map/merge/pallas_call | solution.py:598
  63.3 1.6 %collective-permute-start.2 = (bf16[256,384]{1,0:T(8,128)(2,1)S(1)}, bf16[256,384]{1,0:T(8,128)(2,1)S(1)}, u32[]{:S(2)}, u32[]{:S(2)}) collective-permute-start(bf16[256,384]{1,0:T(8,128)(2,1)S(1)} %get-tuple-element.76.att0), channel_id=1, source_target_pairs={{0,2},{1,3},{2,0},{3,1},{4,6},{5,7},{6,4},{7,5},{8,10},{9,11},{10,... | collective-permute-start | bytes 589832 | tf_op jit(solution)/shard_map/ppermute | solution.py:715
  64.9 5.5 %merge.3 = (bf16[256,384]{1,0:T(8,128)(2,1)S(1)}, bf16[1536,1536]{1,0:T(8,128)(2,1)S(1)}, bf16[1536,1024]{1,0:T(8,128)(2,1)S(1)}, bf16[1536,1024]{1,0:T(8,128)(2,1)S(1)}, bf16[1024,1536]{1,0:T(8,128)(2,1)S(1)}) custom-call(s32[24]{0:T(128)S(1)} %get-tuple-element.66.table_ref, bf16[8,304,128]{2,1,0:T(8,128)(2,1)S(1)} %all-to-all-done.2.back_ref, ...), custom_call_target="tpu_custom_call" | custom-call | flops 3932160 | bytes 8388608 | tf_op jit(solution)/shard_map/merge/pallas_call | solution.py:598
  72.0 4.4 %block.2 = (f32[128,1536]{1,0:T(8,128)S(1)}, f32[128,1536]{1,0:T(8,128)S(1)}, bf16[128,1536]{1,0:T(8,128)(2,1)S(1)}) custom-call(bf16[256,384]{1,0:T(8,128)(2,1)S(1)} %get-tuple-element.76.att0, bf16[256,384]{1,0:T(8,128)(2,1)S(1)} %collective-permute-done.1.att1, bf16[256,384]{1,0:T(8,128)(2,1)S(1)} %collective-permute-done.2.att2, ...), custom_call_target="tpu_custom_call" | custom-call | tf_op jit(solution)/shard_map/block/pallas_call | solution.py:659
  76.4 1.4 %collective-permute-done.6.att2 = bf16[256,384]{1,0:T(8,128)(2,1)S(1)} collective-permute-done((bf16[256,384]{1,0:T(8,128)(2,1)S(1)}, bf16[256,384]{1,0:T(8,128)(2,1)S(1)}, u32[]{:S(2)}, u32[]{:S(2)}) %collective-permute-start.6) | collective-permute-done | bytes 196640 | tf_op jit(solution)/shard_map/ppermute | solution.py:715
  78.4 1.2 %collective-permute-done.7 = bf16[128,1536]{1,0:T(8,128)(2,1)S(1)} collective-permute-done((bf16[128,1536]{1,0:T(8,128)(2,1)S(1)}, bf16[128,1536]{1,0:T(8,128)(2,1)S(1)}, u32[]{:S(2)}, u32[]{:S(2)}) %collective-permute-start.7) | collective-permute-done | bytes 393248 | tf_op jit(solution)/shard_map/ppermute | solution.py:711
  79.7 0.6 collective-permute-start.10
  80.3 1.6 %collective-permute-start.12 = (bf16[80,1536]{1,0:T(8,128)(2,1)S(1)}, bf16[80,1536]{1,0:T(8,128)(2,1)S(1)}, u32[]{:S(2)}, u32[]{:S(2)}) collective-permute-start(bf16[80,1536]{1,0:T(8,128)(2,1)S(1)} %slice.35), channel_id=1, source_target_pairs={{0,2},{1,3},{2,0},{3,1},{4,6},{5,7},{6,4},{7,5},{8,10},{9,11},{10,... | collective-permute-start | bytes 737288 | tf_op jit(solution)/shard_map/ppermute | solution.py:715
  81.9 4.4 %block.3 = (f32[128,1536]{1,0:T(8,128)S(1)}, f32[128,1536]{1,0:T(8,128)S(1)}, bf16[128,1536]{1,0:T(8,128)(2,1)S(1)}) custom-call(bf16[256,384]{1,0:T(8,128)(2,1)S(1)} %get-tuple-element.92.att0, bf16[256,384]{1,0:T(8,128)(2,1)S(1)} %collective-permute-done.8.att1, bf16[256,384]{1,0:T(8,128)(2,1)S(1)} %collective-permute-done.6.att2, ...), custom_call_target="tpu_custom_call" | custom-call | tf_op jit(solution)/shard_map/block/pallas_call | solution.py:659
  87.1 1.1 %collective-permute-done.14 = bf16[128,1536]{1,0:T(8,128)(2,1)S(1)} collective-permute-done((bf16[128,1536]{1,0:T(8,128)(2,1)S(1)}, bf16[128,1536]{1,0:T(8,128)(2,1)S(1)}, u32[]{:S(2)}, u32[]{:S(2)}) %collective-permute-start.14) | collective-permute-done | bytes 393248 | tf_op jit(solution)/shard_map/ppermute | solution.py:711
  88.3 0.6 collective-permute-start.15
  88.9 2.0 %collective-permute-done.12 = bf16[80,1536]{1,0:T(8,128)(2,1)S(1)} collective-permute-done((bf16[80,1536]{1,0:T(8,128)(2,1)S(1)}, bf16[80,1536]{1,0:T(8,128)(2,1)S(1)}, u32[]{:S(2)}, u32[]{:S(2)}) %collective-permute-start.12) | collective-permute-done | bytes 245792 | tf_op jit(solution)/shard_map/ppermute | solution.py:715
  91.1 0.6 collective-permute-start.17
  91.7 6.5 %collective-permute-done.15 = bf16[96,1536]{1,0:T(8,128)(2,1)S(1)} collective-permute-done((bf16[96,1536]{1,0:T(8,128)(2,1)S(1)}, bf16[96,1536]{1,0:T(8,128)(2,1)S(1)}, u32[]{:S(2)}, u32[]{:S(2)}) %collective-permute-start.15) | collective-permute-done | bytes 294944 | tf_op jit(solution)/shard_map/ppermute | solution.py:715
  98.4 1.1 %collective-permute-done.17 = bf16[32,1536]{1,0:T(8,128)(2,1)S(1)} collective-permute-done((bf16[32,1536]{1,0:T(8,128)(2,1)S(1)}, bf16[32,1536]{1,0:T(8,128)(2,1)S(1)}, u32[]{:S(2)}, u32[]{:S(2)}) %collective-permute-start.17) | collective-permute-done | bytes 98336 | tf_op jit(solution)/shard_map/ppermute | solution.py:715
  99.6 0.9 finish.2.refs_0_
  100.9 0.9 finish.3
  (50 shorter events, 4.0 us)
Async XLA Ops:
  0.0 15.1 %copy-start.4 = (s32[48]{0:T(128)S(1)}, s32[48]{0:T(128)}, u32[]{:S(2)}) copy-start(s32[48]{0:T(128)} %request_ref.5) | copy-start | bytes 580
  1.3 13.7 %all-to-all-start = ((s32[8,1,48]{2,1,0:T(1,128)}), s32[8,1,48]{2,1,0:T(1,128)S(1)}, u32[]{:S(2)}, u32[]{:S(2)}) async-start(s32[8,1,48]{2,1,0:T(1,128)} %broadcast_in_dim.3), calls=%async_computation | async-start | bytes 8192 | tf_op jit(solution)/shard_map/all_to_all | solution.py:732
  8.6 0.7 copy-start.3
  9.3 11.7 %copy-start.1 = (bf16[48,6,128]{2,0,1:T(8,128)(2,1)S(1)}, bf16[48,6,128]{2,0,1:T(8,128)(2,1)}, u32[]{:S(2)}) copy-start(bf16[48,6,128]{2,0,1:T(8,128)(2,1)} %param.24) | copy-start | bytes 221188
  9.3 11.7 %copy-start.6 = (s32[48]{0:T(128)S(1)}, s32[48]{0:T(128)}, u32[]{:S(2)}) copy-start(s32[48]{0:T(128)} %fill_ref.3) | copy-start | bytes 580
  17.1 19.4 %all-to-all-start.1 = ((bf16[8,96,384]{2,1,0:T(8,128)(2,1)}), bf16[8,96,384]{2,1,0:T(8,128)(2,1)S(1)}, u32[]{:S(2)}, u32[]{:S(2)}) async-start(bf16[8,96,384]{2,1,0:T(8,128)(2,1)} %bitcast), calls=%async_computation.1 | async-start | bytes 1179648 | tf_op jit(solution)/shard_map/all_to_all | solution.py:732
  21.1 7.0 %copy-start = (bf16[384,1536]{1,0:T(8,128)(2,1)S(1)}, bf16[384,1536]{1,0:T(8,128)(2,1)}, u32[]{:S(2)}) copy-start(bf16[384,1536]{1,0:T(8,128)(2,1)} %refs_0_.1) | copy-start | bytes 3538948
  28.1 26.9 %collective-permute-start = (bf16[384,1536]{1,0:T(8,128)(2,1)S(1)}, bf16[384,1536]{1,0:T(8,128)(2,1)S(1)}, u32[]{:S(2)}, u32[]{:S(2)}) collective-permute-start(bf16[384,1536]{1,0:T(8,128)(2,1)S(1)} %copy-done), channel_id=1, source_target_pairs={{0,2},{1,3},{2,0},{3,1},{4,6},{5,7},{6,4},{7,5},{8,10},{9,11},{10,... | collective-permute-start | bytes 3538952 | tf_op jit(solution)/shard_map/ppermute | solution.py:715
  29.6 35.3 %collective-permute-start.3 = (bf16[384,1536]{1,0:T(8,128)(2,1)S(1)}, bf16[384,1536]{1,0:T(8,128)(2,1)}, u32[]{:S(2)}, u32[]{:S(2)}) collective-permute-start(bf16[384,1536]{1,0:T(8,128)(2,1)S(1)} %copy-done), channel_id=1, source_target_pairs={{0,1},{1,0},{2,3},{3,2},{4,5},{5,4},{6,7},{7,6},{8,9},{9,8},{10,11... | collective-permute-start | bytes 3538952 | tf_op jit(solution)/shard_map/ppermute | solution.py:711
  36.4 8.2 %copy-start.5 = (s32[3,128]{1,0:T(4,128)S(1)}, s32[3,128]{1,0:T(4,128)}, u32[]{:S(2)}) copy-start(s32[3,128]{1,0:T(4,128)} %parents_ref.1) | copy-start | bytes 4612
  36.4 8.2 %copy-start.7 = (f32[6]{0:T(128)S(1)}, f32[6]{0:T(128)}, u32[]{:S(2)}) copy-start(f32[6]{0:T(128)} %param.30) | copy-start | bytes 76
  41.0 20.1 %all-to-all-start.2 = ((bf16[8,304,128]{2,1,0:T(8,128)(2,1)}), bf16[8,304,128]{2,1,0:T(8,128)(2,1)S(1)}, u32[]{:S(2)}, u32[]{:S(2)}) async-start(bf16[8,304,128]{2,1,0:T(8,128)(2,1)} %hosted_pages.1), calls=%async_computation.2 | async-start | bytes 1245184 | tf_op jit(solution)/shard_map/all_to_all | solution.py:732
  54.9 9.9 %collective-permute-start.4 = (bf16[384,1536]{1,0:T(8,128)(2,1)S(1)}, bf16[384,1536]{1,0:T(8,128)(2,1)}, u32[]{:S(2)}, u32[]{:S(2)}) collective-permute-start(bf16[384,1536]{1,0:T(8,128)(2,1)S(1)} %collective-permute-done.refs_2_), channel_id=1, source_target_pairs={{0,1},{1,0},{2,3},{3,2},{4,5},{5,4},{6,7},{7,6},{8,9},{9,8},{10,11... | collective-permute-start | bytes 3538952 | tf_op jit(solution)/shard_map/ppermute | solution.py:711
  63.3 8.8 %copy-start.2 = (f32[1536]{0:T(1024)S(1)}, f32[1536]{0:T(1024)}, u32[]{:S(2)}) copy-start(f32[1536]{0:T(1024)} %gain_ref.5) | copy-start | bytes 18436
  63.3 7.1 %collective-permute-start.2 = (bf16[256,384]{1,0:T(8,128)(2,1)S(1)}, bf16[256,384]{1,0:T(8,128)(2,1)S(1)}, u32[]{:S(2)}, u32[]{:S(2)}) collective-permute-start(bf16[256,384]{1,0:T(8,128)(2,1)S(1)} %get-tuple-element.76.att0), channel_id=1, source_target_pairs={{0,2},{1,3},{2,0},{3,1},{4,6},{5,7},{6,4},{7,5},{8,10},{9,11},{10,... | collective-permute-start | bytes 589832 | tf_op jit(solution)/shard_map/ppermute | solution.py:715
  64.8 6.6 %collective-permute-start.1 = (bf16[256,384]{1,0:T(8,128)(2,1)S(1)}, bf16[256,384]{1,0:T(8,128)(2,1)S(1)}, u32[]{:S(2)}, u32[]{:S(2)}) collective-permute-start(bf16[256,384]{1,0:T(8,128)(2,1)S(1)} %get-tuple-element.76.att0), channel_id=1, source_target_pairs={{0,1},{1,0},{2,3},{3,2},{4,5},{5,4},{6,7},{7,6},{8,9},{9,8},{10,11... | collective-permute-start | bytes 589832 | tf_op jit(solution)/shard_map/ppermute | solution.py:711
  70.4 1.6 %collective-permute-start.5 = (bf16[256,384]{1,0:T(8,128)(2,1)S(1)}, bf16[256,384]{1,0:T(8,128)(2,1)S(1)}, u32[]{:S(2)}, u32[]{:S(2)}) collective-permute-start(bf16[256,384]{1,0:T(8,128)(2,1)S(1)} %collective-permute-done.2.att2), channel_id=1, source_target_pairs={{0,1},{1,0},{2,3},{3,2},{4,5},{5,4},{6,7},{7,6},{8,9},{9,8},{10,11... | collective-permute-start | bytes 589832 | tf_op jit(solution)/shard_map/ppermute | solution.py:711
  71.0 6.9 %collective-permute-start.6 = (bf16[256,384]{1,0:T(8,128)(2,1)S(1)}, bf16[256,384]{1,0:T(8,128)(2,1)S(1)}, u32[]{:S(2)}, u32[]{:S(2)}) collective-permute-start(bf16[256,384]{1,0:T(8,128)(2,1)S(1)} %get-tuple-element.92.att0), channel_id=1, source_target_pairs={{0,2},{1,3},{2,0},{3,1},{4,6},{5,7},{6,4},{7,5},{8,10},{9,11},{10,... | collective-permute-start | bytes 589832 | tf_op jit(solution)/shard_map/ppermute | solution.py:715
  77.8 1.7 %collective-permute-start.7 = (bf16[128,1536]{1,0:T(8,128)(2,1)S(1)}, bf16[128,1536]{1,0:T(8,128)(2,1)S(1)}, u32[]{:S(2)}, u32[]{:S(2)}) collective-permute-start(bf16[128,1536]{1,0:T(8,128)(2,1)S(1)} %get-tuple-element.89), channel_id=1, source_target_pairs={{0,1},{1,0},{2,3},{3,2},{4,5},{5,4},{6,7},{7,6},{8,9},{9,8},{10,11... | collective-permute-start | bytes 1179656 | tf_op jit(solution)/shard_map/ppermute | solution.py:711
  77.9 2.4 %collective-permute-start.8 = (bf16[256,384]{1,0:T(8,128)(2,1)S(1)}, bf16[256,384]{1,0:T(8,128)(2,1)S(1)}, u32[]{:S(2)}, u32[]{:S(2)}) collective-permute-start(bf16[256,384]{1,0:T(8,128)(2,1)S(1)} %get-tuple-element.92.att0), channel_id=1, source_target_pairs={{0,1},{1,0},{2,3},{3,2},{4,5},{5,4},{6,7},{7,6},{8,9},{9,8},{10,11... | collective-permute-start | bytes 589832 | tf_op jit(solution)/shard_map/ppermute | solution.py:711
  78.4 1.9 %collective-permute-start.9 = (bf16[256,384]{1,0:T(8,128)(2,1)S(1)}, bf16[256,384]{1,0:T(8,128)(2,1)S(1)}, u32[]{:S(2)}, u32[]{:S(2)}) collective-permute-start(bf16[256,384]{1,0:T(8,128)(2,1)S(1)} %collective-permute-done.6.att2), channel_id=1, source_target_pairs={{0,1},{1,0},{2,3},{3,2},{4,5},{5,4},{6,7},{7,6},{8,9},{9,8},{10,11... | collective-permute-start | bytes 589832 | tf_op jit(solution)/shard_map/ppermute | solution.py:711
  79.7 6.8 %collective-permute-start.10 = (bf16[48,1536]{1,0:T(8,128)(2,1)S(1)}, bf16[48,1536]{1,0:T(8,128)(2,1)S(1)}, u32[]{:S(2)}, u32[]{:S(2)}) collective-permute-start(bf16[48,1536]{1,0:T(8,128)(2,1)S(1)} %slice.34), channel_id=1, source_target_pairs={{0,2},{1,3},{2,0},{3,1},{4,6},{5,7},{6,4},{7,5},{8,10},{9,11},{10,... | collective-permute-start | bytes 442376 | tf_op jit(solution)/shard_map/ppermute | solution.py:715
  80.3 10.6 %collective-permute-start.12 = (bf16[80,1536]{1,0:T(8,128)(2,1)S(1)}, bf16[80,1536]{1,0:T(8,128)(2,1)S(1)}, u32[]{:S(2)}, u32[]{:S(2)}) collective-permute-start(bf16[80,1536]{1,0:T(8,128)(2,1)S(1)} %slice.35), channel_id=1, source_target_pairs={{0,2},{1,3},{2,0},{3,1},{4,6},{5,7},{6,4},{7,5},{8,10},{9,11},{10,... | collective-permute-start | bytes 737288 | tf_op jit(solution)/shard_map/ppermute | solution.py:715
  86.4 1.7 %collective-permute-start.14 = (bf16[128,1536]{1,0:T(8,128)(2,1)S(1)}, bf16[128,1536]{1,0:T(8,128)(2,1)S(1)}, u32[]{:S(2)}, u32[]{:S(2)}) collective-permute-start(bf16[128,1536]{1,0:T(8,128)(2,1)S(1)} %get-tuple-element.100), channel_id=1, source_target_pairs={{0,1},{1,0},{2,3},{3,2},{4,5},{5,4},{6,7},{7,6},{8,9},{9,8},{10,11... | collective-permute-start | bytes 1179656 | tf_op jit(solution)/shard_map/ppermute | solution.py:711
  86.5 13.1 %collective-permute-start.11 = (bf16[48,1536]{1,0:T(8,128)(2,1)S(1)}, bf16[48,1536]{1,0:T(8,128)(2,1)S(1)}, u32[]{:S(2)}, u32[]{:S(2)}) collective-permute-start(bf16[48,1536]{1,0:T(8,128)(2,1)S(1)} %add_convert_fusion.4.refs_0_), channel_id=1, source_target_pairs={{0,1},{1,0},{2,3},{3,2},{4,5},{5,4},{6,7},{7,6},{8,9},{9,8},{10,11... | collective-permute-start | bytes 442376 | tf_op jit(solution)/shard_map/ppermute | solution.py:711
  88.3 9.9 %collective-permute-start.15 = (bf16[96,1536]{1,0:T(8,128)(2,1)S(1)}, bf16[96,1536]{1,0:T(8,128)(2,1)S(1)}, u32[]{:S(2)}, u32[]{:S(2)}) collective-permute-start(bf16[96,1536]{1,0:T(8,128)(2,1)S(1)} %slice.36), channel_id=1, source_target_pairs={{0,2},{1,3},{2,0},{3,1},{4,6},{5,7},{6,4},{7,5},{8,10},{9,11},{10,... | collective-permute-start | bytes 884744 | tf_op jit(solution)/shard_map/ppermute | solution.py:715
  91.0 8.7 %collective-permute-start.13 = (bf16[80,1536]{1,0:T(8,128)(2,1)S(1)}, bf16[80,1536]{1,0:T(8,128)(2,1)S(1)}, u32[]{:S(2)}, u32[]{:S(2)}) collective-permute-start(bf16[80,1536]{1,0:T(8,128)(2,1)S(1)} %add_convert_fusion.3.refs_2_), channel_id=1, source_target_pairs={{0,1},{1,0},{2,3},{3,2},{4,5},{5,4},{6,7},{7,6},{8,9},{9,8},{10,11... | collective-permute-start | bytes 737288 | tf_op jit(solution)/shard_map/ppermute | solution.py:711
  91.1 8.4 %collective-permute-start.17 = (bf16[32,1536]{1,0:T(8,128)(2,1)S(1)}, bf16[32,1536]{1,0:T(8,128)(2,1)S(1)}, u32[]{:S(2)}, u32[]{:S(2)}) collective-permute-start(bf16[32,1536]{1,0:T(8,128)(2,1)S(1)} %slice.37), channel_id=1, source_target_pairs={{0,2},{1,3},{2,0},{3,1},{4,6},{5,7},{6,4},{7,5},{8,10},{9,11},{10,... | collective-permute-start | bytes 294920 | tf_op jit(solution)/shard_map/ppermute | solution.py:715
  98.3 2.6 %collective-permute-start.16 = (bf16[96,1536]{1,0:T(8,128)(2,1)S(1)}, bf16[96,1536]{1,0:T(8,128)(2,1)S(1)}, u32[]{:S(2)}, u32[]{:S(2)}) collective-permute-start(bf16[96,1536]{1,0:T(8,128)(2,1)S(1)} %add_convert_fusion.2.refs_1_), channel_id=1, source_target_pairs={{0,1},{1,0},{2,3},{3,2},{4,5},{5,4},{6,7},{7,6},{8,9},{9,8},{10,11... | collective-permute-start | bytes 884744 | tf_op jit(solution)/shard_map/ppermute | solution.py:711
  99.5 1.4 %collective-permute-start.18 = (bf16[32,1536]{1,0:T(8,128)(2,1)S(1)}, bf16[32,1536]{1,0:T(8,128)(2,1)S(1)}, u32[]{:S(2)}, u32[]{:S(2)}) collective-permute-start(bf16[32,1536]{1,0:T(8,128)(2,1)S(1)} %add_convert_fusion.5.refs_3_), channel_id=1, source_target_pairs={{0,1},{1,0},{2,3},{3,2},{4,5},{5,4},{6,7},{7,6},{8,9},{9,8},{10,11... | collective-permute-start | bytes 294920 | tf_op jit(solution)/shard_map/ppermute | solution.py:711

commit v14 on v13

--- a/solution.py
+++ b/solution.py
@@ -53,7 +53,7 @@
 
 def fill_table(local_count, capacity, first, ids_ref, table_ref):
     groups = ids_ref.shape[0]
-    for slot in range(groups * capacity):
+    for slot in range(groups * capacity + 1):
         table_ref[slot] = -1
 
     def group(index, carry):
@@ -62,14 +62,12 @@
             local = ids_ref[index, 0, OWNED_SLOTS + page] - first
             mine = (local >= 0) & (local < local_count)
 
-            @pl.when(mine)
-            def _():
-                table_ref[index * capacity + rank] = local
-
+            slot = jnp.where(mine, index * capacity + rank, groups * capacity)
+            table_ref[slot] = local
             rank = rank + mine.astype(jnp.int32)
         return carry
 
-    lax.fori_loop(0, groups, group, 0)
+    lax.fori_loop(0, groups, group, 0, unroll=2)
 
 
 def query_kernel(
@@ -163,7 +161,7 @@
         in_specs=[SMEM, SMEM, vmem],
         out_specs=[SMEM, vmem],
         out_shape=[
-            jax.ShapeDtypeStruct((slots,), jnp.int32),
+            jax.ShapeDtypeStruct((slots + 1,), jnp.int32),
             jax.ShapeDtypeStruct((slots, span, q.shape[1]), bf16),
         ],
         compiler_params=pltpu.CompilerParams(vmem_limit_bytes=8 * MIB),
@@ -774,8 +772,9 @@
 
     chip, residual = [None] * PARTS, [None] * PARTS
     residual[0], mine, other = block_of(0)
-    other, fars[1] = lax.optimization_barrier((other, fars[1]))
-    chip[0] = chip_sum(mine, other)
+    cuts = [0, 48, 96, 128]
+    other = jnp.concatenate([swap_core(other[a:b]) for a, b in zip(cuts, cuts[1:])], axis=0)
+    chip[0] = (mine + other.astype(f32)).astype(bf16)
     most = chip[0].shape[0] // 8 * 3
     chip_most, chip_rest = chip[0][:most], chip[0][most:]
     far_most, far_rest = swap_chip(chip_most), swap_chip(chip_rest)

time: 102 us -> 101 us (level)
  waiting for transfers between devices: 30.9 us -> 28.3 us
  starting transfers between devices: 23.7 us -> 25.1 us
    ppermute x7, waiting for transfers between devices: 12.7 us -> 10.9 us  [swap_chip(): return lax.ppermute(value, 'head', [(i, i ^ 2) for i in range(4)])]
    ppermute x12 -> x14, waiting for transfers between devices: 3.21 us -> 2.42 us  [swap_core(): return lax.ppermute(value, 'head', [(i, i ^ 1) for i in range(4)])]
    ppermute x12 -> x14, starting transfers between devices: 1.87 us -> 2.64 us  [swap_core(): return lax.ppermute(value, 'head', [(i, i ^ 1) for i in range(4)])]
  transfers between devices with their start and end apart: 22 -> 24, of which waited for: 13 -> 13; matrix products, arithmetic and copies ran while one was open for 0% -> 1% of each run, Pallas kernels for 41% -> 41%
where the time goes in v14:
time: 101 us
  Pallas kernels  44.5 us (44%)
  waiting for transfers between devices  28.3 us (28%)
  starting transfers between devices  25.1 us (25%)
  local copies, waits for them, and re-layouts  2.13 us (2%)
    all_to_all x3, waiting for transfers between devices, exchange(): lax.all_to_all(value, 'group', split_axis=0, concat_axis=0, tiled=True)  15 us
    all_to_all x3, starting transfers between devices, exchange(): lax.all_to_all(value, 'group', split_axis=0, concat_axis=0, tiled=True)  14.9 us
    ppermute x7, waiting for transfers between devices, swap_chip(): return lax.ppermute(value, 'head', [(i, i ^ 2) for i in range(4)])  10.9 us
    pallas_call x1, Pallas kernels, fresh(): pl.pallas_call(fresh_kernel, in_specs=[vmem, vmem] + [hbm] * len(big), ou...  8.94 us
    pallas_call x2, Pallas kernels, block(): pl.pallas_call(functools.partial(block_kernel, first), in_specs=[vmem] *...  8.76 us
    pallas_call x2, Pallas kernels, merge(): pl.pallas_call(functools.partial(merge_kernel, capacity, steps, part, inn...  7.75 us
    ppermute x7, starting transfers between devices, swap_chip(): return lax.ppermute(value, 'head', [(i, i ^ 2) for i in range(4)])  7.61 us
    pallas_call x1, Pallas kernels, own_pages(): pl.pallas_call(own_kernel, grid=(OWNED_SLOTS // PAGE_BLOCK,), in_specs=[S...  6.99 us
  transfers between devices with their start and end apart: 24, of which 13 were waited for; matrix products, arithmetic and copies ran while one was open for 1% of the time, Pallas kernels for 41%

profile of v14, /device:TPU:0, one launch (start us, length us, event | category | flops | bytes accessed | tf_op | source)
XLA Modules:
  0.0 100.9 jit_solution(365340364895329189)
XLA Ops:
  0.0 1.3 %broadcast_in_dim.3 = s32[8,1,48]{2,1,0:T(1,128)} broadcast(s32[48]{0:T(128)} %request_ref.5), dimensions={2} | broadcast | bytes 1728 | tf_op jit(solution)/shard_map/broadcast_in_dim | solution.py:732
  1.3 7.3 %all-to-all-start = ((s32[8,1,48]{2,1,0:T(1,128)}), s32[8,1,48]{2,1,0:T(1,128)S(1)}, u32[]{:S(2)}, u32[]{:S(2)}) async-start(s32[8,1,48]{2,1,0:T(1,128)} %broadcast_in_dim.3), calls=%async_computation | async-start | bytes 8192 | tf_op jit(solution)/shard_map/all_to_all | solution.py:730
  8.6 0.7 copy-done.3
  9.3 3.7 %queries.1 = (bf16[512,384]{1,0:T(8,128)(2,1)S(1)}, bf16[512,384]{1,0:T(8,128)(2,1)}, bf16[512,1536]{1,0:T(8,128)(2,1)}) custom-call(bf16[4,128,1536]{2,1,0:T(8,128)(2,1)} %tokens_hbm.1, f32[1536]{0:T(1024)S(1)} %copy-done.3, bf16[384,1536]{1,0:T(8,128)(2,1)} %wq_hbm.1), custom_call_target="tpu_custom_call" | custom-call | flops 603979776 | bytes 6291456 | tf_op jit(solution)/shard_map/queries/pallas_call | solution.py:122
  13.0 2.0 %all-to-all-done.ids_ref = s32[8,1,48]{2,1,0:T(1,128)S(1)} async-done(((s32[8,1,48]{2,1,0:T(1,128)}), s32[8,1,48]{2,1,0:T(1,128)S(1)}, u32[]{:S(2)}, u32[]{:S(2)}) %all-to-all-start) | async-done | bytes 1568 | tf_op jit(solution)/shard_map/all_to_all | solution.py:730
  15.1 2.0 %ask.1 = (s32[25]{0:T(128)S(1)}, bf16[24,32,384]{2,1,0:T(8,128)(2,1)}) custom-call(s32[48]{0:T(128)S(1)} %copy-done.4, s32[8,1,48]{2,1,0:T(1,128)S(1)} %all-to-all-done.ids_ref, bf16[512,384]{1,0:T(8,128)(2,1)S(1)} %get-tuple-element.51.q_ref), custom_call_target="tpu_custom_call" | custom-call | tf_op jit(solution)/shard_map/ask/pallas_call | solution.py:159
  17.1 4.0 %all-to-all-start.1 = ((bf16[8,96,384]{2,1,0:T(8,128)(2,1)}), bf16[8,96,384]{2,1,0:T(8,128)(2,1)S(1)}, u32[]{:S(2)}, u32[]{:S(2)}) async-start(bf16[8,96,384]{2,1,0:T(8,128)(2,1)} %bitcast), calls=%async_computation.1 | async-start | bytes 1179648 | tf_op jit(solution)/shard_map/all_to_all | solution.py:730
  21.1 7.0 %own_pages.1 = (f32[512,384]{1,0:T(8,128)}, f32[512,384]{1,0:T(8,128)}, f32[512,384]{1,0:T(8,128)}) custom-call(s32[48]{0:T(128)S(1)} %copy-done.4, s32[48]{0:T(128)S(1)} %copy-done.6, bf16[512,384]{1,0:T(8,128)(2,1)} %get-tuple-element.54.q_ref.q_hbm, bf16[48,384,128]{2,1,0:T(8,128)(2,1)} %keys_ref.3, bf16[48,384,128]{2,1,0:T(8,128)(2,1)} %values_ref.3, ...), custom_call_target="tpu_custom_call" | custom-call | flops 805306368 | bytes 6291456 | tf_op jit(solution)/shard_map/own_pages/pallas_call | solution.py:439
  28.1 1.5 %collective-permute-start = (bf16[384,1536]{1,0:T(8,128)(2,1)S(1)}, bf16[384,1536]{1,0:T(8,128)(2,1)S(1)}, u32[]{:S(2)}, u32[]{:S(2)}) collective-permute-start(bf16[384,1536]{1,0:T(8,128)(2,1)S(1)} %copy-done), channel_id=1, source_target_pairs={{0,2},{1,3},{2,0},{3,1},{4,6},{5,7},{6,4},{7,5},{8,10},{9,11},{10,... | collective-permute-start | bytes 3538952 | tf_op jit(solution)/shard_map/ppermute | solution.py:713
  29.5 6.9 %all-to-all-done.1 = bf16[8,96,384]{2,1,0:T(8,128)(2,1)S(1)} async-done(((bf16[8,96,384]{2,1,0:T(8,128)(2,1)}), bf16[8,96,384]{2,1,0:T(8,128)(2,1)S(1)}, u32[]{:S(2)}, u32[]{:S(2)}) %all-to-all-start.1) | async-done | bytes 589856 | tf_op jit(solution)/shard_map/all_to_all | solution.py:730
  36.4 4.5 %hosted_pages.1 = bf16[8,304,128]{2,1,0:T(8,128)(2,1)} custom-call(s32[48]{0:T(128)S(1)} %copy-done.4, s32[48]{0:T(128)S(1)} %copy-done.6, bf16[24,32,384]{2,1,0:T(8,128)(2,1)S(1)} %bitcast.9, bf16[48,384,128]{2,1,0:T(8,128)(2,1)} %keys_ref.3, bf16[48,384,128]{2,1,0:T(8,128)(2,1)} %values_ref.3, bf16[6,48,128]{2,1,0:T(8,128)(2,1)S(1)} %bitcast.11), custom_call_target="tpu_custom_call" | custom-call | flops 402653184 | bytes 3145728 | tf_op jit(solution)/shard_map/hosted_pages/pallas_call | solution.py:505
  40.9 3.6 %all-to-all-start.2 = ((bf16[8,304,128]{2,1,0:T(8,128)(2,1)}), bf16[8,304,128]{2,1,0:T(8,128)(2,1)S(1)}, u32[]{:S(2)}, u32[]{:S(2)}) async-start(bf16[8,304,128]{2,1,0:T(8,128)(2,1)} %hosted_pages.1), calls=%async_computation.2 | async-start | bytes 1245184 | tf_op jit(solution)/shard_map/all_to_all | solution.py:730
  44.6 8.9 %fresh.1 = (f32[2,16,16,384]{3,2,1,0:T(8,128)}, f32[2,16,16,384]{3,2,1,0:T(8,128)}) custom-call(s32[3,128]{1,0:T(4,128)S(1)} %copy-done.5, f32[1,6]{1,0:T(1,128)S(1)} %bitcast.12, bf16[512,1536]{1,0:T(8,128)(2,1)} %get-tuple-element.65.normed_hbm, bf16[384,1536]{1,0:T(8,128)(2,1)} %wk_hbm.1, bf16[384,1536]{1,0:T(8,128)(2,1)} %wv_hbm.1, ...), custom_call_target="tpu_custom_call" | custom-call | flops 1207959552 | bytes 12582912 | tf_op jit(solution)/shard_map/fresh/pallas_call | solution.py:324
  53.5 1.4 %collective-permute-done.refs_2_ = bf16[384,1536]{1,0:T(8,128)(2,1)S(1)} collective-permute-done((bf16[384,1536]{1,0:T(8,128)(2,1)S(1)}, bf16[384,1536]{1,0:T(8,128)(2,1)S(1)}, u32[]{:S(2)}, u32[]{:S(2)}) %collective-permute-start) | collective-permute-done | bytes 1179680 | tf_op jit(solution)/shard_map/ppermute | solution.py:713
  54.9 6.1 %all-to-all-done.2.back_ref = bf16[8,304,128]{2,1,0:T(8,128)(2,1)S(1)} async-done(((bf16[8,304,128]{2,1,0:T(8,128)(2,1)}), bf16[8,304,128]{2,1,0:T(8,128)(2,1)S(1)}, u32[]{:S(2)}, u32[]{:S(2)}) %all-to-all-start.2) | async-done | bytes 622624 | tf_op jit(solution)/shard_map/all_to_all | solution.py:730
  61.0 2.2 %merge.2 = (bf16[256,384]{1,0:T(8,128)(2,1)S(1)}, bf16[512,1536]{1,0:T(8,128)(2,1)S(1)}) custom-call(s32[25]{0:T(128)S(1)} %get-tuple-element.64.table_ref, bf16[8,304,128]{2,1,0:T(8,128)(2,1)S(1)} %all-to-all-done.2.back_ref, f32[2,256,384]{2,1,0:T(8,128)} %bitcast.14, f32[2,256,384]{2,1,0:T(8,128)} %bitcast.16, bf16[512,1536]{1,0:T(8,128)(2,1)} %bitcast.13), custom_call_target="tpu_custom_call" | custom-call | flops 3932160 | bytes 8388608 | tf_op jit(solution)/shard_map/merge/pallas_call | solution.py:596
  63.3 1.6 %collective-permute-start.2 = (bf16[256,384]{1,0:T(8,128)(2,1)S(1)}, bf16[256,384]{1,0:T(8,128)(2,1)S(1)}, u32[]{:S(2)}, u32[]{:S(2)}) collective-permute-start(bf16[256,384]{1,0:T(8,128)(2,1)S(1)} %get-tuple-element.74.att0), channel_id=1, source_target_pairs={{0,2},{1,3},{2,0},{3,1},{4,6},{5,7},{6,4},{7,5},{8,10},{9,11},{10,... | collective-permute-start | bytes 589832 | tf_op jit(solution)/shard_map/ppermute | solution.py:713
  64.8 5.5 %merge.3 = (bf16[256,384]{1,0:T(8,128)(2,1)S(1)}, bf16[1536,1536]{1,0:T(8,128)(2,1)S(1)}, bf16[1536,1024]{1,0:T(8,128)(2,1)S(1)}, bf16[1536,1024]{1,0:T(8,128)(2,1)S(1)}, bf16[1024,1536]{1,0:T(8,128)(2,1)S(1)}) custom-call(s32[25]{0:T(128)S(1)} %get-tuple-element.64.table_ref, bf16[8,304,128]{2,1,0:T(8,128)(2,1)S(1)} %all-to-all-done.2.back_ref, ...), custom_call_target="tpu_custom_call" | custom-call | flops 3932160 | bytes 8388608 | tf_op jit(solution)/shard_map/merge/pallas_call | solution.py:596
  70.4 0.6 collective-permute-start.5
  72.0 4.4 %block.2 = (f32[128,1536]{1,0:T(8,128)S(1)}, f32[128,1536]{1,0:T(8,128)S(1)}, bf16[128,1536]{1,0:T(8,128)(2,1)S(1)}) custom-call(bf16[256,384]{1,0:T(8,128)(2,1)S(1)} %get-tuple-element.74.att0, bf16[256,384]{1,0:T(8,128)(2,1)S(1)} %collective-permute-done.1.att1, bf16[256,384]{1,0:T(8,128)(2,1)S(1)} %collective-permute-done.2.att2, ...), custom_call_target="tpu_custom_call" | custom-call | tf_op jit(solution)/shard_map/block/pallas_call | solution.py:657
  78.5 1.0 %collective-permute-start.12 = (bf16[48,1536]{1,0:T(8,128)(2,1)S(1)}, bf16[48,1536]{1,0:T(8,128)(2,1)S(1)}, u32[]{:S(2)}, u32[]{:S(2)}) collective-permute-start(bf16[48,1536]{1,0:T(8,128)(2,1)S(1)} %slice.46), channel_id=1, source_target_pairs={{0,2},{1,3},{2,0},{3,1},{4,6},{5,7},{6,4},{7,5},{8,10},{9,11},{10,... | collective-permute-start | bytes 442376 | tf_op jit(solution)/shard_map/ppermute | solution.py:713
  79.6 1.1 %collective-permute-start.14 = (bf16[80,1536]{1,0:T(8,128)(2,1)S(1)}, bf16[80,1536]{1,0:T(8,128)(2,1)S(1)}, u32[]{:S(2)}, u32[]{:S(2)}) collective-permute-start(bf16[80,1536]{1,0:T(8,128)(2,1)S(1)} %slice.47), channel_id=1, source_target_pairs={{0,2},{1,3},{2,0},{3,1},{4,6},{5,7},{6,4},{7,5},{8,10},{9,11},{10,... | collective-permute-start | bytes 737288 | tf_op jit(solution)/shard_map/ppermute | solution.py:713
  80.7 4.4 %block.3 = (f32[128,1536]{1,0:T(8,128)S(1)}, f32[128,1536]{1,0:T(8,128)S(1)}, bf16[128,1536]{1,0:T(8,128)(2,1)S(1)}) custom-call(bf16[256,384]{1,0:T(8,128)(2,1)S(1)} %get-tuple-element.88.att0, bf16[256,384]{1,0:T(8,128)(2,1)S(1)} %collective-permute-done.9.att1, bf16[256,384]{1,0:T(8,128)(2,1)S(1)} %collective-permute-done.10.att2, ...), custom_call_target="tpu_custom_call" | custom-call | tf_op jit(solution)/shard_map/block/pallas_call | solution.py:657
  85.3 0.6 collective-permute-start.13
  85.9 1.1 %collective-permute-done.16 = bf16[128,1536]{1,0:T(8,128)(2,1)S(1)} collective-permute-done((bf16[128,1536]{1,0:T(8,128)(2,1)S(1)}, bf16[128,1536]{1,0:T(8,128)(2,1)S(1)}, u32[]{:S(2)}, u32[]{:S(2)}) %collective-permute-start.16) | collective-permute-done | bytes 393248 | tf_op jit(solution)/shard_map/ppermute | solution.py:709
  87.1 1.0 %collective-permute-start.17 = (bf16[96,1536]{1,0:T(8,128)(2,1)S(1)}, bf16[96,1536]{1,0:T(8,128)(2,1)S(1)}, u32[]{:S(2)}, u32[]{:S(2)}) collective-permute-start(bf16[96,1536]{1,0:T(8,128)(2,1)S(1)} %slice.48), channel_id=1, source_target_pairs={{0,2},{1,3},{2,0},{3,1},{4,6},{5,7},{6,4},{7,5},{8,10},{9,11},{10,... | collective-permute-start | bytes 884744 | tf_op jit(solution)/shard_map/ppermute | solution.py:713
  88.1 1.8 %collective-permute-done.14 = bf16[80,1536]{1,0:T(8,128)(2,1)S(1)} collective-permute-done((bf16[80,1536]{1,0:T(8,128)(2,1)S(1)}, bf16[80,1536]{1,0:T(8,128)(2,1)S(1)}, u32[]{:S(2)}, u32[]{:S(2)}) %collective-permute-start.14) | collective-permute-done | bytes 245792 | tf_op jit(solution)/shard_map/ppermute | solution.py:713
  90.1 0.8 collective-permute-start.19
  91.0 6.1 %collective-permute-done.17 = bf16[96,1536]{1,0:T(8,128)(2,1)S(1)} collective-permute-done((bf16[96,1536]{1,0:T(8,128)(2,1)S(1)}, bf16[96,1536]{1,0:T(8,128)(2,1)S(1)}, u32[]{:S(2)}, u32[]{:S(2)}) %collective-permute-start.17) | collective-permute-done | bytes 294944 | tf_op jit(solution)/shard_map/ppermute | solution.py:713
  97.2 1.2 %collective-permute-done.19 = bf16[32,1536]{1,0:T(8,128)(2,1)S(1)} collective-permute-done((bf16[32,1536]{1,0:T(8,128)(2,1)S(1)}, bf16[32,1536]{1,0:T(8,128)(2,1)S(1)}, u32[]{:S(2)}, u32[]{:S(2)}) %collective-permute-start.19) | collective-permute-done | bytes 98336 | tf_op jit(solution)/shard_map/ppermute | solution.py:713
  98.5 0.9 finish.2.refs_0_
  99.8 0.9 finish.3
  (56 shorter events, 4.3 us)
Async XLA Ops:
  0.0 15.1 %copy-start.4 = (s32[48]{0:T(128)S(1)}, s32[48]{0:T(128)}, u32[]{:S(2)}) copy-start(s32[48]{0:T(128)} %request_ref.5) | copy-start | bytes 580
  1.3 13.7 %all-to-all-start = ((s32[8,1,48]{2,1,0:T(1,128)}), s32[8,1,48]{2,1,0:T(1,128)S(1)}, u32[]{:S(2)}, u32[]{:S(2)}) async-start(s32[8,1,48]{2,1,0:T(1,128)} %broadcast_in_dim.3), calls=%async_computation | async-start | bytes 8192 | tf_op jit(solution)/shard_map/all_to_all | solution.py:730
  8.6 0.7 copy-start.3
  9.3 11.7 %copy-start.1 = (bf16[48,6,128]{2,0,1:T(8,128)(2,1)S(1)}, bf16[48,6,128]{2,0,1:T(8,128)(2,1)}, u32[]{:S(2)}) copy-start(bf16[48,6,128]{2,0,1:T(8,128)(2,1)} %param.24) | copy-start | bytes 221188
  9.3 11.7 %copy-start.6 = (s32[48]{0:T(128)S(1)}, s32[48]{0:T(128)}, u32[]{:S(2)}) copy-start(s32[48]{0:T(128)} %fill_ref.3) | copy-start | bytes 580
  17.1 19.4 %all-to-all-start.1 = ((bf16[8,96,384]{2,1,0:T(8,128)(2,1)}), bf16[8,96,384]{2,1,0:T(8,128)(2,1)S(1)}, u32[]{:S(2)}, u32[]{:S(2)}) async-start(bf16[8,96,384]{2,1,0:T(8,128)(2,1)} %bitcast), calls=%async_computation.1 | async-start | bytes 1179648 | tf_op jit(solution)/shard_map/all_to_all | solution.py:730
  21.0 7.0 %copy-start = (bf16[384,1536]{1,0:T(8,128)(2,1)S(1)}, bf16[384,1536]{1,0:T(8,128)(2,1)}, u32[]{:S(2)}) copy-start(bf16[384,1536]{1,0:T(8,128)(2,1)} %refs_0_.1) | copy-start | bytes 3538948
  28.1 26.9 %collective-permute-start = (bf16[384,1536]{1,0:T(8,128)(2,1)S(1)}, bf16[384,1536]{1,0:T(8,128)(2,1)S(1)}, u32[]{:S(2)}, u32[]{:S(2)}) collective-permute-start(bf16[384,1536]{1,0:T(8,128)(2,1)S(1)} %copy-done), channel_id=1, source_target_pairs={{0,2},{1,3},{2,0},{3,1},{4,6},{5,7},{6,4},{7,5},{8,10},{9,11},{10,... | collective-permute-start | bytes 3538952 | tf_op jit(solution)/shard_map/ppermute | solution.py:713
  29.5 35.3 %collective-permute-start.3 = (bf16[384,1536]{1,0:T(8,128)(2,1)S(1)}, bf16[384,1536]{1,0:T(8,128)(2,1)}, u32[]{:S(2)}, u32[]{:S(2)}) collective-permute-start(bf16[384,1536]{1,0:T(8,128)(2,1)S(1)} %copy-done), channel_id=1, source_target_pairs={{0,1},{1,0},{2,3},{3,2},{4,5},{5,4},{6,7},{7,6},{8,9},{9,8},{10,11... | collective-permute-start | bytes 3538952 | tf_op jit(solution)/shard_map/ppermute | solution.py:709
  36.4 8.2 %copy-start.5 = (s32[3,128]{1,0:T(4,128)S(1)}, s32[3,128]{1,0:T(4,128)}, u32[]{:S(2)}) copy-start(s32[3,128]{1,0:T(4,128)} %parents_ref.1) | copy-start | bytes 4612
  36.4 8.2 %copy-start.7 = (f32[6]{0:T(128)S(1)}, f32[6]{0:T(128)}, u32[]{:S(2)}) copy-start(f32[6]{0:T(128)} %param.30) | copy-start | bytes 76
  40.9 20.1 %all-to-all-start.2 = ((bf16[8,304,128]{2,1,0:T(8,128)(2,1)}), bf16[8,304,128]{2,1,0:T(8,128)(2,1)S(1)}, u32[]{:S(2)}, u32[]{:S(2)}) async-start(bf16[8,304,128]{2,1,0:T(8,128)(2,1)} %hosted_pages.1), calls=%async_computation.2 | async-start | bytes 1245184 | tf_op jit(solution)/shard_map/all_to_all | solution.py:730
  54.9 9.9 %collective-permute-start.4 = (bf16[384,1536]{1,0:T(8,128)(2,1)S(1)}, bf16[384,1536]{1,0:T(8,128)(2,1)}, u32[]{:S(2)}, u32[]{:S(2)}) collective-permute-start(bf16[384,1536]{1,0:T(8,128)(2,1)S(1)} %collective-permute-done.refs_2_), channel_id=1, source_target_pairs={{0,1},{1,0},{2,3},{3,2},{4,5},{5,4},{6,7},{7,6},{8,9},{9,8},{10,11... | collective-permute-start | bytes 3538952 | tf_op jit(solution)/shard_map/ppermute | solution.py:709
  63.3 8.8 %copy-start.2 = (f32[1536]{0:T(1024)S(1)}, f32[1536]{0:T(1024)}, u32[]{:S(2)}) copy-start(f32[1536]{0:T(1024)} %gain_ref.5) | copy-start | bytes 18436
  63.3 7.1 %collective-permute-start.2 = (bf16[256,384]{1,0:T(8,128)(2,1)S(1)}, bf16[256,384]{1,0:T(8,128)(2,1)S(1)}, u32[]{:S(2)}, u32[]{:S(2)}) collective-permute-start(bf16[256,384]{1,0:T(8,128)(2,1)S(1)} %get-tuple-element.74.att0), channel_id=1, source_target_pairs={{0,2},{1,3},{2,0},{3,1},{4,6},{5,7},{6,4},{7,5},{8,10},{9,11},{10,... | collective-permute-start | bytes 589832 | tf_op jit(solution)/shard_map/ppermute | solution.py:713
  64.8 6.7 %collective-permute-start.1 = (bf16[256,384]{1,0:T(8,128)(2,1)S(1)}, bf16[256,384]{1,0:T(8,128)(2,1)S(1)}, u32[]{:S(2)}, u32[]{:S(2)}) collective-permute-start(bf16[256,384]{1,0:T(8,128)(2,1)S(1)} %get-tuple-element.74.att0), channel_id=1, source_target_pairs={{0,1},{1,0},{2,3},{3,2},{4,5},{5,4},{6,7},{7,6},{8,9},{9,8},{10,11... | collective-permute-start | bytes 589832 | tf_op jit(solution)/shard_map/ppermute | solution.py:709
  70.4 1.6 %collective-permute-start.5 = (bf16[256,384]{1,0:T(8,128)(2,1)S(1)}, bf16[256,384]{1,0:T(8,128)(2,1)S(1)}, u32[]{:S(2)}, u32[]{:S(2)}) collective-permute-start(bf16[256,384]{1,0:T(8,128)(2,1)S(1)} %collective-permute-done.2.att2), channel_id=1, source_target_pairs={{0,1},{1,0},{2,3},{3,2},{4,5},{5,4},{6,7},{7,6},{8,9},{9,8},{10,11... | collective-permute-start | bytes 589832 | tf_op jit(solution)/shard_map/ppermute | solution.py:709
  71.0 6.9 %collective-permute-start.10 = (bf16[256,384]{1,0:T(8,128)(2,1)S(1)}, bf16[256,384]{1,0:T(8,128)(2,1)S(1)}, u32[]{:S(2)}, u32[]{:S(2)}) collective-permute-start(bf16[256,384]{1,0:T(8,128)(2,1)S(1)} %get-tuple-element.88.att0), channel_id=1, source_target_pairs={{0,2},{1,3},{2,0},{3,1},{4,6},{5,7},{6,4},{7,5},{8,10},{9,11},{10,... | collective-permute-start | bytes 589832 | tf_op jit(solution)/shard_map/ppermute | solution.py:713
  76.4 2.0 %collective-permute-start.6 = (bf16[48,1536]{1,0:T(8,128)(2,1)S(1)}, bf16[48,1536]{1,0:T(8,128)(2,1)S(1)}, u32[]{:S(2)}, u32[]{:S(2)}) collective-permute-start(bf16[48,1536]{1,0:T(8,128)(2,1)S(1)} %get-tuple-element.97), channel_id=1, source_target_pairs={{0,1},{1,0},{2,3},{3,2},{4,5},{5,4},{6,7},{7,6},{8,9},{9,8},{10,11... | collective-permute-start | bytes 442376 | tf_op jit(solution)/shard_map/ppermute | solution.py:709
  76.9 1.5 %collective-permute-start.7 = (bf16[48,1536]{1,0:T(8,128)(2,1)S(1)}, bf16[48,1536]{1,0:T(8,128)(2,1)S(1)}, u32[]{:S(2)}, u32[]{:S(2)}) collective-permute-start(bf16[48,1536]{1,0:T(8,128)(2,1)S(1)} %get-tuple-element.98), channel_id=1, source_target_pairs={{0,1},{1,0},{2,3},{3,2},{4,5},{5,4},{6,7},{7,6},{8,9},{9,8},{10,11... | collective-permute-start | bytes 442376 | tf_op jit(solution)/shard_map/ppermute | solution.py:709
  77.0 1.4 %collective-permute-start.8 = (bf16[32,1536]{1,0:T(8,128)(2,1)S(1)}, bf16[32,1536]{1,0:T(8,128)(2,1)S(1)}, u32[]{:S(2)}, u32[]{:S(2)}) collective-permute-start(bf16[32,1536]{1,0:T(8,128)(2,1)S(1)} %slice.38), channel_id=1, source_target_pairs={{0,1},{1,0},{2,3},{3,2},{4,5},{5,4},{6,7},{7,6},{8,9},{9,8},{10,11... | collective-permute-start | bytes 294920 | tf_op jit(solution)/shard_map/ppermute | solution.py:709
  77.5 3.3 %collective-permute-start.9 = (bf16[256,384]{1,0:T(8,128)(2,1)S(1)}, bf16[256,384]{1,0:T(8,128)(2,1)S(1)}, u32[]{:S(2)}, u32[]{:S(2)}) collective-permute-start(bf16[256,384]{1,0:T(8,128)(2,1)S(1)} %get-tuple-element.88.att0), channel_id=1, source_target_pairs={{0,1},{1,0},{2,3},{3,2},{4,5},{5,4},{6,7},{7,6},{8,9},{9,8},{10,11... | collective-permute-start | bytes 589832 | tf_op jit(solution)/shard_map/ppermute | solution.py:709
  77.8 2.9 %collective-permute-start.11 = (bf16[256,384]{1,0:T(8,128)(2,1)S(1)}, bf16[256,384]{1,0:T(8,128)(2,1)S(1)}, u32[]{:S(2)}, u32[]{:S(2)}) collective-permute-start(bf16[256,384]{1,0:T(8,128)(2,1)S(1)} %collective-permute-done.10.att2), channel_id=1, source_target_pairs={{0,1},{1,0},{2,3},{3,2},{4,5},{5,4},{6,7},{7,6},{8,9},{9,8},{10,11... | collective-permute-start | bytes 589832 | tf_op jit(solution)/shard_map/ppermute | solution.py:709
  78.5 6.7 %collective-permute-start.12 = (bf16[48,1536]{1,0:T(8,128)(2,1)S(1)}, bf16[48,1536]{1,0:T(8,128)(2,1)S(1)}, u32[]{:S(2)}, u32[]{:S(2)}) collective-permute-start(bf16[48,1536]{1,0:T(8,128)(2,1)S(1)} %slice.46), channel_id=1, source_target_pairs={{0,2},{1,3},{2,0},{3,1},{4,6},{5,7},{6,4},{7,5},{8,10},{9,11},{10,... | collective-permute-start | bytes 442376 | tf_op jit(solution)/shard_map/ppermute | solution.py:713
  79.6 10.4 %collective-permute-start.14 = (bf16[80,1536]{1,0:T(8,128)(2,1)S(1)}, bf16[80,1536]{1,0:T(8,128)(2,1)S(1)}, u32[]{:S(2)}, u32[]{:S(2)}) collective-permute-start(bf16[80,1536]{1,0:T(8,128)(2,1)S(1)} %slice.47), channel_id=1, source_target_pairs={{0,2},{1,3},{2,0},{3,1},{4,6},{5,7},{6,4},{7,5},{8,10},{9,11},{10,... | collective-permute-start | bytes 737288 | tf_op jit(solution)/shard_map/ppermute | solution.py:713
  85.3 1.7 %collective-permute-start.16 = (bf16[128,1536]{1,0:T(8,128)(2,1)S(1)}, bf16[128,1536]{1,0:T(8,128)(2,1)S(1)}, u32[]{:S(2)}, u32[]{:S(2)}) collective-permute-start(bf16[128,1536]{1,0:T(8,128)(2,1)S(1)} %get-tuple-element.96), channel_id=1, source_target_pairs={{0,1},{1,0},{2,3},{3,2},{4,5},{5,4},{6,7},{7,6},{8,9},{9,8},{10,11... | collective-permute-start | bytes 1179656 | tf_op jit(solution)/shard_map/ppermute | solution.py:709
  85.3 13.2 %collective-permute-start.13 = (bf16[48,1536]{1,0:T(8,128)(2,1)S(1)}, bf16[48,1536]{1,0:T(8,128)(2,1)S(1)}, u32[]{:S(2)}, u32[]{:S(2)}) collective-permute-start(bf16[48,1536]{1,0:T(8,128)(2,1)S(1)} %add_convert_fusion.4.refs_0_), channel_id=1, source_target_pairs={{0,1},{1,0},{2,3},{3,2},{4,5},{5,4},{6,7},{7,6},{8,9},{9,8},{10,11... | collective-permute-start | bytes 442376 | tf_op jit(solution)/shard_map/ppermute | solution.py:709
  87.1 9.9 %collective-permute-start.17 = (bf16[96,1536]{1,0:T(8,128)(2,1)S(1)}, bf16[96,1536]{1,0:T(8,128)(2,1)S(1)}, u32[]{:S(2)}, u32[]{:S(2)}) collective-permute-start(bf16[96,1536]{1,0:T(8,128)(2,1)S(1)} %slice.48), channel_id=1, source_target_pairs={{0,2},{1,3},{2,0},{3,1},{4,6},{5,7},{6,4},{7,5},{8,10},{9,11},{10,... | collective-permute-start | bytes 884744 | tf_op jit(solution)/shard_map/ppermute | solution.py:713
  90.0 8.5 %collective-permute-start.15 = (bf16[80,1536]{1,0:T(8,128)(2,1)S(1)}, bf16[80,1536]{1,0:T(8,128)(2,1)S(1)}, u32[]{:S(2)}, u32[]{:S(2)}) collective-permute-start(bf16[80,1536]{1,0:T(8,128)(2,1)S(1)} %add_convert_fusion.3.refs_2_), channel_id=1, source_target_pairs={{0,1},{1,0},{2,3},{3,2},{4,5},{5,4},{6,7},{7,6},{8,9},{9,8},{10,11... | collective-permute-start | bytes 737288 | tf_op jit(solution)/shard_map/ppermute | solution.py:709
  90.1 8.3 %collective-permute-start.19 = (bf16[32,1536]{1,0:T(8,128)(2,1)S(1)}, bf16[32,1536]{1,0:T(8,128)(2,1)S(1)}, u32[]{:S(2)}, u32[]{:S(2)}) collective-permute-start(bf16[32,1536]{1,0:T(8,128)(2,1)S(1)} %slice.49), channel_id=1, source_target_pairs={{0,2},{1,3},{2,0},{3,1},{4,6},{5,7},{6,4},{7,5},{8,10},{9,11},{10,... | collective-permute-start | bytes 294920 | tf_op jit(solution)/shard_map/ppermute | solution.py:713
  97.1 2.7 %collective-permute-start.18 = (bf16[96,1536]{1,0:T(8,128)(2,1)S(1)}, bf16[96,1536]{1,0:T(8,128)(2,1)S(1)}, u32[]{:S(2)}, u32[]{:S(2)}) collective-permute-start(bf16[96,1536]{1,0:T(8,128)(2,1)S(1)} %add_convert_fusion.2.refs_1_), channel_id=1, source_target_pairs={{0,1},{1,0},{2,3},{3,2},{4,5},{5,4},{6,7},{7,6},{8,9},{9,8},{10,11... | collective-permute-start | bytes 884744 | tf_op jit(solution)/shard_map/ppermute | solution.py:709
  98.4 1.4 %collective-permute-start.20 = (bf16[32,1536]{1,0:T(8,128)(2,1)S(1)}, bf16[32,1536]{1,0:T(8,128)(2,1)S(1)}, u32[]{:S(2)}, u32[]{:S(2)}) collective-permute-start(bf16[32,1536]{1,0:T(8,128)(2,1)S(1)} %add_convert_fusion.5.refs_3_), channel_id=1, source_target_pairs={{0,1},{1,0},{2,3},{3,2},{4,5},{5,4},{6,7},{7,6},{8,9},{9,8},{10,11... | collective-permute-start | bytes 294920 | tf_op jit(solution)/shard_map/ppermute | solution.py:709

commit v15 on v14

--- a/solution.py
+++ b/solution.py
@@ -750,11 +750,11 @@
     flat = tokens.reshape(steps * rows, width)
     each = steps // PARTS
     sums = (table, back, logs, averages, each, capacity)
-    here, flat = merge(0, *sums, [flat])
+    here, flat, w_down = merge(0, *sums, [flat, w_down])
     heres = [here]
     back, heres[0] = lax.optimization_barrier((back, heres[0]))
     sums = (table, back, logs, averages, each, capacity)
-    here, weight, w_gate, w_up, w_down = merge(1, *sums, mixes + [w_gate, w_up, w_down])
+    here, weight, w_gate, w_up = merge(1, *sums, mixes + [w_gate, w_up])
     heres.append(here)
     fars = [swap_chip(here) for here in heres]
     fars[0], heres[1] = lax.optimization_barrier((fars[0], heres[1]))

time: 101 us -> 101 us (level)
  no operation moved by 1% of the time
where the time goes in v15:
time: 101 us
  Pallas kernels  44.7 us (44%)
  waiting for transfers between devices  28.1 us (28%)
  starting transfers between devices  25.2 us (25%)
  local copies, waits for them, and re-layouts  2.13 us (2%)
    all_to_all x3, waiting for transfers between devices, exchange(): lax.all_to_all(value, 'group', split_axis=0, concat_axis=0, tiled=True)  15 us
    all_to_all x3, starting transfers between devices, exchange(): lax.all_to_all(value, 'group', split_axis=0, concat_axis=0, tiled=True)  14.9 us
    ppermute x7, waiting for transfers between devices, swap_chip(): return lax.ppermute(value, 'head', [(i, i ^ 2) for i in range(4)])  10.7 us
    pallas_call x1, Pallas kernels, fresh(): pl.pallas_call(fresh_kernel, in_specs=[vmem, vmem] + [hbm] * len(big), ou...  8.94 us
    pallas_call x2, Pallas kernels, block(): pl.pallas_call(functools.partial(block_kernel, first), in_specs=[vmem] *...  8.89 us
    pallas_call x2, Pallas kernels, merge(): pl.pallas_call(functools.partial(merge_kernel, capacity, steps, part, inn...  7.82 us
    ppermute x7, starting transfers between devices, swap_chip(): return lax.ppermute(value, 'head', [(i, i ^ 2) for i in range(4)])  7.58 us
    pallas_call x1, Pallas kernels, own_pages(): pl.pallas_call(own_kernel, grid=(OWNED_SLOTS // PAGE_BLOCK,), in_specs=[S...  6.99 us
  transfers between devices with their start and end apart: 24, of which 13 were waited for; matrix products, arithmetic and copies ran while one was open for 1% of the time, Pallas kernels for 41%

profile of v15, /device:TPU:0, one launch (start us, length us, event | category | flops | bytes accessed | tf_op | source)
XLA Modules:
  0.0 101.0 jit_solution(1842049802276466667)
XLA Ops:
  0.0 1.3 %broadcast_in_dim.3 = s32[8,1,48]{2,1,0:T(1,128)} broadcast(s32[48]{0:T(128)} %request_ref.5), dimensions={2} | broadcast | bytes 1728 | tf_op jit(solution)/shard_map/broadcast_in_dim | solution.py:732
  1.3 7.3 %all-to-all-start = ((s32[8,1,48]{2,1,0:T(1,128)}), s32[8,1,48]{2,1,0:T(1,128)S(1)}, u32[]{:S(2)}, u32[]{:S(2)}) async-start(s32[8,1,48]{2,1,0:T(1,128)} %broadcast_in_dim.3), calls=%async_computation | async-start | bytes 8192 | tf_op jit(solution)/shard_map/all_to_all | solution.py:730
  8.6 0.7 copy-done.3
  9.3 3.7 %queries.1 = (bf16[512,384]{1,0:T(8,128)(2,1)S(1)}, bf16[512,384]{1,0:T(8,128)(2,1)}, bf16[512,1536]{1,0:T(8,128)(2,1)}) custom-call(bf16[4,128,1536]{2,1,0:T(8,128)(2,1)} %tokens_hbm.1, f32[1536]{0:T(1024)S(1)} %copy-done.3, bf16[384,1536]{1,0:T(8,128)(2,1)} %wq_hbm.1), custom_call_target="tpu_custom_call" | custom-call | flops 603979776 | bytes 6291456 | tf_op jit(solution)/shard_map/queries/pallas_call | solution.py:122
  13.0 2.0 %all-to-all-done.ids_ref = s32[8,1,48]{2,1,0:T(1,128)S(1)} async-done(((s32[8,1,48]{2,1,0:T(1,128)}), s32[8,1,48]{2,1,0:T(1,128)S(1)}, u32[]{:S(2)}, u32[]{:S(2)}) %all-to-all-start) | async-done | bytes 1568 | tf_op jit(solution)/shard_map/all_to_all | solution.py:730
  15.1 2.0 %ask.1 = (s32[25]{0:T(128)S(1)}, bf16[24,32,384]{2,1,0:T(8,128)(2,1)}) custom-call(s32[48]{0:T(128)S(1)} %copy-done.4, s32[8,1,48]{2,1,0:T(1,128)S(1)} %all-to-all-done.ids_ref, bf16[512,384]{1,0:T(8,128)(2,1)S(1)} %get-tuple-element.51.q_ref), custom_call_target="tpu_custom_call" | custom-call | tf_op jit(solution)/shard_map/ask/pallas_call | solution.py:159
  17.1 4.0 %all-to-all-start.1 = ((bf16[8,96,384]{2,1,0:T(8,128)(2,1)}), bf16[8,96,384]{2,1,0:T(8,128)(2,1)S(1)}, u32[]{:S(2)}, u32[]{:S(2)}) async-start(bf16[8,96,384]{2,1,0:T(8,128)(2,1)} %bitcast), calls=%async_computation.1 | async-start | bytes 1179648 | tf_op jit(solution)/shard_map/all_to_all | solution.py:730
  21.1 7.0 %own_pages.1 = (f32[512,384]{1,0:T(8,128)}, f32[512,384]{1,0:T(8,128)}, f32[512,384]{1,0:T(8,128)}) custom-call(s32[48]{0:T(128)S(1)} %copy-done.4, s32[48]{0:T(128)S(1)} %copy-done.6, bf16[512,384]{1,0:T(8,128)(2,1)} %get-tuple-element.54.q_ref.q_hbm, bf16[48,384,128]{2,1,0:T(8,128)(2,1)} %keys_ref.3, bf16[48,384,128]{2,1,0:T(8,128)(2,1)} %values_ref.3, ...), custom_call_target="tpu_custom_call" | custom-call | flops 805306368 | bytes 6291456 | tf_op jit(solution)/shard_map/own_pages/pallas_call | solution.py:439
  28.1 1.5 %collective-permute-start = (bf16[384,1536]{1,0:T(8,128)(2,1)S(1)}, bf16[384,1536]{1,0:T(8,128)(2,1)S(1)}, u32[]{:S(2)}, u32[]{:S(2)}) collective-permute-start(bf16[384,1536]{1,0:T(8,128)(2,1)S(1)} %copy-done), channel_id=1, source_target_pairs={{0,2},{1,3},{2,0},{3,1},{4,6},{5,7},{6,4},{7,5},{8,10},{9,11},{10,... | collective-permute-start | bytes 3538952 | tf_op jit(solution)/shard_map/ppermute | solution.py:713
  29.6 6.9 %all-to-all-done.1 = bf16[8,96,384]{2,1,0:T(8,128)(2,1)S(1)} async-done(((bf16[8,96,384]{2,1,0:T(8,128)(2,1)}), bf16[8,96,384]{2,1,0:T(8,128)(2,1)S(1)}, u32[]{:S(2)}, u32[]{:S(2)}) %all-to-all-start.1) | async-done | bytes 589856 | tf_op jit(solution)/shard_map/all_to_all | solution.py:730
  36.4 4.5 %hosted_pages.1 = bf16[8,304,128]{2,1,0:T(8,128)(2,1)} custom-call(s32[48]{0:T(128)S(1)} %copy-done.4, s32[48]{0:T(128)S(1)} %copy-done.6, bf16[24,32,384]{2,1,0:T(8,128)(2,1)S(1)} %bitcast.9, bf16[48,384,128]{2,1,0:T(8,128)(2,1)} %keys_ref.3, bf16[48,384,128]{2,1,0:T(8,128)(2,1)} %values_ref.3, bf16[6,48,128]{2,1,0:T(8,128)(2,1)S(1)} %bitcast.11), custom_call_target="tpu_custom_call" | custom-call | flops 402653184 | bytes 3145728 | tf_op jit(solution)/shard_map/hosted_pages/pallas_call | solution.py:505
  40.9 3.6 %all-to-all-start.2 = ((bf16[8,304,128]{2,1,0:T(8,128)(2,1)}), bf16[8,304,128]{2,1,0:T(8,128)(2,1)S(1)}, u32[]{:S(2)}, u32[]{:S(2)}) async-start(bf16[8,304,128]{2,1,0:T(8,128)(2,1)} %hosted_pages.1), calls=%async_computation.2 | async-start | bytes 1245184 | tf_op jit(solution)/shard_map/all_to_all | solution.py:730
  44.6 8.9 %fresh.1 = (f32[2,16,16,384]{3,2,1,0:T(8,128)}, f32[2,16,16,384]{3,2,1,0:T(8,128)}) custom-call(s32[3,128]{1,0:T(4,128)S(1)} %copy-done.5, f32[1,6]{1,0:T(1,128)S(1)} %bitcast.12, bf16[512,1536]{1,0:T(8,128)(2,1)} %get-tuple-element.65.normed_hbm, bf16[384,1536]{1,0:T(8,128)(2,1)} %wk_hbm.1, bf16[384,1536]{1,0:T(8,128)(2,1)} %wv_hbm.1, ...), custom_call_target="tpu_custom_call" | custom-call | flops 1207959552 | bytes 12582912 | tf_op jit(solution)/shard_map/fresh/pallas_call | solution.py:324
  53.5 1.4 %collective-permute-done.refs_2_ = bf16[384,1536]{1,0:T(8,128)(2,1)S(1)} collective-permute-done((bf16[384,1536]{1,0:T(8,128)(2,1)S(1)}, bf16[384,1536]{1,0:T(8,128)(2,1)S(1)}, u32[]{:S(2)}, u32[]{:S(2)}) %collective-permute-start) | collective-permute-done | bytes 1179680 | tf_op jit(solution)/shard_map/ppermute | solution.py:713
  54.9 6.1 %all-to-all-done.2.back_ref = bf16[8,304,128]{2,1,0:T(8,128)(2,1)S(1)} async-done(((bf16[8,304,128]{2,1,0:T(8,128)(2,1)}), bf16[8,304,128]{2,1,0:T(8,128)(2,1)S(1)}, u32[]{:S(2)}, u32[]{:S(2)}) %all-to-all-start.2) | async-done | bytes 622624 | tf_op jit(solution)/shard_map/all_to_all | solution.py:730
  61.0 3.2 %merge.2 = (bf16[256,384]{1,0:T(8,128)(2,1)S(1)}, bf16[512,1536]{1,0:T(8,128)(2,1)S(1)}, bf16[1024,1536]{1,0:T(8,128)(2,1)S(1)}) custom-call(s32[25]{0:T(128)S(1)} %get-tuple-element.64.table_ref, bf16[8,304,128]{2,1,0:T(8,128)(2,1)S(1)} %all-to-all-done.2.back_ref, f32[2,256,384]{2,1,0:T(8,128)} %bitcast.14, f32[2,256,384]{2,1,0:T(8,128)} %bitcast.16, ...), custom_call_target="tpu_custom_call" | custom-call | flops 3932160 | bytes 8388608 | tf_op jit(solution)/shard_map/merge/pallas_call | solution.py:596
  64.3 1.6 %collective-permute-start.2 = (bf16[256,384]{1,0:T(8,128)(2,1)S(1)}, bf16[256,384]{1,0:T(8,128)(2,1)S(1)}, u32[]{:S(2)}, u32[]{:S(2)}) collective-permute-start(bf16[256,384]{1,0:T(8,128)(2,1)S(1)} %get-tuple-element.74.att0), channel_id=1, source_target_pairs={{0,2},{1,3},{2,0},{3,1},{4,6},{5,7},{6,4},{7,5},{8,10},{9,11},{10,... | collective-permute-start | bytes 589832 | tf_op jit(solution)/shard_map/ppermute | solution.py:713
  65.8 4.6 %merge.3 = (bf16[256,384]{1,0:T(8,128)(2,1)S(1)}, bf16[1536,1536]{1,0:T(8,128)(2,1)S(1)}, bf16[1536,1024]{1,0:T(8,128)(2,1)S(1)}, bf16[1536,1024]{1,0:T(8,128)(2,1)S(1)}) custom-call(s32[25]{0:T(128)S(1)} %get-tuple-element.64.table_ref, bf16[8,304,128]{2,1,0:T(8,128)(2,1)S(1)} %all-to-all-done.2.back_ref, f32[2,256,384]{2,1,0:T(8,128)} %bitcast.15, ...), custom_call_target="tpu_custom_call" | custom-call | flops 3932160 | bytes 8388608 | tf_op jit(solution)/shard_map/merge/pallas_call | solution.py:596
  70.4 0.6 collective-permute-start.5
  72.1 4.4 %block.2 = (f32[128,1536]{1,0:T(8,128)S(1)}, f32[128,1536]{1,0:T(8,128)S(1)}, bf16[128,1536]{1,0:T(8,128)(2,1)S(1)}) custom-call(bf16[256,384]{1,0:T(8,128)(2,1)S(1)} %get-tuple-element.74.att0, bf16[256,384]{1,0:T(8,128)(2,1)S(1)} %collective-permute-done.1.att1, bf16[256,384]{1,0:T(8,128)(2,1)S(1)} %collective-permute-done.2.att2, ...), custom_call_target="tpu_custom_call" | custom-call | tf_op jit(solution)/shard_map/block/pallas_call | solution.py:657
  78.6 1.0 %collective-permute-start.12 = (bf16[48,1536]{1,0:T(8,128)(2,1)S(1)}, bf16[48,1536]{1,0:T(8,128)(2,1)S(1)}, u32[]{:S(2)}, u32[]{:S(2)}) collective-permute-start(bf16[48,1536]{1,0:T(8,128)(2,1)S(1)} %slice.46), channel_id=1, source_target_pairs={{0,2},{1,3},{2,0},{3,1},{4,6},{5,7},{6,4},{7,5},{8,10},{9,11},{10,... | collective-permute-start | bytes 442376 | tf_op jit(solution)/shard_map/ppermute | solution.py:713
  79.7 1.2 %collective-permute-start.14 = (bf16[80,1536]{1,0:T(8,128)(2,1)S(1)}, bf16[80,1536]{1,0:T(8,128)(2,1)S(1)}, u32[]{:S(2)}, u32[]{:S(2)}) collective-permute-start(bf16[80,1536]{1,0:T(8,128)(2,1)S(1)} %slice.47), channel_id=1, source_target_pairs={{0,2},{1,3},{2,0},{3,1},{4,6},{5,7},{6,4},{7,5},{8,10},{9,11},{10,... | collective-permute-start | bytes 737288 | tf_op jit(solution)/shard_map/ppermute | solution.py:713
  80.8 4.5 %block.3 = (f32[128,1536]{1,0:T(8,128)S(1)}, f32[128,1536]{1,0:T(8,128)S(1)}, bf16[128,1536]{1,0:T(8,128)(2,1)S(1)}) custom-call(bf16[256,384]{1,0:T(8,128)(2,1)S(1)} %get-tuple-element.88.att0, bf16[256,384]{1,0:T(8,128)(2,1)S(1)} %collective-permute-done.9.att1, bf16[256,384]{1,0:T(8,128)(2,1)S(1)} %collective-permute-done.10.att2, ...), custom_call_target="tpu_custom_call" | custom-call | tf_op jit(solution)/shard_map/block/pallas_call | solution.py:657
  85.5 0.6 collective-permute-start.13
  86.0 1.1 %collective-permute-done.16 = bf16[128,1536]{1,0:T(8,128)(2,1)S(1)} collective-permute-done((bf16[128,1536]{1,0:T(8,128)(2,1)S(1)}, bf16[128,1536]{1,0:T(8,128)(2,1)S(1)}, u32[]{:S(2)}, u32[]{:S(2)}) %collective-permute-start.16) | collective-permute-done | bytes 393248 | tf_op jit(solution)/shard_map/ppermute | solution.py:709
  87.2 1.0 %collective-permute-start.17 = (bf16[96,1536]{1,0:T(8,128)(2,1)S(1)}, bf16[96,1536]{1,0:T(8,128)(2,1)S(1)}, u32[]{:S(2)}, u32[]{:S(2)}) collective-permute-start(bf16[96,1536]{1,0:T(8,128)(2,1)S(1)} %slice.48), channel_id=1, source_target_pairs={{0,2},{1,3},{2,0},{3,1},{4,6},{5,7},{6,4},{7,5},{8,10},{9,11},{10,... | collective-permute-start | bytes 884744 | tf_op jit(solution)/shard_map/ppermute | solution.py:713
  88.3 1.8 %collective-permute-done.14 = bf16[80,1536]{1,0:T(8,128)(2,1)S(1)} collective-permute-done((bf16[80,1536]{1,0:T(8,128)(2,1)S(1)}, bf16[80,1536]{1,0:T(8,128)(2,1)S(1)}, u32[]{:S(2)}, u32[]{:S(2)}) %collective-permute-start.14) | collective-permute-done | bytes 245792 | tf_op jit(solution)/shard_map/ppermute | solution.py:713
  90.3 0.8 collective-permute-start.19
  91.1 6.1 %collective-permute-done.17 = bf16[96,1536]{1,0:T(8,128)(2,1)S(1)} collective-permute-done((bf16[96,1536]{1,0:T(8,128)(2,1)S(1)}, bf16[96,1536]{1,0:T(8,128)(2,1)S(1)}, u32[]{:S(2)}, u32[]{:S(2)}) %collective-permute-start.17) | collective-permute-done | bytes 294944 | tf_op jit(solution)/shard_map/ppermute | solution.py:713
  97.3 1.2 %collective-permute-done.19 = bf16[32,1536]{1,0:T(8,128)(2,1)S(1)} collective-permute-done((bf16[32,1536]{1,0:T(8,128)(2,1)S(1)}, bf16[32,1536]{1,0:T(8,128)(2,1)S(1)}, u32[]{:S(2)}, u32[]{:S(2)}) %collective-permute-start.19) | collective-permute-done | bytes 98336 | tf_op jit(solution)/shard_map/ppermute | solution.py:713
  98.7 0.9 finish.2.refs_0_
  99.9 0.9 finish.3
  (56 shorter events, 4.3 us)
Async XLA Ops:
  0.0 15.1 %copy-start.4 = (s32[48]{0:T(128)S(1)}, s32[48]{0:T(128)}, u32[]{:S(2)}) copy-start(s32[48]{0:T(128)} %request_ref.5) | copy-start | bytes 580
  1.3 13.7 %all-to-all-start = ((s32[8,1,48]{2,1,0:T(1,128)}), s32[8,1,48]{2,1,0:T(1,128)S(1)}, u32[]{:S(2)}, u32[]{:S(2)}) async-start(s32[8,1,48]{2,1,0:T(1,128)} %broadcast_in_dim.3), calls=%async_computation | async-start | bytes 8192 | tf_op jit(solution)/shard_map/all_to_all | solution.py:730
  8.6 0.7 copy-start.3
  9.3 11.7 %copy-start.1 = (bf16[48,6,128]{2,0,1:T(8,128)(2,1)S(1)}, bf16[48,6,128]{2,0,1:T(8,128)(2,1)}, u32[]{:S(2)}) copy-start(bf16[48,6,128]{2,0,1:T(8,128)(2,1)} %param.24) | copy-start | bytes 221188
  9.3 11.7 %copy-start.6 = (s32[48]{0:T(128)S(1)}, s32[48]{0:T(128)}, u32[]{:S(2)}) copy-start(s32[48]{0:T(128)} %fill_ref.3) | copy-start | bytes 580
  17.1 19.4 %all-to-all-start.1 = ((bf16[8,96,384]{2,1,0:T(8,128)(2,1)}), bf16[8,96,384]{2,1,0:T(8,128)(2,1)S(1)}, u32[]{:S(2)}, u32[]{:S(2)}) async-start(bf16[8,96,384]{2,1,0:T(8,128)(2,1)} %bitcast), calls=%async_computation.1 | async-start | bytes 1179648 | tf_op jit(solution)/shard_map/all_to_all | solution.py:730
  21.0 7.0 %copy-start = (bf16[384,1536]{1,0:T(8,128)(2,1)S(1)}, bf16[384,1536]{1,0:T(8,128)(2,1)}, u32[]{:S(2)}) copy-start(bf16[384,1536]{1,0:T(8,128)(2,1)} %refs_0_.1) | copy-start | bytes 3538948
  28.1 26.9 %collective-permute-start = (bf16[384,1536]{1,0:T(8,128)(2,1)S(1)}, bf16[384,1536]{1,0:T(8,128)(2,1)S(1)}, u32[]{:S(2)}, u32[]{:S(2)}) collective-permute-start(bf16[384,1536]{1,0:T(8,128)(2,1)S(1)} %copy-done), channel_id=1, source_target_pairs={{0,2},{1,3},{2,0},{3,1},{4,6},{5,7},{6,4},{7,5},{8,10},{9,11},{10,... | collective-permute-start | bytes 3538952 | tf_op jit(solution)/shard_map/ppermute | solution.py:713
  29.5 36.3 %collective-permute-start.3 = (bf16[384,1536]{1,0:T(8,128)(2,1)S(1)}, bf16[384,1536]{1,0:T(8,128)(2,1)}, u32[]{:S(2)}, u32[]{:S(2)}) collective-permute-start(bf16[384,1536]{1,0:T(8,128)(2,1)S(1)} %copy-done), channel_id=1, source_target_pairs={{0,1},{1,0},{2,3},{3,2},{4,5},{5,4},{6,7},{7,6},{8,9},{9,8},{10,11... | collective-permute-start | bytes 3538952 | tf_op jit(solution)/shard_map/ppermute | solution.py:709
  36.4 8.2 %copy-start.5 = (s32[3,128]{1,0:T(4,128)S(1)}, s32[3,128]{1,0:T(4,128)}, u32[]{:S(2)}) copy-start(s32[3,128]{1,0:T(4,128)} %parents_ref.1) | copy-start | bytes 4612
  36.4 8.2 %copy-start.7 = (f32[6]{0:T(128)S(1)}, f32[6]{0:T(128)}, u32[]{:S(2)}) copy-start(f32[6]{0:T(128)} %param.30) | copy-start | bytes 76
  40.9 20.1 %all-to-all-start.2 = ((bf16[8,304,128]{2,1,0:T(8,128)(2,1)}), bf16[8,304,128]{2,1,0:T(8,128)(2,1)S(1)}, u32[]{:S(2)}, u32[]{:S(2)}) async-start(bf16[8,304,128]{2,1,0:T(8,128)(2,1)} %hosted_pages.1), calls=%async_computation.2 | async-start | bytes 1245184 | tf_op jit(solution)/shard_map/all_to_all | solution.py:730
  54.9 10.9 %collective-permute-start.4 = (bf16[384,1536]{1,0:T(8,128)(2,1)S(1)}, bf16[384,1536]{1,0:T(8,128)(2,1)}, u32[]{:S(2)}, u32[]{:S(2)}) collective-permute-start(bf16[384,1536]{1,0:T(8,128)(2,1)S(1)} %collective-permute-done.refs_2_), channel_id=1, source_target_pairs={{0,1},{1,0},{2,3},{3,2},{4,5},{5,4},{6,7},{7,6},{8,9},{9,8},{10,11... | collective-permute-start | bytes 3538952 | tf_op jit(solution)/shard_map/ppermute | solution.py:709
  64.2 7.9 %copy-start.2 = (f32[1536]{0:T(1024)S(1)}, f32[1536]{0:T(1024)}, u32[]{:S(2)}) copy-start(f32[1536]{0:T(1024)} %gain_ref.5) | copy-start | bytes 18436
  64.3 6.2 %collective-permute-start.2 = (bf16[256,384]{1,0:T(8,128)(2,1)S(1)}, bf16[256,384]{1,0:T(8,128)(2,1)S(1)}, u32[]{:S(2)}, u32[]{:S(2)}) collective-permute-start(bf16[256,384]{1,0:T(8,128)(2,1)S(1)} %get-tuple-element.74.att0), channel_id=1, source_target_pairs={{0,2},{1,3},{2,0},{3,1},{4,6},{5,7},{6,4},{7,5},{8,10},{9,11},{10,... | collective-permute-start | bytes 589832 | tf_op jit(solution)/shard_map/ppermute | solution.py:713
  65.8 5.8 %collective-permute-start.1 = (bf16[256,384]{1,0:T(8,128)(2,1)S(1)}, bf16[256,384]{1,0:T(8,128)(2,1)S(1)}, u32[]{:S(2)}, u32[]{:S(2)}) collective-permute-start(bf16[256,384]{1,0:T(8,128)(2,1)S(1)} %get-tuple-element.74.att0), channel_id=1, source_target_pairs={{0,1},{1,0},{2,3},{3,2},{4,5},{5,4},{6,7},{7,6},{8,9},{9,8},{10,11... | collective-permute-start | bytes 589832 | tf_op jit(solution)/shard_map/ppermute | solution.py:709
  70.4 1.6 %collective-permute-start.5 = (bf16[256,384]{1,0:T(8,128)(2,1)S(1)}, bf16[256,384]{1,0:T(8,128)(2,1)S(1)}, u32[]{:S(2)}, u32[]{:S(2)}) collective-permute-start(bf16[256,384]{1,0:T(8,128)(2,1)S(1)} %collective-permute-done.2.att2), channel_id=1, source_target_pairs={{0,1},{1,0},{2,3},{3,2},{4,5},{5,4},{6,7},{7,6},{8,9},{9,8},{10,11... | collective-permute-start | bytes 589832 | tf_op jit(solution)/shard_map/ppermute | solution.py:709
  71.0 6.9 %collective-permute-start.10 = (bf16[256,384]{1,0:T(8,128)(2,1)S(1)}, bf16[256,384]{1,0:T(8,128)(2,1)S(1)}, u32[]{:S(2)}, u32[]{:S(2)}) collective-permute-start(bf16[256,384]{1,0:T(8,128)(2,1)S(1)} %get-tuple-element.88.att0), channel_id=1, source_target_pairs={{0,2},{1,3},{2,0},{3,1},{4,6},{5,7},{6,4},{7,5},{8,10},{9,11},{10,... | collective-permute-start | bytes 589832 | tf_op jit(solution)/shard_map/ppermute | solution.py:713
  76.6 2.0 %collective-permute-start.6 = (bf16[48,1536]{1,0:T(8,128)(2,1)S(1)}, bf16[48,1536]{1,0:T(8,128)(2,1)S(1)}, u32[]{:S(2)}, u32[]{:S(2)}) collective-permute-start(bf16[48,1536]{1,0:T(8,128)(2,1)S(1)} %get-tuple-element.97), channel_id=1, source_target_pairs={{0,1},{1,0},{2,3},{3,2},{4,5},{5,4},{6,7},{7,6},{8,9},{9,8},{10,11... | collective-permute-start | bytes 442376 | tf_op jit(solution)/shard_map/ppermute | solution.py:709
  77.0 1.5 %collective-permute-start.7 = (bf16[48,1536]{1,0:T(8,128)(2,1)S(1)}, bf16[48,1536]{1,0:T(8,128)(2,1)S(1)}, u32[]{:S(2)}, u32[]{:S(2)}) collective-permute-start(bf16[48,1536]{1,0:T(8,128)(2,1)S(1)} %get-tuple-element.98), channel_id=1, source_target_pairs={{0,1},{1,0},{2,3},{3,2},{4,5},{5,4},{6,7},{7,6},{8,9},{9,8},{10,11... | collective-permute-start | bytes 442376 | tf_op jit(solution)/shard_map/ppermute | solution.py:709
  77.2 1.4 %collective-permute-start.8 = (bf16[32,1536]{1,0:T(8,128)(2,1)S(1)}, bf16[32,1536]{1,0:T(8,128)(2,1)S(1)}, u32[]{:S(2)}, u32[]{:S(2)}) collective-permute-start(bf16[32,1536]{1,0:T(8,128)(2,1)S(1)} %slice.38), channel_id=1, source_target_pairs={{0,1},{1,0},{2,3},{3,2},{4,5},{5,4},{6,7},{7,6},{8,9},{9,8},{10,11... | collective-permute-start | bytes 294920 | tf_op jit(solution)/shard_map/ppermute | solution.py:709
  77.6 3.3 %collective-permute-start.9 = (bf16[256,384]{1,0:T(8,128)(2,1)S(1)}, bf16[256,384]{1,0:T(8,128)(2,1)S(1)}, u32[]{:S(2)}, u32[]{:S(2)}) collective-permute-start(bf16[256,384]{1,0:T(8,128)(2,1)S(1)} %get-tuple-element.88.att0), channel_id=1, source_target_pairs={{0,1},{1,0},{2,3},{3,2},{4,5},{5,4},{6,7},{7,6},{8,9},{9,8},{10,11... | collective-permute-start | bytes 589832 | tf_op jit(solution)/shard_map/ppermute | solution.py:709
  77.9 2.9 %collective-permute-start.11 = (bf16[256,384]{1,0:T(8,128)(2,1)S(1)}, bf16[256,384]{1,0:T(8,128)(2,1)S(1)}, u32[]{:S(2)}, u32[]{:S(2)}) collective-permute-start(bf16[256,384]{1,0:T(8,128)(2,1)S(1)} %collective-permute-done.10.att2), channel_id=1, source_target_pairs={{0,1},{1,0},{2,3},{3,2},{4,5},{5,4},{6,7},{7,6},{8,9},{9,8},{10,11... | collective-permute-start | bytes 589832 | tf_op jit(solution)/shard_map/ppermute | solution.py:709
  78.6 6.7 %collective-permute-start.12 = (bf16[48,1536]{1,0:T(8,128)(2,1)S(1)}, bf16[48,1536]{1,0:T(8,128)(2,1)S(1)}, u32[]{:S(2)}, u32[]{:S(2)}) collective-permute-start(bf16[48,1536]{1,0:T(8,128)(2,1)S(1)} %slice.46), channel_id=1, source_target_pairs={{0,2},{1,3},{2,0},{3,1},{4,6},{5,7},{6,4},{7,5},{8,10},{9,11},{10,... | collective-permute-start | bytes 442376 | tf_op jit(solution)/shard_map/ppermute | solution.py:713
  79.7 10.4 %collective-permute-start.14 = (bf16[80,1536]{1,0:T(8,128)(2,1)S(1)}, bf16[80,1536]{1,0:T(8,128)(2,1)S(1)}, u32[]{:S(2)}, u32[]{:S(2)}) collective-permute-start(bf16[80,1536]{1,0:T(8,128)(2,1)S(1)} %slice.47), channel_id=1, source_target_pairs={{0,2},{1,3},{2,0},{3,1},{4,6},{5,7},{6,4},{7,5},{8,10},{9,11},{10,... | collective-permute-start | bytes 737288 | tf_op jit(solution)/shard_map/ppermute | solution.py:713
  85.4 1.7 %collective-permute-start.16 = (bf16[128,1536]{1,0:T(8,128)(2,1)S(1)}, bf16[128,1536]{1,0:T(8,128)(2,1)S(1)}, u32[]{:S(2)}, u32[]{:S(2)}) collective-permute-start(bf16[128,1536]{1,0:T(8,128)(2,1)S(1)} %get-tuple-element.96), channel_id=1, source_target_pairs={{0,1},{1,0},{2,3},{3,2},{4,5},{5,4},{6,7},{7,6},{8,9},{9,8},{10,11... | collective-permute-start | bytes 1179656 | tf_op jit(solution)/shard_map/ppermute | solution.py:709
  85.5 13.2 %collective-permute-start.13 = (bf16[48,1536]{1,0:T(8,128)(2,1)S(1)}, bf16[48,1536]{1,0:T(8,128)(2,1)S(1)}, u32[]{:S(2)}, u32[]{:S(2)}) collective-permute-start(bf16[48,1536]{1,0:T(8,128)(2,1)S(1)} %add_convert_fusion.4.refs_0_), channel_id=1, source_target_pairs={{0,1},{1,0},{2,3},{3,2},{4,5},{5,4},{6,7},{7,6},{8,9},{9,8},{10,11... | collective-permute-start | bytes 442376 | tf_op jit(solution)/shard_map/ppermute | solution.py:709
  87.2 9.9 %collective-permute-start.17 = (bf16[96,1536]{1,0:T(8,128)(2,1)S(1)}, bf16[96,1536]{1,0:T(8,128)(2,1)S(1)}, u32[]{:S(2)}, u32[]{:S(2)}) collective-permute-start(bf16[96,1536]{1,0:T(8,128)(2,1)S(1)} %slice.48), channel_id=1, source_target_pairs={{0,2},{1,3},{2,0},{3,1},{4,6},{5,7},{6,4},{7,5},{8,10},{9,11},{10,... | collective-permute-start | bytes 884744 | tf_op jit(solution)/shard_map/ppermute | solution.py:713
  90.2 8.5 %collective-permute-start.15 = (bf16[80,1536]{1,0:T(8,128)(2,1)S(1)}, bf16[80,1536]{1,0:T(8,128)(2,1)S(1)}, u32[]{:S(2)}, u32[]{:S(2)}) collective-permute-start(bf16[80,1536]{1,0:T(8,128)(2,1)S(1)} %add_convert_fusion.3.refs_2_), channel_id=1, source_target_pairs={{0,1},{1,0},{2,3},{3,2},{4,5},{5,4},{6,7},{7,6},{8,9},{9,8},{10,11... | collective-permute-start | bytes 737288 | tf_op jit(solution)/shard_map/ppermute | solution.py:709
  90.3 8.2 %collective-permute-start.19 = (bf16[32,1536]{1,0:T(8,128)(2,1)S(1)}, bf16[32,1536]{1,0:T(8,128)(2,1)S(1)}, u32[]{:S(2)}, u32[]{:S(2)}) collective-permute-start(bf16[32,1536]{1,0:T(8,128)(2,1)S(1)} %slice.49), channel_id=1, source_target_pairs={{0,2},{1,3},{2,0},{3,1},{4,6},{5,7},{6,4},{7,5},{8,10},{9,11},{10,... | collective-permute-start | bytes 294920 | tf_op jit(solution)/shard_map/ppermute | solution.py:713
  97.3 2.7 %collective-permute-start.18 = (bf16[96,1536]{1,0:T(8,128)(2,1)S(1)}, bf16[96,1536]{1,0:T(8,128)(2,1)S(1)}, u32[]{:S(2)}, u32[]{:S(2)}) collective-permute-start(bf16[96,1536]{1,0:T(8,128)(2,1)S(1)} %add_convert_fusion.2.refs_1_), channel_id=1, source_target_pairs={{0,1},{1,0},{2,3},{3,2},{4,5},{5,4},{6,7},{7,6},{8,9},{9,8},{10,11... | collective-permute-start | bytes 884744 | tf_op jit(solution)/shard_map/ppermute | solution.py:709
  98.6 1.4 %collective-permute-start.20 = (bf16[32,1536]{1,0:T(8,128)(2,1)S(1)}, bf16[32,1536]{1,0:T(8,128)(2,1)S(1)}, u32[]{:S(2)}, u32[]{:S(2)}) collective-permute-start(bf16[32,1536]{1,0:T(8,128)(2,1)S(1)} %add_convert_fusion.5.refs_3_), channel_id=1, source_target_pairs={{0,1},{1,0},{2,3},{3,2},{4,5},{5,4},{6,7},{7,6},{8,9},{9,8},{10,11... | collective-permute-start | bytes 294920 | tf_op jit(solution)/shard_map/ppermute | solution.py:709
